TPU v7x, 128 devices: a whole 4x4x4 slice. The times are simulated.
128 devices in a mesh: lat: 8 (over x, core), lon: 16 (over y, z).
Axes of the slice: x: 4, y: 4, z: 4, core: 2. Of those that a mesh axis runs over, the one named last changes fastest.
Arguments:
- spectrum: float32 [36, 2, 256, 4096], P(None, None, 'lat', 'lon'), may hold values from 0.05 to 2
- speed_factor: float32 [256, 4096], P('lat', 'lon'), may hold values from 0.3 to 1
- land_sea_mask: int32 [256, 4096], P('lat', 'lon'), may hold values 0 or 1
- courant: float32 [2], replicated, may hold values from 0.25 to 0.65
- depth_kernel: float32 [64, 72], replicated, may hold values from -0.75 to 0.75
- send_rows: int32 [128, 128, 128], P(('lat', 'lon')), may hold values from -1 to 8191, as said below
- recv_rows: int32 [128, 128, 128], P(('lat', 'lon')), may hold values from -1 to 4095, as said below
Outputs:
- propagated: float32 [36, 2, 256, 4096], P(None, None, 'lat', 'lon')
- stokes_tiles: float32 [64, 524288], P(None, ('lat', 'lon'))
Inputs may be any that keep to these rules, and one draw needn't show every extreme that they name: Slots 0 to n - 1 of send_rows[s, o] hold the listed local cells (repeats allowed) and the rest -1, with n at most 128; in every draw some owner receives a full list of 128 from every source. recv_rows[o, s, k] is -1 exactly where send_rows[s, o, k] is -1.
All inputs are finite; a program needn't handle non-finite values. No bound on the sum of `land_sea_mask` on one device may be relied on, other than what follows from the above.
Results may differ from a plain program's by a relative error of at most 0.002.
Values may be sent and summed in bfloat16 or wider, within the bound.
No kernel may reach another device: no remote copies, remote signals or barrier semaphores. Data moves between devices by JAX's collectives and lax.ppermute only.
A program may use at most 64 MiB of HBM per device.

v0:
```python
import math

import jax
import jax.numpy as jnp
from jax import lax
from jax.sharding import PartitionSpec as P

DIRS = 36
FREQ = 2
OUT_DEV = 4096


def partner_2(value, axis, apart):
    mask = 2**apart
    pairs = [(source, source ^ mask) for source in range(lax.axis_size(axis))]
    return lax.ppermute(value, axis, pairs)


def padded(shard, sides, width, wrap):
    for axis, dim in sides:
        size, length = (lax.axis_size(axis), shard.shape[dim])
        up = [(i, (i + 1) % size) for i in range(size if wrap else size - 1)]
        down = [(j, i) for i, j in up]
        last = lax.slice_in_dim(shard, length - width, length, axis=dim)
        leading = lax.slice_in_dim(shard, 0, width, axis=dim)
        before = lax.ppermute(last, axis, up)
        after = lax.ppermute(leading, axis, down)
        shard = jnp.concatenate([before, shard, after], axis=dim)
    return shard


def shift_dirs(planes_in):
    return jnp.roll(planes_in, DIRS // 2 * FREQ, axis=0)


def fold_rows(border):
    moved = border
    for bit_index in range(lax.axis_size("lon").bit_length() - 1):
        moved = partner_2(moved.astype(jnp.bfloat16), "lon", bit_index).astype(moved.dtype)
    return moved


def margins(source, margin):
    height = source.shape[1]
    plane_count = DIRS * FREQ
    lon_wide = padded(source, (("lon", 2),), margin, True)
    partner = fold_rows(lon_wide[:, height - margin :, :])
    mirror = partner[:, ::-1, ::-1]
    folded = jnp.concatenate([shift_dirs(mirror), mirror[plane_count:]], axis=0)
    entire = padded(lon_wide, (("lat", 1),), margin, False)
    at_top = lax.axis_index("lat") == lax.axis_size("lat") - 1
    north_rim = jnp.where(at_top, folded, entire[:, height + margin :, :])
    return jnp.concatenate([entire[:, : height + margin, :], north_rim], axis=1)


def divergence(extended, courant_x, courant_y):
    centre = extended[:, 1:-1, 1:-1]
    east_plus = jnp.maximum(courant_x, 0.0)[:, None, None]
    east_minus = jnp.minimum(courant_x, 0.0)[:, None, None]
    north_plus = jnp.maximum(courant_y, 0.0)[:, None, None]
    north_minus = jnp.minimum(courant_y, 0.0)[:, None, None]
    flux_east = east_plus * (centre - extended[:, 1:-1, :-2]) + east_minus * (
        extended[:, 1:-1, 2:] - centre
    )
    flux_north = north_plus * (centre - extended[:, :-2, 1:-1]) + north_minus * (
        extended[:, 2:, 1:-1] - centre
    )
    return (flux_east, flux_north)


def body(spectrum, speed_factor, land_sea_mask, courant, depth_kernel, send_rows, recv_rows):
    height, breadth = speed_factor.shape
    plane_count = DIRS * FREQ
    planes = spectrum.reshape(plane_count, height, breadth)
    sea_mask = land_sea_mask.astype(jnp.float32)
    moving = speed_factor * sea_mask
    heading = (jnp.arange(DIRS, dtype=jnp.float32) + 0.5) * (2.0 * math.pi / DIRS)
    courant_x = (jnp.cos(heading)[:, None] * courant[None, :]).reshape(-1)
    courant_y = (jnp.sin(heading)[:, None] * courant[None, :]).reshape(-1)
    for substep in range(2):
        extended = margins(moving * planes, 1)
        flux_east, flux_north = divergence(extended, courant_x, courant_y)
        planes = sea_mask * (planes - flux_east - flux_north)
    flattened = planes.reshape(plane_count, height * breadth)
    profiles = lax.dot_general(
        flattened,
        depth_kernel,
        (((0,), (1,)), ((), ())),
        precision=lax.Precision.HIGHEST,
        preferred_element_type=jnp.float32,
    ).astype(jnp.bfloat16)
    owner_lists = send_rows[0]
    device_count = owner_lists.shape[0]
    slot_count = owner_lists.shape[1]
    components = profiles.shape[1]
    picked = jnp.take(profiles, jnp.maximum(owner_lists, 0).reshape(-1), axis=0).reshape(
        device_count, slot_count, components
    )
    received = lax.all_to_all(picked, ("lat", "lon"), split_axis=0, concat_axis=0, tiled=True)
    row_lists = recv_rows[0]
    group = math.gcd(device_count, max(1, 2048 // slot_count))
    block_count = device_count // group
    block_rows = group * slot_count
    value_blocks = received.reshape(block_count, block_rows, components)
    target_blocks = row_lists.reshape(block_count, block_rows)
    columns = jnp.arange(OUT_DEV, dtype=jnp.int32)[None, :]

    def accumulate(total, block):
        values, targets = block
        selector = (targets[:, None] == columns).astype(jnp.bfloat16)
        term = lax.dot_general(
            values, selector, (((0,), (0,)), ((), ())), preferred_element_type=jnp.float32
        )
        return (total + term, None)

    empty = jnp.zeros((components, OUT_DEV), jnp.float32)
    stokes_tiles, unused = lax.scan(accumulate, empty, (value_blocks, target_blocks))
    return (planes.reshape(DIRS, FREQ, height, breadth), stokes_tiles)


def solution(mesh):
    placed = (
        P(None, None, "lat", "lon"),
        P("lat", "lon"),
        P("lat", "lon"),
        P(),
        P(),
        P(("lat", "lon"), None, None),
        P(("lat", "lon"), None, None),
    )
    return jax.shard_map(
        body,
        mesh=mesh,
        in_specs=placed,
        out_specs=(P(None, None, "lat", "lon"), P(None, ("lat", "lon"))),
        check_vma=False,
    )
```

profile of v0, /device:TPU:1, one launch (start us, length us, event | category | flops | bytes accessed | tf_op | source)
XLA Modules:
  0.0 279.4 jit_solution(6396655326584890401)
XLA Ops:
  1.4 1.9 bitcast_multiply_fusion
  3.3 1.8 fusion.40
  5.1 1.9 copy.17
  7.0 2.5 collective-permute-start
  9.5 1.9 copy.19
  11.4 4.6 %collective-permute-start.1 = (f32[72,32,1]{0,1,2:T(8,128)S(1)}, f32[72,32,1]{0,1,2:T(8,128)S(1)}, u32[]{:S(2)}, u32[]{:S(2)}) collective-permute-start(f32[72,32,1]{0,1,2:T(8,128)S(1)} %copy.19), channel_id=1, source_target_pairs={{1,0},{2,1},{3,2},{4,3},{5,4},{6,5},{7,6},{8,7},{9,8},{10,9},{11,1... | collective-permute-start | bytes 27656 | tf_op jit(solution)/shard_map/ppermute | solution.py:27
  16.0 1.9 copy.18
  18.0 2.0 copy.20
  19.9 1.9 fusion.38
  21.9 3.6 %collective-permute-done.3 = bf16[72,1,258]{2,1,0:T(2,128)(2,1)S(1)} collective-permute-done((bf16[72,1,258]{2,1,0:T(2,128)(2,1)S(1)}, bf16[72,1,258]{2,1,0:T(2,128)(2,1)S(1)}, u32[]{:S(2)}, u32[]{:S(2)}) %collective-permute-start.3) | collective-permute-done | bytes 37184 | tf_op jit(solution)/shard_map/ppermute | solution.py:16
  25.5 5.1 %collective-permute-done.4 = bf16[72,1,258]{2,1,0:T(2,128)(2,1)S(1)} collective-permute-done((bf16[72,1,258]{2,1,0:T(2,128)(2,1)S(1)}, bf16[72,1,258]{2,1,0:T(2,128)(2,1)S(1)}, u32[]{:S(2)}, u32[]{:S(2)}) %collective-permute-start.4) | collective-permute-done | bytes 37184 | tf_op jit(solution)/shard_map/ppermute | solution.py:16
  30.7 3.5 %collective-permute-done.5 = bf16[72,1,258]{2,1,0:T(2,128)(2,1)S(1)} collective-permute-done((bf16[72,1,258]{2,1,0:T(2,128)(2,1)S(1)}, bf16[72,1,258]{2,1,0:T(2,128)(2,1)S(1)}, u32[]{:S(2)}, u32[]{:S(2)}) %collective-permute-start.5) | collective-permute-done | bytes 37184 | tf_op jit(solution)/shard_map/ppermute | solution.py:16
  34.2 1.8 collective-permute-start.6
  36.6 6.7 %collective-permute-start.7 = (f32[72,1,258]{2,1,0:T(1,128)S(1)}, f32[72,1,258]{2,1,0:T(1,128)S(1)}, u32[]{:S(2)}, u32[]{:S(2)}) collective-permute-start(f32[72,1,258]{2,1,0:T(1,128)S(1)} %get-tuple-element.68), channel_id=1, source_target_pairs={{16,0},{32,16},{48,32},{64,48},{80,64},{96,80},{112,96},{17,1},{33... | collective-permute-start | bytes 222920 | tf_op jit(solution)/shard_map/ppermute | solution.py:27
  43.3 3.0 %collective-permute-start.2 = (f32[72,1,258]{2,1,0:T(1,128)S(1)}, f32[72,1,258]{2,1,0:T(1,128)S(1)}, u32[]{:S(2)}, u32[]{:S(2)}) collective-permute-start(f32[72,1,258]{2,1,0:T(1,128)S(1)} %get-tuple-element.66), channel_id=1, source_target_pairs={{0,16},{16,32},{32,48},{48,64},{64,80},{80,96},{96,112},{1,17},{17... | collective-permute-start | bytes 222920 | tf_op jit(solution)/shard_map/ppermute | solution.py:26
  48.3 7.2 %broadcast_multiply_fusion = (f32[72,32,256]{2,1,0:T(8,128)S(1)}, f32[72,32,256]{2,1,0:T(8,128)}) fusion(f32[32,256]{1,0:T(8,128)S(1)} %convert_multiply_fusion, f32[72,32,256]{2,1,0:T(8,128)S(1)} %bitcast_multiply_fusion, f32[72,1,258]{2,1,0:T(1,128)S(1)} %broadcast_select_fusion.2, f32[72,32,1]{2,1,0:T(8,128)} %copy.20, f32[72,32,1]{2,1,0:T(8,128)} %copy.18, ...), kind=kLoop, calls=%fused_computation.55 | loop fusion | flops 12976128 | bytes 9670912 | tf_op jit(solution)/shard_map/mul | solution.py:81
  55.5 2.1 fusion.39
  57.6 2.0 copy.23
  59.7 1.7 collective-permute-start.8
  61.4 1.9 copy.25
  63.3 3.5 %collective-permute-start.9 = (f32[72,32,1]{0,1,2:T(8,128)S(1)}, f32[72,32,1]{0,1,2:T(8,128)S(1)}, u32[]{:S(2)}, u32[]{:S(2)}) collective-permute-start(f32[72,32,1]{0,1,2:T(8,128)S(1)} %copy.25), channel_id=1, source_target_pairs={{1,0},{2,1},{3,2},{4,3},{5,4},{6,5},{7,6},{8,7},{9,8},{10,9},{11,1... | collective-permute-start | bytes 27656 | tf_op jit(solution)/shard_map/ppermute | solution.py:27
  66.8 1.9 copy.24
  68.7 1.9 copy.26
  70.7 1.9 fusion.36
  72.7 4.8 %collective-permute-done.11 = bf16[72,1,258]{2,1,0:T(2,128)(2,1)S(1)} collective-permute-done((bf16[72,1,258]{2,1,0:T(2,128)(2,1)S(1)}, bf16[72,1,258]{2,1,0:T(2,128)(2,1)S(1)}, u32[]{:S(2)}, u32[]{:S(2)}) %collective-permute-start.11) | collective-permute-done | bytes 37184 | tf_op jit(solution)/shard_map/ppermute | solution.py:16
  78.9 4.1 %collective-permute-done.12 = bf16[72,1,258]{2,1,0:T(2,128)(2,1)S(1)} collective-permute-done((bf16[72,1,258]{2,1,0:T(2,128)(2,1)S(1)}, bf16[72,1,258]{2,1,0:T(2,128)(2,1)S(1)}, u32[]{:S(2)}, u32[]{:S(2)}) %collective-permute-start.12) | collective-permute-done | bytes 37184 | tf_op jit(solution)/shard_map/ppermute | solution.py:16
  83.0 3.6 %collective-permute-done.13 = bf16[72,1,258]{2,1,0:T(2,128)(2,1)S(1)} collective-permute-done((bf16[72,1,258]{2,1,0:T(2,128)(2,1)S(1)}, bf16[72,1,258]{2,1,0:T(2,128)(2,1)S(1)}, u32[]{:S(2)}, u32[]{:S(2)}) %collective-permute-start.13) | collective-permute-done | bytes 37184 | tf_op jit(solution)/shard_map/ppermute | solution.py:16
  86.6 1.6 collective-permute-start.14
  88.2 4.7 %collective-permute-start.15 = (f32[72,1,258]{2,1,0:T(1,128)S(1)}, f32[72,1,258]{2,1,0:T(1,128)S(1)}, u32[]{:S(2)}, u32[]{:S(2)}) collective-permute-start(f32[72,1,258]{2,1,0:T(1,128)S(1)} %get-tuple-element.67), channel_id=1, source_target_pairs={{16,0},{32,16},{48,32},{64,48},{80,64},{96,80},{112,96},{17,1},{33... | collective-permute-start | bytes 222920 | tf_op jit(solution)/shard_map/ppermute | solution.py:27
  93.0 3.5 %collective-permute-start.10 = (f32[72,1,258]{2,1,0:T(1,128)S(1)}, f32[72,1,258]{2,1,0:T(1,128)S(1)}, u32[]{:S(2)}, u32[]{:S(2)}) collective-permute-start(f32[72,1,258]{2,1,0:T(1,128)S(1)} %get-tuple-element.62), channel_id=1, source_target_pairs={{0,16},{16,32},{32,48},{48,64},{64,80},{80,96},{96,112},{1,17},{17... | collective-permute-start | bytes 222920 | tf_op jit(solution)/shard_map/ppermute | solution.py:26
  98.5 6.1 %fusion.12 = f32[72,32,256]{2,1,0:T(8,128)S(1)} fusion(f32[72,32,256]{2,1,0:T(8,128)S(1)} %copy-done.2, f32[72,1,258]{2,1,0:T(1,128)S(1)} %broadcast_select_fusion.1, f32[72,32,1]{2,1,0:T(8,128)} %copy.26, f32[72,32,1]{2,1,0:T(8,128)} %copy.24, f32[72,1,258]{2,1,0:T(1,128)S(1)} %collective-permute-done.10, f32[72,32,256]{2,1,0:T(8,128)} %get-tuple-element.64, ...), kind=kLoop, calls=%fused_computation.16 | loop fusion | flops 12386304 | bytes 7278848 | tf_op jit(solution)/shard_map/mul | solution.py:83
  104.6 1.4 copy.35
  106.0 2.1 convolution_convert_fusion
  109.2 57.8 %gather_fusion = bf16[16384,64]{1,0:T(8,128)(2,1)} fusion(bf16[8192,64]{1,0:T(8,128)(2,1)S(1)} %copy.29, s32[16384]{0:T(1024)S(1)} %bitcast_clamp_fusion), kind=kCustom, calls=%fused_computation | custom fusion | bytes 4259840 | tf_op jit(solution)/shard_map/jit(_take)/gather | solution.py:96
  167.0 3.7 %copy.30 = bf16[128,128,64]{1,2,0:T(8,128)(2,1)S(1)} copy(bf16[128,128,64]{2,1,0:T(8,128)(2,1)} %bitcast.27) | data formatting | bytes 4194304 | tf_op jit(solution)/shard_map/jit(_take)/gather | solution.py:96
  170.7 1.6 broadcast_select_fusion
  172.3 10.0 %all-to-all-start = ((bf16[128,128,64]{1,2,0:T(8,128)(2,1)}), bf16[128,128,64]{1,2,0:T(8,128)(2,1)S(1)}, u32[]{:S(2)}, u32[]{:S(2)}) async-start(bf16[128,128,64]{1,2,0:T(8,128)(2,1)} %broadcast_select_fusion), calls=%async_computation | async-start | bytes 4194304 | tf_op jit(solution)/shard_map/all_to_all | solution.py:99
  182.4 29.4 %all-to-all-done = bf16[128,128,64]{1,2,0:T(8,128)(2,1)S(1)} async-done(((bf16[128,128,64]{1,2,0:T(8,128)(2,1)}), bf16[128,128,64]{1,2,0:T(8,128)(2,1)S(1)}, u32[]{:S(2)}, u32[]{:S(2)}) %all-to-all-start) | async-done | bytes 2097184 | tf_op jit(solution)/shard_map/all_to_all | solution.py:99
  211.8 3.1 %copy.33 = bf16[128,128,64]{2,1,0:T(8,128)(2,1)} copy(bf16[128,128,64]{1,2,0:T(8,128)(2,1)S(1)} %all-to-all-done) | data formatting | bytes 4194304
  214.9 63.5 %while.11 = (s32[]{:T(128)}, f32[64,4096]{1,0:T(8,128)S(1)}, bf16[8,2048,64]{2,1,0:T(8,128)(2,1)}, s32[8,2048]{1,0:T(8,128)S(1)}, s32[]{:T(128)}, /*index=5*/s32[]{:T(128)}) while((s32[]{:T(128)}, f32[64,4096]{1,0:T(8,128)S(1)}, bf16[8,2048,64]{2,1,0:T(8,128)(2,1)}, s32[8,2048]{1,0:T(8,128)S(1)}, s32[]{:T(128)}, ...), condition=%wide.region_1.2_spmd.clone, body=%wide.region_0.1_spmd.clone.sunk | while | flops 1082654720 | bytes 2646611 | solution.py:117
  214.9 7.9 %fusion.48 = f32[64,4096]{1,0:T(8,128)S(1)} fusion(s32[2048]{0:T(1024)S(1)} %bitcast.36, f32[64,4096]{1,0:T(8,128)S(1)} %get-tuple-element.117, bf16[8,2048,64]{2,1,0:T(8,128)(2,1)} %get-tuple-element.124, s32[]{:T(128)} %get-tuple-element.116, pred[]{:T(512)S(6)} %compare.3), kind=kOutput, calls=%fused_computation.5.clone.1 | convolution fusion | flops 1082654720 | bytes 2630145 | tf_op jit(solution)/shard_map/while/body/eval_jaxpr/dot_general | solution.py:111
  222.9 7.9 %fusion.48 = f32[64,4096]{1,0:T(8,128)S(1)} fusion(s32[2048]{0:T(1024)S(1)} %bitcast.36, f32[64,4096]{1,0:T(8,128)S(1)} %get-tuple-element.117, bf16[8,2048,64]{2,1,0:T(8,128)(2,1)} %get-tuple-element.124, s32[]{:T(128)} %get-tuple-element.116, pred[]{:T(512)S(6)} %compare.3), kind=kOutput, calls=%fused_computation.5.clone.1 | convolution fusion | flops 1082654720 | bytes 2630145 | tf_op jit(solution)/shard_map/while/body/eval_jaxpr/dot_general | solution.py:111
  230.8 7.9 %fusion.48 = f32[64,4096]{1,0:T(8,128)S(1)} fusion(s32[2048]{0:T(1024)S(1)} %bitcast.36, f32[64,4096]{1,0:T(8,128)S(1)} %get-tuple-element.117, bf16[8,2048,64]{2,1,0:T(8,128)(2,1)} %get-tuple-element.124, s32[]{:T(128)} %get-tuple-element.116, pred[]{:T(512)S(6)} %compare.3), kind=kOutput, calls=%fused_computation.5.clone.1 | convolution fusion | flops 1082654720 | bytes 2630145 | tf_op jit(solution)/shard_map/while/body/eval_jaxpr/dot_general | solution.py:111
  238.8 7.9 %fusion.48 = f32[64,4096]{1,0:T(8,128)S(1)} fusion(s32[2048]{0:T(1024)S(1)} %bitcast.36, f32[64,4096]{1,0:T(8,128)S(1)} %get-tuple-element.117, bf16[8,2048,64]{2,1,0:T(8,128)(2,1)} %get-tuple-element.124, s32[]{:T(128)} %get-tuple-element.116, pred[]{:T(512)S(6)} %compare.3), kind=kOutput, calls=%fused_computation.5.clone.1 | convolution fusion | flops 1082654720 | bytes 2630145 | tf_op jit(solution)/shard_map/while/body/eval_jaxpr/dot_general | solution.py:111
  246.7 7.9 %fusion.48 = f32[64,4096]{1,0:T(8,128)S(1)} fusion(s32[2048]{0:T(1024)S(1)} %bitcast.36, f32[64,4096]{1,0:T(8,128)S(1)} %get-tuple-element.117, bf16[8,2048,64]{2,1,0:T(8,128)(2,1)} %get-tuple-element.124, s32[]{:T(128)} %get-tuple-element.116, pred[]{:T(512)S(6)} %compare.3), kind=kOutput, calls=%fused_computation.5.clone.1 | convolution fusion | flops 1082654720 | bytes 2630145 | tf_op jit(solution)/shard_map/while/body/eval_jaxpr/dot_general | solution.py:111
  254.6 7.9 %fusion.48 = f32[64,4096]{1,0:T(8,128)S(1)} fusion(s32[2048]{0:T(1024)S(1)} %bitcast.36, f32[64,4096]{1,0:T(8,128)S(1)} %get-tuple-element.117, bf16[8,2048,64]{2,1,0:T(8,128)(2,1)} %get-tuple-element.124, s32[]{:T(128)} %get-tuple-element.116, pred[]{:T(512)S(6)} %compare.3), kind=kOutput, calls=%fused_computation.5.clone.1 | convolution fusion | flops 1082654720 | bytes 2630145 | tf_op jit(solution)/shard_map/while/body/eval_jaxpr/dot_general | solution.py:111
  262.6 7.9 %fusion.48 = f32[64,4096]{1,0:T(8,128)S(1)} fusion(s32[2048]{0:T(1024)S(1)} %bitcast.36, f32[64,4096]{1,0:T(8,128)S(1)} %get-tuple-element.117, bf16[8,2048,64]{2,1,0:T(8,128)(2,1)} %get-tuple-element.124, s32[]{:T(128)} %get-tuple-element.116, pred[]{:T(512)S(6)} %compare.3), kind=kOutput, calls=%fused_computation.5.clone.1 | convolution fusion | flops 1082654720 | bytes 2630145 | tf_op jit(solution)/shard_map/while/body/eval_jaxpr/dot_general | solution.py:111
  270.5 7.9 %fusion.48 = f32[64,4096]{1,0:T(8,128)S(1)} fusion(s32[2048]{0:T(1024)S(1)} %bitcast.36, f32[64,4096]{1,0:T(8,128)S(1)} %get-tuple-element.117, bf16[8,2048,64]{2,1,0:T(8,128)(2,1)} %get-tuple-element.124, s32[]{:T(128)} %get-tuple-element.116, pred[]{:T(512)S(6)} %compare.3), kind=kOutput, calls=%fused_computation.5.clone.1 | convolution fusion | flops 1082654720 | bytes 2630145 | tf_op jit(solution)/shard_map/while/body/eval_jaxpr/dot_general | solution.py:111
  (67 shorter events, 9.1 us)
Async XLA Ops:
  0.6 105.4 %copy-start = (f32[64,72]{1,0:T(8,128)S(1)}, f32[64,72]{1,0:T(8,128)}, u32[]{:S(2)}) copy-start(f32[64,72]{1,0:T(8,128)} %param.13) | copy-start | bytes 55300
  7.0 9.0 %collective-permute-start = (f32[72,32,1]{0,1,2:T(8,128)S(1)}, f32[72,32,1]{0,1,2:T(8,128)S(1)}, u32[]{:S(2)}, u32[]{:S(2)}) collective-permute-start(f32[72,32,1]{0,1,2:T(8,128)S(1)} %copy.17), channel_id=1, source_target_pairs={{0,1},{1,2},{2,3},{3,4},{4,5},{5,6},{6,7},{7,8},{8,9},{9,10},{10,1... | collective-permute-start | bytes 27656 | tf_op jit(solution)/shard_map/ppermute | solution.py:26
  11.4 6.6 %collective-permute-start.1 = (f32[72,32,1]{0,1,2:T(8,128)S(1)}, f32[72,32,1]{0,1,2:T(8,128)S(1)}, u32[]{:S(2)}, u32[]{:S(2)}) collective-permute-start(f32[72,32,1]{0,1,2:T(8,128)S(1)} %copy.19), channel_id=1, source_target_pairs={{1,0},{2,1},{3,2},{4,3},{5,4},{6,5},{7,6},{8,7},{9,8},{10,9},{11,1... | collective-permute-start | bytes 27656 | tf_op jit(solution)/shard_map/ppermute | solution.py:27
  19.9 16.1 %copy-start.7 = (f32[2]{0:T(128)S(1)}, f32[2]{0:T(128)}, u32[]{:S(2)}) copy-start(f32[2]{0:T(128)} %param.12) | copy-start | bytes 28
  19.9 16.2 %copy-start.5 = (s32[32,256]{1,0:T(8,128)S(1)}, s32[32,256]{1,0:T(8,128)}, u32[]{:S(2)}) copy-start(s32[32,256]{1,0:T(8,128)} %param.11) | copy-start | bytes 98308
  21.9 3.7 %collective-permute-start.3 = (bf16[72,1,258]{2,1,0:T(2,128)(2,1)S(1)}, bf16[72,1,258]{2,1,0:T(2,128)(2,1)S(1)}, u32[]{:S(2)}, u32[]{:S(2)}) collective-permute-start(bf16[72,1,258]{2,1,0:T(2,128)(2,1)S(1)} %get-tuple-element.65), channel_id=1, source_target_pairs={{0,1},{1,0},{2,3},{3,2},{4,5},{5,4},{6,7},{7,6},{8,9},{9,8},{10,11... | collective-permute-start | bytes 111464 | tf_op jit(solution)/shard_map/ppermute | solution.py:16
  25.5 5.1 %collective-permute-start.4 = (bf16[72,1,258]{2,1,0:T(2,128)(2,1)S(1)}, bf16[72,1,258]{2,1,0:T(2,128)(2,1)S(1)}, u32[]{:S(2)}, u32[]{:S(2)}) collective-permute-start(bf16[72,1,258]{2,1,0:T(2,128)(2,1)S(1)} %collective-permute-done.3), channel_id=1, source_target_pairs={{0,2},{1,3},{2,0},{3,1},{4,6},{5,7},{6,4},{7,5},{8,10},{9,11},{10,... | collective-permute-start | bytes 111464 | tf_op jit(solution)/shard_map/ppermute | solution.py:16
  30.6 3.6 %collective-permute-start.5 = (bf16[72,1,258]{2,1,0:T(2,128)(2,1)S(1)}, bf16[72,1,258]{2,1,0:T(2,128)(2,1)S(1)}, u32[]{:S(2)}, u32[]{:S(2)}) collective-permute-start(bf16[72,1,258]{2,1,0:T(2,128)(2,1)S(1)} %collective-permute-done.4), channel_id=1, source_target_pairs={{0,4},{1,5},{2,6},{3,7},{4,0},{5,1},{6,2},{7,3},{8,12},{9,13},{10,... | collective-permute-start | bytes 111464 | tf_op jit(solution)/shard_map/ppermute | solution.py:16
  34.2 12.1 %collective-permute-start.6 = (bf16[72,1,258]{2,1,0:T(2,128)(2,1)S(1)}, bf16[72,1,258]{2,1,0:T(2,128)(2,1)S(1)}, u32[]{:S(2)}, u32[]{:S(2)}) collective-permute-start(bf16[72,1,258]{2,1,0:T(2,128)(2,1)S(1)} %collective-permute-done.5), channel_id=1, source_target_pairs={{0,8},{1,9},{2,10},{3,11},{4,12},{5,13},{6,14},{7,15},{8,0},{9,1},... | collective-permute-start | bytes 111464 | tf_op jit(solution)/shard_map/ppermute | solution.py:16
  36.6 11.6 %collective-permute-start.7 = (f32[72,1,258]{2,1,0:T(1,128)S(1)}, f32[72,1,258]{2,1,0:T(1,128)S(1)}, u32[]{:S(2)}, u32[]{:S(2)}) collective-permute-start(f32[72,1,258]{2,1,0:T(1,128)S(1)} %get-tuple-element.68), channel_id=1, source_target_pairs={{16,0},{32,16},{48,32},{64,48},{80,64},{96,80},{112,96},{17,1},{33... | collective-permute-start | bytes 222920 | tf_op jit(solution)/shard_map/ppermute | solution.py:27
  43.3 5.0 %collective-permute-start.2 = (f32[72,1,258]{2,1,0:T(1,128)S(1)}, f32[72,1,258]{2,1,0:T(1,128)S(1)}, u32[]{:S(2)}, u32[]{:S(2)}) collective-permute-start(f32[72,1,258]{2,1,0:T(1,128)S(1)} %get-tuple-element.66), channel_id=1, source_target_pairs={{0,16},{16,32},{32,48},{48,64},{64,80},{80,96},{96,112},{1,17},{17... | collective-permute-start | bytes 222920 | tf_op jit(solution)/shard_map/ppermute | solution.py:26
  55.5 2.1 copy-start.1
  57.6 13.0 %copy-start.2 = (f32[72,32,256]{2,1,0:T(8,128)S(1)}, f32[72,32,256]{2,1,0:T(8,128)}, u32[]{:S(2)}) copy-start(f32[72,32,256]{2,1,0:T(8,128)} %copy-done.1) | copy-start | bytes 7077892
  59.7 7.1 %collective-permute-start.8 = (f32[72,32,1]{0,1,2:T(8,128)S(1)}, f32[72,32,1]{0,1,2:T(8,128)S(1)}, u32[]{:S(2)}, u32[]{:S(2)}) collective-permute-start(f32[72,32,1]{0,1,2:T(8,128)S(1)} %copy.23), channel_id=1, source_target_pairs={{0,1},{1,2},{2,3},{3,4},{4,5},{5,6},{6,7},{7,8},{8,9},{9,10},{10,1... | collective-permute-start | bytes 27656 | tf_op jit(solution)/shard_map/ppermute | solution.py:26
  63.3 5.4 %collective-permute-start.9 = (f32[72,32,1]{0,1,2:T(8,128)S(1)}, f32[72,32,1]{0,1,2:T(8,128)S(1)}, u32[]{:S(2)}, u32[]{:S(2)}) collective-permute-start(f32[72,32,1]{0,1,2:T(8,128)S(1)} %copy.25), channel_id=1, source_target_pairs={{1,0},{2,1},{3,2},{4,3},{5,4},{6,5},{7,6},{8,7},{9,8},{10,9},{11,1... | collective-permute-start | bytes 27656 | tf_op jit(solution)/shard_map/ppermute | solution.py:27
  70.7 12.3 %copy-start.4 = (s32[1,128,128]{2,1,0:T(8,128)S(1)}, s32[1,128,128]{2,1,0:T(8,128)}, u32[]{:S(2)}) copy-start(s32[1,128,128]{2,1,0:T(8,128)} %param.14) | copy-start | bytes 196612
  72.6 4.9 %collective-permute-start.11 = (bf16[72,1,258]{2,1,0:T(2,128)(2,1)S(1)}, bf16[72,1,258]{2,1,0:T(2,128)(2,1)S(1)}, u32[]{:S(2)}, u32[]{:S(2)}) collective-permute-start(bf16[72,1,258]{2,1,0:T(2,128)(2,1)S(1)} %get-tuple-element.61), channel_id=1, source_target_pairs={{0,1},{1,0},{2,3},{3,2},{4,5},{5,4},{6,7},{7,6},{8,9},{9,8},{10,11... | collective-permute-start | bytes 111464 | tf_op jit(solution)/shard_map/ppermute | solution.py:16
  77.5 5.5 %collective-permute-start.12 = (bf16[72,1,258]{2,1,0:T(2,128)(2,1)S(1)}, bf16[72,1,258]{2,1,0:T(2,128)(2,1)S(1)}, u32[]{:S(2)}, u32[]{:S(2)}) collective-permute-start(bf16[72,1,258]{2,1,0:T(2,128)(2,1)S(1)} %collective-permute-done.11), channel_id=1, source_target_pairs={{0,2},{1,3},{2,0},{3,1},{4,6},{5,7},{6,4},{7,5},{8,10},{9,11},{10,... | collective-permute-start | bytes 111464 | tf_op jit(solution)/shard_map/ppermute | solution.py:16
  83.0 3.6 %collective-permute-start.13 = (bf16[72,1,258]{2,1,0:T(2,128)(2,1)S(1)}, bf16[72,1,258]{2,1,0:T(2,128)(2,1)S(1)}, u32[]{:S(2)}, u32[]{:S(2)}) collective-permute-start(bf16[72,1,258]{2,1,0:T(2,128)(2,1)S(1)} %collective-permute-done.12), channel_id=1, source_target_pairs={{0,4},{1,5},{2,6},{3,7},{4,0},{5,1},{6,2},{7,3},{8,12},{9,13},{10,... | collective-permute-start | bytes 111464 | tf_op jit(solution)/shard_map/ppermute | solution.py:16
  86.6 9.9 %collective-permute-start.14 = (bf16[72,1,258]{2,1,0:T(2,128)(2,1)S(1)}, bf16[72,1,258]{2,1,0:T(2,128)(2,1)S(1)}, u32[]{:S(2)}, u32[]{:S(2)}) collective-permute-start(bf16[72,1,258]{2,1,0:T(2,128)(2,1)S(1)} %collective-permute-done.13), channel_id=1, source_target_pairs={{0,8},{1,9},{2,10},{3,11},{4,12},{5,13},{6,14},{7,15},{8,0},{9,1},... | collective-permute-start | bytes 111464 | tf_op jit(solution)/shard_map/ppermute | solution.py:16
  88.2 10.1 %collective-permute-start.15 = (f32[72,1,258]{2,1,0:T(1,128)S(1)}, f32[72,1,258]{2,1,0:T(1,128)S(1)}, u32[]{:S(2)}, u32[]{:S(2)}) collective-permute-start(f32[72,1,258]{2,1,0:T(1,128)S(1)} %get-tuple-element.67), channel_id=1, source_target_pairs={{16,0},{32,16},{48,32},{64,48},{80,64},{96,80},{112,96},{17,1},{33... | collective-permute-start | bytes 222920 | tf_op jit(solution)/shard_map/ppermute | solution.py:27
  93.0 5.5 %collective-permute-start.10 = (f32[72,1,258]{2,1,0:T(1,128)S(1)}, f32[72,1,258]{2,1,0:T(1,128)S(1)}, u32[]{:S(2)}, u32[]{:S(2)}) collective-permute-start(f32[72,1,258]{2,1,0:T(1,128)S(1)} %get-tuple-element.62), channel_id=1, source_target_pairs={{0,16},{16,32},{32,48},{48,64},{64,80},{80,96},{96,112},{1,17},{17... | collective-permute-start | bytes 222920 | tf_op jit(solution)/shard_map/ppermute | solution.py:26
  104.6 1.4 copy-start.3
  172.3 10.0 %copy-start.6 = (s32[1,128,128]{2,1,0:T(8,128)S(1)}, s32[1,128,128]{2,1,0:T(8,128)}, u32[]{:S(2)}) copy-start(s32[1,128,128]{2,1,0:T(8,128)} %param.15) | copy-start | bytes 196612
  172.3 39.5 %all-to-all-start = ((bf16[128,128,64]{1,2,0:T(8,128)(2,1)}), bf16[128,128,64]{1,2,0:T(8,128)(2,1)S(1)}, u32[]{:S(2)}, u32[]{:S(2)}) async-start(bf16[128,128,64]{1,2,0:T(8,128)(2,1)} %broadcast_select_fusion), calls=%async_computation | async-start | bytes 4194304 | tf_op jit(solution)/shard_map/all_to_all | solution.py:99
  278.4 1.0 copy-start.8
where the time goes:
time: 280 us; the launch traced here: 279 us
  local copies, waits for them, and re-layouts  91.7 us (33%)
  matrix products  65.3 us (23%)
  waiting for transfers between devices  54.2 us (19%)
  starting transfers between devices  45.1 us (16%)
  other arithmetic  21.9 us (8%)
    dot_general x8, matrix products, accumulate(): lax.dot_general(values, selector, (((0,), (0,)), ((), ())), preferred_ele...  63.2 us
    gather x2, local copies, waits for them, and re-layouts, body(): jnp.take(profiles, jnp.maximum(owner_lists, 0).reshape(-1), axis=0)  61.5 us
    all_to_all x1, waiting for transfers between devices, body(): lax.all_to_all(picked, ('lat', 'lon'), split_axis=0, concat_axis=0, tiled...  29.4 us
    ppermute x8, waiting for transfers between devices, partner_2(): return lax.ppermute(value, axis, pairs)  24.7 us
    ppermute x4, starting transfers between devices, padded(): after = lax.ppermute(leading, axis, down)  19.6 us
    ppermute x4, starting transfers between devices, padded(): before = lax.ppermute(last, axis, up)  10.7 us
    all_to_all x1, starting transfers between devices, body(): lax.all_to_all(picked, ('lat', 'lon'), split_axis=0, concat_axis=0, tiled...  9.99 us
    mul x2, other arithmetic, body(): extended = margins(moving * planes, 1)  9.04 us
  transfers between devices with their start and end apart: 17, of which 7 were waited for; matrix products, arithmetic and copies ran while one was open for 4% of the time, Pallas kernels for 0%

commit v1 on v0

v1 whole, which is shorter than its diff:
```python
import functools
import math

import jax
import jax.numpy as jnp
import numpy as np
from jax import lax
from jax.experimental import pallas as pl
from jax.experimental.pallas import tpu as pltpu
from jax.sharding import PartitionSpec as P

DIRS = 36
FREQ = 2
PLANES = DIRS * FREQ
HALF = PLANES // 2
QUAD = PLANES // 4
OUT_DEV = 4096
N_ACC = 4
VMEM_LIMIT = 48 * 1024 * 1024


def chain_perms(n_lat, n_lon):
    top = n_lat - 1

    def flat(j, i):
        return j * n_lon + i % n_lon

    def build(step, fold):
        first, second = [], []
        for j in range(n_lat):
            for i in range(n_lon):
                start = (i + (top - j) * step) % n_lon
                partner = fold(start) % n_lon
                rising = start <= partner
                up = (flat(j, i), flat(j + 1, i + step)) if j < top else (flat(j, i), flat(j, partner))
                down = (flat(j, i), flat(j - 1, i - step)) if j > 0 else None
                if j == top and start == partner:
                    up = None
                a, b = (up, down) if rising else (down, up)
                first += [a] if a else []
                second += [b] if b else []
        return first, second

    return (
        build(0, lambda i: n_lon - 1 - i),
        build(1, lambda i: n_lon - 2 - i),
        build(-1, lambda i: n_lon - i),
    )


def rising_flags(n_lat, n_lon):
    j, i = lax.axis_index("lat"), lax.axis_index("lon")
    left = n_lat - 1 - j
    row = i <= n_lon - 1 - i
    start = lax.rem(i + left, n_lon)
    partner = lax.rem(2 * n_lon - 2 - start, n_lon)
    start_l = lax.rem(i - left + n_lon, n_lon)
    partner_l = lax.rem(n_lon - start_l, n_lon)
    return row, start <= partner, start_l <= partner_l, j == n_lat - 1, start == partner, start_l == partner_l


def pack_kernel(n_lat, n_lon, x_ref, speed_ref, mask_ref, a_ref, b_ref, c_ref, d_ref, xa_ref, xb_ref, ya_ref, yb_ref,
                mov_ref, sea_ref, up_ref, down_ref):
    height, breadth = speed_ref.shape
    row_asc, right_asc, left_asc, _, _, _ = rising_flags(n_lat, n_lon)
    sea = mask_ref[...].astype(jnp.float32)
    moving = speed_ref[...] * sea
    mov_ref[...] = moving
    sea_ref[...] = sea
    for k in range(2):
        for q in range(HALF):
            up_ref[k, q : q + 1, :] = x_ref[q, height - 1 - k : height - k, :]
            down_ref[k, q : q + 1, :] = x_ref[HALF + q, k : k + 1, :]
        up_ref[k, HALF : HALF + 1, :] = moving[height - 1 - k : height - k, :]
        down_ref[k, HALF : HALF + 1, :] = moving[k : k + 1, :]
        up_ref[k, HALF + 1 : HALF + 2, :] = sea[height - 1 - k : height - k, :]
        down_ref[k, HALF + 1 : HALF + 2, :] = sea[k : k + 1, :]
        up_ref[k, HALF + 2 :, :] = jnp.zeros((2, breadth), jnp.float32)
        down_ref[k, HALF + 2 :, :] = jnp.zeros((2, breadth), jnp.float32)

    @pl.when(row_asc)
    def _():
        a_ref[...] = up_ref[...]
        b_ref[...] = down_ref[...]

    @pl.when(jnp.logical_not(row_asc))
    def _():
        a_ref[...] = down_ref[...]
        b_ref[...] = up_ref[...]

    lane = lax.broadcasted_iota(jnp.int32, (height, 128), 1)
    east = jnp.zeros((height, 128), jnp.float32)
    west = jnp.zeros((height, 128), jnp.float32)
    for q in range(HALF + 2):
        mine = lane // 2 == q
        if q < HALF:
            p_e = q if q < QUAD else q + HALF
            p_w = q + QUAD
            edge_e, edge_w = x_ref[p_e, :, breadth - 128 :], x_ref[p_w, :, :128]
        else:
            field = moving if q == HALF else sea
            edge_e, edge_w = field[:, breadth - 128 :], field[:, :128]
        east = jnp.where(mine, pltpu.roll(edge_e, (2 * q + 2) % 128, axis=1), east)
        west = jnp.where(mine, pltpu.roll(edge_w, 2 * q, axis=1), west)
    c_ref[...] = east
    d_ref[...] = west
    up_right, up_left = east[height - 8 :], west[height - 8 :]
    down_right, down_left = east[:8], west[:8]
    xa_ref[...] = jnp.where(right_asc, up_right, down_left)
    xb_ref[...] = jnp.where(right_asc, down_left, up_right)
    ya_ref[...] = jnp.where(left_asc, up_left, down_right)
    yb_ref[...] = jnp.where(left_asc, down_right, up_left)


def wave_kernel(n_lat, n_lon, slots, courant_ref, cos_ref, sin_ref, cells_ref, x_ref, mov_ref, sea_ref, kernel_ref,
                a_ref, b_ref, c_ref, d_ref, xa_ref, xb_ref, ya_ref, yb_ref, own_c_ref, own_d_ref,
                lanes_ref, subs_ref, out_ref, picked_ref,
                south0, south1, north0, north1, west0, west1, east0, east1, halves, table, owner_rows, wide_kernel):
    height, breadth = mov_ref.shape
    row_asc, right_asc, left_asc, at_top, right_self, left_self = rising_flags(n_lat, n_lon)
    c0, c1 = courant_ref[0], courant_ref[1]

    xa, xb, ya, yb = xa_ref[...], xb_ref[...], ya_ref[...], yb_ref[...]
    sw = jnp.where(right_asc, xa, xb)[7:8]
    se = jnp.where(left_asc, ya, yb)[7:8]
    ne_in = jnp.where(right_asc, xb, xa)
    nw_in = jnp.where(left_asc, yb, ya)
    ne_fold = jnp.where(right_self, own_c_ref[height - 1 :, :], ne_in[7:8])
    nw_fold = jnp.where(left_self, own_d_ref[height - 1 :, :], nw_in[7:8])
    near_c, near_d = 2 * HALF + 1, 2 * HALF

    def with_moving(row, lane_of):
        return row * row[:, lane_of : lane_of + 1]

    sw = with_moving(sw, near_c)
    se = with_moving(se, near_d)
    ne = jnp.where(at_top, pltpu.roll(with_moving(ne_fold, near_c), HALF - 1, axis=1), with_moving(ne_in[0:1], near_d))
    nw = jnp.where(at_top, pltpu.roll(with_moving(nw_fold, near_d), HALF + 1, axis=1), with_moving(nw_in[0:1], near_c))

    lane = lax.broadcasted_iota(jnp.int32, (height, 128), 1)
    row = lax.broadcasted_iota(jnp.int32, (height, 128), 0)
    odd = lane % 2 == 1

    def columns(ref, near, far, southern, northern, cx, cy, sign, flux0, flux1):
        e0 = ref[...]
        mov = jnp.where(odd, e0[:, 2 * HALF + 1 : 2 * HALF + 2], e0[:, 2 * HALF : 2 * HALF + 1])
        sea = e0[:, 2 * HALF + 2 + near : 2 * HALF + 3 + near]
        f0 = mov * e0
        f_far = pltpu.roll(f0, 1 if near > far else 127, axis=1)
        f_south = jnp.where(row == 0, southern, pltpu.roll(f0, 1, axis=0))
        f_north = jnp.where(row == height - 1, northern, pltpu.roll(f0, height - 1, axis=0))
        div_x = cx * (f0 - f_far) if sign > 0 else cx * (f_far - f0)
        div_y = jnp.where(lane < HALF, cy * (f0 - f_south), cy * (f_north - f0))
        flux0[...] = f0
        flux1[...] = mov * (sea * ((e0 - div_x) - div_y))

    lanes = lanes_ref[...]
    lane_courant = jnp.where(lanes[4:5] > 0.5, c1, c0)
    columns(c_ref, 1, 0, sw, nw, lanes[0:1] * lane_courant, lanes[1:2] * lane_courant, 1, west0, west1)
    columns(d_ref, 0, 1, se, ne, lanes[2:3] * lane_courant, lanes[3:4] * lane_courant, -1, east0, east1)

    wide = lax.broadcasted_iota(jnp.int32, (HALF + 4, breadth), 1)
    plane = lax.broadcasted_iota(jnp.int32, (HALF + 4, 1), 0)
    plane_l = lax.broadcasted_iota(jnp.int32, (HALF + 4, 128), 0)
    lane_l = lax.broadcasted_iota(jnp.int32, (HALF + 4, 128), 1)
    subs = subs_ref[...]
    sub_courant = jnp.where(plane % 2 == 1, c1, c0)

    def to_sublanes(corner, lane_of):
        return jnp.sum(jnp.where(lane_l == lane_of, corner, 0.0), axis=1, keepdims=True)

    def rows(near, far, first_west, west_corner, east_corner, cx, cy, sign, flux0, flux1):
        mov, sea = near[HALF : HALF + 1], near[HALF + 1 : HALF + 2]
        f0 = mov * near
        f_far = far[HALF : HALF + 1] * far
        f_west = jnp.where(wide == 0, west_corner, pltpu.roll(f0, 1, axis=1))
        f_east = jnp.where(wide == breadth - 1, east_corner, pltpu.roll(f0, breadth - 1, axis=1))
        from_west = (plane < QUAD) if first_west else (plane >= QUAD)
        div_x = jnp.where(from_west, cx * (f0 - f_west), cx * (f_east - f0))
        div_y = cy * (f0 - f_far) if sign > 0 else cy * (f_far - f0)
        flux0[...] = f0
        flux1[...] = mov * (sea * ((near - div_x) - div_y))

    south = jnp.where(row_asc, a_ref[...], b_ref[...])
    north0[...] = jnp.where(row_asc, b_ref[0], a_ref[0])
    north1[...] = jnp.where(row_asc, b_ref[1], a_ref[1])

    @pl.when(at_top)
    def _():
        flip_i = lax.broadcasted_iota(jnp.int32, (breadth, breadth), 0)
        flip_j = lax.broadcasted_iota(jnp.int32, (breadth, breadth), 1)
        flip = (flip_i + flip_j == breadth - 1).astype(jnp.float32)
        for ref in (north0, north1):
            ref[...] = jnp.dot(ref[...], flip, precision=lax.Precision.HIGHEST, preferred_element_type=jnp.float32)

    sw_s = to_sublanes(sw, 2 * plane_l + 1)
    se_s = to_sublanes(se, 2 * plane_l - HALF)
    ne_s = to_sublanes(ne, 2 * plane_l + HALF)
    nw_s = to_sublanes(nw, 2 * plane_l + 1)
    rows(south[0], south[1], True, sw_s, se_s, subs[:, 0:1] * sub_courant, subs[:, 1:2] * sub_courant, 1, south0, south1)
    rows(north0[...], north1[...], False, nw_s, ne_s, subs[:, 2:3] * sub_courant, subs[:, 3:4] * sub_courant, -1,
         north0, north1)

    moving = mov_ref[...]
    sea_all = sea_ref[...]
    lane_edge = lax.broadcasted_iota(jnp.int32, (height, 128), 1)
    row_edge = lax.broadcasted_iota(jnp.int32, (8, breadth), 0)

    def quadrant(first, from_west, from_south, column0, column1, lane_first, row0, row1, row_first):
        def upstream(flux, column, line):
            if from_west:
                moved = pltpu.roll(flux, 1, axis=1)
                side = jnp.concatenate([jnp.where(lane_edge == 0, column, moved[:, :128]), moved[:, 128:]], axis=1)
            else:
                moved = pltpu.roll(flux, breadth - 1, axis=1)
                edge = jnp.where(lane_edge == 127, column, moved[:, breadth - 128 :])
                side = jnp.concatenate([moved[:, : breadth - 128], edge], axis=1)
            if from_south:
                moved = pltpu.roll(flux, 1, axis=0)
                below = jnp.concatenate([jnp.where(row_edge == 0, line, moved[:8]), moved[8:]], axis=0)
            else:
                moved = pltpu.roll(flux, height - 1, axis=0)
                edge = jnp.where(row_edge == 7, line, moved[height - 8 :])
                below = jnp.concatenate([moved[: height - 8], edge], axis=0)
            return side, below

        def step(t, carry):
            p = first + t
            courant = jnp.where(p % 2 == 1, c1, c0)
            cx = cos_ref[p] * courant
            cy = sin_ref[p] * courant
            place = lane_first + 2 * t
            turn = (128 - place) if from_west else (127 - place)
            energy = x_ref[p]
            for column_ref, row_ref in ((column0, row0), (column1, row1)):
                flux = moving * energy
                column = pltpu.roll(column_ref[...], turn, axis=1)
                side, below = upstream(flux, column, row_ref[pl.ds(row_first + t, 1), :])
                div_x = cx * (flux - side) if from_west else cx * (side - flux)
                div_y = cy * (flux - below) if from_south else cy * (below - flux)
                energy = sea_all * ((energy - div_x) - div_y)
            out_ref[p] = energy
            start = pl.ds(pl.multiple_of(p * height, height), height)
            for h in range(breadth // 128):
                halves[h, start, :] = energy[:, h * 128 : (h + 1) * 128]
            return carry

        lax.fori_loop(0, QUAD, step, 0)

    quadrant(0, True, True, west0, west1, 1, south0, south1, 0)
    quadrant(QUAD, False, True, east0, east1, 0, south0, south1, QUAD)
    quadrant(2 * QUAD, False, False, east0, east1, HALF, north0, north1, 0)
    quadrant(3 * QUAD, True, False, west0, west1, HALF + 1, north0, north1, QUAD)

    pad = jnp.zeros((8, 128), jnp.bfloat16)
    wide_kernel[...] = jnp.zeros((128, 128), jnp.float32)
    wide_kernel[:64, :PLANES] = kernel_ref[...]
    wide_kernel[64:, :PLANES] = kernel_ref[...]
    turned = wide_kernel[...].T[:PLANES]
    weight_high = turned.astype(jnp.bfloat16)
    weight_low = (turned - weight_high.astype(jnp.float32)).astype(jnp.bfloat16)
    weight = jnp.concatenate([weight_high, pad, weight_high, pad, weight_low, pad], axis=0)

    @pl.loop(0, height)
    def _(r):
        for h in range(breadth // 128):
            spectra = halves[h, pl.ds(r, PLANES, stride=height), :]
            high = spectra.astype(jnp.bfloat16)
            low = (spectra - high.astype(jnp.float32)).astype(jnp.bfloat16)
            stacked = jnp.concatenate([high, pad, low, pad, high, pad], axis=0)
            profile = lax.dot_general(stacked, weight, (((0,), (0,)), ((), ())), preferred_element_type=jnp.float32)
            start = pl.multiple_of(r * breadth + h * 128, 128)
            table[pl.ds(start, 128), :] = profile.astype(jnp.bfloat16).astype(jnp.float32)

    first_half = lax.broadcasted_iota(jnp.int32, (1, 128), 1) < 64

    @pl.loop(0, picked_ref.shape[0])
    def _(owner):
        for g in range(slots // 16):
            for j in range(8):
                one = cells_ref[owner * slots + g * 16 + j]
                two = cells_ref[owner * slots + g * 16 + 8 + j]
                line = jnp.where(first_half, table[pl.ds(one, 1), :], table[pl.ds(two, 1), :])
                owner_rows[g * 8 + j : g * 8 + j + 1, :] = line
        picked_ref[owner] = owner_rows[...].astype(jnp.bfloat16)


def add_kernel(slots, rows_ref, values_ref, out_ref, lines, *sums):
    n_acc = len(sums) // 2
    tile = out_ref.shape[1]
    block = 512
    for total in sums:

        @pl.loop(0, tile // block)
        def _(i):
            total[pl.ds(pl.multiple_of(i * block, block), block), :] = jnp.zeros((block, 128), jnp.float32)

    @pl.loop(0, values_ref.shape[0])
    def _(source):
        lines[...] = values_ref[source].astype(jnp.float32)
        for g in range(slots // 16):
            for j in range(8):
                one = rows_ref[source * slots + g * 16 + j]
                two = rows_ref[source * slots + g * 16 + 8 + j]
                line = lines[g * 8 + j : g * 8 + j + 1, :]
                left, right = sums[j % n_acc], sums[n_acc + j % n_acc]
                left[pl.ds(one, 1), :] = left[pl.ds(one, 1), :] + line
                right[pl.ds(two, 1), :] = right[pl.ds(two, 1), :] + line

    first_half = lax.broadcasted_iota(jnp.int32, (block, 128), 1) < 64

    @pl.loop(0, tile // block)
    def _(i):
        here = pl.ds(pl.multiple_of(i * block, block), block)
        left, right = sums[0][here, :], sums[n_acc][here, :]
        for q in range(1, n_acc):
            left = left + sums[q][here, :]
            right = right + sums[n_acc + q][here, :]
        both = jnp.where(first_half, left, right).T
        out_ref[:, here] = both[:64] + both[64:]


def constant_tables():
    heading = (np.arange(DIRS) + 0.5) * (2.0 * math.pi / DIRS)
    cos = np.repeat(np.cos(heading), FREQ)
    sin = np.repeat(np.sin(heading), FREQ)
    lanes = np.zeros((8, 128))
    q = np.arange(HALF)
    from_west = np.where(q < QUAD, q, q + HALF)
    from_east = q + QUAD
    for column in range(2):
        lanes[0, 2 * q + column] = cos[from_west]
        lanes[1, 2 * q + column] = sin[from_west]
        lanes[2, 2 * q + column] = cos[from_east]
        lanes[3, 2 * q + column] = sin[from_east]
        lanes[4, 2 * q + column] = q % 2
    subs = np.zeros((HALF + 4, 128))
    subs[:HALF, 0], subs[:HALF, 1] = cos[:HALF], sin[:HALF]
    subs[:HALF, 2], subs[:HALF, 3] = cos[HALF:], sin[HALF:]
    return [t.astype(np.float32) for t in (cos, sin, lanes, subs)]


def body(n_lat, n_lon, spectrum, speed_factor, land_sea_mask, courant, depth_kernel, send_rows, recv_rows):
    height, breadth = speed_factor.shape
    devices, slots = send_rows.shape[1:]
    x = spectrum.reshape(PLANES, height, breadth)
    f32 = jnp.float32
    vmem = pl.BlockSpec(memory_space=pltpu.VMEM)
    smem = pl.BlockSpec(memory_space=pltpu.SMEM)
    params = pltpu.CompilerParams(vmem_limit_bytes=VMEM_LIMIT)

    def shape(*dims, kind=f32):
        return jax.ShapeDtypeStruct(dims, kind)

    row_message = shape(2, HALF + 4, breadth)
    column_message = shape(height, 128)
    corner_message = shape(8, 128)
    a, b, c, d, xa, xb, ya, yb, moving, sea = pl.pallas_call(
        functools.partial(pack_kernel, n_lat, n_lon),
        out_shape=[row_message] * 2 + [column_message] * 2 + [corner_message] * 4 + [shape(height, breadth)] * 2,
        in_specs=[vmem] * 3,
        out_specs=[vmem] * 10,
        scratch_shapes=[pltpu.VMEM((2, HALF + 4, breadth), f32)] * 2,
        compiler_params=params,
        name="pack_halos",
    )(x, speed_factor, land_sea_mask)

    both = ("lat", "lon")
    row_perms, right_perms, left_perms = chain_perms(n_lat, n_lon)
    east = [(i, (i + 1) % n_lon) for i in range(n_lon)]
    west = [(j, i) for i, j in east]
    got = [lax.ppermute(m, both, perm) for m, perm in zip((a, b), row_perms)]
    got += [lax.ppermute(c, "lon", east), lax.ppermute(d, "lon", west)]
    got += [lax.ppermute(m, both, perm) for m, perm in zip((xa, xb, ya, yb), right_perms + left_perms)]

    cos, sin, lanes, subs = constant_tables()
    cells = jnp.maximum(send_rows, 0).reshape(-1)
    targets = jnp.where(recv_rows < 0, OUT_DEV, recv_rows).reshape(-1)
    propagated, picked = pl.pallas_call(
        functools.partial(wave_kernel, n_lat, n_lon, slots),
        out_shape=[shape(PLANES, height, breadth), shape(devices, slots // 2, 128, kind=jnp.bfloat16)],
        in_specs=[smem] * 4 + [vmem] * 16,
        out_specs=[vmem] * 2,
        scratch_shapes=[pltpu.VMEM((HALF + 4, breadth), f32)] * 4
        + [pltpu.VMEM((height, 128), f32)] * 4
        + [
            pltpu.VMEM((breadth // 128, PLANES * height, 128), f32),
            pltpu.VMEM((height * breadth, 128), f32),
            pltpu.VMEM((slots // 2, 128), f32),
            pltpu.VMEM((128, 128), f32),
        ],
        compiler_params=params,
        name="propagate_and_pick",
    )(courant, cos, sin, cells, x, moving, sea, depth_kernel, *got, c, d, lanes, subs)

    received = lax.all_to_all(picked, both, split_axis=0, concat_axis=0, tiled=True)

    stokes = pl.pallas_call(
        functools.partial(add_kernel, slots),
        out_shape=shape(depth_kernel.shape[0], OUT_DEV),
        in_specs=[smem, vmem],
        out_specs=vmem,
        scratch_shapes=[pltpu.VMEM((slots // 2, 128), f32)] + [pltpu.VMEM((OUT_DEV + 8, 128), f32)] * (2 * N_ACC),
        compiler_params=params,
        name="add_profiles",
    )(targets, received)
    return propagated.reshape(DIRS, FREQ, height, breadth), stokes


def solution(mesh):
    placed = (
        P(None, None, "lat", "lon"),
        P("lat", "lon"),
        P("lat", "lon"),
        P(),
        P(),
        P(("lat", "lon"), None, None),
        P(("lat", "lon"), None, None),
    )
    return jax.shard_map(
        functools.partial(body, mesh.shape["lat"], mesh.shape["lon"]),
        mesh=mesh,
        in_specs=placed,
        out_specs=(P(None, None, "lat", "lon"), P(None, ("lat", "lon"))),
        check_vma=False,
    )
```

time: 280 us -> 135 us (0.48)
  local copies, waits for them, and re-layouts: 91.7 us -> 4.55 us
  matrix products: 65.3 us -> 0 us
  Pallas kernels: 0 us -> 59.6 us
  waiting for transfers between devices: 54.2 us -> 30.9 us
  other arithmetic: 21.9 us -> 0.02 us
  starting transfers between devices: 45.1 us -> 38.8 us
    dot_general x9 -> x0, matrix products: 65.3 us -> none  [the longest x8 63.2 us: accumulate(): lax.dot_general(values, selector, (((0,), (0,)), ((), ())), preferred_ele...]
    gather x2 -> x0, local copies, waits for them, and re-layouts: 61.5 us -> none  [body(): jnp.take(profiles, jnp.maximum(owner_lists, 0).reshape(-1), axis=0)]
    pallas_call x0 -> x3, Pallas kernels: none -> 59.6 us  [the longest x1 39.3 us: body(): pl.pallas_call(functools.partial(wave_kernel, n_lat, n_lon, slots), out_s...]
    ppermute x16 -> x8, waiting for transfers between devices: 24.8 us -> 1.47 us  [the longest x4 1.46 us: body(): lax.ppermute(m, both, perm)]
    mul x4 -> x0, other arithmetic: 15.9 us -> none  [the longest x2 9.04 us: body(): extended = margins(moving * planes, 1)]
    slice x8 -> x0, local copies, waits for them, and re-layouts: 11.8 us -> none  [the longest x4 7.84 us: padded(): last = lax.slice_in_dim(shard, length - width, length, axis=dim)]
    ppermute x16 -> x8, starting transfers between devices: 35.2 us -> 27 us  [the longest x4 16.2 us: body(): lax.ppermute(m, both, perm)]
    ppermute x4 -> x0, local copies, waits for them, and re-layouts: 7.8 us -> none  [the longest x2 3.9 us: padded(): before = lax.ppermute(last, axis, up)]
  transfers between devices with their start and end apart: 17 -> 9, of which waited for: 7 -> 2; matrix products, arithmetic and copies ran while one was open for 4% -> 0% of each run, Pallas kernels for 0% -> 0%
where the time goes in v1:
time: 135 us
  Pallas kernels  59.6 us (44%)
  starting transfers between devices  38.8 us (29%)
  waiting for transfers between devices  30.9 us (23%)
  local copies, waits for them, and re-layouts  4.55 us (3%)
    pallas_call x1, Pallas kernels, body(): pl.pallas_call(functools.partial(wave_kernel, n_lat, n_lon, slots), out_s...  39.3 us
    all_to_all x1, waiting for transfers between devices, body(): lax.all_to_all(picked, both, split_axis=0, concat_axis=0, tiled=True)  29.5 us
    pallas_call x1, Pallas kernels, body(): pl.pallas_call(functools.partial(add_kernel, slots), out_shape=shape(dept...  19.8 us
    ppermute x4, starting transfers between devices, body(): lax.ppermute(m, both, perm)  16.2 us
    all_to_all x1, starting transfers between devices, body(): lax.all_to_all(picked, both, split_axis=0, concat_axis=0, tiled=True)  11.8 us
    ppermute x2, starting transfers between devices, body(): got = [lax.ppermute(m, both, perm) for m, perm in zip((a, b), row_perms)]  5.98 us
    ppermute x2, starting transfers between devices, body(): got += [lax.ppermute(c, 'lon', east), lax.ppermute(d, 'lon', west)]  4.85 us
    unnamed x24, local copies, waits for them, and re-layouts  4.55 us
  transfers between devices with their start and end apart: 9, of which 2 were waited for; matrix products, arithmetic and copies ran while one was open for 0% of the time, Pallas kernels for 0%

profile of v1, /device:TPU:1, one launch (start us, length us, event | category | flops | bytes accessed | tf_op | source)
XLA Modules:
  0.0 134.7 jit_solution(6409072087572969015)
XLA Ops:
  0.6 0.0 copy-start.8
  0.6 0.0 copy-start.9
  0.7 0.0 copy-start.7
  0.7 0.0 copy-start
  0.7 1.7 %copy-done = f32[36,2,32,256]{3,2,1,0:T(8,128)S(1)} copy-done((f32[36,2,32,256]{3,2,1,0:T(8,128)S(1)}, f32[36,2,32,256]{3,2,1,0:T(8,128)}, u32[]{:S(2)}) %copy-start) | copy-done | bytes 2359320
  2.3 0.0 copy-start.2
  2.4 0.8 copy-done.2
  3.1 0.0 copy-start.3
  3.1 0.8 copy-done.3
  3.9 0.0 copy-start.10
  3.9 0.0 copy-start.4
  3.9 0.0 copy-start.5
  3.9 0.0 copy-start.6
  3.9 0.5 pack_halos.1
  4.4 5.9 %collective-permute-start.4 = (f32[8,128]{1,0:T(8,128)S(1)}, f32[8,128]{1,0:T(8,128)S(1)}, u32[]{:S(2)}, u32[]{:S(2)}) collective-permute-start(f32[8,128]{1,0:T(8,128)S(1)} %get-tuple-element.20), channel_id=1, source_target_pairs={{0,17},{8,25},{9,26},{10,27},{11,28},{12,29},{13,30},{14,31},{15,1... | collective-permute-start | bytes 12296 | tf_op jit(solution)/shard_map/ppermute | solution.py:374
  10.2 4.9 %collective-permute-start.5 = (f32[8,128]{1,0:T(8,128)S(1)}, f32[8,128]{1,0:T(8,128)S(1)}, u32[]{:S(2)}, u32[]{:S(2)}) collective-permute-start(f32[8,128]{1,0:T(8,128)S(1)} %get-tuple-element.21), channel_id=1, source_target_pairs={{1,18},{2,19},{3,20},{4,21},{5,22},{6,23},{7,24},{16,15},{17,0},{1... | collective-permute-start | bytes 12296 | tf_op jit(solution)/shard_map/ppermute | solution.py:374
  15.2 1.9 %collective-permute-start.6 = (f32[8,128]{1,0:T(8,128)S(1)}, f32[8,128]{1,0:T(8,128)S(1)}, u32[]{:S(2)}, u32[]{:S(2)}) collective-permute-start(f32[8,128]{1,0:T(8,128)S(1)} %get-tuple-element.22), channel_id=1, source_target_pairs={{7,22},{8,23},{9,24},{10,25},{11,26},{12,27},{13,28},{14,29},{15,3... | collective-permute-start | bytes 12296 | tf_op jit(solution)/shard_map/ppermute | solution.py:374
  17.1 0.1 collective-permute-start.2
  17.2 4.8 %collective-permute-start.3 = (f32[32,128]{1,0:T(8,128)S(1)}, f32[32,128]{1,0:T(8,128)S(1)}, u32[]{:S(2)}, u32[]{:S(2)}) collective-permute-start(f32[32,128]{1,0:T(8,128)S(1)} %get-tuple-element.19.own_d_ref), channel_id=1, source_target_pairs={{1,0},{2,1},{3,2},{4,3},{5,4},{6,5},{7,6},{8,7},{9,8},{10,9},{11,1... | collective-permute-start | bytes 49160 | tf_op jit(solution)/shard_map/ppermute | solution.py:373
  22.0 0.0 collective-permute-done.4.xa_ref
  22.0 4.1 %collective-permute-start = (f32[2,40,256]{2,1,0:T(8,128)S(1)}, f32[2,40,256]{2,1,0:T(8,128)S(1)}, u32[]{:S(2)}, u32[]{:S(2)}) collective-permute-start(f32[2,40,256]{2,1,0:T(8,128)S(1)} %get-tuple-element.16), channel_id=1, source_target_pairs={{0,16},{1,17},{2,18},{3,19},{4,20},{5,21},{6,22},{7,23},{16,32},{1... | collective-permute-start | bytes 245768 | tf_op jit(solution)/shard_map/ppermute | solution.py:372
  26.0 0.0 collective-permute-done.5.xb_ref
  26.0 1.9 %collective-permute-start.1 = (f32[2,40,256]{2,1,0:T(8,128)S(1)}, f32[2,40,256]{2,1,0:T(8,128)S(1)}, u32[]{:S(2)}, u32[]{:S(2)}) collective-permute-start(f32[2,40,256]{2,1,0:T(8,128)S(1)} %get-tuple-element.17), channel_id=1, source_target_pairs={{8,24},{9,25},{10,26},{11,27},{12,28},{13,29},{14,30},{15,31},{16,... | collective-permute-start | bytes 245768 | tf_op jit(solution)/shard_map/ppermute | solution.py:372
  28.0 0.0 collective-permute-done.6.ya_ref
  28.0 3.4 %collective-permute-start.7 = (f32[8,128]{1,0:T(8,128)S(1)}, f32[8,128]{1,0:T(8,128)S(1)}, u32[]{:S(2)}, u32[]{:S(2)}) collective-permute-start(f32[8,128]{1,0:T(8,128)S(1)} %get-tuple-element.23), channel_id=1, source_target_pairs={{0,31},{1,16},{2,17},{3,18},{4,19},{5,20},{6,21},{16,47},{17,32},{... | collective-permute-start | bytes 12296 | tf_op jit(solution)/shard_map/ppermute | solution.py:374
  31.4 0.0 copy-done.10
  31.5 1.5 %collective-permute-done.7.yb_ref = f32[8,128]{1,0:T(8,128)S(1)} collective-permute-done((f32[8,128]{1,0:T(8,128)S(1)}, f32[8,128]{1,0:T(8,128)S(1)}, u32[]{:S(2)}, u32[]{:S(2)}) %collective-permute-start.7) | collective-permute-done | bytes 4128 | tf_op jit(solution)/shard_map/ppermute | solution.py:374
  32.9 0.0 collective-permute-done.2.c_ref
  32.9 0.0 collective-permute-done.3.d_ref
  32.9 0.0 collective-permute-done.a_ref
  32.9 0.0 collective-permute-done.1.b_ref
  32.9 0.0 copy-done.8
  32.9 0.0 copy-done.9
  33.0 0.0 copy-done.7
  33.0 0.0 copy-done.4
  33.0 0.0 copy-done.5
  33.0 0.0 copy-done.6
  33.0 39.3 %propagate_and_pick.1 = (f32[72,32,256]{2,1,0:T(8,128)}, bf16[128,64,128]{2,1,0:T(8,128)(2,1)S(1)}) custom-call(f32[2]{0:T(128)S(1)} %copy-done.7, f32[72]{0:T(128)S(1)} %copy-done.8, f32[72]{0:T(128)S(1)} %copy-done.9, s32[16384]{0:T(1024)S(1)} %maximum_bitcast_fusion.cells_ref, f32[72,32,256]{2,1,0:T(8,128)S(1)} %bitcast.7, ...), custom_call_target="tpu_custom_call" | custom-call | tf_op jit(solution)/shard_map/propagate_and_pick/pallas_call | solution.py:379
  72.3 0.0 copy-start.1
  72.3 1.3 copy-done.1
  73.6 0.0 copy-start.11
  73.6 11.8 %all-to-all-start = ((bf16[128,64,128]{2,1,0:T(8,128)(2,1)}), bf16[128,64,128]{2,1,0:T(8,128)(2,1)S(1)}, u32[]{:S(2)}, u32[]{:S(2)}) async-start(bf16[128,64,128]{2,1,0:T(8,128)(2,1)} %copy-done.1), calls=%async_computation | async-start | bytes 4194304 | tf_op jit(solution)/shard_map/all_to_all | solution.py:396
  85.5 0.0 copy-done.11
  85.5 29.5 %all-to-all-done.values_ref = bf16[128,64,128]{2,1,0:T(8,128)(2,1)S(1)} async-done(((bf16[128,64,128]{2,1,0:T(8,128)(2,1)}), bf16[128,64,128]{2,1,0:T(8,128)(2,1)S(1)}, u32[]{:S(2)}, u32[]{:S(2)}) %all-to-all-start) | async-done | bytes 2097184 | tf_op jit(solution)/shard_map/all_to_all | solution.py:396
  114.9 19.8 %add_profiles.1 = f32[64,4096]{1,0:T(8,128)} custom-call(s32[16384]{0:T(1024)S(1)} %fusion.rows_ref, bf16[128,64,128]{2,1,0:T(8,128)(2,1)S(1)} %all-to-all-done.values_ref), custom_call_target="tpu_custom_call" | custom-call | tf_op jit(solution)/shard_map/add_profiles/pallas_call | solution.py:398
  (2 shorter events, 0.0 us)
Async XLA Ops:
  0.6 32.3 %copy-start.8 = (f32[72]{0:T(128)S(1)}, f32[72]{0:T(128)}, u32[]{:S(2)}) copy-start(f32[72]{0:T(128)} %constant.12.clone.cos_ref) | copy-start | bytes 868
  0.6 32.3 %copy-start.9 = (f32[72]{0:T(128)S(1)}, f32[72]{0:T(128)}, u32[]{:S(2)}) copy-start(f32[72]{0:T(128)} %constant.13.clone.sin_ref) | copy-start | bytes 868
  0.7 32.3 %copy-start.7 = (f32[2]{0:T(128)S(1)}, f32[2]{0:T(128)}, u32[]{:S(2)}) copy-start(f32[2]{0:T(128)} %courant_ref.1) | copy-start | bytes 28
  0.7 1.7 %copy-start = (f32[36,2,32,256]{3,2,1,0:T(8,128)S(1)}, f32[36,2,32,256]{3,2,1,0:T(8,128)}, u32[]{:S(2)}) copy-start(f32[36,2,32,256]{3,2,1,0:T(8,128)} %param.11) | copy-start | bytes 7077892
  2.3 0.8 copy-start.2
  3.1 0.8 copy-start.3
  3.9 27.6 %copy-start.10 = (s32[1,128,128]{2,1,0:T(8,128)S(1)}, s32[1,128,128]{2,1,0:T(8,128)}, u32[]{:S(2)}) copy-start(s32[1,128,128]{2,1,0:T(8,128)} %param.16) | copy-start | bytes 196612
  3.9 29.1 %copy-start.4 = (f32[64,72]{1,0:T(8,128)S(1)}, f32[64,72]{1,0:T(8,128)}, u32[]{:S(2)}) copy-start(f32[64,72]{1,0:T(8,128)} %kernel_ref.1) | copy-start | bytes 55300
  3.9 29.1 %copy-start.5 = (f32[40,128]{1,0:T(8,128)S(1)}, f32[40,128]{1,0:T(8,128)}, u32[]{:S(2)}) copy-start(f32[40,128]{1,0:T(8,128)} %constant.15.clone.subs_ref) | copy-start | bytes 61444
  3.9 29.1 %copy-start.6 = (f32[8,128]{1,0:T(8,128)S(1)}, f32[8,128]{1,0:T(8,128)}, u32[]{:S(2)}) copy-start(f32[8,128]{1,0:T(8,128)} %constant.14.clone.lanes_ref) | copy-start | bytes 12292
  4.4 17.6 %collective-permute-start.4 = (f32[8,128]{1,0:T(8,128)S(1)}, f32[8,128]{1,0:T(8,128)S(1)}, u32[]{:S(2)}, u32[]{:S(2)}) collective-permute-start(f32[8,128]{1,0:T(8,128)S(1)} %get-tuple-element.20), channel_id=1, source_target_pairs={{0,17},{8,25},{9,26},{10,27},{11,28},{12,29},{13,30},{14,31},{15,1... | collective-permute-start | bytes 12296 | tf_op jit(solution)/shard_map/ppermute | solution.py:374
  10.2 15.8 %collective-permute-start.5 = (f32[8,128]{1,0:T(8,128)S(1)}, f32[8,128]{1,0:T(8,128)S(1)}, u32[]{:S(2)}, u32[]{:S(2)}) collective-permute-start(f32[8,128]{1,0:T(8,128)S(1)} %get-tuple-element.21), channel_id=1, source_target_pairs={{1,18},{2,19},{3,20},{4,21},{5,22},{6,23},{7,24},{16,15},{17,0},{1... | collective-permute-start | bytes 12296 | tf_op jit(solution)/shard_map/ppermute | solution.py:374
  15.2 12.8 %collective-permute-start.6 = (f32[8,128]{1,0:T(8,128)S(1)}, f32[8,128]{1,0:T(8,128)S(1)}, u32[]{:S(2)}, u32[]{:S(2)}) collective-permute-start(f32[8,128]{1,0:T(8,128)S(1)} %get-tuple-element.22), channel_id=1, source_target_pairs={{7,22},{8,23},{9,24},{10,25},{11,26},{12,27},{13,28},{14,29},{15,3... | collective-permute-start | bytes 12296 | tf_op jit(solution)/shard_map/ppermute | solution.py:374
  17.1 15.8 %collective-permute-start.2 = (f32[32,128]{1,0:T(8,128)S(1)}, f32[32,128]{1,0:T(8,128)S(1)}, u32[]{:S(2)}, u32[]{:S(2)}) collective-permute-start(f32[32,128]{1,0:T(8,128)S(1)} %get-tuple-element.18.own_c_ref), channel_id=1, source_target_pairs={{0,1},{1,2},{2,3},{3,4},{4,5},{5,6},{6,7},{7,8},{8,9},{9,10},{10,1... | collective-permute-start | bytes 49160 | tf_op jit(solution)/shard_map/ppermute | solution.py:373
  17.2 15.7 %collective-permute-start.3 = (f32[32,128]{1,0:T(8,128)S(1)}, f32[32,128]{1,0:T(8,128)S(1)}, u32[]{:S(2)}, u32[]{:S(2)}) collective-permute-start(f32[32,128]{1,0:T(8,128)S(1)} %get-tuple-element.19.own_d_ref), channel_id=1, source_target_pairs={{1,0},{2,1},{3,2},{4,3},{5,4},{6,5},{7,6},{8,7},{9,8},{10,9},{11,1... | collective-permute-start | bytes 49160 | tf_op jit(solution)/shard_map/ppermute | solution.py:373
  22.0 11.0 %collective-permute-start = (f32[2,40,256]{2,1,0:T(8,128)S(1)}, f32[2,40,256]{2,1,0:T(8,128)S(1)}, u32[]{:S(2)}, u32[]{:S(2)}) collective-permute-start(f32[2,40,256]{2,1,0:T(8,128)S(1)} %get-tuple-element.16), channel_id=1, source_target_pairs={{0,16},{1,17},{2,18},{3,19},{4,20},{5,21},{6,22},{7,23},{16,32},{1... | collective-permute-start | bytes 245768 | tf_op jit(solution)/shard_map/ppermute | solution.py:372
  26.0 6.9 %collective-permute-start.1 = (f32[2,40,256]{2,1,0:T(8,128)S(1)}, f32[2,40,256]{2,1,0:T(8,128)S(1)}, u32[]{:S(2)}, u32[]{:S(2)}) collective-permute-start(f32[2,40,256]{2,1,0:T(8,128)S(1)} %get-tuple-element.17), channel_id=1, source_target_pairs={{8,24},{9,25},{10,26},{11,27},{12,28},{13,29},{14,30},{15,31},{16,... | collective-permute-start | bytes 245768 | tf_op jit(solution)/shard_map/ppermute | solution.py:372
  28.0 4.9 %collective-permute-start.7 = (f32[8,128]{1,0:T(8,128)S(1)}, f32[8,128]{1,0:T(8,128)S(1)}, u32[]{:S(2)}, u32[]{:S(2)}) collective-permute-start(f32[8,128]{1,0:T(8,128)S(1)} %get-tuple-element.23), channel_id=1, source_target_pairs={{0,31},{1,16},{2,17},{3,18},{4,19},{5,20},{6,21},{16,47},{17,32},{... | collective-permute-start | bytes 12296 | tf_op jit(solution)/shard_map/ppermute | solution.py:374
  72.3 1.3 copy-start.1
  73.6 11.8 %copy-start.11 = (s32[1,128,128]{2,1,0:T(8,128)S(1)}, s32[1,128,128]{2,1,0:T(8,128)}, u32[]{:S(2)}) copy-start(s32[1,128,128]{2,1,0:T(8,128)} %param.17) | copy-start | bytes 196612
  73.6 41.3 %all-to-all-start = ((bf16[128,64,128]{2,1,0:T(8,128)(2,1)}), bf16[128,64,128]{2,1,0:T(8,128)(2,1)S(1)}, u32[]{:S(2)}, u32[]{:S(2)}) async-start(bf16[128,64,128]{2,1,0:T(8,128)(2,1)} %copy-done.1), calls=%async_computation | async-start | bytes 4194304 | tf_op jit(solution)/shard_map/all_to_all | solution.py:396

commit v2 on v1

v2 whole, which is shorter than its diff:
```python
import functools
import math

import jax
import jax.numpy as jnp
import numpy as np
from jax import lax
from jax.experimental import pallas as pl
from jax.experimental.pallas import tpu as pltpu
from jax.sharding import PartitionSpec as P

DIRS = 36
FREQ = 2
PLANES = DIRS * FREQ
HALF = PLANES // 2
QUAD = PLANES // 4
OUT_DEV = 4096
N_ACC = 4
VMEM_LIMIT = 48 * 1024 * 1024


def exchange_pairs(n_lat, n_lon):
    def flat(j, i):
        return j * n_lon + i % n_lon

    row_first = [(j, j ^ 1) for j in range(n_lat)]
    row_second = []
    for i in range(n_lon):
        row_second += [(flat(0, i), flat(0, i)), (flat(n_lat - 1, i), flat(n_lat - 1, n_lon - 1 - i))]
        for j in range(1, n_lat - 1, 2):
            row_second += [(flat(j, i), flat(j + 1, i)), (flat(j + 1, i), flat(j, i))]
    column_first = [(i, i ^ 1) for i in range(n_lon)]
    column_second = [(i, (i + 1 if i % 2 else i - 1) % n_lon) for i in range(n_lon)]
    return row_first, row_second, column_first, column_second


def pack_kernel(x_ref, speed_ref, mask_ref, first_ref, second_ref, east_ref, west_ref, mov_ref, sea_ref, up_ref, down_ref):
    height, breadth = speed_ref.shape
    even = lax.axis_index("lat") % 2 == 0
    sea = mask_ref[...].astype(jnp.float32)
    moving = speed_ref[...] * sea
    mov_ref[...] = moving
    sea_ref[...] = sea
    for k in range(2):
        for q in range(HALF):
            up_ref[k, q : q + 1, :] = x_ref[q, height - 1 - k : height - k, :]
            down_ref[k, q : q + 1, :] = x_ref[HALF + q, k : k + 1, :]
        up_ref[k, HALF : HALF + 1, :] = moving[height - 1 - k : height - k, :]
        down_ref[k, HALF : HALF + 1, :] = moving[k : k + 1, :]
        up_ref[k, HALF + 1 : HALF + 2, :] = sea[height - 1 - k : height - k, :]
        down_ref[k, HALF + 1 : HALF + 2, :] = sea[k : k + 1, :]
        up_ref[k, HALF + 2 :, :] = jnp.zeros((2, breadth), jnp.float32)
        down_ref[k, HALF + 2 :, :] = jnp.zeros((2, breadth), jnp.float32)

    @pl.when(even)
    def _():
        first_ref[...] = up_ref[...]
        second_ref[...] = down_ref[...]

    @pl.when(jnp.logical_not(even))
    def _():
        first_ref[...] = down_ref[...]
        second_ref[...] = up_ref[...]

    lane = lax.broadcasted_iota(jnp.int32, (height, 128), 1)
    east = jnp.zeros((height, 128), jnp.float32)
    west = jnp.zeros((height, 128), jnp.float32)
    for q in range(HALF + 2):
        mine = lane // 2 == q
        if q < HALF:
            p_e = q if q < QUAD else q + HALF
            p_w = q + QUAD
            edge_e, edge_w = x_ref[p_e, :, breadth - 128 :], x_ref[p_w, :, :128]
        else:
            field = moving if q == HALF else sea
            edge_e, edge_w = field[:, breadth - 128 :], field[:, :128]
        east = jnp.where(mine, pltpu.roll(edge_e, (2 * q + 2) % 128, axis=1), east)
        west = jnp.where(mine, pltpu.roll(edge_w, 2 * q, axis=1), west)
    east_ref[...] = east
    west_ref[...] = west


def corner_kernel(n_lat, first_ref, second_ref, east_ref, west_ref, south_ref, north_ref, out_first, out_second):
    height = east_ref.shape[0]
    breadth = first_ref.shape[2]
    lat = lax.axis_index("lat")
    even = lat % 2 == 0

    @pl.when(even)
    def _():
        north_ref[...] = first_ref[...]
        south_ref[...] = second_ref[...]

    @pl.when(jnp.logical_not(even))
    def _():
        south_ref[...] = first_ref[...]
        north_ref[...] = second_ref[...]

    @pl.when(lat == 0)
    def _():
        south_ref[...] = jnp.zeros_like(south_ref)

    @pl.when(lat == n_lat - 1)
    def _():
        flip_i = lax.broadcasted_iota(jnp.int32, (breadth, breadth), 0)
        flip_j = lax.broadcasted_iota(jnp.int32, (breadth, breadth), 1)
        flip = (flip_i + flip_j == breadth - 1).astype(jnp.float32)
        for k in range(2):
            north_ref[k] = jnp.dot(
                north_ref[k], flip, precision=lax.Precision.HIGHEST, preferred_element_type=jnp.float32
            )

    plane = lax.broadcasted_iota(jnp.int32, (HALF + 4, 128), 0)
    lane = lax.broadcasted_iota(jnp.int32, (HALF + 4, 128), 1)
    south = south_ref[0] * south_ref[0, HALF : HALF + 1, :]
    north = north_ref[0] * north_ref[0, HALF : HALF + 1, :]

    def to_lanes(column, low, high, place):
        mine = (plane >= low) & (plane < high) & (lane == place)
        return jnp.where(mine, column, 0.0)

    east_edge = to_lanes(south[:, breadth - 1 :], 0, QUAD, 2 * plane + 1)
    east_edge += to_lanes(north[:, breadth - 1 :], QUAD, HALF, 2 * plane + 1)
    west_edge = to_lanes(south[:, :1], QUAD, HALF, 2 * plane - HALF)
    west_edge += to_lanes(north[:, :1], 0, QUAD, 2 * plane + HALF)
    east_edge = jnp.broadcast_to(jnp.sum(east_edge, axis=0, keepdims=True), (8, 128))
    west_edge = jnp.broadcast_to(jnp.sum(west_edge, axis=0, keepdims=True), (8, 128))
    even_lon = lax.axis_index("lon") % 2 == 0
    out_first[:height] = jnp.where(even_lon, east_ref[...], west_ref[...])
    out_second[:height] = jnp.where(even_lon, west_ref[...], east_ref[...])
    out_first[height:] = jnp.where(even_lon, east_edge, west_edge)
    out_second[height:] = jnp.where(even_lon, west_edge, east_edge)


def wave_kernel(slots, courant_ref, cos_ref, sin_ref, cells_ref, x_ref, mov_ref, sea_ref, kernel_ref,
                south_ref, north_ref, first_ref, second_ref, lanes_ref, subs_ref, out_ref, picked_ref,
                south0, south1, north0, north1, west0, west1, east0, east1, halves, table, owner_rows, wide_kernel,
                out_sems):
    height, breadth = mov_ref.shape
    c0, c1 = courant_ref[0], courant_ref[1]
    even_lon = lax.axis_index("lon") % 2 == 0
    from_west = jnp.where(even_lon, second_ref[...], first_ref[...])
    from_east = jnp.where(even_lon, first_ref[...], second_ref[...])
    corner_w, corner_e = from_west[height : height + 1], from_east[height : height + 1]

    lane = lax.broadcasted_iota(jnp.int32, (height, 128), 1)
    row = lax.broadcasted_iota(jnp.int32, (height, 128), 0)
    odd = lane % 2 == 1

    def columns(e0, near, far, corner, cx, cy, sign, flux0, flux1):
        mov = jnp.where(odd, e0[:, 2 * HALF + 1 : 2 * HALF + 2], e0[:, 2 * HALF : 2 * HALF + 1])
        sea = e0[:, 2 * HALF + 2 + near : 2 * HALF + 3 + near]
        f0 = mov * e0
        f_far = pltpu.roll(f0, 1 if near > far else 127, axis=1)
        f_south = jnp.where(row == 0, corner, pltpu.roll(f0, 1, axis=0))
        f_north = jnp.where(row == height - 1, corner, pltpu.roll(f0, height - 1, axis=0))
        div_x = cx * (f0 - f_far) if sign > 0 else cx * (f_far - f0)
        div_y = jnp.where(lane < HALF, cy * (f0 - f_south), cy * (f_north - f0))
        flux0[...] = f0
        flux1[...] = mov * (sea * ((e0 - div_x) - div_y))

    lanes = lanes_ref[...]
    lane_courant = jnp.where(lanes[4:5] > 0.5, c1, c0)
    columns(from_west[:height], 1, 0, corner_w, lanes[0:1] * lane_courant, lanes[1:2] * lane_courant, 1, west0, west1)
    columns(from_east[:height], 0, 1, corner_e, lanes[2:3] * lane_courant, lanes[3:4] * lane_courant, -1, east0, east1)

    wide = lax.broadcasted_iota(jnp.int32, (HALF + 4, breadth), 1)
    plane = lax.broadcasted_iota(jnp.int32, (HALF + 4, 1), 0)
    plane_l = lax.broadcasted_iota(jnp.int32, (HALF + 4, 128), 0)
    lane_l = lax.broadcasted_iota(jnp.int32, (HALF + 4, 128), 1)
    subs = subs_ref[...]
    sub_courant = jnp.where(plane % 2 == 1, c1, c0)

    def to_sublanes(corner, lane_of):
        return jnp.sum(jnp.where(lane_l == lane_of, corner, 0.0), axis=1, keepdims=True)

    def rows(near, far, first_west, west_corner, east_corner, cx, cy, sign, flux0, flux1):
        mov, sea = near[HALF : HALF + 1], near[HALF + 1 : HALF + 2]
        f0 = mov * near
        f_far = far[HALF : HALF + 1] * far
        f_west = jnp.where(wide == 0, west_corner, pltpu.roll(f0, 1, axis=1))
        f_east = jnp.where(wide == breadth - 1, east_corner, pltpu.roll(f0, breadth - 1, axis=1))
        from_west = (plane < QUAD) if first_west else (plane >= QUAD)
        div_x = jnp.where(from_west, cx * (f0 - f_west), cx * (f_east - f0))
        div_y = cy * (f0 - f_far) if sign > 0 else cy * (f_far - f0)
        flux0[...] = f0
        flux1[...] = mov * (sea * ((near - div_x) - div_y))

    sw = to_sublanes(corner_w, 2 * plane_l + 1)
    se = to_sublanes(corner_e, 2 * plane_l - HALF)
    ne = to_sublanes(corner_e, 2 * plane_l + HALF)
    nw = sw
    rows(south_ref[0], south_ref[1], True, sw, se, subs[:, 0:1] * sub_courant, subs[:, 1:2] * sub_courant, 1,
         south0, south1)
    rows(north_ref[0], north_ref[1], False, nw, ne, subs[:, 2:3] * sub_courant, subs[:, 3:4] * sub_courant, -1,
         north0, north1)

    moving = mov_ref[...]
    sea_all = sea_ref[...]
    lane_edge = lax.broadcasted_iota(jnp.int32, (height, 128), 1)
    row_edge = lax.broadcasted_iota(jnp.int32, (8, breadth), 0)

    def write_out(planes, h):
        target = out_ref.at[planes, pl.ds(h * 128, 128)]
        return pltpu.make_async_copy(halves.at[h, planes, :], target, out_sems.at[h])

    def quadrant(first, from_west, from_south, column0, column1, lane_first, row0, row1, row_first):
        def upstream(flux, column, line):
            if from_west:
                moved = pltpu.roll(flux, 1, axis=1)
                side = jnp.concatenate([jnp.where(lane_edge == 0, column, moved[:, :128]), moved[:, 128:]], axis=1)
            else:
                moved = pltpu.roll(flux, breadth - 1, axis=1)
                edge = jnp.where(lane_edge == 127, column, moved[:, breadth - 128 :])
                side = jnp.concatenate([moved[:, : breadth - 128], edge], axis=1)
            if from_south:
                moved = pltpu.roll(flux, 1, axis=0)
                below = jnp.concatenate([jnp.where(row_edge == 0, line, moved[:8]), moved[8:]], axis=0)
            else:
                moved = pltpu.roll(flux, height - 1, axis=0)
                edge = jnp.where(row_edge == 7, line, moved[height - 8 :])
                below = jnp.concatenate([moved[: height - 8], edge], axis=0)
            return side, below

        def step(t, carry):
            p = first + t
            courant = jnp.where(p % 2 == 1, c1, c0)
            cx = cos_ref[p] * courant
            cy = sin_ref[p] * courant
            place = lane_first + 2 * t
            turn = (128 - place) if from_west else (127 - place)
            energy = x_ref[p]
            for column_ref, row_ref in ((column0, row0), (column1, row1)):
                flux = moving * energy
                column = pltpu.roll(column_ref[...], turn, axis=1)
                side, below = upstream(flux, column, row_ref[pl.ds(row_first + t, 1), :])
                div_x = cx * (flux - side) if from_west else cx * (side - flux)
                div_y = cy * (flux - below) if from_south else cy * (below - flux)
                energy = sea_all * ((energy - div_x) - div_y)
            start = pl.ds(pl.multiple_of(p * height, height), height)
            for h in range(breadth // 128):
                halves[h, start, :] = energy[:, h * 128 : (h + 1) * 128]
            return carry

        lax.fori_loop(0, QUAD, step, 0, unroll=6)
        planes = pl.ds(first * height, QUAD * height)
        for h in range(breadth // 128):
            write_out(planes, h).start()

    quadrant(0, True, True, west0, west1, 1, south0, south1, 0)
    quadrant(QUAD, False, True, east0, east1, 0, south0, south1, QUAD)
    quadrant(2 * QUAD, False, False, east0, east1, HALF, north0, north1, 0)
    quadrant(3 * QUAD, True, False, west0, west1, HALF + 1, north0, north1, QUAD)

    pad = jnp.zeros((8, 128), jnp.bfloat16)
    wide_kernel[...] = jnp.zeros((128, 128), jnp.float32)
    wide_kernel[:64, :PLANES] = kernel_ref[...]
    wide_kernel[64:, :PLANES] = kernel_ref[...]
    turned = wide_kernel[...].T[:PLANES]
    weight_high = turned.astype(jnp.bfloat16)
    weight_low = (turned - weight_high.astype(jnp.float32)).astype(jnp.bfloat16)
    weight = jnp.concatenate([weight_high, pad, weight_high, pad, weight_low, pad], axis=0)

    group = 8

    @pl.loop(0, height // group)
    def _(r):
        blocks = []
        for k in range(group):
            for h in range(breadth // 128):
                spectra = halves[h, pl.ds(r * group + k, PLANES, stride=height), :]
                high = spectra.astype(jnp.bfloat16)
                low = (spectra - high.astype(jnp.float32)).astype(jnp.bfloat16)
                blocks.append(jnp.concatenate([high, pad, low, pad, high, pad], axis=0))
        stacked = jnp.concatenate(blocks, axis=1)
        profile = lax.dot_general(stacked, weight, (((0,), (0,)), ((), ())), preferred_element_type=jnp.float32)
        start = pl.multiple_of(r * group * breadth, 128)
        table[pl.ds(start, group * breadth), :] = profile

    first_half = lax.broadcasted_iota(jnp.int32, (1, 128), 1) < 64
    cell_count = height * breadth
    table[cell_count:, :] = jnp.zeros((8, 128), jnp.float32)
    owner_rows[...] = jnp.zeros_like(owner_rows)

    @pl.loop(0, picked_ref.shape[0])
    def _(owner):
        base = owner * slots
        for s in range(0, slots, 32):

            @pl.when(cells_ref[base + s] < cell_count)
            def _():
                for g in range(s, s + 32, 16):
                    for j in range(8):
                        one, two = cells_ref[base + g + j], cells_ref[base + g + 8 + j]
                        line = jnp.where(first_half, table[pl.ds(one, 1), :], table[pl.ds(two, 1), :])
                        owner_rows[g // 2 + j : g // 2 + j + 1, :] = line

        picked_ref[owner] = owner_rows[...].astype(jnp.bfloat16)

    whole = pl.ds(0, PLANES * height)
    for h in range(breadth // 128):
        write_out(whole, h).wait()


def add_kernel(slots, rows_ref, values_ref, out_ref, lines, *sums):
    n_acc = len(sums) // 2
    tile = out_ref.shape[1]
    block = 512
    for total in sums:

        @pl.loop(0, tile // block)
        def _(i):
            total[pl.ds(pl.multiple_of(i * block, block), block), :] = jnp.zeros((block, 128), jnp.float32)

    @pl.loop(0, values_ref.shape[0])
    def _(source):
        lines[...] = values_ref[source].astype(jnp.float32)
        for g in range(slots // 16):
            for j in range(8):
                one = rows_ref[source * slots + g * 16 + j]
                two = rows_ref[source * slots + g * 16 + 8 + j]
                line = lines[g * 8 + j : g * 8 + j + 1, :]
                left, right = sums[j % n_acc], sums[n_acc + j % n_acc]
                left[pl.ds(one, 1), :] = left[pl.ds(one, 1), :] + line
                right[pl.ds(two, 1), :] = right[pl.ds(two, 1), :] + line

    first_half = lax.broadcasted_iota(jnp.int32, (block, 128), 1) < 64

    @pl.loop(0, tile // block)
    def _(i):
        here = pl.ds(pl.multiple_of(i * block, block), block)
        left, right = sums[0][here, :], sums[n_acc][here, :]
        for q in range(1, n_acc):
            left = left + sums[q][here, :]
            right = right + sums[n_acc + q][here, :]
        both = jnp.where(first_half, left, right).T
        out_ref[:, here] = both[:64] + both[64:]


def constant_tables():
    heading = (np.arange(DIRS) + 0.5) * (2.0 * math.pi / DIRS)
    cos = np.repeat(np.cos(heading), FREQ)
    sin = np.repeat(np.sin(heading), FREQ)
    lanes = np.zeros((8, 128))
    q = np.arange(HALF)
    from_west = np.where(q < QUAD, q, q + HALF)
    from_east = q + QUAD
    for column in range(2):
        lanes[0, 2 * q + column] = cos[from_west]
        lanes[1, 2 * q + column] = sin[from_west]
        lanes[2, 2 * q + column] = cos[from_east]
        lanes[3, 2 * q + column] = sin[from_east]
        lanes[4, 2 * q + column] = q % 2
    subs = np.zeros((HALF + 4, 128))
    subs[:HALF, 0], subs[:HALF, 1] = cos[:HALF], sin[:HALF]
    subs[:HALF, 2], subs[:HALF, 3] = cos[HALF:], sin[HALF:]
    return [t.astype(np.float32) for t in (cos, sin, lanes, subs)]


def body(n_lat, n_lon, spectrum, speed_factor, land_sea_mask, courant, depth_kernel, send_rows, recv_rows):
    height, breadth = speed_factor.shape
    devices, slots = send_rows.shape[1:]
    x = spectrum.reshape(PLANES, height, breadth)
    f32 = jnp.float32
    vmem = pl.BlockSpec(memory_space=pltpu.VMEM)
    smem = pl.BlockSpec(memory_space=pltpu.SMEM)
    params = pltpu.CompilerParams(vmem_limit_bytes=VMEM_LIMIT)

    both = ("lat", "lon")

    def shape(*dims, kind=f32):
        return jax.ShapeDtypeStruct(dims, kind)

    row_message = shape(2, HALF + 4, breadth)
    columns = shape(height, 128)
    column_message = shape(height + 8, 128)
    row_first, row_second, column_first, column_second = exchange_pairs(n_lat, n_lon)
    first, second, east, west, moving, sea = pl.pallas_call(
        pack_kernel,
        out_shape=[row_message] * 2 + [columns] * 2 + [shape(height, breadth)] * 2,
        in_specs=[vmem] * 3,
        out_specs=[vmem] * 6,
        scratch_shapes=[pltpu.VMEM((2, HALF + 4, breadth), f32)] * 2,
        compiler_params=params,
        name="pack_halos",
    )(x, speed_factor, land_sea_mask)
    first = lax.ppermute(first, "lat", row_first)
    second = lax.ppermute(second, both, row_second)
    south, north, first, second = pl.pallas_call(
        functools.partial(corner_kernel, n_lat),
        out_shape=[row_message] * 2 + [column_message] * 2,
        in_specs=[vmem] * 4,
        out_specs=[vmem] * 4,
        compiler_params=params,
        name="add_corners",
    )(first, second, east, west)
    first = lax.ppermute(first, "lon", column_first)
    second = lax.ppermute(second, "lon", column_second)

    cos, sin, lanes, subs = constant_tables()
    cells = jnp.where(send_rows < 0, height * breadth, send_rows).reshape(-1)
    targets = jnp.where(recv_rows < 0, OUT_DEV, recv_rows).reshape(-1)
    propagated, picked = pl.pallas_call(
        functools.partial(wave_kernel, slots),
        out_shape=[shape(PLANES * height, breadth), shape(devices, slots // 2, 128, kind=jnp.bfloat16)],
        in_specs=[smem] * 4 + [vmem] * 10,
        out_specs=[pl.BlockSpec(memory_space=pl.ANY), vmem],
        scratch_shapes=[pltpu.VMEM((HALF + 4, breadth), f32)] * 4
        + [pltpu.VMEM((height, 128), f32)] * 4
        + [
            pltpu.VMEM((breadth // 128, PLANES * height, 128), f32),
            pltpu.VMEM((height * breadth + 8, 128), f32),
            pltpu.VMEM((slots // 2, 128), f32),
            pltpu.VMEM((128, 128), f32),
            pltpu.SemaphoreType.DMA((breadth // 128,)),
        ],
        compiler_params=params,
        name="propagate_and_pick",
    )(courant, cos, sin, cells, x, moving, sea, depth_kernel, south, north, first, second, lanes, subs)

    received = lax.all_to_all(picked, both, split_axis=0, concat_axis=0, tiled=True)

    stokes = pl.pallas_call(
        functools.partial(add_kernel, slots),
        out_shape=shape(depth_kernel.shape[0], OUT_DEV),
        in_specs=[smem, vmem],
        out_specs=vmem,
        scratch_shapes=[pltpu.VMEM((slots // 2, 128), f32)] + [pltpu.VMEM((OUT_DEV + 8, 128), f32)] * (2 * N_ACC),
        compiler_params=params,
        name="add_profiles",
    )(targets, received)
    return propagated.reshape(DIRS, FREQ, height, breadth), stokes


def solution(mesh):
    placed = (
        P(None, None, "lat", "lon"),
        P("lat", "lon"),
        P("lat", "lon"),
        P(),
        P(),
        P(("lat", "lon"), None, None),
        P(("lat", "lon"), None, None),
    )
    return jax.shard_map(
        functools.partial(body, mesh.shape["lat"], mesh.shape["lon"]),
        mesh=mesh,
        in_specs=placed,
        out_specs=(P(None, None, "lat", "lon"), P(None, ("lat", "lon"))),
        check_vma=False,
    )
```

time: 135 us -> 104 us (0.77)
  Pallas kernels: 59.6 us -> 42.1 us
  starting transfers between devices: 38.8 us -> 23 us
  waiting for transfers between devices: 30.9 us -> 33.2 us
    pallas_call x2 -> x3, Pallas kernels: 39.8 us -> 22.3 us  [the longest x1 21.7 us: body(): pl.pallas_call(functools.partial(wave_kernel, slots), out_shape=[shape(PL...]
    ppermute x8 -> x4, starting transfers between devices: 27 us -> 11.2 us  [the longest x1 4.69 us: body(): second = lax.ppermute(second, 'lon', column_second)]
    ppermute x8 -> x4, waiting for transfers between devices: 1.47 us -> 3.74 us  [the longest x1 2.5 us: body(): second = lax.ppermute(second, both, row_second)]
    unnamed x24 -> x26, local copies, waits for them, and re-layouts: 4.55 us -> 4.56 us
  transfers between devices with their start and end apart: 9 -> 5, of which waited for: 2 -> 3; matrix products, arithmetic and copies ran while one was open for 0% -> 0% of each run, Pallas kernels for 0% -> 0%
where the time goes in v2:
time: 104 us
  Pallas kernels  42.1 us (40%)
  waiting for transfers between devices  33.2 us (32%)
  starting transfers between devices  23 us (22%)
  local copies, waits for them, and re-layouts  4.56 us (4%)
    all_to_all x1, waiting for transfers between devices, body(): lax.all_to_all(picked, both, split_axis=0, concat_axis=0, tiled=True)  29.5 us
    pallas_call x1, Pallas kernels, body(): pl.pallas_call(functools.partial(wave_kernel, slots), out_shape=[shape(PL...  21.7 us
    pallas_call x1, Pallas kernels, body(): pl.pallas_call(functools.partial(add_kernel, slots), out_shape=shape(dept...  19.8 us
    all_to_all x1, starting transfers between devices, body(): lax.all_to_all(picked, both, split_axis=0, concat_axis=0, tiled=True)  11.7 us
    ppermute x1, starting transfers between devices, body(): second = lax.ppermute(second, 'lon', column_second)  4.69 us
    unnamed x26, local copies, waits for them, and re-layouts  4.56 us
    ppermute x1, starting transfers between devices, body(): second = lax.ppermute(second, both, row_second)  3.23 us
    ppermute x1, waiting for transfers between devices, body(): second = lax.ppermute(second, both, row_second)  2.5 us
  transfers between devices with their start and end apart: 5, of which 3 were waited for; matrix products, arithmetic and copies ran while one was open for 0% of the time, Pallas kernels for 0%

profile of v2, /device:TPU:1, one launch (start us, length us, event | category | flops | bytes accessed | tf_op | source)
XLA Modules:
  0.0 103.7 jit_solution(17263032387165457567)
XLA Ops:
  0.6 0.0 copy-start.9
  0.6 0.0 copy-start.10
  0.7 0.0 copy-start.8
  0.7 0.0 copy-start
  0.7 1.7 %copy-done = f32[36,2,32,256]{3,2,1,0:T(8,128)S(1)} copy-done((f32[36,2,32,256]{3,2,1,0:T(8,128)S(1)}, f32[36,2,32,256]{3,2,1,0:T(8,128)}, u32[]{:S(2)}) %copy-start) | copy-done | bytes 2359320
  2.3 0.0 copy-start.3
  2.4 0.8 copy-done.3
  3.1 0.0 copy-start.4
  3.1 0.8 copy-done.4
  3.9 0.0 copy-start.11
  3.9 0.0 copy-start.1
  3.9 0.0 copy-start.5
  3.9 0.0 copy-start.6
  3.9 0.0 copy-start.7
  3.9 0.5 pack_halos.1
  4.4 1.5 %collective-permute-start = (f32[2,40,256]{2,1,0:T(8,128)S(1)}, f32[2,40,256]{2,1,0:T(8,128)S(1)}, u32[]{:S(2)}, u32[]{:S(2)}) collective-permute-start(f32[2,40,256]{2,1,0:T(8,128)S(1)} %get-tuple-element.16), channel_id=1, source_target_pairs={{0,16},{16,0},{32,48},{48,32},{64,80},{80,64},{96,112},{112,96},{1... | collective-permute-start | bytes 245768 | tf_op jit(solution)/shard_map/ppermute | solution.py:387
  5.9 3.2 %collective-permute-start.1 = (f32[2,40,256]{2,1,0:T(8,128)S(1)}, f32[2,40,256]{2,1,0:T(8,128)S(1)}, u32[]{:S(2)}, u32[]{:S(2)}) collective-permute-start(f32[2,40,256]{2,1,0:T(8,128)S(1)} %get-tuple-element.17), channel_id=1, source_target_pairs={{0,0},{112,127},{16,32},{32,16},{48,64},{64,48},{80,96},{96,80},{1... | collective-permute-start | bytes 245768 | tf_op jit(solution)/shard_map/ppermute | solution.py:388
  9.1 0.0 collective-permute-done.first_ref
  9.1 2.5 %collective-permute-done.1.second_ref = f32[2,40,256]{2,1,0:T(8,128)S(1)} collective-permute-done((f32[2,40,256]{2,1,0:T(8,128)S(1)}, f32[2,40,256]{2,1,0:T(8,128)S(1)}, u32[]{:S(2)}, u32[]{:S(2)}) %collective-permute-start.1) | collective-permute-done | bytes 81952 | tf_op jit(solution)/shard_map/ppermute | solution.py:388
  11.6 0.1 add_corners.1
  11.7 1.8 %collective-permute-start.2 = (f32[40,128]{1,0:T(8,128)S(1)}, f32[40,128]{1,0:T(8,128)S(1)}, u32[]{:S(2)}, u32[]{:S(2)}) collective-permute-start(f32[40,128]{1,0:T(8,128)S(1)} %get-tuple-element.22), channel_id=1, source_target_pairs={{0,1},{1,0},{2,3},{3,2},{4,5},{5,4},{6,7},{7,6},{8,9},{9,8},{10,11... | collective-permute-start | bytes 61448 | tf_op jit(solution)/shard_map/ppermute | solution.py:397
  13.5 4.7 %collective-permute-start.3 = (f32[40,128]{1,0:T(8,128)S(1)}, f32[40,128]{1,0:T(8,128)S(1)}, u32[]{:S(2)}, u32[]{:S(2)}) collective-permute-start(f32[40,128]{1,0:T(8,128)S(1)} %get-tuple-element.23), channel_id=1, source_target_pairs={{0,15},{1,2},{2,1},{3,4},{4,3},{5,6},{6,5},{7,8},{8,7},{9,10},{10,... | collective-permute-start | bytes 61448 | tf_op jit(solution)/shard_map/ppermute | solution.py:398
  18.2 0.0 copy-done.11
  18.2 0.0 collective-permute-done.2.first_ref
  18.3 1.2 %collective-permute-done.3.second_ref = f32[40,128]{1,0:T(8,128)S(1)} collective-permute-done((f32[40,128]{1,0:T(8,128)S(1)}, f32[40,128]{1,0:T(8,128)S(1)}, u32[]{:S(2)}, u32[]{:S(2)}) %collective-permute-start.3) | collective-permute-done | bytes 20512 | tf_op jit(solution)/shard_map/ppermute | solution.py:398
  19.5 0.0 copy-done.9
  19.5 0.0 copy-done.10
  19.5 0.0 copy-done.8
  19.5 0.0 copy-done.1
  19.5 0.0 copy-done.5
  19.5 0.0 copy-done.6
  19.5 0.0 copy-done.7
  19.5 21.7 %propagate_and_pick.1 = (f32[2304,256]{1,0:T(8,128)}, bf16[128,64,128]{2,1,0:T(8,128)(2,1)S(1)}) custom-call(f32[2]{0:T(128)S(1)} %copy-done.8, f32[72]{0:T(128)S(1)} %copy-done.9, f32[72]{0:T(128)S(1)} %copy-done.10, s32[16384]{0:T(1024)S(1)} %fusion.cells_ref, f32[72,32,256]{2,1,0:T(8,128)S(1)} %bitcast.7, f32[32,256]{1,0:T(8,128)S(1)} %get-tuple-element.14.mov_ref, ...), custom_call_target="tpu_custom_call" | custom-call | tf_op jit(solution)/shard_map/propagate_and_pick/pallas_call | solution.py:403
  41.2 0.0 copy-start.2
  41.3 1.3 %copy-done.2 = bf16[128,64,128]{2,1,0:T(8,128)(2,1)} copy-done((bf16[128,64,128]{2,1,0:T(8,128)(2,1)}, bf16[128,64,128]{2,1,0:T(8,128)(2,1)S(1)}, u32[]{:S(2)}) %copy-start.2) | copy-done | bytes 2097176
  42.6 0.0 copy-start.12
  42.6 11.7 %all-to-all-start = ((bf16[128,64,128]{2,1,0:T(8,128)(2,1)}), bf16[128,64,128]{2,1,0:T(8,128)(2,1)S(1)}, u32[]{:S(2)}, u32[]{:S(2)}) async-start(bf16[128,64,128]{2,1,0:T(8,128)(2,1)} %copy-done.2), calls=%async_computation | async-start | bytes 4194304 | tf_op jit(solution)/shard_map/all_to_all | solution.py:421
  54.3 0.0 copy-done.12
  54.4 29.5 %all-to-all-done.values_ref = bf16[128,64,128]{2,1,0:T(8,128)(2,1)S(1)} async-done(((bf16[128,64,128]{2,1,0:T(8,128)(2,1)}), bf16[128,64,128]{2,1,0:T(8,128)(2,1)S(1)}, u32[]{:S(2)}, u32[]{:S(2)}) %all-to-all-start) | async-done | bytes 2097184 | tf_op jit(solution)/shard_map/all_to_all | solution.py:421
  83.8 19.8 %add_profiles.1 = f32[64,4096]{1,0:T(8,128)} custom-call(s32[16384]{0:T(1024)S(1)} %fusion.1.rows_ref, bf16[128,64,128]{2,1,0:T(8,128)(2,1)S(1)} %all-to-all-done.values_ref), custom_call_target="tpu_custom_call" | custom-call | tf_op jit(solution)/shard_map/add_profiles/pallas_call | solution.py:423
  (2 shorter events, 0.0 us)
Async XLA Ops:
  0.6 18.9 %copy-start.9 = (f32[72]{0:T(128)S(1)}, f32[72]{0:T(128)}, u32[]{:S(2)}) copy-start(f32[72]{0:T(128)} %constant.14.clone.cos_ref) | copy-start | bytes 868
  0.6 18.9 %copy-start.10 = (f32[72]{0:T(128)S(1)}, f32[72]{0:T(128)}, u32[]{:S(2)}) copy-start(f32[72]{0:T(128)} %constant.15.clone.sin_ref) | copy-start | bytes 868
  0.7 18.8 %copy-start.8 = (f32[2]{0:T(128)S(1)}, f32[2]{0:T(128)}, u32[]{:S(2)}) copy-start(f32[2]{0:T(128)} %courant_ref.1) | copy-start | bytes 28
  0.7 1.7 %copy-start = (f32[36,2,32,256]{3,2,1,0:T(8,128)S(1)}, f32[36,2,32,256]{3,2,1,0:T(8,128)}, u32[]{:S(2)}) copy-start(f32[36,2,32,256]{3,2,1,0:T(8,128)} %param.11) | copy-start | bytes 7077892
  2.3 0.8 copy-start.3
  3.1 0.8 copy-start.4
  3.9 14.4 %copy-start.11 = (s32[1,128,128]{2,1,0:T(8,128)S(1)}, s32[1,128,128]{2,1,0:T(8,128)}, u32[]{:S(2)}) copy-start(s32[1,128,128]{2,1,0:T(8,128)} %param.16) | copy-start | bytes 196612
  3.9 15.6 %copy-start.1 = (f32[36,2,32,256]{3,2,1,0:T(8,128)S(1)}, f32[36,2,32,256]{3,2,1,0:T(8,128)}, u32[]{:S(2)}) copy-start(f32[36,2,32,256]{3,2,1,0:T(8,128)} %param.11) | copy-start | bytes 7077892
  3.9 15.6 %copy-start.5 = (f32[64,72]{1,0:T(8,128)S(1)}, f32[64,72]{1,0:T(8,128)}, u32[]{:S(2)}) copy-start(f32[64,72]{1,0:T(8,128)} %kernel_ref.1) | copy-start | bytes 55300
  3.9 15.7 %copy-start.6 = (f32[40,128]{1,0:T(8,128)S(1)}, f32[40,128]{1,0:T(8,128)}, u32[]{:S(2)}) copy-start(f32[40,128]{1,0:T(8,128)} %constant.17.clone.subs_ref) | copy-start | bytes 61444
  3.9 15.7 %copy-start.7 = (f32[8,128]{1,0:T(8,128)S(1)}, f32[8,128]{1,0:T(8,128)}, u32[]{:S(2)}) copy-start(f32[8,128]{1,0:T(8,128)} %constant.16.clone.lanes_ref) | copy-start | bytes 12292
  4.4 4.7 %collective-permute-start = (f32[2,40,256]{2,1,0:T(8,128)S(1)}, f32[2,40,256]{2,1,0:T(8,128)S(1)}, u32[]{:S(2)}, u32[]{:S(2)}) collective-permute-start(f32[2,40,256]{2,1,0:T(8,128)S(1)} %get-tuple-element.16), channel_id=1, source_target_pairs={{0,16},{16,0},{32,48},{48,32},{64,80},{80,64},{96,112},{112,96},{1... | collective-permute-start | bytes 245768 | tf_op jit(solution)/shard_map/ppermute | solution.py:387
  5.9 5.7 %collective-permute-start.1 = (f32[2,40,256]{2,1,0:T(8,128)S(1)}, f32[2,40,256]{2,1,0:T(8,128)S(1)}, u32[]{:S(2)}, u32[]{:S(2)}) collective-permute-start(f32[2,40,256]{2,1,0:T(8,128)S(1)} %get-tuple-element.17), channel_id=1, source_target_pairs={{0,0},{112,127},{16,32},{32,16},{48,64},{64,48},{80,96},{96,80},{1... | collective-permute-start | bytes 245768 | tf_op jit(solution)/shard_map/ppermute | solution.py:388
  11.7 6.5 %collective-permute-start.2 = (f32[40,128]{1,0:T(8,128)S(1)}, f32[40,128]{1,0:T(8,128)S(1)}, u32[]{:S(2)}, u32[]{:S(2)}) collective-permute-start(f32[40,128]{1,0:T(8,128)S(1)} %get-tuple-element.22), channel_id=1, source_target_pairs={{0,1},{1,0},{2,3},{3,2},{4,5},{5,4},{6,7},{7,6},{8,9},{9,8},{10,11... | collective-permute-start | bytes 61448 | tf_op jit(solution)/shard_map/ppermute | solution.py:397
  13.5 6.0 %collective-permute-start.3 = (f32[40,128]{1,0:T(8,128)S(1)}, f32[40,128]{1,0:T(8,128)S(1)}, u32[]{:S(2)}, u32[]{:S(2)}) collective-permute-start(f32[40,128]{1,0:T(8,128)S(1)} %get-tuple-element.23), channel_id=1, source_target_pairs={{0,15},{1,2},{2,1},{3,4},{4,3},{5,6},{6,5},{7,8},{8,7},{9,10},{10,... | collective-permute-start | bytes 61448 | tf_op jit(solution)/shard_map/ppermute | solution.py:398
  41.2 1.3 %copy-start.2 = (bf16[128,64,128]{2,1,0:T(8,128)(2,1)}, bf16[128,64,128]{2,1,0:T(8,128)(2,1)S(1)}, u32[]{:S(2)}) copy-start(bf16[128,64,128]{2,1,0:T(8,128)(2,1)S(1)} %get-tuple-element.25) | copy-start | bytes 6291460
  42.6 11.8 %copy-start.12 = (s32[1,128,128]{2,1,0:T(8,128)S(1)}, s32[1,128,128]{2,1,0:T(8,128)}, u32[]{:S(2)}) copy-start(s32[1,128,128]{2,1,0:T(8,128)} %param.17) | copy-start | bytes 196612
  42.6 41.3 %all-to-all-start = ((bf16[128,64,128]{2,1,0:T(8,128)(2,1)}), bf16[128,64,128]{2,1,0:T(8,128)(2,1)S(1)}, u32[]{:S(2)}, u32[]{:S(2)}) async-start(bf16[128,64,128]{2,1,0:T(8,128)(2,1)} %copy-done.2), calls=%async_computation | async-start | bytes 4194304 | tf_op jit(solution)/shard_map/all_to_all | solution.py:421

commit v3 on v2

--- a/solution.py
+++ b/solution.py
@@ -16,6 +16,7 @@
 QUAD = PLANES // 4
 OUT_DEV = 4096
 N_ACC = 4
+WINDOW = 1024
 VMEM_LIMIT = 48 * 1024 * 1024
 
 
@@ -34,17 +35,36 @@
     return row_first, row_second, column_first, column_second
 
 
-def pack_kernel(x_ref, speed_ref, mask_ref, first_ref, second_ref, east_ref, west_ref, mov_ref, sea_ref, up_ref, down_ref):
+def pack_kernel(x_hbm, speed_hbm, mask_hbm, first_ref, second_ref, east_ref, west_ref, mov_ref, sea_ref,
+                up_ref, down_ref, top_rows, bottom_rows, east_edge, west_edge, speed_ref, mask_ref, sems):
     height, breadth = speed_ref.shape
+    first_quad, mid_quads, last_quad = pl.ds(0, QUAD), pl.ds(QUAD, HALF), pl.ds(3 * QUAD, QUAD)
+    last_lanes = pl.ds(breadth - 128, 128)
+    copies = [
+        pltpu.make_async_copy(source, target, sems.at[k])
+        for k, (source, target) in enumerate((
+            (speed_hbm, speed_ref),
+            (mask_hbm, mask_ref),
+            (x_hbm.at[pl.ds(0, HALF), pl.ds(height - 8, 8), :], top_rows),
+            (x_hbm.at[pl.ds(HALF, HALF), pl.ds(0, 8), :], bottom_rows),
+            (x_hbm.at[first_quad, :, last_lanes], east_edge.at[first_quad]),
+            (x_hbm.at[last_quad, :, last_lanes], east_edge.at[pl.ds(QUAD, QUAD)]),
+            (x_hbm.at[mid_quads, :, pl.ds(0, 128)], west_edge),
+        ))
+    ]
+    for copy in copies:
+        copy.start()
     even = lax.axis_index("lat") % 2 == 0
+    for copy in copies[:4]:
+        copy.wait()
     sea = mask_ref[...].astype(jnp.float32)
     moving = speed_ref[...] * sea
     mov_ref[...] = moving
     sea_ref[...] = sea
     for k in range(2):
         for q in range(HALF):
-            up_ref[k, q : q + 1, :] = x_ref[q, height - 1 - k : height - k, :]
-            down_ref[k, q : q + 1, :] = x_ref[HALF + q, k : k + 1, :]
+            up_ref[k, q : q + 1, :] = top_rows[q, 7 - k : 8 - k, :]
+            down_ref[k, q : q + 1, :] = bottom_rows[q, k : k + 1, :]
         up_ref[k, HALF : HALF + 1, :] = moving[height - 1 - k : height - k, :]
         down_ref[k, HALF : HALF + 1, :] = moving[k : k + 1, :]
         up_ref[k, HALF + 1 : HALF + 2, :] = sea[height - 1 - k : height - k, :]
@@ -62,15 +82,15 @@
         first_ref[...] = down_ref[...]
         second_ref[...] = up_ref[...]
 
+    for copy in copies[4:]:
+        copy.wait()
     lane = lax.broadcasted_iota(jnp.int32, (height, 128), 1)
     east = jnp.zeros((height, 128), jnp.float32)
     west = jnp.zeros((height, 128), jnp.float32)
     for q in range(HALF + 2):
         mine = lane // 2 == q
         if q < HALF:
-            p_e = q if q < QUAD else q + HALF
-            p_w = q + QUAD
-            edge_e, edge_w = x_ref[p_e, :, breadth - 128 :], x_ref[p_w, :, :128]
+            edge_e, edge_w = east_edge[q], west_edge[q]
         else:
             field = moving if q == HALF else sea
             edge_e, edge_w = field[:, breadth - 128 :], field[:, :128]
@@ -132,10 +152,32 @@
     out_second[height:] = jnp.where(even_lon, west_edge, east_edge)
 
 
-def wave_kernel(slots, courant_ref, cos_ref, sin_ref, cells_ref, x_ref, mov_ref, sea_ref, kernel_ref,
+def for_windows(list_ref, window, sems, work):
+    count = list_ref.shape[0] // WINDOW
+
+    def fetch(i, w):
+        source = list_ref.at[pl.ds(pl.multiple_of(i * WINDOW, WINDOW), WINDOW)]
+        return pltpu.make_async_copy(source, window.at[pl.ds(w * WINDOW, WINDOW)], sems.at[w])
+
+    for w in range(2):
+        fetch(w, w).start()
+
+    @pl.loop(0, count // 2)
+    def _(t):
+        for w in range(2):
+            i = 2 * t + w
+            fetch(i, w).wait()
+            work(lambda k, start=w * WINDOW: window[start + k], i)
+
+            @pl.when(i + 2 < count)
+            def _():
+                fetch(i + 2, w).start()
+
+
+def wave_kernel( courant_ref, cos_ref, sin_ref, cells_ref, x_ref, mov_ref, sea_ref, kernel_ref,
                 south_ref, north_ref, first_ref, second_ref, lanes_ref, subs_ref, out_ref, picked_ref,
-                south0, south1, north0, north1, west0, west1, east0, east1, halves, table, owner_rows, wide_kernel,
-                out_sems):
+                south0, south1, north0, north1, west0, west1, east0, east1, halves, table, lines, picks, wide_kernel,
+                window, out_sems, window_sems, pick_sem):
     height, breadth = mov_ref.shape
     c0, c1 = courant_ref[0], courant_ref[1]
     even_lon = lax.axis_index("lon") % 2 == 0
@@ -278,52 +320,55 @@
         table[pl.ds(start, group * breadth), :] = profile
 
     first_half = lax.broadcasted_iota(jnp.int32, (1, 128), 1) < 64
-    cell_count = height * breadth
-    table[cell_count:, :] = jnp.zeros((8, 128), jnp.float32)
-    owner_rows[...] = jnp.zeros_like(owner_rows)
-
-    @pl.loop(0, picked_ref.shape[0])
-    def _(owner):
-        base = owner * slots
-        for s in range(0, slots, 32):
-
-            @pl.when(cells_ref[base + s] < cell_count)
-            def _():
-                for g in range(s, s + 32, 16):
-                    for j in range(8):
-                        one, two = cells_ref[base + g + j], cells_ref[base + g + 8 + j]
-                        line = jnp.where(first_half, table[pl.ds(one, 1), :], table[pl.ds(two, 1), :])
-                        owner_rows[g // 2 + j : g // 2 + j + 1, :] = line
-
-        picked_ref[owner] = owner_rows[...].astype(jnp.bfloat16)
-
+    half = WINDOW // 2
+
+    def pick(cell, i):
+        for g in range(WINDOW // 16):
+            for j in range(8):
+                one, two = cell(16 * g + j), cell(16 * g + 8 + j)
+                line = jnp.where(first_half, table[pl.ds(one, 1), :], table[pl.ds(two, 1), :])
+                lines[8 * g + j : 8 * g + j + 1, :] = line
+        here = pl.ds(pl.multiple_of(i * half, half), half)
+        picks[here, :] = lines[...].astype(jnp.bfloat16)
+        pltpu.make_async_copy(picks.at[here, :], picked_ref.at[here, :], pick_sem).start()
+
+    for_windows(cells_ref, window, window_sems, pick)
+    pltpu.make_async_copy(picks, picked_ref, pick_sem).wait()
     whole = pl.ds(0, PLANES * height)
     for h in range(breadth // 128):
         write_out(whole, h).wait()
 
 
-def add_kernel(slots, rows_ref, values_ref, out_ref, lines, *sums):
+def add_kernel(rows_ref, values_ref, out_ref, values, lines, tile_sums, window, value_sems, window_sems, out_sem, *sums):
     n_acc = len(sums) // 2
     tile = out_ref.shape[1]
     block = 512
-    for total in sums:
-
-        @pl.loop(0, tile // block)
-        def _(i):
+    half = WINDOW // 2
+
+    def fetch(i):
+        here = pl.ds(pl.multiple_of(i * half, half), half)
+        return pltpu.make_async_copy(values_ref.at[here, :], values.at[here, :], value_sems.at[i])
+
+    for i in range(value_sems.shape[0]):
+        fetch(i).start()
+
+    @pl.loop(0, tile // block)
+    def _(i):
+        for total in sums:
             total[pl.ds(pl.multiple_of(i * block, block), block), :] = jnp.zeros((block, 128), jnp.float32)
 
-    @pl.loop(0, values_ref.shape[0])
-    def _(source):
-        lines[...] = values_ref[source].astype(jnp.float32)
-        for g in range(slots // 16):
+    def add(row, i):
+        fetch(i).wait()
+        lines[...] = values[pl.ds(pl.multiple_of(i * half, half), half), :].astype(jnp.float32)
+        for g in range(WINDOW // 16):
             for j in range(8):
-                one = rows_ref[source * slots + g * 16 + j]
-                two = rows_ref[source * slots + g * 16 + 8 + j]
-                line = lines[g * 8 + j : g * 8 + j + 1, :]
+                one, two = row(16 * g + j), row(16 * g + 8 + j)
+                line = lines[8 * g + j : 8 * g + j + 1, :]
                 left, right = sums[j % n_acc], sums[n_acc + j % n_acc]
                 left[pl.ds(one, 1), :] = left[pl.ds(one, 1), :] + line
                 right[pl.ds(two, 1), :] = right[pl.ds(two, 1), :] + line
 
+    for_windows(rows_ref, window, window_sems, add)
     first_half = lax.broadcasted_iota(jnp.int32, (block, 128), 1) < 64
 
     @pl.loop(0, tile // block)
@@ -334,7 +379,10 @@
             left = left + sums[q][here, :]
             right = right + sums[n_acc + q][here, :]
         both = jnp.where(first_half, left, right).T
-        out_ref[:, here] = both[:64] + both[64:]
+        tile_sums[:, here] = both[:64] + both[64:]
+        pltpu.make_async_copy(tile_sums.at[:, here], out_ref.at[:, here], out_sem).start()
+
+    pltpu.make_async_copy(tile_sums, out_ref, out_sem).wait()
 
 
 def constant_tables():
@@ -364,6 +412,7 @@
     f32 = jnp.float32
     vmem = pl.BlockSpec(memory_space=pltpu.VMEM)
     smem = pl.BlockSpec(memory_space=pltpu.SMEM)
+    hbm = pl.BlockSpec(memory_space=pltpu.HBM)
     params = pltpu.CompilerParams(vmem_limit_bytes=VMEM_LIMIT)
 
     both = ("lat", "lon")
@@ -378,9 +427,12 @@
     first, second, east, west, moving, sea = pl.pallas_call(
         pack_kernel,
         out_shape=[row_message] * 2 + [columns] * 2 + [shape(height, breadth)] * 2,
-        in_specs=[vmem] * 3,
+        in_specs=[hbm] * 3,
         out_specs=[vmem] * 6,
-        scratch_shapes=[pltpu.VMEM((2, HALF + 4, breadth), f32)] * 2,
+        scratch_shapes=[pltpu.VMEM((2, HALF + 4, breadth), f32)] * 2
+        + [pltpu.VMEM((HALF, 8, breadth), f32)] * 2
+        + [pltpu.VMEM((HALF, height, 128), f32)] * 2
+        + [pltpu.VMEM((height, breadth), f32), pltpu.VMEM((height, breadth), jnp.int32), pltpu.SemaphoreType.DMA((7,))],
         compiler_params=params,
         name="pack_halos",
     )(x, speed_factor, land_sea_mask)
@@ -398,37 +450,53 @@
     second = lax.ppermute(second, "lon", column_second)
 
     cos, sin, lanes, subs = constant_tables()
-    cells = jnp.where(send_rows < 0, height * breadth, send_rows).reshape(-1)
+    cells = jnp.maximum(send_rows, 0).reshape(-1)
     targets = jnp.where(recv_rows < 0, OUT_DEV, recv_rows).reshape(-1)
     propagated, picked = pl.pallas_call(
-        functools.partial(wave_kernel, slots),
-        out_shape=[shape(PLANES * height, breadth), shape(devices, slots // 2, 128, kind=jnp.bfloat16)],
-        in_specs=[smem] * 4 + [vmem] * 10,
-        out_specs=[pl.BlockSpec(memory_space=pl.ANY), vmem],
+        wave_kernel,
+        out_shape=[shape(PLANES * height, breadth), shape(devices * slots // 2, 128, kind=jnp.bfloat16)],
+        in_specs=[smem] * 3 + [hbm] + [vmem] * 10,
+        out_specs=[hbm] * 2,
         scratch_shapes=[pltpu.VMEM((HALF + 4, breadth), f32)] * 4
         + [pltpu.VMEM((height, 128), f32)] * 4
         + [
             pltpu.VMEM((breadth // 128, PLANES * height, 128), f32),
-            pltpu.VMEM((height * breadth + 8, 128), f32),
-            pltpu.VMEM((slots // 2, 128), f32),
+            pltpu.VMEM((height * breadth, 128), f32),
+            pltpu.VMEM((WINDOW // 2, 128), f32),
+            pltpu.VMEM((devices * slots // 2, 128), jnp.bfloat16),
             pltpu.VMEM((128, 128), f32),
+            pltpu.SMEM((2 * WINDOW,), jnp.int32),
             pltpu.SemaphoreType.DMA((breadth // 128,)),
+            pltpu.SemaphoreType.DMA((2,)),
+            pltpu.SemaphoreType.DMA,
         ],
         compiler_params=params,
         name="propagate_and_pick",
     )(courant, cos, sin, cells, x, moving, sea, depth_kernel, south, north, first, second, lanes, subs)
 
+    picked = picked.reshape(devices, slots // 2, 128)
     received = lax.all_to_all(picked, both, split_axis=0, concat_axis=0, tiled=True)
 
+    slot_rows = devices * slots // 2
+    components = depth_kernel.shape[0]
     stokes = pl.pallas_call(
-        functools.partial(add_kernel, slots),
-        out_shape=shape(depth_kernel.shape[0], OUT_DEV),
-        in_specs=[smem, vmem],
-        out_specs=vmem,
-        scratch_shapes=[pltpu.VMEM((slots // 2, 128), f32)] + [pltpu.VMEM((OUT_DEV + 8, 128), f32)] * (2 * N_ACC),
+        add_kernel,
+        out_shape=shape(components, OUT_DEV),
+        in_specs=[hbm] * 2,
+        out_specs=hbm,
+        scratch_shapes=[
+            pltpu.VMEM((slot_rows, 128), jnp.bfloat16),
+            pltpu.VMEM((WINDOW // 2, 128), f32),
+            pltpu.VMEM((components, OUT_DEV), f32),
+            pltpu.SMEM((2 * WINDOW,), jnp.int32),
+            pltpu.SemaphoreType.DMA((slot_rows // (WINDOW // 2),)),
+            pltpu.SemaphoreType.DMA((2,)),
+            pltpu.SemaphoreType.DMA,
+        ]
+        + [pltpu.VMEM((OUT_DEV + 8, 128), f32)] * (2 * N_ACC),
         compiler_params=params,
         name="add_profiles",
-    )(targets, received)
+    )(targets, received.reshape(slot_rows, 128))
     return propagated.reshape(DIRS, FREQ, height, breadth), stokes
 
 

time: 104 us -> 102 us (0.981)
    pallas_call x2, Pallas kernels: 41.5 us -> 40.3 us  [the longest x1 21.1 us: body(): pl.pallas_call(add_kernel, out_shape=shape(components, OUT_DEV), in_specs...]
where the time goes in v3:
time: 102 us
  Pallas kernels  41.2 us (40%)
  waiting for transfers between devices  33.3 us (33%)
  starting transfers between devices  22.3 us (22%)
  local copies, waits for them, and re-layouts  4.56 us (4%)
    all_to_all x1, waiting for transfers between devices, body(): lax.all_to_all(picked, both, split_axis=0, concat_axis=0, tiled=True)  29.5 us
    pallas_call x1, Pallas kernels, body(): pl.pallas_call(add_kernel, out_shape=shape(components, OUT_DEV), in_specs...  21.1 us
    pallas_call x1, Pallas kernels, body(): pl.pallas_call(wave_kernel, out_shape=[shape(PLANES * height, breadth), s...  19.2 us
    all_to_all x1, starting transfers between devices, body(): lax.all_to_all(picked, both, split_axis=0, concat_axis=0, tiled=True)  11.2 us
    ppermute x1, starting transfers between devices, body(): second = lax.ppermute(second, 'lon', column_second)  4.69 us
    unnamed x26, local copies, waits for them, and re-layouts  4.56 us
    ppermute x1, starting transfers between devices, body(): second = lax.ppermute(second, both, row_second)  3.1 us
    ppermute x1, waiting for transfers between devices, body(): second = lax.ppermute(second, both, row_second)  2.63 us
  transfers between devices with their start and end apart: 5, of which 3 were waited for; matrix products, arithmetic and copies ran while one was open for 0% of the time, Pallas kernels for 0%

profile of v3, /device:TPU:1, one launch (start us, length us, event | category | flops | bytes accessed | tf_op | source)
XLA Modules:
  0.0 102.2 jit_solution(1407388371640325825)
XLA Ops:
  0.6 0.0 copy-start.9
  0.6 0.0 copy-start.10
  0.7 0.0 copy-start.8
  0.7 0.0 copy-start
  0.7 1.7 %copy-done = f32[36,2,32,256]{3,2,1,0:T(8,128)S(1)} copy-done((f32[36,2,32,256]{3,2,1,0:T(8,128)S(1)}, f32[36,2,32,256]{3,2,1,0:T(8,128)}, u32[]{:S(2)}) %copy-start) | copy-done | bytes 2359320
  2.3 0.0 copy-start.3
  2.4 0.8 copy-done.3
  3.1 0.0 copy-start.4
  3.1 0.8 copy-done.4
  3.9 0.0 copy-start.11
  3.9 0.0 copy-start.1
  3.9 0.0 copy-start.5
  3.9 0.0 copy-start.6
  3.9 0.0 copy-start.7
  3.9 0.8 pack_halos.1
  4.7 1.5 %collective-permute-start = (f32[2,40,256]{2,1,0:T(8,128)S(1)}, f32[2,40,256]{2,1,0:T(8,128)S(1)}, u32[]{:S(2)}, u32[]{:S(2)}) collective-permute-start(f32[2,40,256]{2,1,0:T(8,128)S(1)} %get-tuple-element.16), channel_id=1, source_target_pairs={{0,16},{16,0},{32,48},{48,32},{64,80},{80,64},{96,112},{112,96},{1... | collective-permute-start | bytes 245768 | tf_op jit(solution)/shard_map/ppermute | solution.py:439
  6.2 3.1 %collective-permute-start.1 = (f32[2,40,256]{2,1,0:T(8,128)S(1)}, f32[2,40,256]{2,1,0:T(8,128)S(1)}, u32[]{:S(2)}, u32[]{:S(2)}) collective-permute-start(f32[2,40,256]{2,1,0:T(8,128)S(1)} %get-tuple-element.17), channel_id=1, source_target_pairs={{0,0},{112,127},{16,32},{32,16},{48,64},{64,48},{80,96},{96,80},{1... | collective-permute-start | bytes 245768 | tf_op jit(solution)/shard_map/ppermute | solution.py:440
  9.3 0.0 collective-permute-done.first_ref
  9.3 2.6 %collective-permute-done.1.second_ref = f32[2,40,256]{2,1,0:T(8,128)S(1)} collective-permute-done((f32[2,40,256]{2,1,0:T(8,128)S(1)}, f32[2,40,256]{2,1,0:T(8,128)S(1)}, u32[]{:S(2)}, u32[]{:S(2)}) %collective-permute-start.1) | collective-permute-done | bytes 81952 | tf_op jit(solution)/shard_map/ppermute | solution.py:440
  11.9 0.1 add_corners.1
  12.0 1.8 %collective-permute-start.2 = (f32[40,128]{1,0:T(8,128)S(1)}, f32[40,128]{1,0:T(8,128)S(1)}, u32[]{:S(2)}, u32[]{:S(2)}) collective-permute-start(f32[40,128]{1,0:T(8,128)S(1)} %get-tuple-element.22), channel_id=1, source_target_pairs={{0,1},{1,0},{2,3},{3,2},{4,5},{5,4},{6,7},{7,6},{8,9},{9,8},{10,11... | collective-permute-start | bytes 61448 | tf_op jit(solution)/shard_map/ppermute | solution.py:449
  13.8 4.7 %collective-permute-start.3 = (f32[40,128]{1,0:T(8,128)S(1)}, f32[40,128]{1,0:T(8,128)S(1)}, u32[]{:S(2)}, u32[]{:S(2)}) collective-permute-start(f32[40,128]{1,0:T(8,128)S(1)} %get-tuple-element.23), channel_id=1, source_target_pairs={{0,15},{1,2},{2,1},{3,4},{4,3},{5,6},{6,5},{7,8},{8,7},{9,10},{10,... | collective-permute-start | bytes 61448 | tf_op jit(solution)/shard_map/ppermute | solution.py:450
  18.5 0.0 copy-done.11
  18.5 0.0 collective-permute-done.2.first_ref
  18.6 1.2 %collective-permute-done.3.second_ref = f32[40,128]{1,0:T(8,128)S(1)} collective-permute-done((f32[40,128]{1,0:T(8,128)S(1)}, f32[40,128]{1,0:T(8,128)S(1)}, u32[]{:S(2)}, u32[]{:S(2)}) %collective-permute-start.3) | collective-permute-done | bytes 20512 | tf_op jit(solution)/shard_map/ppermute | solution.py:450
  19.8 0.0 copy-done.9
  19.8 0.0 copy-done.10
  19.8 0.0 copy-done.8
  19.8 0.0 copy-done.1
  19.8 0.0 copy-done.5
  19.8 0.0 copy-done.6
  19.8 0.0 copy-done.7
  19.8 19.2 %propagate_and_pick.1 = (f32[2304,256]{1,0:T(8,128)}, bf16[8192,128]{1,0:T(8,128)(2,1)S(1)}) custom-call(f32[2]{0:T(128)S(1)} %copy-done.8, f32[72]{0:T(128)S(1)} %copy-done.9, f32[72]{0:T(128)S(1)} %copy-done.10, s32[16384]{0:T(1024)S(1)} %maximum_bitcast_fusion.cells_ref, f32[72,32,256]{2,1,0:T(8,128)S(1)} %bitcast.9, ...), custom_call_target="tpu_custom_call" | custom-call | tf_op jit(solution)/shard_map/propagate_and_pick/pallas_call | solution.py:455
  39.0 0.0 copy-start.2
  39.0 1.3 %copy-done.2 = bf16[8192,128]{1,0:T(8,128)(2,1)} copy-done((bf16[8192,128]{1,0:T(8,128)(2,1)}, bf16[8192,128]{1,0:T(8,128)(2,1)S(1)}, u32[]{:S(2)}) %copy-start.2) | copy-done | bytes 2097176
  40.4 0.0 copy-start.12
  40.4 11.2 %all-to-all-start = ((bf16[128,64,128]{2,1,0:T(8,128)(2,1)}), bf16[128,64,128]{2,1,0:T(8,128)(2,1)S(1)}, u32[]{:S(2)}, u32[]{:S(2)}) async-start(bf16[128,64,128]{2,1,0:T(8,128)(2,1)} %bitcast.11), calls=%async_computation | async-start | bytes 4194304 | tf_op jit(solution)/shard_map/all_to_all | solution.py:478
  51.6 0.0 copy-done.12
  51.6 29.5 %all-to-all-done = bf16[128,64,128]{2,1,0:T(8,128)(2,1)S(1)} async-done(((bf16[128,64,128]{2,1,0:T(8,128)(2,1)}), bf16[128,64,128]{2,1,0:T(8,128)(2,1)S(1)}, u32[]{:S(2)}, u32[]{:S(2)}) %all-to-all-start) | async-done | bytes 2097184 | tf_op jit(solution)/shard_map/all_to_all | solution.py:478
  81.1 21.1 %add_profiles.1 = f32[64,4096]{1,0:T(8,128)} custom-call(s32[16384]{0:T(1024)S(1)} %fusion.rows_ref, bf16[8192,128]{1,0:T(8,128)(2,1)S(1)} %bitcast.10), custom_call_target="tpu_custom_call" | custom-call | tf_op jit(solution)/shard_map/add_profiles/pallas_call | solution.py:482
  (2 shorter events, 0.0 us)
Async XLA Ops:
  0.6 19.2 %copy-start.9 = (f32[72]{0:T(128)S(1)}, f32[72]{0:T(128)}, u32[]{:S(2)}) copy-start(f32[72]{0:T(128)} %constant.12.clone.cos_ref) | copy-start | bytes 868
  0.6 19.1 %copy-start.10 = (f32[72]{0:T(128)S(1)}, f32[72]{0:T(128)}, u32[]{:S(2)}) copy-start(f32[72]{0:T(128)} %constant.13.clone.sin_ref) | copy-start | bytes 868
  0.7 19.1 %copy-start.8 = (f32[2]{0:T(128)S(1)}, f32[2]{0:T(128)}, u32[]{:S(2)}) copy-start(f32[2]{0:T(128)} %courant_ref.1) | copy-start | bytes 28
  0.7 1.7 %copy-start = (f32[36,2,32,256]{3,2,1,0:T(8,128)S(1)}, f32[36,2,32,256]{3,2,1,0:T(8,128)}, u32[]{:S(2)}) copy-start(f32[36,2,32,256]{3,2,1,0:T(8,128)} %param.11) | copy-start | bytes 7077892
  2.3 0.8 copy-start.3
  3.1 0.8 copy-start.4
  3.9 14.7 %copy-start.11 = (s32[1,128,128]{2,1,0:T(8,128)S(1)}, s32[1,128,128]{2,1,0:T(8,128)}, u32[]{:S(2)}) copy-start(s32[1,128,128]{2,1,0:T(8,128)} %param.16) | copy-start | bytes 196612
  3.9 15.9 %copy-start.1 = (f32[36,2,32,256]{3,2,1,0:T(8,128)S(1)}, f32[36,2,32,256]{3,2,1,0:T(8,128)}, u32[]{:S(2)}) copy-start(f32[36,2,32,256]{3,2,1,0:T(8,128)} %param.11) | copy-start | bytes 7077892
  3.9 15.9 %copy-start.5 = (f32[64,72]{1,0:T(8,128)S(1)}, f32[64,72]{1,0:T(8,128)}, u32[]{:S(2)}) copy-start(f32[64,72]{1,0:T(8,128)} %kernel_ref.1) | copy-start | bytes 55300
  3.9 16.0 %copy-start.6 = (f32[40,128]{1,0:T(8,128)S(1)}, f32[40,128]{1,0:T(8,128)}, u32[]{:S(2)}) copy-start(f32[40,128]{1,0:T(8,128)} %constant.15.clone.subs_ref) | copy-start | bytes 61444
  3.9 16.0 %copy-start.7 = (f32[8,128]{1,0:T(8,128)S(1)}, f32[8,128]{1,0:T(8,128)}, u32[]{:S(2)}) copy-start(f32[8,128]{1,0:T(8,128)} %constant.14.clone.lanes_ref) | copy-start | bytes 12292
  4.7 4.6 %collective-permute-start = (f32[2,40,256]{2,1,0:T(8,128)S(1)}, f32[2,40,256]{2,1,0:T(8,128)S(1)}, u32[]{:S(2)}, u32[]{:S(2)}) collective-permute-start(f32[2,40,256]{2,1,0:T(8,128)S(1)} %get-tuple-element.16), channel_id=1, source_target_pairs={{0,16},{16,0},{32,48},{48,32},{64,80},{80,64},{96,112},{112,96},{1... | collective-permute-start | bytes 245768 | tf_op jit(solution)/shard_map/ppermute | solution.py:439
  6.2 5.7 %collective-permute-start.1 = (f32[2,40,256]{2,1,0:T(8,128)S(1)}, f32[2,40,256]{2,1,0:T(8,128)S(1)}, u32[]{:S(2)}, u32[]{:S(2)}) collective-permute-start(f32[2,40,256]{2,1,0:T(8,128)S(1)} %get-tuple-element.17), channel_id=1, source_target_pairs={{0,0},{112,127},{16,32},{32,16},{48,64},{64,48},{80,96},{96,80},{1... | collective-permute-start | bytes 245768 | tf_op jit(solution)/shard_map/ppermute | solution.py:440
  12.0 6.5 %collective-permute-start.2 = (f32[40,128]{1,0:T(8,128)S(1)}, f32[40,128]{1,0:T(8,128)S(1)}, u32[]{:S(2)}, u32[]{:S(2)}) collective-permute-start(f32[40,128]{1,0:T(8,128)S(1)} %get-tuple-element.22), channel_id=1, source_target_pairs={{0,1},{1,0},{2,3},{3,2},{4,5},{5,4},{6,7},{7,6},{8,9},{9,8},{10,11... | collective-permute-start | bytes 61448 | tf_op jit(solution)/shard_map/ppermute | solution.py:449
  13.8 6.0 %collective-permute-start.3 = (f32[40,128]{1,0:T(8,128)S(1)}, f32[40,128]{1,0:T(8,128)S(1)}, u32[]{:S(2)}, u32[]{:S(2)}) collective-permute-start(f32[40,128]{1,0:T(8,128)S(1)} %get-tuple-element.23), channel_id=1, source_target_pairs={{0,15},{1,2},{2,1},{3,4},{4,3},{5,6},{6,5},{7,8},{8,7},{9,10},{10,... | collective-permute-start | bytes 61448 | tf_op jit(solution)/shard_map/ppermute | solution.py:450
  39.0 1.3 %copy-start.2 = (bf16[8192,128]{1,0:T(8,128)(2,1)}, bf16[8192,128]{1,0:T(8,128)(2,1)S(1)}, u32[]{:S(2)}) copy-start(bf16[8192,128]{1,0:T(8,128)(2,1)S(1)} %get-tuple-element.25) | copy-start | bytes 6291460
  40.4 11.2 %copy-start.12 = (s32[1,128,128]{2,1,0:T(8,128)S(1)}, s32[1,128,128]{2,1,0:T(8,128)}, u32[]{:S(2)}) copy-start(s32[1,128,128]{2,1,0:T(8,128)} %param.17) | copy-start | bytes 196612
  40.4 40.7 %all-to-all-start = ((bf16[128,64,128]{2,1,0:T(8,128)(2,1)}), bf16[128,64,128]{2,1,0:T(8,128)(2,1)S(1)}, u32[]{:S(2)}, u32[]{:S(2)}) async-start(bf16[128,64,128]{2,1,0:T(8,128)(2,1)} %bitcast.11), calls=%async_computation | async-start | bytes 4194304 | tf_op jit(solution)/shard_map/all_to_all | solution.py:478

commit v4 on v3

--- a/solution.py
+++ b/solution.py
@@ -17,7 +17,7 @@
 OUT_DEV = 4096
 N_ACC = 4
 WINDOW = 1024
-VMEM_LIMIT = 48 * 1024 * 1024
+VMEM_LIMIT = 32 * 1024 * 1024
 
 
 def exchange_pairs(n_lat, n_lon):
@@ -174,10 +174,61 @@
                 fetch(i + 2, w).start()
 
 
-def wave_kernel( courant_ref, cos_ref, sin_ref, cells_ref, x_ref, mov_ref, sea_ref, kernel_ref,
-                south_ref, north_ref, first_ref, second_ref, lanes_ref, subs_ref, out_ref, picked_ref,
-                south0, south1, north0, north1, west0, west1, east0, east1, halves, table, lines, picks, wide_kernel,
-                window, out_sems, window_sems, pick_sem):
+def inside_kernel(courant_ref, cos_ref, sin_ref, x_ref, mov_ref, sea_ref, halves):
+    height, breadth = mov_ref.shape
+    c0, c1 = courant_ref[0], courant_ref[1]
+    moving = mov_ref[...]
+    sea = sea_ref[...]
+    lane = lax.broadcasted_iota(jnp.int32, (height, 128), 1)
+    row = lax.broadcasted_iota(jnp.int32, (8, breadth), 0)
+    for h in range(breadth // 128):
+        halves[h, PLANES * height :, :] = jnp.zeros((4 * height, 128), jnp.float32)
+
+    def quadrant(first, from_west, from_south):
+        def upstream(flux):
+            if from_west:
+                moved = pltpu.roll(flux, 1, axis=1)
+                side = jnp.concatenate([jnp.where(lane == 0, 0.0, moved[:, :128]), moved[:, 128:]], axis=1)
+            else:
+                moved = pltpu.roll(flux, breadth - 1, axis=1)
+                edge = jnp.where(lane == 127, 0.0, moved[:, breadth - 128 :])
+                side = jnp.concatenate([moved[:, : breadth - 128], edge], axis=1)
+            if from_south:
+                moved = pltpu.roll(flux, 1, axis=0)
+                below = jnp.concatenate([jnp.where(row == 0, 0.0, moved[:8]), moved[8:]], axis=0)
+            else:
+                moved = pltpu.roll(flux, height - 1, axis=0)
+                below = jnp.concatenate([moved[: height - 8], jnp.where(row == 7, 0.0, moved[height - 8 :])], axis=0)
+            return side, below
+
+        def step(t, carry):
+            p = first + t
+            courant = jnp.where(p % 2 == 1, c1, c0)
+            cx = cos_ref[p] * courant
+            cy = sin_ref[p] * courant
+            energy = x_ref[p]
+            for _ in range(2):
+                flux = moving * energy
+                side, below = upstream(flux)
+                div_x = cx * (flux - side) if from_west else cx * (side - flux)
+                div_y = cy * (flux - below) if from_south else cy * (below - flux)
+                energy = sea * ((energy - div_x) - div_y)
+            start = pl.ds(pl.multiple_of(p * height, height), height)
+            for h in range(breadth // 128):
+                halves[h, start, :] = energy[:, h * 128 : (h + 1) * 128]
+            return carry
+
+        lax.fori_loop(0, QUAD, step, 0, unroll=6)
+
+    quadrant(0, True, True)
+    quadrant(QUAD, False, True)
+    quadrant(2 * QUAD, False, False)
+    quadrant(3 * QUAD, True, False)
+
+
+def finish_kernel(courant_ref, cells_ref, mov_ref, sea_ref, kernel_ref, south_ref, north_ref, first_ref, second_ref,
+                  lanes_ref, subs_ref, halves_in, out_ref, picked_ref, halves,
+                  table, lines, picks, wide_kernel, window, out_sems, window_sems, pick_sem):
     height, breadth = mov_ref.shape
     c0, c1 = courant_ref[0], courant_ref[1]
     even_lon = lax.axis_index("lon") % 2 == 0
@@ -189,7 +240,7 @@
     row = lax.broadcasted_iota(jnp.int32, (height, 128), 0)
     odd = lane % 2 == 1
 
-    def columns(e0, near, far, corner, cx, cy, sign, flux0, flux1):
+    def columns(e0, near, far, corner, cx, cy, sign):
         mov = jnp.where(odd, e0[:, 2 * HALF + 1 : 2 * HALF + 2], e0[:, 2 * HALF : 2 * HALF + 1])
         sea = e0[:, 2 * HALF + 2 + near : 2 * HALF + 3 + near]
         f0 = mov * e0
@@ -198,13 +249,13 @@
         f_north = jnp.where(row == height - 1, corner, pltpu.roll(f0, height - 1, axis=0))
         div_x = cx * (f0 - f_far) if sign > 0 else cx * (f_far - f0)
         div_y = jnp.where(lane < HALF, cy * (f0 - f_south), cy * (f_north - f0))
-        flux0[...] = f0
-        flux1[...] = mov * (sea * ((e0 - div_x) - div_y))
+        return f0, mov * (sea * ((e0 - div_x) - div_y))
 
     lanes = lanes_ref[...]
     lane_courant = jnp.where(lanes[4:5] > 0.5, c1, c0)
-    columns(from_west[:height], 1, 0, corner_w, lanes[0:1] * lane_courant, lanes[1:2] * lane_courant, 1, west0, west1)
-    columns(from_east[:height], 0, 1, corner_e, lanes[2:3] * lane_courant, lanes[3:4] * lane_courant, -1, east0, east1)
+    cx_w, cy_w, cx_e, cy_e = (lanes[k : k + 1] * lane_courant for k in range(4))
+    west_flux0, west_flux1 = columns(from_west[:height], 1, 0, corner_w, cx_w, cy_w, 1)
+    east_flux0, east_flux1 = columns(from_east[:height], 0, 1, corner_e, cx_e, cy_e, -1)
 
     wide = lax.broadcasted_iota(jnp.int32, (HALF + 4, breadth), 1)
     plane = lax.broadcasted_iota(jnp.int32, (HALF + 4, 1), 0)
@@ -216,7 +267,7 @@
     def to_sublanes(corner, lane_of):
         return jnp.sum(jnp.where(lane_l == lane_of, corner, 0.0), axis=1, keepdims=True)
 
-    def rows(near, far, first_west, west_corner, east_corner, cx, cy, sign, flux0, flux1):
+    def rows(near, far, first_west, west_corner, east_corner, cx, cy, sign):
         mov, sea = near[HALF : HALF + 1], near[HALF + 1 : HALF + 2]
         f0 = mov * near
         f_far = far[HALF : HALF + 1] * far
@@ -225,74 +276,62 @@
         from_west = (plane < QUAD) if first_west else (plane >= QUAD)
         div_x = jnp.where(from_west, cx * (f0 - f_west), cx * (f_east - f0))
         div_y = cy * (f0 - f_far) if sign > 0 else cy * (f_far - f0)
-        flux0[...] = f0
-        flux1[...] = mov * (sea * ((near - div_x) - div_y))
+        return f0, mov * (sea * ((near - div_x) - div_y))
 
     sw = to_sublanes(corner_w, 2 * plane_l + 1)
     se = to_sublanes(corner_e, 2 * plane_l - HALF)
     ne = to_sublanes(corner_e, 2 * plane_l + HALF)
     nw = sw
-    rows(south_ref[0], south_ref[1], True, sw, se, subs[:, 0:1] * sub_courant, subs[:, 1:2] * sub_courant, 1,
-         south0, south1)
-    rows(north_ref[0], north_ref[1], False, nw, ne, subs[:, 2:3] * sub_courant, subs[:, 3:4] * sub_courant, -1,
-         north0, north1)
-
-    moving = mov_ref[...]
-    sea_all = sea_ref[...]
-    lane_edge = lax.broadcasted_iota(jnp.int32, (height, 128), 1)
-    row_edge = lax.broadcasted_iota(jnp.int32, (8, breadth), 0)
-
-    def write_out(planes, h):
-        target = out_ref.at[planes, pl.ds(h * 128, 128)]
-        return pltpu.make_async_copy(halves.at[h, planes, :], target, out_sems.at[h])
-
-    def quadrant(first, from_west, from_south, column0, column1, lane_first, row0, row1, row_first):
-        def upstream(flux, column, line):
-            if from_west:
-                moved = pltpu.roll(flux, 1, axis=1)
-                side = jnp.concatenate([jnp.where(lane_edge == 0, column, moved[:, :128]), moved[:, 128:]], axis=1)
-            else:
-                moved = pltpu.roll(flux, breadth - 1, axis=1)
-                edge = jnp.where(lane_edge == 127, column, moved[:, breadth - 128 :])
-                side = jnp.concatenate([moved[:, : breadth - 128], edge], axis=1)
-            if from_south:
-                moved = pltpu.roll(flux, 1, axis=0)
-                below = jnp.concatenate([jnp.where(row_edge == 0, line, moved[:8]), moved[8:]], axis=0)
-            else:
-                moved = pltpu.roll(flux, height - 1, axis=0)
-                edge = jnp.where(row_edge == 7, line, moved[height - 8 :])
-                below = jnp.concatenate([moved[: height - 8], edge], axis=0)
-            return side, below
-
-        def step(t, carry):
-            p = first + t
-            courant = jnp.where(p % 2 == 1, c1, c0)
-            cx = cos_ref[p] * courant
-            cy = sin_ref[p] * courant
-            place = lane_first + 2 * t
-            turn = (128 - place) if from_west else (127 - place)
-            energy = x_ref[p]
-            for column_ref, row_ref in ((column0, row0), (column1, row1)):
-                flux = moving * energy
-                column = pltpu.roll(column_ref[...], turn, axis=1)
-                side, below = upstream(flux, column, row_ref[pl.ds(row_first + t, 1), :])
-                div_x = cx * (flux - side) if from_west else cx * (side - flux)
-                div_y = cy * (flux - below) if from_south else cy * (below - flux)
-                energy = sea_all * ((energy - div_x) - div_y)
-            start = pl.ds(pl.multiple_of(p * height, height), height)
+    cx_s, cy_s, cx_n, cy_n = (subs[:, k : k + 1] * sub_courant for k in range(4))
+    south_flux0, south_flux1 = rows(south_ref[0], south_ref[1], True, sw, se, cx_s, cy_s, 1)
+    north_flux0, north_flux1 = rows(north_ref[0], north_ref[1], False, nw, ne, cx_n, cy_n, -1)
+
+    def add_rows(first, near, next_row, flux0, flux1, cx, cy, first_west):
+        sea0, sea1 = sea_ref[near : near + 1, :], sea_ref[next_row : next_row + 1, :]
+        change = sea0 * (cy * flux0)
+        flux = mov_ref[near : near + 1, :] * change
+        west_flux = jnp.where(wide == 0, 0.0, pltpu.roll(flux, 1, axis=1))
+        east_flux = jnp.where(wide == breadth - 1, 0.0, pltpu.roll(flux, breadth - 1, axis=1))
+        from_west = (plane < QUAD) if first_west else (plane >= QUAD)
+        div_x = jnp.where(from_west, cx * (flux - west_flux), cx * (east_flux - flux))
+        near_change = sea0 * (((change - div_x) - cy * flux) + cy * flux1)
+        next_change = sea1 * (cy * flux)
+        for at, delta in ((near, near_change), (next_row, next_change)):
             for h in range(breadth // 128):
-                halves[h, start, :] = energy[:, h * 128 : (h + 1) * 128]
-            return carry
-
-        lax.fori_loop(0, QUAD, step, 0, unroll=6)
-        planes = pl.ds(first * height, QUAD * height)
-        for h in range(breadth // 128):
-            write_out(planes, h).start()
-
-    quadrant(0, True, True, west0, west1, 1, south0, south1, 0)
-    quadrant(QUAD, False, True, east0, east1, 0, south0, south1, QUAD)
-    quadrant(2 * QUAD, False, False, east0, east1, HALF, north0, north1, 0)
-    quadrant(3 * QUAD, True, False, west0, west1, HALF + 1, north0, north1, QUAD)
+                place = pl.ds(first * height + at, HALF + 4, stride=height)
+                halves[h, place, :] = halves[h, place, :] + delta[:, h * 128 : (h + 1) * 128]
+
+    def add_columns(half, near, next_column, flux0, flux1, cx, cy, from_west):
+        sea0, sea1 = sea_ref[:, near : near + 1], sea_ref[:, next_column : next_column + 1]
+        change = sea0 * (cx * flux0)
+        flux = mov_ref[:, near : near + 1] * change
+        south_flux = jnp.where(row == 0, 0.0, pltpu.roll(flux, 1, axis=0))
+        north_flux = jnp.where(row == height - 1, 0.0, pltpu.roll(flux, height - 1, axis=0))
+        div_y = jnp.where(lane < HALF, cy * (flux - south_flux), cy * (north_flux - flux))
+        near_change = sea0 * (((change - cx * flux) - div_y) + cx * flux1)
+        next_change = sea1 * (cx * flux)
+        if from_west:
+            both = jnp.where(odd, next_change, pltpu.roll(near_change, 127, axis=1))
+        else:
+            both = jnp.where(odd, pltpu.roll(near_change, 1, axis=1), next_change)
+        edge = lane < 2 if from_west else lane >= 126
+        for q in range(HALF):
+            p = q + QUAD if not from_west else (q if q < QUAD else q + HALF)
+            turned = pltpu.roll(both, ((128 if from_west else 126) - 2 * q) % 128, axis=1)
+            place = pl.ds(p * height, height)
+            halves[half, place, :] = halves[half, place, :] + jnp.where(edge, turned, 0.0)
+
+    add_rows(0, 0, 1, south_flux0, south_flux1, cx_s, cy_s, True)
+    add_rows(HALF, height - 1, height - 2, north_flux0, north_flux1, cx_n, -cy_n, False)
+    add_columns(0, 0, 1, west_flux0, west_flux1, cx_w, cy_w, True)
+    add_columns(breadth // 128 - 1, breadth - 1, breadth - 2, east_flux0, east_flux1, -cx_e, cy_e, False)
+    whole = pl.ds(0, PLANES * height)
+    writes = [
+        pltpu.make_async_copy(halves.at[h, whole, :], out_ref.at[:, pl.ds(h * 128, 128)], out_sems.at[h])
+        for h in range(breadth // 128)
+    ]
+    for write in writes:
+        write.start()
 
     pad = jnp.zeros((8, 128), jnp.bfloat16)
     wide_kernel[...] = jnp.zeros((128, 128), jnp.float32)
@@ -334,32 +373,23 @@
 
     for_windows(cells_ref, window, window_sems, pick)
     pltpu.make_async_copy(picks, picked_ref, pick_sem).wait()
-    whole = pl.ds(0, PLANES * height)
-    for h in range(breadth // 128):
-        write_out(whole, h).wait()
-
-
-def add_kernel(rows_ref, values_ref, out_ref, values, lines, tile_sums, window, value_sems, window_sems, out_sem, *sums):
+    for write in writes:
+        write.wait()
+
+
+def add_kernel(rows_ref, values_ref, out_ref, lines, tile_sums, window, window_sems, out_sem, *sums):
     n_acc = len(sums) // 2
     tile = out_ref.shape[1]
     block = 512
     half = WINDOW // 2
 
-    def fetch(i):
-        here = pl.ds(pl.multiple_of(i * half, half), half)
-        return pltpu.make_async_copy(values_ref.at[here, :], values.at[here, :], value_sems.at[i])
-
-    for i in range(value_sems.shape[0]):
-        fetch(i).start()
-
     @pl.loop(0, tile // block)
     def _(i):
         for total in sums:
             total[pl.ds(pl.multiple_of(i * block, block), block), :] = jnp.zeros((block, 128), jnp.float32)
 
     def add(row, i):
-        fetch(i).wait()
-        lines[...] = values[pl.ds(pl.multiple_of(i * half, half), half), :].astype(jnp.float32)
+        lines[...] = values_ref[pl.ds(pl.multiple_of(i * half, half), half), :].astype(jnp.float32)
         for g in range(WINDOW // 16):
             for j in range(8):
                 one, two = row(16 * g + j), row(16 * g + 8 + j)
@@ -420,6 +450,7 @@
     def shape(*dims, kind=f32):
         return jax.ShapeDtypeStruct(dims, kind)
 
+    cos, sin, lanes, subs = constant_tables()
     row_message = shape(2, HALF + 4, breadth)
     columns = shape(height, 128)
     column_message = shape(height + 8, 128)
@@ -435,9 +466,18 @@
         + [pltpu.VMEM((height, breadth), f32), pltpu.VMEM((height, breadth), jnp.int32), pltpu.SemaphoreType.DMA((7,))],
         compiler_params=params,
         name="pack_halos",
-    )(x, speed_factor, land_sea_mask)
+    )(*(pltpu.with_memory_space_constraint(v, pltpu.HBM) for v in (x, speed_factor, land_sea_mask)))
+    second = lax.ppermute(second, both, row_second)
     first = lax.ppermute(first, "lat", row_first)
-    second = lax.ppermute(second, both, row_second)
+    halves = pl.pallas_call(
+        inside_kernel,
+        out_shape=pltpu.VMEM((breadth // 128, (PLANES + 4) * height, 128), f32),
+        in_specs=[smem] * 3 + [vmem] * 3,
+        out_specs=vmem,
+        compiler_params=params,
+        cost_estimate=pl.CostEstimate(flops=4_000_000_000, bytes_accessed=5_000_000, transcendentals=0),
+        name="advance_inside",
+    )(courant, cos, sin, x, moving, sea)
     south, north, first, second = pl.pallas_call(
         functools.partial(corner_kernel, n_lat),
         out_shape=[row_message] * 2 + [column_message] * 2,
@@ -446,24 +486,26 @@
         compiler_params=params,
         name="add_corners",
     )(first, second, east, west)
+    second = lax.ppermute(second, "lon", column_second)
     first = lax.ppermute(first, "lon", column_first)
-    second = lax.ppermute(second, "lon", column_second)
-
-    cos, sin, lanes, subs = constant_tables()
+
     cells = jnp.maximum(send_rows, 0).reshape(-1)
     targets = jnp.where(recv_rows < 0, OUT_DEV, recv_rows).reshape(-1)
-    propagated, picked = pl.pallas_call(
-        wave_kernel,
-        out_shape=[shape(PLANES * height, breadth), shape(devices * slots // 2, 128, kind=jnp.bfloat16)],
-        in_specs=[smem] * 3 + [hbm] + [vmem] * 10,
-        out_specs=[hbm] * 2,
-        scratch_shapes=[pltpu.VMEM((HALF + 4, breadth), f32)] * 4
-        + [pltpu.VMEM((height, 128), f32)] * 4
-        + [
-            pltpu.VMEM((breadth // 128, PLANES * height, 128), f32),
+    slot_rows = devices * slots // 2
+    propagated, picked, _ = pl.pallas_call(
+        finish_kernel,
+        out_shape=[
+            pltpu.HBM((PLANES * height, breadth), f32),
+            pltpu.HBM((slot_rows, 128), jnp.bfloat16),
+            pltpu.VMEM(halves.shape, f32),
+        ],
+        in_specs=[smem, hbm] + [vmem] * 10,
+        out_specs=[hbm, hbm, vmem],
+        input_output_aliases={11: 2},
+        scratch_shapes=[
             pltpu.VMEM((height * breadth, 128), f32),
             pltpu.VMEM((WINDOW // 2, 128), f32),
-            pltpu.VMEM((devices * slots // 2, 128), jnp.bfloat16),
+            pltpu.VMEM((slot_rows, 128), jnp.bfloat16),
             pltpu.VMEM((128, 128), f32),
             pltpu.SMEM((2 * WINDOW,), jnp.int32),
             pltpu.SemaphoreType.DMA((breadth // 128,)),
@@ -471,25 +513,22 @@
             pltpu.SemaphoreType.DMA,
         ],
         compiler_params=params,
-        name="propagate_and_pick",
-    )(courant, cos, sin, cells, x, moving, sea, depth_kernel, south, north, first, second, lanes, subs)
+        name="finish_and_pick",
+    )(courant, cells, moving, sea, depth_kernel, south, north, first, second, lanes, subs, halves)
 
     picked = picked.reshape(devices, slots // 2, 128)
     received = lax.all_to_all(picked, both, split_axis=0, concat_axis=0, tiled=True)
 
-    slot_rows = devices * slots // 2
     components = depth_kernel.shape[0]
     stokes = pl.pallas_call(
         add_kernel,
-        out_shape=shape(components, OUT_DEV),
-        in_specs=[hbm] * 2,
+        out_shape=pltpu.HBM((components, OUT_DEV), f32),
+        in_specs=[hbm, vmem],
         out_specs=hbm,
         scratch_shapes=[
-            pltpu.VMEM((slot_rows, 128), jnp.bfloat16),
             pltpu.VMEM((WINDOW // 2, 128), f32),
             pltpu.VMEM((components, OUT_DEV), f32),
             pltpu.SMEM((2 * WINDOW,), jnp.int32),
-            pltpu.SemaphoreType.DMA((slot_rows // (WINDOW // 2),)),
             pltpu.SemaphoreType.DMA((2,)),
             pltpu.SemaphoreType.DMA,
         ]

time: 102 us -> 90.7 us (0.89)
  local copies, waits for them, and re-layouts: 4.56 us -> 0.05 us
  Pallas kernels: 41.2 us -> 37.9 us
  starting transfers between devices: 22.3 us -> 20.1 us
  waiting for transfers between devices: 33.3 us -> 32.1 us
    pallas_call x2 -> x3, Pallas kernels: 40.3 us -> 35.7 us  [the longest x1 18.2 us: body(): pl.pallas_call(add_kernel, out_shape=pltpu.HBM((components, OUT_DEV), f32...]
    unnamed x26 -> x18, local copies, waits for them, and re-layouts: 4.56 us -> 0.05 us
    all_to_all x1, starting transfers between devices: 11.2 us -> 9.04 us  [body(): lax.all_to_all(picked, both, split_axis=0, concat_axis=0, tiled=True)]
    pallas_call x1, Pallas kernels: 0.78 us -> 2.06 us  [body(): pl.pallas_call(pack_kernel, out_shape=[row_message] * 2 + [columns] * 2 +...]
    ppermute x1, waiting for transfers between devices: 1.24 us -> 0.01 us  [body(): second = lax.ppermute(second, 'lon', column_second)]
  transfers between devices with their start and end apart: 5 -> 5, of which waited for: 3 -> 2; matrix products, arithmetic and copies ran while one was open for 0% -> 0% of each run, Pallas kernels for 0% -> 4%
where the time goes in v4:
time: 90.7 us; the launch traced here: 91 us
  Pallas kernels  37.9 us (42%)
  waiting for transfers between devices  32.1 us (35%)
  starting transfers between devices  20.1 us (22%)
    all_to_all x1, waiting for transfers between devices, body(): lax.all_to_all(picked, both, split_axis=0, concat_axis=0, tiled=True)  29.5 us
    pallas_call x1, Pallas kernels, body(): pl.pallas_call(add_kernel, out_shape=pltpu.HBM((components, OUT_DEV), f32...  18.2 us
    pallas_call x1, Pallas kernels, body(): pl.pallas_call(finish_kernel, out_shape=[pltpu.HBM((PLANES * height, brea...  14.1 us
    all_to_all x1, starting transfers between devices, body(): lax.all_to_all(picked, both, split_axis=0, concat_axis=0, tiled=True)  9.04 us
    ppermute x1, starting transfers between devices, body(): second = lax.ppermute(second, 'lon', column_second)  4.69 us
    pallas_call x1, Pallas kernels, body(): pl.pallas_call(inside_kernel, out_shape=pltpu.VMEM((breadth // 128, (PLAN...  3.36 us
    ppermute x1, starting transfers between devices, body(): second = lax.ppermute(second, both, row_second)  3.1 us
    ppermute x1, waiting for transfers between devices, body(): second = lax.ppermute(second, both, row_second)  2.6 us
  transfers between devices with their start and end apart: 5, of which 2 were waited for; matrix products, arithmetic and copies ran while one was open for 0% of the time, Pallas kernels for 4%

profile of v4, /device:TPU:1, one launch (start us, length us, event | category | flops | bytes accessed | tf_op | source)
XLA Modules:
  0.0 91.0 jit_solution(6941508489634669395)
XLA Ops:
  0.6 0.0 copy-start.5
  0.6 0.0 copy-start.6
  0.7 0.0 copy-start
  0.7 0.0 copy-start.7
  0.7 0.0 copy-start.4
  0.7 2.1 %pack_halos.1 = (f32[2,40,256]{2,1,0:T(8,128)S(1)}, f32[2,40,256]{2,1,0:T(8,128)S(1)}, f32[32,128]{1,0:T(8,128)S(1)}, f32[32,128]{1,0:T(8,128)S(1)}, f32[32,256]{1,0:T(8,128)S(1)}, /*index=5*/f32[32,256]{1,0:T(8,128)S(1)}) custom-call(f32[72,32,256]{2,1,0:T(8,128)} %bitcast.9, f32[32,256]{1,0:T(8,128)} %speed_hbm.1, s32[32,256]{1,0:T(8,128)} %mask_hbm.1), custom_call_target="tpu_custom_call" | custom-call | tf_op jit(solution)/shard_map/pack_halos/pallas_call | solution.py:458
  2.8 1.5 %collective-permute-start = (f32[2,40,256]{2,1,0:T(8,128)S(1)}, f32[2,40,256]{2,1,0:T(8,128)S(1)}, u32[]{:S(2)}, u32[]{:S(2)}) collective-permute-start(f32[2,40,256]{2,1,0:T(8,128)S(1)} %get-tuple-element.16), channel_id=1, source_target_pairs={{0,16},{16,0},{32,48},{48,32},{64,80},{80,64},{96,112},{112,96},{1... | collective-permute-start | bytes 245768 | tf_op jit(solution)/shard_map/ppermute | solution.py:471
  4.3 3.1 %collective-permute-start.1 = (f32[2,40,256]{2,1,0:T(8,128)S(1)}, f32[2,40,256]{2,1,0:T(8,128)S(1)}, u32[]{:S(2)}, u32[]{:S(2)}) collective-permute-start(f32[2,40,256]{2,1,0:T(8,128)S(1)} %get-tuple-element.17), channel_id=1, source_target_pairs={{0,0},{112,127},{16,32},{32,16},{48,64},{64,48},{80,96},{96,80},{1... | collective-permute-start | bytes 245768 | tf_op jit(solution)/shard_map/ppermute | solution.py:470
  7.4 0.0 copy-done.7
  7.4 0.0 collective-permute-done.first_ref
  7.4 2.6 %collective-permute-done.1.second_ref = f32[2,40,256]{2,1,0:T(8,128)S(1)} collective-permute-done((f32[2,40,256]{2,1,0:T(8,128)S(1)}, f32[2,40,256]{2,1,0:T(8,128)S(1)}, u32[]{:S(2)}, u32[]{:S(2)}) %collective-permute-start.1) | collective-permute-done | bytes 81952 | tf_op jit(solution)/shard_map/ppermute | solution.py:470
  10.0 0.1 add_corners.1
  10.1 1.8 %collective-permute-start.2 = (f32[40,128]{1,0:T(8,128)S(1)}, f32[40,128]{1,0:T(8,128)S(1)}, u32[]{:S(2)}, u32[]{:S(2)}) collective-permute-start(f32[40,128]{1,0:T(8,128)S(1)} %get-tuple-element.22), channel_id=1, source_target_pairs={{0,1},{1,0},{2,3},{3,2},{4,5},{5,4},{6,7},{7,6},{8,9},{9,8},{10,11... | collective-permute-start | bytes 61448 | tf_op jit(solution)/shard_map/ppermute | solution.py:490
  11.9 4.7 %collective-permute-start.3 = (f32[40,128]{1,0:T(8,128)S(1)}, f32[40,128]{1,0:T(8,128)S(1)}, u32[]{:S(2)}, u32[]{:S(2)}) collective-permute-start(f32[40,128]{1,0:T(8,128)S(1)} %get-tuple-element.23), channel_id=1, source_target_pairs={{0,15},{1,2},{2,1},{3,4},{4,3},{5,6},{6,5},{7,8},{8,7},{9,10},{10,... | collective-permute-start | bytes 61448 | tf_op jit(solution)/shard_map/ppermute | solution.py:489
  16.6 0.0 copy-done.5
  16.6 0.0 copy-done.6
  16.6 0.0 copy-done
  16.6 0.0 copy-done.4
  16.6 0.0 copy-start.1
  16.6 0.0 copy-start.2
  16.6 0.0 copy-start.3
  16.7 3.4 %advance_inside.1.halves_in = f32[2,2432,128]{2,1,0:T(8,128)S(1)} custom-call(f32[2]{0:T(128)S(1)} %copy-done.4, f32[72]{0:T(128)S(1)} %copy-done.5, f32[72]{0:T(128)S(1)} %copy-done.6, f32[72,32,256]{2,1,0:T(8,128)S(1)} %bitcast.10, f32[32,256]{1,0:T(8,128)S(1)} %get-tuple-element.14.mov_ref, f32[32,256]{1,0:T(8,128)S(1)} %get-tuple-element.15.sea_ref), custom_call_target="tpu_custom_call" | custom-call | flops 4000000000 | bytes 5000000 | tf_op jit(solution)/shard_map/advance_inside/pallas_call | solution.py:472
  20.0 0.0 collective-permute-done.2.first_ref
  20.0 0.0 collective-permute-done.3.second_ref
  20.1 0.0 copy-done.1
  20.1 0.0 copy-done.2
  20.1 0.0 copy-done.3
  20.1 14.1 %finish_and_pick.1 = (f32[2304,256]{1,0:T(8,128)}, bf16[8192,128]{1,0:T(8,128)(2,1)}, f32[2,2432,128]{2,1,0:T(8,128)S(1)}) custom-call(f32[2]{0:T(128)S(1)} %copy-done.4, s32[16384]{0:T(1024)S(1)} %maximum_bitcast_fusion.cells_ref, f32[32,256]{1,0:T(8,128)S(1)} %get-tuple-element.14.mov_ref, ...), custom_call_target="tpu_custom_call", output_to_operand_aliasing={{2}: (11, {})} | custom-call | tf_op jit(solution)/shard_map/finish_and_pick/pallas_call | solution.py:495
  34.2 0.0 copy-start.8
  34.2 9.0 %all-to-all-start = ((bf16[128,64,128]{2,1,0:T(8,128)(2,1)}), bf16[128,64,128]{2,1,0:T(8,128)(2,1)S(1)}, u32[]{:S(2)}, u32[]{:S(2)}) async-start(bf16[128,64,128]{2,1,0:T(8,128)(2,1)} %bitcast.11), calls=%async_computation | async-start | bytes 4194304 | tf_op jit(solution)/shard_map/all_to_all | solution.py:520
  43.3 0.0 copy-done.8
  43.3 29.5 %all-to-all-done = bf16[128,64,128]{2,1,0:T(8,128)(2,1)S(1)} async-done(((bf16[128,64,128]{2,1,0:T(8,128)(2,1)}), bf16[128,64,128]{2,1,0:T(8,128)(2,1)S(1)}, u32[]{:S(2)}, u32[]{:S(2)}) %all-to-all-start) | async-done | bytes 2097184 | tf_op jit(solution)/shard_map/all_to_all | solution.py:520
  72.8 18.2 %add_profiles.1 = f32[64,4096]{1,0:T(8,128)} custom-call(s32[16384]{0:T(1024)S(1)} %fusion.rows_ref, bf16[8192,128]{1,0:T(8,128)(2,1)S(1)} %bitcast.8), custom_call_target="tpu_custom_call" | custom-call | tf_op jit(solution)/shard_map/add_profiles/pallas_call | solution.py:523
  (2 shorter events, 0.0 us)
Async XLA Ops:
  0.6 16.0 %copy-start.5 = (f32[72]{0:T(128)S(1)}, f32[72]{0:T(128)}, u32[]{:S(2)}) copy-start(f32[72]{0:T(128)} %constant.12.clone.cos_ref) | copy-start | bytes 868
  0.6 16.0 %copy-start.6 = (f32[72]{0:T(128)S(1)}, f32[72]{0:T(128)}, u32[]{:S(2)}) copy-start(f32[72]{0:T(128)} %constant.13.clone.sin_ref) | copy-start | bytes 868
  0.7 16.0 %copy-start = (f32[36,2,32,256]{3,2,1,0:T(8,128)S(1)}, f32[36,2,32,256]{3,2,1,0:T(8,128)}, u32[]{:S(2)}) copy-start(f32[36,2,32,256]{3,2,1,0:T(8,128)} %param.11) | copy-start | bytes 7077892
  0.7 6.7 %copy-start.7 = (s32[1,128,128]{2,1,0:T(8,128)S(1)}, s32[1,128,128]{2,1,0:T(8,128)}, u32[]{:S(2)}) copy-start(s32[1,128,128]{2,1,0:T(8,128)} %param.16) | copy-start | bytes 196612
  0.7 15.9 %copy-start.4 = (f32[2]{0:T(128)S(1)}, f32[2]{0:T(128)}, u32[]{:S(2)}) copy-start(f32[2]{0:T(128)} %courant_ref.3) | copy-start | bytes 28
  2.8 4.6 %collective-permute-start = (f32[2,40,256]{2,1,0:T(8,128)S(1)}, f32[2,40,256]{2,1,0:T(8,128)S(1)}, u32[]{:S(2)}, u32[]{:S(2)}) collective-permute-start(f32[2,40,256]{2,1,0:T(8,128)S(1)} %get-tuple-element.16), channel_id=1, source_target_pairs={{0,16},{16,0},{32,48},{48,32},{64,80},{80,64},{96,112},{112,96},{1... | collective-permute-start | bytes 245768 | tf_op jit(solution)/shard_map/ppermute | solution.py:471
  4.3 5.7 %collective-permute-start.1 = (f32[2,40,256]{2,1,0:T(8,128)S(1)}, f32[2,40,256]{2,1,0:T(8,128)S(1)}, u32[]{:S(2)}, u32[]{:S(2)}) collective-permute-start(f32[2,40,256]{2,1,0:T(8,128)S(1)} %get-tuple-element.17), channel_id=1, source_target_pairs={{0,0},{112,127},{16,32},{32,16},{48,64},{64,48},{80,96},{96,80},{1... | collective-permute-start | bytes 245768 | tf_op jit(solution)/shard_map/ppermute | solution.py:470
  10.1 9.9 %collective-permute-start.2 = (f32[40,128]{1,0:T(8,128)S(1)}, f32[40,128]{1,0:T(8,128)S(1)}, u32[]{:S(2)}, u32[]{:S(2)}) collective-permute-start(f32[40,128]{1,0:T(8,128)S(1)} %get-tuple-element.22), channel_id=1, source_target_pairs={{0,1},{1,0},{2,3},{3,2},{4,5},{5,4},{6,7},{7,6},{8,9},{9,8},{10,11... | collective-permute-start | bytes 61448 | tf_op jit(solution)/shard_map/ppermute | solution.py:490
  11.9 8.1 %collective-permute-start.3 = (f32[40,128]{1,0:T(8,128)S(1)}, f32[40,128]{1,0:T(8,128)S(1)}, u32[]{:S(2)}, u32[]{:S(2)}) collective-permute-start(f32[40,128]{1,0:T(8,128)S(1)} %get-tuple-element.23), channel_id=1, source_target_pairs={{0,15},{1,2},{2,1},{3,4},{4,3},{5,6},{6,5},{7,8},{8,7},{9,10},{10,... | collective-permute-start | bytes 61448 | tf_op jit(solution)/shard_map/ppermute | solution.py:489
  16.6 3.4 %copy-start.1 = (f32[64,72]{1,0:T(8,128)S(1)}, f32[64,72]{1,0:T(8,128)}, u32[]{:S(2)}) copy-start(f32[64,72]{1,0:T(8,128)} %kernel_ref.1) | copy-start | bytes 55300
  16.6 3.4 %copy-start.2 = (f32[40,128]{1,0:T(8,128)S(1)}, f32[40,128]{1,0:T(8,128)}, u32[]{:S(2)}) copy-start(f32[40,128]{1,0:T(8,128)} %constant.15.clone.subs_ref) | copy-start | bytes 61444
  16.6 3.4 %copy-start.3 = (f32[8,128]{1,0:T(8,128)S(1)}, f32[8,128]{1,0:T(8,128)}, u32[]{:S(2)}) copy-start(f32[8,128]{1,0:T(8,128)} %constant.14.clone.lanes_ref) | copy-start | bytes 12292
  34.2 9.1 %copy-start.8 = (s32[1,128,128]{2,1,0:T(8,128)S(1)}, s32[1,128,128]{2,1,0:T(8,128)}, u32[]{:S(2)}) copy-start(s32[1,128,128]{2,1,0:T(8,128)} %param.17) | copy-start | bytes 196612
  34.2 38.5 %all-to-all-start = ((bf16[128,64,128]{2,1,0:T(8,128)(2,1)}), bf16[128,64,128]{2,1,0:T(8,128)(2,1)S(1)}, u32[]{:S(2)}, u32[]{:S(2)}) async-start(bf16[128,64,128]{2,1,0:T(8,128)(2,1)} %bitcast.11), calls=%async_computation | async-start | bytes 4194304 | tf_op jit(solution)/shard_map/all_to_all | solution.py:520

commit v5 on v4

--- a/solution.py
+++ b/solution.py
@@ -15,9 +15,10 @@
 HALF = PLANES // 2
 QUAD = PLANES // 4
 OUT_DEV = 4096
+SPARE = 64
 N_ACC = 4
 WINDOW = 1024
-VMEM_LIMIT = 32 * 1024 * 1024
+VMEM_LIMIT = 16 * 1024 * 1024
 
 
 def exchange_pairs(n_lat, n_lon):
@@ -35,11 +36,9 @@
     return row_first, row_second, column_first, column_second
 
 
-def pack_kernel(x_hbm, speed_hbm, mask_hbm, first_ref, second_ref, east_ref, west_ref, mov_ref, sea_ref,
-                up_ref, down_ref, top_rows, bottom_rows, east_edge, west_edge, speed_ref, mask_ref, sems):
+def pack_rows_kernel(x_hbm, speed_hbm, mask_hbm, first_ref, second_ref, mov_ref, sea_ref,
+                     up_ref, down_ref, top_rows, bottom_rows, speed_ref, mask_ref, sems):
     height, breadth = speed_ref.shape
-    first_quad, mid_quads, last_quad = pl.ds(0, QUAD), pl.ds(QUAD, HALF), pl.ds(3 * QUAD, QUAD)
-    last_lanes = pl.ds(breadth - 128, 128)
     copies = [
         pltpu.make_async_copy(source, target, sems.at[k])
         for k, (source, target) in enumerate((
@@ -47,15 +46,12 @@
             (mask_hbm, mask_ref),
             (x_hbm.at[pl.ds(0, HALF), pl.ds(height - 8, 8), :], top_rows),
             (x_hbm.at[pl.ds(HALF, HALF), pl.ds(0, 8), :], bottom_rows),
-            (x_hbm.at[first_quad, :, last_lanes], east_edge.at[first_quad]),
-            (x_hbm.at[last_quad, :, last_lanes], east_edge.at[pl.ds(QUAD, QUAD)]),
-            (x_hbm.at[mid_quads, :, pl.ds(0, 128)], west_edge),
         ))
     ]
     for copy in copies:
         copy.start()
     even = lax.axis_index("lat") % 2 == 0
-    for copy in copies[:4]:
+    for copy in copies:
         copy.wait()
     sea = mask_ref[...].astype(jnp.float32)
     moving = speed_ref[...] * sea
@@ -82,17 +78,19 @@
         first_ref[...] = down_ref[...]
         second_ref[...] = up_ref[...]
 
-    for copy in copies[4:]:
-        copy.wait()
+
+def pack_columns_kernel(x_ref, mov_ref, sea_ref, east_ref, west_ref):
+    height, breadth = mov_ref.shape
     lane = lax.broadcasted_iota(jnp.int32, (height, 128), 1)
     east = jnp.zeros((height, 128), jnp.float32)
     west = jnp.zeros((height, 128), jnp.float32)
     for q in range(HALF + 2):
         mine = lane // 2 == q
         if q < HALF:
-            edge_e, edge_w = east_edge[q], west_edge[q]
+            p_e = q if q < QUAD else q + HALF
+            edge_e, edge_w = x_ref[p_e, :, breadth - 128 :], x_ref[q + QUAD, :, :128]
         else:
-            field = moving if q == HALF else sea
+            field = (mov_ref if q == HALF else sea_ref)[...]
             edge_e, edge_w = field[:, breadth - 128 :], field[:, :128]
         east = jnp.where(mine, pltpu.roll(edge_e, (2 * q + 2) % 128, axis=1), east)
         west = jnp.where(mine, pltpu.roll(edge_w, 2 * q, axis=1), west)
@@ -377,16 +375,22 @@
         write.wait()
 
 
-def add_kernel(rows_ref, values_ref, out_ref, lines, tile_sums, window, window_sems, out_sem, *sums):
-    n_acc = len(sums) // 2
+def clear_kernel(_, *sums):
+    block = 520
+
+    @pl.loop(0, sums[0].shape[0] // block)
+    def _(i):
+        for total in sums:
+            total[pl.ds(pl.multiple_of(i * block, 8), block), :] = jnp.zeros((block, 128), jnp.float32)
+
+
+def add_kernel(rows_ref, values_ref, *refs):
+    n_acc = N_ACC
+    out_ref, sums = refs[2 * n_acc], refs[2 * n_acc + 1 : 4 * n_acc + 1]
+    lines, tile_sums, window, window_sems, out_sem = refs[4 * n_acc + 1 :]
     tile = out_ref.shape[1]
     block = 512
     half = WINDOW // 2
-
-    @pl.loop(0, tile // block)
-    def _(i):
-        for total in sums:
-            total[pl.ds(pl.multiple_of(i * block, block), block), :] = jnp.zeros((block, 128), jnp.float32)
 
     def add(row, i):
         lines[...] = values_ref[pl.ds(pl.multiple_of(i * half, half), half), :].astype(jnp.float32)
@@ -455,20 +459,28 @@
     columns = shape(height, 128)
     column_message = shape(height + 8, 128)
     row_first, row_second, column_first, column_second = exchange_pairs(n_lat, n_lon)
-    first, second, east, west, moving, sea = pl.pallas_call(
-        pack_kernel,
-        out_shape=[row_message] * 2 + [columns] * 2 + [shape(height, breadth)] * 2,
+    first, second, moving, sea = pl.pallas_call(
+        pack_rows_kernel,
+        out_shape=[row_message] * 2 + [shape(height, breadth)] * 2,
         in_specs=[hbm] * 3,
-        out_specs=[vmem] * 6,
+        out_specs=[vmem] * 4,
         scratch_shapes=[pltpu.VMEM((2, HALF + 4, breadth), f32)] * 2
         + [pltpu.VMEM((HALF, 8, breadth), f32)] * 2
-        + [pltpu.VMEM((HALF, height, 128), f32)] * 2
-        + [pltpu.VMEM((height, breadth), f32), pltpu.VMEM((height, breadth), jnp.int32), pltpu.SemaphoreType.DMA((7,))],
-        compiler_params=params,
-        name="pack_halos",
+        + [pltpu.VMEM((height, breadth), f32), pltpu.VMEM((height, breadth), jnp.int32), pltpu.SemaphoreType.DMA((4,))],
+        compiler_params=params,
+        name="pack_rows",
     )(*(pltpu.with_memory_space_constraint(v, pltpu.HBM) for v in (x, speed_factor, land_sea_mask)))
     second = lax.ppermute(second, both, row_second)
     first = lax.ppermute(first, "lat", row_first)
+    east, west = pl.pallas_call(
+        pack_columns_kernel,
+        out_shape=[columns] * 2,
+        in_specs=[vmem] * 3,
+        out_specs=[vmem] * 2,
+        compiler_params=params,
+        cost_estimate=pl.CostEstimate(flops=2_000_000_000, bytes_accessed=5_000_000, transcendentals=0),
+        name="pack_columns",
+    )(x, moving, sea)
     halves = pl.pallas_call(
         inside_kernel,
         out_shape=pltpu.VMEM((breadth // 128, (PLANES + 4) * height, 128), f32),
@@ -490,7 +502,9 @@
     first = lax.ppermute(first, "lon", column_first)
 
     cells = jnp.maximum(send_rows, 0).reshape(-1)
-    targets = jnp.where(recv_rows < 0, OUT_DEV, recv_rows).reshape(-1)
+    slot = jnp.arange(slots, dtype=jnp.int32)
+    spare = OUT_DEV + (slot // 16 * 8 + slot % 8) % SPARE
+    targets = jnp.where(recv_rows < 0, spare, recv_rows).reshape(-1)
     slot_rows = devices * slots // 2
     propagated, picked, _ = pl.pallas_call(
         finish_kernel,
@@ -520,22 +534,32 @@
     received = lax.all_to_all(picked, both, split_axis=0, concat_axis=0, tiled=True)
 
     components = depth_kernel.shape[0]
-    stokes = pl.pallas_call(
+    sums = [pltpu.VMEM((OUT_DEV + SPARE, 128), f32)] * (2 * N_ACC)
+    cleared = pl.pallas_call(
+        clear_kernel,
+        out_shape=sums,
+        in_specs=[hbm],
+        out_specs=[vmem] * len(sums),
+        compiler_params=params,
+        cost_estimate=pl.CostEstimate(flops=2_000_000_000, bytes_accessed=17_000_000, transcendentals=0),
+        name="clear_sums",
+    )(pltpu.with_memory_space_constraint(picked, pltpu.HBM))
+    stokes, *_ = pl.pallas_call(
         add_kernel,
-        out_shape=pltpu.HBM((components, OUT_DEV), f32),
-        in_specs=[hbm, vmem],
-        out_specs=hbm,
+        out_shape=[pltpu.HBM((components, OUT_DEV), f32)] + sums,
+        in_specs=[hbm, vmem] + [vmem] * len(sums),
+        out_specs=[hbm] + [vmem] * len(sums),
+        input_output_aliases={2 + k: 1 + k for k in range(len(sums))},
         scratch_shapes=[
             pltpu.VMEM((WINDOW // 2, 128), f32),
             pltpu.VMEM((components, OUT_DEV), f32),
             pltpu.SMEM((2 * WINDOW,), jnp.int32),
             pltpu.SemaphoreType.DMA((2,)),
             pltpu.SemaphoreType.DMA,
-        ]
-        + [pltpu.VMEM((OUT_DEV + 8, 128), f32)] * (2 * N_ACC),
+        ],
         compiler_params=params,
         name="add_profiles",
-    )(targets, received.reshape(slot_rows, 128))
+    )(targets, received.reshape(slot_rows, 128), *cleared)
     return propagated.reshape(DIRS, FREQ, height, breadth), stokes
 
 

time: 90.7 us -> 99.4 us (1.096)
  local copies, waits for them, and re-layouts: 0.05 us -> 23.7 us
  waiting for transfers between devices: 32.1 us -> 19.6 us
  Pallas kernels: 37.9 us -> 34.4 us
    unnamed x18 -> x50, local copies, waits for them, and re-layouts: 0.05 us -> 23.7 us
    all_to_all x1, waiting for transfers between devices: 29.5 us -> 17.4 us  [body(): lax.all_to_all(picked, both, split_axis=0, concat_axis=0, tiled=True)]
    pallas_call x2 -> x4, Pallas kernels: 20.3 us -> 16.9 us  [the longest x1 14 us: body(): pl.pallas_call(add_kernel, out_shape=[pltpu.HBM((components, OUT_DEV), f3...]
  transfers between devices with their start and end apart: 5 -> 5, of which waited for: 2 -> 2; matrix products, arithmetic and copies ran while one was open for 0% -> 0% of each run, Pallas kernels for 4% -> 5%
where the time goes in v5:
time: 99.4 us; the launch traced here: 98.9 us
  Pallas kernels  34.4 us (35%)
  local copies, waits for them, and re-layouts  23.7 us (24%)
  starting transfers between devices  20.2 us (20%)
  waiting for transfers between devices  19.6 us (20%)
    unnamed x50, local copies, waits for them, and re-layouts  23.7 us
    all_to_all x1, waiting for transfers between devices, body(): lax.all_to_all(picked, both, split_axis=0, concat_axis=0, tiled=True)  17.4 us
    pallas_call x1, Pallas kernels, body(): pl.pallas_call(finish_kernel, out_shape=[pltpu.HBM((PLANES * height, brea...  14.1 us
    pallas_call x1, Pallas kernels, body(): pl.pallas_call(add_kernel, out_shape=[pltpu.HBM((components, OUT_DEV), f3...  14 us
    all_to_all x1, starting transfers between devices, body(): lax.all_to_all(picked, both, split_axis=0, concat_axis=0, tiled=True)  9.12 us
    ppermute x1, starting transfers between devices, body(): second = lax.ppermute(second, 'lon', column_second)  4.71 us
    pallas_call x1, Pallas kernels, body(): pl.pallas_call(inside_kernel, out_shape=pltpu.VMEM((breadth // 128, (PLAN...  3.33 us
    ppermute x1, starting transfers between devices, body(): second = lax.ppermute(second, both, row_second)  3.1 us
  transfers between devices with their start and end apart: 5, of which 2 were waited for; matrix products, arithmetic and copies ran while one was open for 0% of the time, Pallas kernels for 5%

profile of v5, /device:TPU:1, one launch (start us, length us, event | category | flops | bytes accessed | tf_op | source)
XLA Modules:
  0.0 98.9 jit_solution(17931364945741828208)
XLA Ops:
  0.6 0.0 copy-start
  0.6 0.0 copy-start.23
  0.7 1.4 %pack_rows.1 = (f32[2,40,256]{2,1,0:T(8,128)S(1)}, f32[2,40,256]{2,1,0:T(8,128)S(1)}, f32[32,256]{1,0:T(8,128)S(1)}, f32[32,256]{1,0:T(8,128)S(1)}) custom-call(f32[72,32,256]{2,1,0:T(8,128)} %bitcast.9, f32[32,256]{1,0:T(8,128)} %speed_hbm.1, s32[32,256]{1,0:T(8,128)} %mask_hbm.1), custom_call_target="tpu_custom_call" | custom-call | tf_op jit(solution)/shard_map/pack_rows/pallas_call | solution.py:462
  2.0 1.5 %collective-permute-start = (f32[2,40,256]{2,1,0:T(8,128)S(1)}, f32[2,40,256]{2,1,0:T(8,128)S(1)}, u32[]{:S(2)}, u32[]{:S(2)}) collective-permute-start(f32[2,40,256]{2,1,0:T(8,128)S(1)} %get-tuple-element.25), channel_id=1, source_target_pairs={{0,16},{16,0},{32,48},{48,32},{64,80},{80,64},{96,112},{112,96},{1... | collective-permute-start | bytes 245768 | tf_op jit(solution)/shard_map/ppermute | solution.py:474
  3.5 3.1 %collective-permute-start.1 = (f32[2,40,256]{2,1,0:T(8,128)S(1)}, f32[2,40,256]{2,1,0:T(8,128)S(1)}, u32[]{:S(2)}, u32[]{:S(2)}) collective-permute-start(f32[2,40,256]{2,1,0:T(8,128)S(1)} %get-tuple-element.26), channel_id=1, source_target_pairs={{0,0},{112,127},{16,32},{32,16},{48,64},{64,48},{80,96},{96,80},{1... | collective-permute-start | bytes 245768 | tf_op jit(solution)/shard_map/ppermute | solution.py:473
  6.7 0.0 copy-done.23
  6.7 0.0 copy-done
  6.7 0.0 copy-start.20
  6.7 0.0 copy-start.21
  6.7 0.0 copy-start.22
  6.7 0.4 pack_columns.1
  7.1 0.0 collective-permute-done.first_ref
  7.1 2.2 %collective-permute-done.1.second_ref = f32[2,40,256]{2,1,0:T(8,128)S(1)} collective-permute-done((f32[2,40,256]{2,1,0:T(8,128)S(1)}, f32[2,40,256]{2,1,0:T(8,128)S(1)}, u32[]{:S(2)}, u32[]{:S(2)}) %collective-permute-start.1) | collective-permute-done | bytes 81952 | tf_op jit(solution)/shard_map/ppermute | solution.py:473
  9.3 0.1 add_corners.1
  9.4 1.8 %collective-permute-start.2 = (f32[40,128]{1,0:T(8,128)S(1)}, f32[40,128]{1,0:T(8,128)S(1)}, u32[]{:S(2)}, u32[]{:S(2)}) collective-permute-start(f32[40,128]{1,0:T(8,128)S(1)} %get-tuple-element.31), channel_id=1, source_target_pairs={{0,1},{1,0},{2,3},{3,2},{4,5},{5,4},{6,7},{7,6},{8,9},{9,8},{10,11... | collective-permute-start | bytes 61448 | tf_op jit(solution)/shard_map/ppermute | solution.py:502
  11.2 4.7 %collective-permute-start.3 = (f32[40,128]{1,0:T(8,128)S(1)}, f32[40,128]{1,0:T(8,128)S(1)}, u32[]{:S(2)}, u32[]{:S(2)}) collective-permute-start(f32[40,128]{1,0:T(8,128)S(1)} %get-tuple-element.32), channel_id=1, source_target_pairs={{0,15},{1,2},{2,1},{3,4},{4,3},{5,6},{6,5},{7,8},{8,7},{9,10},{10,... | collective-permute-start | bytes 61448 | tf_op jit(solution)/shard_map/ppermute | solution.py:501
  15.9 0.0 copy-done.20
  15.9 0.0 copy-done.21
  15.9 0.0 copy-done.22
  15.9 3.3 %advance_inside.1.halves_in = f32[2,2432,128]{2,1,0:T(8,128)S(1)} custom-call(f32[2]{0:T(128)S(1)} %copy-done.20, f32[72]{0:T(128)S(1)} %copy-done.22, f32[72]{0:T(128)S(1)} %copy-done.21, f32[72,32,256]{2,1,0:T(8,128)S(1)} %bitcast.11, f32[32,256]{1,0:T(8,128)S(1)} %get-tuple-element.23.mov_ref, f32[32,256]{1,0:T(8,128)S(1)} %get-tuple-element.24.sea_ref), custom_call_target="tpu_custom_call" | custom-call | flops 4000000000 | bytes 5000000 | tf_op jit(solution)/shard_map/advance_inside/pallas_call | solution.py:484
  19.3 0.0 collective-permute-done.2.first_ref
  19.3 0.0 collective-permute-done.3.second_ref
  19.3 0.0 copy-done.17
  19.3 0.0 copy-done.18
  19.3 0.0 copy-done.19
  19.3 14.1 %finish_and_pick.1 = (f32[2304,256]{1,0:T(8,128)}, bf16[8192,128]{1,0:T(8,128)(2,1)}, f32[2,2432,128]{2,1,0:T(8,128)S(1)}) custom-call(f32[2]{0:T(128)S(1)} %copy-done.20, s32[16384]{0:T(1024)S(1)} %maximum_bitcast_fusion.cells_ref, f32[32,256]{1,0:T(8,128)S(1)} %get-tuple-element.23.mov_ref, ...), custom_call_target="tpu_custom_call", output_to_operand_aliasing={{2}: (11, {})} | custom-call | tf_op jit(solution)/shard_map/finish_and_pick/pallas_call | solution.py:509
  33.4 0.0 copy-start.24
  33.4 9.1 %all-to-all-start = ((bf16[128,64,128]{2,1,0:T(8,128)(2,1)}), bf16[128,64,128]{2,1,0:T(8,128)(2,1)S(1)}, u32[]{:S(2)}, u32[]{:S(2)}) async-start(bf16[128,64,128]{2,1,0:T(8,128)(2,1)} %bitcast.12), calls=%async_computation | async-start | bytes 4194304 | tf_op jit(solution)/shard_map/all_to_all | solution.py:534
  42.6 0.0 copy-done.24
  42.6 1.1 %clear_sums.1 = (f32[4160,128]{1,0:T(8,128)S(1)}, f32[4160,128]{1,0:T(8,128)S(1)}, f32[4160,128]{1,0:T(8,128)S(1)}, f32[4160,128]{1,0:T(8,128)S(1)}, f32[4160,12...) custom-call(bf16[128,64,128]{2,1,0:T(8,128)(2,1)} %bitcast.13), custom_call_target="tpu_custom_call" | custom-call | flops 2000000000 | bytes 17000000 | tf_op jit(solution)/shard_map/clear_sums/pallas_call | solution.py:538
  43.7 1.4 %copy-done.1 = f32[4160,128]{1,0:T(8,128)} copy-done((f32[4160,128]{1,0:T(8,128)}, f32[4160,128]{1,0:T(8,128)S(1)}, u32[]{:S(2)}) %copy-start.1) | copy-done | bytes 2129944
  45.1 1.3 %copy-done.3 = f32[4160,128]{1,0:T(8,128)} copy-done((f32[4160,128]{1,0:T(8,128)}, f32[4160,128]{1,0:T(8,128)S(1)}, u32[]{:S(2)}) %copy-start.3) | copy-done | bytes 2129944
  46.5 1.4 %copy-done.5 = f32[4160,128]{1,0:T(8,128)} copy-done((f32[4160,128]{1,0:T(8,128)}, f32[4160,128]{1,0:T(8,128)S(1)}, u32[]{:S(2)}) %copy-start.5) | copy-done | bytes 2129944
  47.8 1.4 %copy-done.7 = f32[4160,128]{1,0:T(8,128)} copy-done((f32[4160,128]{1,0:T(8,128)}, f32[4160,128]{1,0:T(8,128)S(1)}, u32[]{:S(2)}) %copy-start.7) | copy-done | bytes 2129944
  49.3 1.3 %copy-done.9 = f32[4160,128]{1,0:T(8,128)} copy-done((f32[4160,128]{1,0:T(8,128)}, f32[4160,128]{1,0:T(8,128)S(1)}, u32[]{:S(2)}) %copy-start.9) | copy-done | bytes 2129944
  50.6 1.4 %copy-done.11 = f32[4160,128]{1,0:T(8,128)} copy-done((f32[4160,128]{1,0:T(8,128)}, f32[4160,128]{1,0:T(8,128)S(1)}, u32[]{:S(2)}) %copy-start.11) | copy-done | bytes 2129944
  52.0 1.3 %copy-done.13 = f32[4160,128]{1,0:T(8,128)} copy-done((f32[4160,128]{1,0:T(8,128)}, f32[4160,128]{1,0:T(8,128)S(1)}, u32[]{:S(2)}) %copy-start.13) | copy-done | bytes 2129944
  53.3 1.3 %copy-done.15 = f32[4160,128]{1,0:T(8,128)} copy-done((f32[4160,128]{1,0:T(8,128)}, f32[4160,128]{1,0:T(8,128)S(1)}, u32[]{:S(2)}) %copy-start.15) | copy-done | bytes 2129944
  54.6 17.4 %all-to-all-done = bf16[128,64,128]{2,1,0:T(8,128)(2,1)S(1)} async-done(((bf16[128,64,128]{2,1,0:T(8,128)(2,1)}), bf16[128,64,128]{2,1,0:T(8,128)(2,1)S(1)}, u32[]{:S(2)}, u32[]{:S(2)}) %all-to-all-start) | async-done | bytes 2097184 | tf_op jit(solution)/shard_map/all_to_all | solution.py:534
  72.1 1.6 %copy-done.2 = f32[4160,128]{1,0:T(8,128)S(1)} copy-done((f32[4160,128]{1,0:T(8,128)S(1)}, f32[4160,128]{1,0:T(8,128)}, u32[]{:S(2)}) %copy-start.2) | copy-done | bytes 2129944
  73.7 1.6 %copy-done.4 = f32[4160,128]{1,0:T(8,128)S(1)} copy-done((f32[4160,128]{1,0:T(8,128)S(1)}, f32[4160,128]{1,0:T(8,128)}, u32[]{:S(2)}) %copy-start.4) | copy-done | bytes 2129944
  75.3 1.6 %copy-done.6 = f32[4160,128]{1,0:T(8,128)S(1)} copy-done((f32[4160,128]{1,0:T(8,128)S(1)}, f32[4160,128]{1,0:T(8,128)}, u32[]{:S(2)}) %copy-start.6) | copy-done | bytes 2129944
  76.9 1.6 %copy-done.8 = f32[4160,128]{1,0:T(8,128)S(1)} copy-done((f32[4160,128]{1,0:T(8,128)S(1)}, f32[4160,128]{1,0:T(8,128)}, u32[]{:S(2)}) %copy-start.8) | copy-done | bytes 2129944
  78.5 1.6 %copy-done.10 = f32[4160,128]{1,0:T(8,128)S(1)} copy-done((f32[4160,128]{1,0:T(8,128)S(1)}, f32[4160,128]{1,0:T(8,128)}, u32[]{:S(2)}) %copy-start.10) | copy-done | bytes 2129944
  80.1 1.6 %copy-done.12 = f32[4160,128]{1,0:T(8,128)S(1)} copy-done((f32[4160,128]{1,0:T(8,128)S(1)}, f32[4160,128]{1,0:T(8,128)}, u32[]{:S(2)}) %copy-start.12) | copy-done | bytes 2129944
  81.7 1.6 %copy-done.14 = f32[4160,128]{1,0:T(8,128)S(1)} copy-done((f32[4160,128]{1,0:T(8,128)S(1)}, f32[4160,128]{1,0:T(8,128)}, u32[]{:S(2)}) %copy-start.14) | copy-done | bytes 2129944
  83.3 1.6 %copy-done.16 = f32[4160,128]{1,0:T(8,128)S(1)} copy-done((f32[4160,128]{1,0:T(8,128)S(1)}, f32[4160,128]{1,0:T(8,128)}, u32[]{:S(2)}) %copy-start.16) | copy-done | bytes 2129944
  84.9 14.0 %add_profiles.1 = (f32[64,4096]{1,0:T(8,128)}, f32[4160,128]{1,0:T(8,128)S(1)}, f32[4160,128]{1,0:T(8,128)S(1)}, f32[4160,128]{1,0:T(8,128)S(1)}, f32[4160,128]{...) custom-call(s32[16384]{0:T(1024)S(1)} %fusion.rows_ref, ...), custom_call_target="tpu_custom_call", output_to_operand_aliasing={{1}: (2, {}), {2}: (3, {}), {3}: (4, {}), {4}: (5, {}), {5}... | custom-call | tf_op jit(solution)/shard_map/add_profiles/pallas_call | solution.py:547
  (22 shorter events, 0.1 us)
Async XLA Ops:
  0.6 6.1 %copy-start = (f32[36,2,32,256]{3,2,1,0:T(8,128)S(1)}, f32[36,2,32,256]{3,2,1,0:T(8,128)}, u32[]{:S(2)}) copy-start(f32[36,2,32,256]{3,2,1,0:T(8,128)} %param.11) | copy-start | bytes 7077892
  0.6 6.0 %copy-start.23 = (s32[1,128,128]{2,1,0:T(8,128)S(1)}, s32[1,128,128]{2,1,0:T(8,128)}, u32[]{:S(2)}) copy-start(s32[1,128,128]{2,1,0:T(8,128)} %param.16) | copy-start | bytes 196612
  2.0 5.1 %collective-permute-start = (f32[2,40,256]{2,1,0:T(8,128)S(1)}, f32[2,40,256]{2,1,0:T(8,128)S(1)}, u32[]{:S(2)}, u32[]{:S(2)}) collective-permute-start(f32[2,40,256]{2,1,0:T(8,128)S(1)} %get-tuple-element.25), channel_id=1, source_target_pairs={{0,16},{16,0},{32,48},{48,32},{64,80},{80,64},{96,112},{112,96},{1... | collective-permute-start | bytes 245768 | tf_op jit(solution)/shard_map/ppermute | solution.py:474
  3.5 5.7 %collective-permute-start.1 = (f32[2,40,256]{2,1,0:T(8,128)S(1)}, f32[2,40,256]{2,1,0:T(8,128)S(1)}, u32[]{:S(2)}, u32[]{:S(2)}) collective-permute-start(f32[2,40,256]{2,1,0:T(8,128)S(1)} %get-tuple-element.26), channel_id=1, source_target_pairs={{0,0},{112,127},{16,32},{32,16},{48,64},{64,48},{80,96},{96,80},{1... | collective-permute-start | bytes 245768 | tf_op jit(solution)/shard_map/ppermute | solution.py:473
  6.7 9.2 %copy-start.20 = (f32[2]{0:T(128)S(1)}, f32[2]{0:T(128)}, u32[]{:S(2)}) copy-start(f32[2]{0:T(128)} %courant_ref.3) | copy-start | bytes 28
  6.7 9.2 %copy-start.21 = (f32[72]{0:T(128)S(1)}, f32[72]{0:T(128)}, u32[]{:S(2)}) copy-start(f32[72]{0:T(128)} %constant.57.clone.sin_ref) | copy-start | bytes 868
  6.7 9.2 %copy-start.22 = (f32[72]{0:T(128)S(1)}, f32[72]{0:T(128)}, u32[]{:S(2)}) copy-start(f32[72]{0:T(128)} %constant.56.clone.cos_ref) | copy-start | bytes 868
  9.4 9.9 %collective-permute-start.2 = (f32[40,128]{1,0:T(8,128)S(1)}, f32[40,128]{1,0:T(8,128)S(1)}, u32[]{:S(2)}, u32[]{:S(2)}) collective-permute-start(f32[40,128]{1,0:T(8,128)S(1)} %get-tuple-element.31), channel_id=1, source_target_pairs={{0,1},{1,0},{2,3},{3,2},{4,5},{5,4},{6,7},{7,6},{8,9},{9,8},{10,11... | collective-permute-start | bytes 61448 | tf_op jit(solution)/shard_map/ppermute | solution.py:502
  11.2 8.1 %copy-start.17 = (f32[64,72]{1,0:T(8,128)S(1)}, f32[64,72]{1,0:T(8,128)}, u32[]{:S(2)}) copy-start(f32[64,72]{1,0:T(8,128)} %kernel_ref.1) | copy-start | bytes 55300
  11.2 8.1 %copy-start.18 = (f32[40,128]{1,0:T(8,128)S(1)}, f32[40,128]{1,0:T(8,128)}, u32[]{:S(2)}) copy-start(f32[40,128]{1,0:T(8,128)} %constant.59.clone.subs_ref) | copy-start | bytes 61444
  11.2 8.1 %copy-start.19 = (f32[8,128]{1,0:T(8,128)S(1)}, f32[8,128]{1,0:T(8,128)}, u32[]{:S(2)}) copy-start(f32[8,128]{1,0:T(8,128)} %constant.58.clone.lanes_ref) | copy-start | bytes 12292
  11.2 8.1 %collective-permute-start.3 = (f32[40,128]{1,0:T(8,128)S(1)}, f32[40,128]{1,0:T(8,128)S(1)}, u32[]{:S(2)}, u32[]{:S(2)}) collective-permute-start(f32[40,128]{1,0:T(8,128)S(1)} %get-tuple-element.32), channel_id=1, source_target_pairs={{0,15},{1,2},{2,1},{3,4},{4,3},{5,6},{6,5},{7,8},{8,7},{9,10},{10,... | collective-permute-start | bytes 61448 | tf_op jit(solution)/shard_map/ppermute | solution.py:501
  33.4 9.2 %copy-start.24 = (s32[1,128,128]{2,1,0:T(8,128)S(1)}, s32[1,128,128]{2,1,0:T(8,128)}, u32[]{:S(2)}) copy-start(s32[1,128,128]{2,1,0:T(8,128)} %param.17) | copy-start | bytes 196612
  33.4 38.6 %all-to-all-start = ((bf16[128,64,128]{2,1,0:T(8,128)(2,1)}), bf16[128,64,128]{2,1,0:T(8,128)(2,1)S(1)}, u32[]{:S(2)}, u32[]{:S(2)}) async-start(bf16[128,64,128]{2,1,0:T(8,128)(2,1)} %bitcast.12), calls=%async_computation | async-start | bytes 4194304 | tf_op jit(solution)/shard_map/all_to_all | solution.py:534
  43.7 1.4 %copy-start.1 = (f32[4160,128]{1,0:T(8,128)}, f32[4160,128]{1,0:T(8,128)S(1)}, u32[]{:S(2)}) copy-start(f32[4160,128]{1,0:T(8,128)S(1)} %get-tuple-element.35.refs_0_) | copy-start | bytes 6389764
  45.1 1.3 %copy-start.3 = (f32[4160,128]{1,0:T(8,128)}, f32[4160,128]{1,0:T(8,128)S(1)}, u32[]{:S(2)}) copy-start(f32[4160,128]{1,0:T(8,128)S(1)} %get-tuple-element.36.refs_1_) | copy-start | bytes 6389764
  46.5 1.4 %copy-start.5 = (f32[4160,128]{1,0:T(8,128)}, f32[4160,128]{1,0:T(8,128)S(1)}, u32[]{:S(2)}) copy-start(f32[4160,128]{1,0:T(8,128)S(1)} %get-tuple-element.37.refs_2_) | copy-start | bytes 6389764
  47.8 1.4 %copy-start.7 = (f32[4160,128]{1,0:T(8,128)}, f32[4160,128]{1,0:T(8,128)S(1)}, u32[]{:S(2)}) copy-start(f32[4160,128]{1,0:T(8,128)S(1)} %get-tuple-element.38.refs_3_) | copy-start | bytes 6389764
  49.3 1.3 %copy-start.9 = (f32[4160,128]{1,0:T(8,128)}, f32[4160,128]{1,0:T(8,128)S(1)}, u32[]{:S(2)}) copy-start(f32[4160,128]{1,0:T(8,128)S(1)} %get-tuple-element.39.refs_4_) | copy-start | bytes 6389764
  50.6 1.4 %copy-start.11 = (f32[4160,128]{1,0:T(8,128)}, f32[4160,128]{1,0:T(8,128)S(1)}, u32[]{:S(2)}) copy-start(f32[4160,128]{1,0:T(8,128)S(1)} %get-tuple-element.40.refs_5_) | copy-start | bytes 6389764
  52.0 1.3 %copy-start.13 = (f32[4160,128]{1,0:T(8,128)}, f32[4160,128]{1,0:T(8,128)S(1)}, u32[]{:S(2)}) copy-start(f32[4160,128]{1,0:T(8,128)S(1)} %get-tuple-element.41.refs_6_) | copy-start | bytes 6389764
  53.3 1.3 %copy-start.15 = (f32[4160,128]{1,0:T(8,128)}, f32[4160,128]{1,0:T(8,128)S(1)}, u32[]{:S(2)}) copy-start(f32[4160,128]{1,0:T(8,128)S(1)} %get-tuple-element.42.refs_7_) | copy-start | bytes 6389764
  72.1 1.6 %copy-start.2 = (f32[4160,128]{1,0:T(8,128)S(1)}, f32[4160,128]{1,0:T(8,128)}, u32[]{:S(2)}) copy-start(f32[4160,128]{1,0:T(8,128)} %copy-done.1) | copy-start | bytes 6389764
  73.7 1.6 %copy-start.4 = (f32[4160,128]{1,0:T(8,128)S(1)}, f32[4160,128]{1,0:T(8,128)}, u32[]{:S(2)}) copy-start(f32[4160,128]{1,0:T(8,128)} %copy-done.3) | copy-start | bytes 6389764
  75.3 1.6 %copy-start.6 = (f32[4160,128]{1,0:T(8,128)S(1)}, f32[4160,128]{1,0:T(8,128)}, u32[]{:S(2)}) copy-start(f32[4160,128]{1,0:T(8,128)} %copy-done.5) | copy-start | bytes 6389764
  76.9 1.6 %copy-start.8 = (f32[4160,128]{1,0:T(8,128)S(1)}, f32[4160,128]{1,0:T(8,128)}, u32[]{:S(2)}) copy-start(f32[4160,128]{1,0:T(8,128)} %copy-done.7) | copy-start | bytes 6389764
  78.5 1.6 %copy-start.10 = (f32[4160,128]{1,0:T(8,128)S(1)}, f32[4160,128]{1,0:T(8,128)}, u32[]{:S(2)}) copy-start(f32[4160,128]{1,0:T(8,128)} %copy-done.9) | copy-start | bytes 6389764
  80.1 1.6 %copy-start.12 = (f32[4160,128]{1,0:T(8,128)S(1)}, f32[4160,128]{1,0:T(8,128)}, u32[]{:S(2)}) copy-start(f32[4160,128]{1,0:T(8,128)} %copy-done.11) | copy-start | bytes 6389764
  81.7 1.6 %copy-start.14 = (f32[4160,128]{1,0:T(8,128)S(1)}, f32[4160,128]{1,0:T(8,128)}, u32[]{:S(2)}) copy-start(f32[4160,128]{1,0:T(8,128)} %copy-done.13) | copy-start | bytes 6389764
  83.3 1.6 %copy-start.16 = (f32[4160,128]{1,0:T(8,128)S(1)}, f32[4160,128]{1,0:T(8,128)}, u32[]{:S(2)}) copy-start(f32[4160,128]{1,0:T(8,128)} %copy-done.15) | copy-start | bytes 6389764

commit v6 on v5

--- a/solution.py
+++ b/solution.py
@@ -17,8 +17,10 @@
 OUT_DEV = 4096
 SPARE = 64
 N_ACC = 4
+ROWS = HALF + 12
 WINDOW = 1024
 VMEM_LIMIT = 16 * 1024 * 1024
+ADD_VMEM_LIMIT = 32 * 1024 * 1024
 
 
 def exchange_pairs(n_lat, n_lon):
@@ -65,18 +67,18 @@
         down_ref[k, HALF : HALF + 1, :] = moving[k : k + 1, :]
         up_ref[k, HALF + 1 : HALF + 2, :] = sea[height - 1 - k : height - k, :]
         down_ref[k, HALF + 1 : HALF + 2, :] = sea[k : k + 1, :]
-        up_ref[k, HALF + 2 :, :] = jnp.zeros((2, breadth), jnp.float32)
-        down_ref[k, HALF + 2 :, :] = jnp.zeros((2, breadth), jnp.float32)
+        up_ref[k, HALF + 2 :, :] = jnp.zeros((ROWS - HALF - 2, breadth), jnp.float32)
+        down_ref[k, HALF + 2 :, :] = jnp.zeros((ROWS - HALF - 2, breadth), jnp.float32)
 
     @pl.when(even)
     def _():
-        first_ref[...] = up_ref[...]
-        second_ref[...] = down_ref[...]
+        first_ref[...] = up_ref[...].astype(jnp.bfloat16)
+        second_ref[...] = down_ref[...].astype(jnp.bfloat16)
 
     @pl.when(jnp.logical_not(even))
     def _():
-        first_ref[...] = down_ref[...]
-        second_ref[...] = up_ref[...]
+        first_ref[...] = down_ref[...].astype(jnp.bfloat16)
+        second_ref[...] = up_ref[...].astype(jnp.bfloat16)
 
 
 def pack_columns_kernel(x_ref, mov_ref, sea_ref, east_ref, west_ref):
@@ -104,15 +106,17 @@
     lat = lax.axis_index("lat")
     even = lat % 2 == 0
 
+    used = HALF + 4
+
     @pl.when(even)
     def _():
-        north_ref[...] = first_ref[...]
-        south_ref[...] = second_ref[...]
+        north_ref[...] = first_ref[...].astype(jnp.float32)[:, :used]
+        south_ref[...] = second_ref[...].astype(jnp.float32)[:, :used]
 
     @pl.when(jnp.logical_not(even))
     def _():
-        south_ref[...] = first_ref[...]
-        north_ref[...] = second_ref[...]
+        south_ref[...] = first_ref[...].astype(jnp.float32)[:, :used]
+        north_ref[...] = second_ref[...].astype(jnp.float32)[:, :used]
 
     @pl.when(lat == 0)
     def _():
@@ -122,11 +126,11 @@
     def _():
         flip_i = lax.broadcasted_iota(jnp.int32, (breadth, breadth), 0)
         flip_j = lax.broadcasted_iota(jnp.int32, (breadth, breadth), 1)
-        flip = (flip_i + flip_j == breadth - 1).astype(jnp.float32)
-        for k in range(2):
-            north_ref[k] = jnp.dot(
-                north_ref[k], flip, precision=lax.Precision.HIGHEST, preferred_element_type=jnp.float32
-            )
+        flip = (flip_i + flip_j == breadth - 1).astype(jnp.bfloat16)
+        both = jnp.concatenate([second_ref[0], second_ref[1]], axis=0)
+        flipped = jnp.dot(both, flip, preferred_element_type=jnp.float32)
+        north_ref[0] = flipped[:used]
+        north_ref[1] = flipped[ROWS : ROWS + used]
 
     plane = lax.broadcasted_iota(jnp.int32, (HALF + 4, 128), 0)
     lane = lax.broadcasted_iota(jnp.int32, (HALF + 4, 128), 1)
@@ -224,9 +228,55 @@
     quadrant(3 * QUAD, True, False)
 
 
-def finish_kernel(courant_ref, cells_ref, mov_ref, sea_ref, kernel_ref, south_ref, north_ref, first_ref, second_ref,
-                  lanes_ref, subs_ref, halves_in, out_ref, picked_ref, halves,
-                  table, lines, picks, wide_kernel, window, out_sems, window_sems, pick_sem):
+def profile_rows(halves, weight, table, first_row, count, height, breadth):
+    pad = jnp.zeros((8, 128), jnp.bfloat16)
+    blocks = []
+    for k in range(count):
+        for h in range(breadth // 128):
+            spectra = halves[h, pl.ds(first_row + k, PLANES, stride=height), :]
+            high = spectra.astype(jnp.bfloat16)
+            low = (spectra - high.astype(jnp.float32)).astype(jnp.bfloat16)
+            blocks.append(jnp.concatenate([high, pad, low, pad, high, pad], axis=0))
+    stacked = jnp.concatenate(blocks, axis=1)
+    profile = lax.dot_general(stacked, weight, (((0,), (0,)), ((), ())), preferred_element_type=jnp.float32)
+    start = first_row * breadth
+    if not isinstance(start, int):
+        start = pl.multiple_of(start, 128)
+    table[pl.ds(start, count * breadth), :] = profile
+
+
+def profile_kernel(halves, kernel_ref, table, weight_ref, edge_ref, wide_kernel):
+    height, breadth = halves.shape[1] // (PLANES + 4), table.shape[0] // (halves.shape[1] // (PLANES + 4))
+    pad = jnp.zeros((8, 128), jnp.bfloat16)
+    wide_kernel[...] = jnp.zeros((128, 128), jnp.float32)
+    wide_kernel[:64, :PLANES] = kernel_ref[...]
+    wide_kernel[64:, :PLANES] = kernel_ref[...]
+    turned = wide_kernel[...].T
+    weight_high = turned[:PLANES].astype(jnp.bfloat16)
+    weight_low = (turned[:PLANES] - weight_high.astype(jnp.float32)).astype(jnp.bfloat16)
+    weight = jnp.concatenate([weight_high, pad, weight_high, pad, weight_low, pad], axis=0)
+    weight_ref[...] = weight
+
+    lane = lax.broadcasted_iota(jnp.int32, (128, 128), 0)
+    plane = lax.broadcasted_iota(jnp.int32, (128, 128), 1)
+    q = lane // 2
+    used = lane < 2 * HALF
+    for side, owner in ((0, jnp.where(q < QUAD, q, q + HALF)), (1, q + QUAD)):
+        for k in range(2):
+            chosen = used & (plane == owner) & (lane % 2 == (k if side == 0 else 1 - k))
+            edge_ref[side, :, k * 128 : (k + 1) * 128] = jnp.dot(
+                chosen.astype(jnp.float32), turned, precision=lax.Precision.HIGHEST, preferred_element_type=jnp.float32
+            )
+    group = 8
+
+    @pl.loop(0, height // group)
+    def _(r):
+        profile_rows(halves, weight, table, r * group, group, height, breadth)
+
+
+def finish_kernel(courant_ref, cells_ref, mov_ref, sea_ref, weight_ref, edge_ref, south_ref, north_ref, first_ref,
+                  second_ref, lanes_ref, subs_ref, halves_in, table_in, out_ref, picked_ref, halves, table,
+                  lines, picks, window, out_sems, window_sems, pick_sem):
     height, breadth = mov_ref.shape
     c0, c1 = courant_ref[0], courant_ref[1]
     even_lon = lax.axis_index("lon") % 2 == 0
@@ -318,11 +368,12 @@
             turned = pltpu.roll(both, ((128 if from_west else 126) - 2 * q) % 128, axis=1)
             place = pl.ds(p * height, height)
             halves[half, place, :] = halves[half, place, :] + jnp.where(edge, turned, 0.0)
+        return jnp.where(lane < 2 * HALF, both, 0.0)
 
     add_rows(0, 0, 1, south_flux0, south_flux1, cx_s, cy_s, True)
     add_rows(HALF, height - 1, height - 2, north_flux0, north_flux1, cx_n, -cy_n, False)
-    add_columns(0, 0, 1, west_flux0, west_flux1, cx_w, cy_w, True)
-    add_columns(breadth // 128 - 1, breadth - 1, breadth - 2, east_flux0, east_flux1, -cx_e, cy_e, False)
+    change_w = add_columns(0, 0, 1, west_flux0, west_flux1, cx_w, cy_w, True)
+    change_e = add_columns(breadth // 128 - 1, breadth - 1, breadth - 2, east_flux0, east_flux1, -cx_e, cy_e, False)
     whole = pl.ds(0, PLANES * height)
     writes = [
         pltpu.make_async_copy(halves.at[h, whole, :], out_ref.at[:, pl.ds(h * 128, 128)], out_sems.at[h])
@@ -331,30 +382,15 @@
     for write in writes:
         write.start()
 
-    pad = jnp.zeros((8, 128), jnp.bfloat16)
-    wide_kernel[...] = jnp.zeros((128, 128), jnp.float32)
-    wide_kernel[:64, :PLANES] = kernel_ref[...]
-    wide_kernel[64:, :PLANES] = kernel_ref[...]
-    turned = wide_kernel[...].T[:PLANES]
-    weight_high = turned.astype(jnp.bfloat16)
-    weight_low = (turned - weight_high.astype(jnp.float32)).astype(jnp.bfloat16)
-    weight = jnp.concatenate([weight_high, pad, weight_high, pad, weight_low, pad], axis=0)
-
-    group = 8
-
-    @pl.loop(0, height // group)
-    def _(r):
-        blocks = []
-        for k in range(group):
-            for h in range(breadth // 128):
-                spectra = halves[h, pl.ds(r * group + k, PLANES, stride=height), :]
-                high = spectra.astype(jnp.bfloat16)
-                low = (spectra - high.astype(jnp.float32)).astype(jnp.bfloat16)
-                blocks.append(jnp.concatenate([high, pad, low, pad, high, pad], axis=0))
-        stacked = jnp.concatenate(blocks, axis=1)
-        profile = lax.dot_general(stacked, weight, (((0,), (0,)), ((), ())), preferred_element_type=jnp.float32)
-        start = pl.multiple_of(r * group * breadth, 128)
-        table[pl.ds(start, group * breadth), :] = profile
+    for change, columns_of, near, next_column in ((change_w, 0, 0, 1), (change_e, 1, breadth - 1, breadth - 2)):
+        profile = jnp.dot(
+            change, edge_ref[columns_of], precision=lax.Precision.HIGHEST, preferred_element_type=jnp.float32
+        )
+        for k, column in enumerate((near, next_column)):
+            place = pl.ds(column, height, stride=breadth)
+            table[place, :] = table[place, :] + profile[:, k * 128 : (k + 1) * 128]
+    for first_row in (0, height - 2):
+        profile_rows(halves, weight_ref[...], table, first_row, 2, height, breadth)
 
     first_half = lax.broadcasted_iota(jnp.int32, (1, 128), 1) < 64
     half = WINDOW // 2
@@ -375,22 +411,16 @@
         write.wait()
 
 
-def clear_kernel(_, *sums):
-    block = 520
-
-    @pl.loop(0, sums[0].shape[0] // block)
-    def _(i):
-        for total in sums:
-            total[pl.ds(pl.multiple_of(i * block, 8), block), :] = jnp.zeros((block, 128), jnp.float32)
-
-
-def add_kernel(rows_ref, values_ref, *refs):
-    n_acc = N_ACC
-    out_ref, sums = refs[2 * n_acc], refs[2 * n_acc + 1 : 4 * n_acc + 1]
-    lines, tile_sums, window, window_sems, out_sem = refs[4 * n_acc + 1 :]
+def add_kernel(rows_ref, values_ref, out_ref, lines, tile_sums, window, window_sems, out_sem, *sums):
+    n_acc = len(sums) // 2
     tile = out_ref.shape[1]
     block = 512
     half = WINDOW // 2
+
+    @pl.loop(0, tile // block)
+    def _(i):
+        for total in sums:
+            total[pl.ds(pl.multiple_of(i * block, block), block), :] = jnp.zeros((block, 128), jnp.float32)
 
     def add(row, i):
         lines[...] = values_ref[pl.ds(pl.multiple_of(i * half, half), half), :].astype(jnp.float32)
@@ -455,7 +485,8 @@
         return jax.ShapeDtypeStruct(dims, kind)
 
     cos, sin, lanes, subs = constant_tables()
-    row_message = shape(2, HALF + 4, breadth)
+    row_message = shape(2, ROWS, breadth, kind=jnp.bfloat16)
+    row_halo = shape(2, HALF + 4, breadth)
     columns = shape(height, 128)
     column_message = shape(height + 8, 128)
     row_first, row_second, column_first, column_second = exchange_pairs(n_lat, n_lon)
@@ -464,7 +495,7 @@
         out_shape=[row_message] * 2 + [shape(height, breadth)] * 2,
         in_specs=[hbm] * 3,
         out_specs=[vmem] * 4,
-        scratch_shapes=[pltpu.VMEM((2, HALF + 4, breadth), f32)] * 2
+        scratch_shapes=[pltpu.VMEM((2, ROWS, breadth), f32)] * 2
         + [pltpu.VMEM((HALF, 8, breadth), f32)] * 2
         + [pltpu.VMEM((height, breadth), f32), pltpu.VMEM((height, breadth), jnp.int32), pltpu.SemaphoreType.DMA((4,))],
         compiler_params=params,
@@ -492,7 +523,7 @@
     )(courant, cos, sin, x, moving, sea)
     south, north, first, second = pl.pallas_call(
         functools.partial(corner_kernel, n_lat),
-        out_shape=[row_message] * 2 + [column_message] * 2,
+        out_shape=[row_halo] * 2 + [column_message] * 2,
         in_specs=[vmem] * 4,
         out_specs=[vmem] * 4,
         compiler_params=params,
@@ -506,21 +537,32 @@
     spare = OUT_DEV + (slot // 16 * 8 + slot % 8) % SPARE
     targets = jnp.where(recv_rows < 0, spare, recv_rows).reshape(-1)
     slot_rows = devices * slots // 2
-    propagated, picked, _ = pl.pallas_call(
+    slot_rows = devices * slots // 2
+    table_shape = pltpu.VMEM((height * breadth, 128), f32)
+    table, weight, edges = pl.pallas_call(
+        profile_kernel,
+        out_shape=[table_shape, shape(3 * (PLANES + 8), 128, kind=jnp.bfloat16), shape(2, 128, 256)],
+        in_specs=[vmem] * 2,
+        out_specs=[vmem] * 3,
+        scratch_shapes=[pltpu.VMEM((128, 128), f32)],
+        compiler_params=params,
+        cost_estimate=pl.CostEstimate(flops=2_000_000_000, bytes_accessed=5_000_000, transcendentals=0),
+        name="profiles_inside",
+    )(halves, depth_kernel)
+    propagated, picked, *_ = pl.pallas_call(
         finish_kernel,
         out_shape=[
             pltpu.HBM((PLANES * height, breadth), f32),
             pltpu.HBM((slot_rows, 128), jnp.bfloat16),
             pltpu.VMEM(halves.shape, f32),
+            table_shape,
         ],
-        in_specs=[smem, hbm] + [vmem] * 10,
-        out_specs=[hbm, hbm, vmem],
-        input_output_aliases={11: 2},
+        in_specs=[smem, hbm] + [vmem] * 12,
+        out_specs=[hbm, hbm, vmem, vmem],
+        input_output_aliases={12: 2, 13: 3},
         scratch_shapes=[
-            pltpu.VMEM((height * breadth, 128), f32),
             pltpu.VMEM((WINDOW // 2, 128), f32),
             pltpu.VMEM((slot_rows, 128), jnp.bfloat16),
-            pltpu.VMEM((128, 128), f32),
             pltpu.SMEM((2 * WINDOW,), jnp.int32),
             pltpu.SemaphoreType.DMA((breadth // 128,)),
             pltpu.SemaphoreType.DMA((2,)),
@@ -528,38 +570,28 @@
         ],
         compiler_params=params,
         name="finish_and_pick",
-    )(courant, cells, moving, sea, depth_kernel, south, north, first, second, lanes, subs, halves)
+    )(courant, cells, moving, sea, weight, edges, south, north, first, second, lanes, subs, halves, table)
 
     picked = picked.reshape(devices, slots // 2, 128)
     received = lax.all_to_all(picked, both, split_axis=0, concat_axis=0, tiled=True)
 
     components = depth_kernel.shape[0]
-    sums = [pltpu.VMEM((OUT_DEV + SPARE, 128), f32)] * (2 * N_ACC)
-    cleared = pl.pallas_call(
-        clear_kernel,
-        out_shape=sums,
-        in_specs=[hbm],
-        out_specs=[vmem] * len(sums),
-        compiler_params=params,
-        cost_estimate=pl.CostEstimate(flops=2_000_000_000, bytes_accessed=17_000_000, transcendentals=0),
-        name="clear_sums",
-    )(pltpu.with_memory_space_constraint(picked, pltpu.HBM))
-    stokes, *_ = pl.pallas_call(
+    stokes = pl.pallas_call(
         add_kernel,
-        out_shape=[pltpu.HBM((components, OUT_DEV), f32)] + sums,
-        in_specs=[hbm, vmem] + [vmem] * len(sums),
-        out_specs=[hbm] + [vmem] * len(sums),
-        input_output_aliases={2 + k: 1 + k for k in range(len(sums))},
+        out_shape=pltpu.HBM((components, OUT_DEV), f32),
+        in_specs=[hbm, vmem],
+        out_specs=hbm,
         scratch_shapes=[
             pltpu.VMEM((WINDOW // 2, 128), f32),
             pltpu.VMEM((components, OUT_DEV), f32),
             pltpu.SMEM((2 * WINDOW,), jnp.int32),
             pltpu.SemaphoreType.DMA((2,)),
             pltpu.SemaphoreType.DMA,
-        ],
-        compiler_params=params,
+        ]
+        + [pltpu.VMEM((OUT_DEV + SPARE, 128), f32)] * (2 * N_ACC),
+        compiler_params=pltpu.CompilerParams(vmem_limit_bytes=ADD_VMEM_LIMIT),
         name="add_profiles",
-    )(targets, received.reshape(slot_rows, 128), *cleared)
+    )(targets, received.reshape(slot_rows, 128))
     return propagated.reshape(DIRS, FREQ, height, breadth), stokes
 
 

time: 99.4 us -> 85.6 us (0.86)
  local copies, waits for them, and re-layouts: 23.7 us -> 0.04 us
  waiting for transfers between devices: 19.6 us -> 29.5 us
  starting transfers between devices: 20.2 us -> 18.7 us
  Pallas kernels: 34.4 us -> 35.4 us
    unnamed x50 -> x16, local copies, waits for them, and re-layouts: 23.7 us -> 0.04 us
    all_to_all x1, waiting for transfers between devices: 17.4 us -> 29.5 us  [body(): lax.all_to_all(picked, both, split_axis=0, concat_axis=0, tiled=True)]
    pallas_call x3, Pallas kernels: 15.2 us -> 17.9 us  [the longest x1 14.8 us: body(): pl.pallas_call(add_kernel, out_shape=pltpu.HBM((components, OUT_DEV), f32...]
    ppermute x1, waiting for transfers between devices: 2.17 us -> 0.01 us  [body(): second = lax.ppermute(second, both, row_second)]
    pallas_call x1, Pallas kernels: 14.1 us -> 12.3 us  [body(): pl.pallas_call(finish_kernel, out_shape=[pltpu.HBM((PLANES * height, brea...]
    all_to_all x1, starting transfers between devices: 9.12 us -> 7.72 us  [body(): lax.all_to_all(picked, both, split_axis=0, concat_axis=0, tiled=True)]
  transfers between devices with their start and end apart: 5 -> 5, of which waited for: 2 -> 1; matrix products, arithmetic and copies ran while one was open for 0% -> 1% of each run, Pallas kernels for 5% -> 8%
where the time goes in v6:
time: 85.6 us; the launch traced here: 85.3 us
  Pallas kernels  35.4 us (41%)
  waiting for transfers between devices  29.5 us (34%)
  starting transfers between devices  18.7 us (22%)
  other arithmetic  0.87 us (1%)
    all_to_all x1, waiting for transfers between devices, body(): lax.all_to_all(picked, both, split_axis=0, concat_axis=0, tiled=True)  29.5 us
    pallas_call x1, Pallas kernels, body(): pl.pallas_call(add_kernel, out_shape=pltpu.HBM((components, OUT_DEV), f32...  14.8 us
    pallas_call x1, Pallas kernels, body(): pl.pallas_call(finish_kernel, out_shape=[pltpu.HBM((PLANES * height, brea...  12.3 us
    all_to_all x1, starting transfers between devices, body(): lax.all_to_all(picked, both, split_axis=0, concat_axis=0, tiled=True)  7.72 us
    ppermute x1, starting transfers between devices, body(): second = lax.ppermute(second, 'lon', column_second)  4.69 us
    pallas_call x1, Pallas kernels, body(): pl.pallas_call(inside_kernel, out_shape=pltpu.VMEM((breadth // 128, (PLAN...  3.38 us
    ppermute x1, starting transfers between devices, body(): second = lax.ppermute(second, both, row_second)  3.1 us
    pallas_call x1, Pallas kernels, body(): pl.pallas_call(profile_kernel, out_shape=[table_shape, shape(3 * (PLANES...  2.97 us
  transfers between devices with their start and end apart: 5, of which 1 were waited for; matrix products, arithmetic and copies ran while one was open for 1% of the time, Pallas kernels for 8%

profile of v6, /device:TPU:1, one launch (start us, length us, event | category | flops | bytes accessed | tf_op | source)
XLA Modules:
  0.0 85.3 jit_solution(17366114498758544498)
XLA Ops:
  0.6 0.0 copy-start.5
  0.6 0.0 copy-start.6
  0.7 0.0 copy-start
  0.7 0.0 copy-start.3
  0.7 1.4 %pack_rows.1 = (bf16[2,48,256]{2,1,0:T(8,128)(2,1)S(1)}, bf16[2,48,256]{2,1,0:T(8,128)(2,1)S(1)}, f32[32,256]{1,0:T(8,128)S(1)}, f32[32,256]{1,0:T(8,128)S(1)}) custom-call(f32[72,32,256]{2,1,0:T(8,128)} %bitcast.9, f32[32,256]{1,0:T(8,128)} %speed_hbm.1, s32[32,256]{1,0:T(8,128)} %mask_hbm.1), custom_call_target="tpu_custom_call" | custom-call | tf_op jit(solution)/shard_map/pack_rows/pallas_call | solution.py:493
  2.1 1.5 %collective-permute-start = (bf16[2,48,256]{2,1,0:T(8,128)(2,1)S(1)}, bf16[2,48,256]{2,1,0:T(8,128)(2,1)S(1)}, u32[]{:S(2)}, u32[]{:S(2)}) collective-permute-start(bf16[2,48,256]{2,1,0:T(8,128)(2,1)S(1)} %get-tuple-element.21), channel_id=1, source_target_pairs={{0,16},{16,0},{32,48},{48,32},{64,80},{80,64},{96,112},{112,96},{1... | collective-permute-start | bytes 147464 | tf_op jit(solution)/shard_map/ppermute | solution.py:505
  3.6 3.1 %collective-permute-start.1 = (bf16[2,48,256]{2,1,0:T(8,128)(2,1)S(1)}, bf16[2,48,256]{2,1,0:T(8,128)(2,1)S(1)}, u32[]{:S(2)}, u32[]{:S(2)}) collective-permute-start(bf16[2,48,256]{2,1,0:T(8,128)(2,1)S(1)} %get-tuple-element.22), channel_id=1, source_target_pairs={{0,0},{112,127},{16,32},{32,16},{48,64},{64,48},{80,96},{96,80},{1... | collective-permute-start | bytes 147464 | tf_op jit(solution)/shard_map/ppermute | solution.py:504
  6.7 0.8 maximum_bitcast_fusion.cells_ref
  7.5 0.0 copy-done.5
  7.5 0.0 copy-done.6
  7.5 0.0 copy-done
  7.5 0.0 copy-done.3
  7.5 3.4 %advance_inside.1.halves.halves_in = f32[2,2432,128]{2,1,0:T(8,128)S(1)} custom-call(f32[2]{0:T(128)S(1)} %copy-done.3, f32[72]{0:T(128)S(1)} %copy-done.5, f32[72]{0:T(128)S(1)} %copy-done.6, f32[72,32,256]{2,1,0:T(8,128)S(1)} %bitcast.10, f32[32,256]{1,0:T(8,128)S(1)} %get-tuple-element.17.mov_ref, f32[32,256]{1,0:T(8,128)S(1)} %get-tuple-element.18.sea_ref), custom_call_target="tpu_custom_call" | custom-call | flops 4000000000 | bytes 5000000 | tf_op jit(solution)/shard_map/advance_inside/pallas_call | solution.py:515
  10.9 0.0 copy-start.4
  10.9 0.4 pack_columns.1
  11.3 0.0 collective-permute-done.first_ref
  11.4 0.0 collective-permute-done.1.second_ref
  11.4 0.1 add_corners.1
  11.5 1.7 %collective-permute-start.2 = (f32[40,128]{1,0:T(8,128)S(1)}, f32[40,128]{1,0:T(8,128)S(1)}, u32[]{:S(2)}, u32[]{:S(2)}) collective-permute-start(f32[40,128]{1,0:T(8,128)S(1)} %get-tuple-element.27), channel_id=1, source_target_pairs={{0,1},{1,0},{2,3},{3,2},{4,5},{5,4},{6,7},{7,6},{8,9},{9,8},{10,11... | collective-permute-start | bytes 61448 | tf_op jit(solution)/shard_map/ppermute | solution.py:533
  13.2 0.0 copy-start.1
  13.2 0.0 copy-start.2
  13.2 4.7 %collective-permute-start.3 = (f32[40,128]{1,0:T(8,128)S(1)}, f32[40,128]{1,0:T(8,128)S(1)}, u32[]{:S(2)}, u32[]{:S(2)}) collective-permute-start(f32[40,128]{1,0:T(8,128)S(1)} %get-tuple-element.28), channel_id=1, source_target_pairs={{0,15},{1,2},{2,1},{3,4},{4,3},{5,6},{6,5},{7,8},{8,7},{9,10},{10,... | collective-permute-start | bytes 61448 | tf_op jit(solution)/shard_map/ppermute | solution.py:532
  17.9 0.0 copy-done.4
  17.9 3.0 %profiles_inside.1 = (f32[8192,128]{1,0:T(8,128)S(1)}, bf16[240,128]{1,0:T(8,128)(2,1)S(1)}, f32[2,128,256]{2,1,0:T(8,128)S(1)}) custom-call(f32[2,2432,128]{2,1,0:T(8,128)S(1)} %advance_inside.1.halves.halves_in, f32[64,72]{1,0:T(8,128)S(1)} %copy-done.4), custom_call_target="tpu_custom_call" | custom-call | flops 2000000000 | bytes 5000000 | tf_op jit(solution)/shard_map/profiles_inside/pallas_call | solution.py:542
  20.9 0.0 collective-permute-done.2.first_ref
  20.9 0.0 collective-permute-done.3.second_ref
  20.9 0.0 copy-done.1
  20.9 0.0 copy-done.2
  20.9 12.3 %finish_and_pick.1 = (f32[2304,256]{1,0:T(8,128)}, bf16[8192,128]{1,0:T(8,128)(2,1)}, f32[2,2432,128]{2,1,0:T(8,128)S(1)}, f32[8192,128]{1,0:T(8,128)S(1)}) custom-call(f32[2]{0:T(128)S(1)} %copy-done.3, s32[16384]{0:T(1024)S(1)} %maximum_bitcast_fusion.cells_ref, ...), custom_call_target="tpu_custom_call", output_to_operand_aliasing={{2}: (12, {}), {3}: (13, {})} | custom-call | tf_op jit(solution)/shard_map/finish_and_pick/pallas_call | solution.py:552
  33.3 0.0 copy-start.7
  33.3 7.7 %all-to-all-start = ((bf16[128,64,128]{2,1,0:T(8,128)(2,1)}), bf16[128,64,128]{2,1,0:T(8,128)(2,1)S(1)}, u32[]{:S(2)}, u32[]{:S(2)}) async-start(bf16[128,64,128]{2,1,0:T(8,128)(2,1)} %bitcast.12), calls=%async_computation | async-start | bytes 4194304 | tf_op jit(solution)/shard_map/all_to_all | solution.py:576
  41.0 0.0 copy-done.7
  41.0 29.5 %all-to-all-done = bf16[128,64,128]{2,1,0:T(8,128)(2,1)S(1)} async-done(((bf16[128,64,128]{2,1,0:T(8,128)(2,1)}), bf16[128,64,128]{2,1,0:T(8,128)(2,1)S(1)}, u32[]{:S(2)}, u32[]{:S(2)}) %all-to-all-start) | async-done | bytes 2097184 | tf_op jit(solution)/shard_map/all_to_all | solution.py:576
  70.5 14.8 %add_profiles.1 = f32[64,4096]{1,0:T(8,128)} custom-call(s32[16384]{0:T(1024)S(1)} %fusion.rows_ref, bf16[8192,128]{1,0:T(8,128)(2,1)S(1)} %bitcast.8), custom_call_target="tpu_custom_call" | custom-call | tf_op jit(solution)/shard_map/add_profiles/pallas_call | solution.py:579
  (2 shorter events, 0.0 us)
Async XLA Ops:
  0.6 6.9 %copy-start.5 = (f32[72]{0:T(128)S(1)}, f32[72]{0:T(128)}, u32[]{:S(2)}) copy-start(f32[72]{0:T(128)} %constant.56.clone.cos_ref) | copy-start | bytes 868
  0.6 6.9 %copy-start.6 = (f32[72]{0:T(128)S(1)}, f32[72]{0:T(128)}, u32[]{:S(2)}) copy-start(f32[72]{0:T(128)} %constant.57.clone.sin_ref) | copy-start | bytes 868
  0.7 6.9 %copy-start = (f32[36,2,32,256]{3,2,1,0:T(8,128)S(1)}, f32[36,2,32,256]{3,2,1,0:T(8,128)}, u32[]{:S(2)}) copy-start(f32[36,2,32,256]{3,2,1,0:T(8,128)} %param.11) | copy-start | bytes 7077892
  0.7 6.9 %copy-start.3 = (f32[2]{0:T(128)S(1)}, f32[2]{0:T(128)}, u32[]{:S(2)}) copy-start(f32[2]{0:T(128)} %courant_ref.3) | copy-start | bytes 28
  2.1 9.3 %collective-permute-start = (bf16[2,48,256]{2,1,0:T(8,128)(2,1)S(1)}, bf16[2,48,256]{2,1,0:T(8,128)(2,1)S(1)}, u32[]{:S(2)}, u32[]{:S(2)}) collective-permute-start(bf16[2,48,256]{2,1,0:T(8,128)(2,1)S(1)} %get-tuple-element.21), channel_id=1, source_target_pairs={{0,16},{16,0},{32,48},{48,32},{64,80},{80,64},{96,112},{112,96},{1... | collective-permute-start | bytes 147464 | tf_op jit(solution)/shard_map/ppermute | solution.py:505
  3.6 7.8 %collective-permute-start.1 = (bf16[2,48,256]{2,1,0:T(8,128)(2,1)S(1)}, bf16[2,48,256]{2,1,0:T(8,128)(2,1)S(1)}, u32[]{:S(2)}, u32[]{:S(2)}) collective-permute-start(bf16[2,48,256]{2,1,0:T(8,128)(2,1)S(1)} %get-tuple-element.22), channel_id=1, source_target_pairs={{0,0},{112,127},{16,32},{32,16},{48,64},{64,48},{80,96},{96,80},{1... | collective-permute-start | bytes 147464 | tf_op jit(solution)/shard_map/ppermute | solution.py:504
  10.9 7.0 %copy-start.4 = (f32[64,72]{1,0:T(8,128)S(1)}, f32[64,72]{1,0:T(8,128)}, u32[]{:S(2)}) copy-start(f32[64,72]{1,0:T(8,128)} %kernel_ref.1) | copy-start | bytes 55300
  11.5 9.4 %collective-permute-start.2 = (f32[40,128]{1,0:T(8,128)S(1)}, f32[40,128]{1,0:T(8,128)S(1)}, u32[]{:S(2)}, u32[]{:S(2)}) collective-permute-start(f32[40,128]{1,0:T(8,128)S(1)} %get-tuple-element.27), channel_id=1, source_target_pairs={{0,1},{1,0},{2,3},{3,2},{4,5},{5,4},{6,7},{7,6},{8,9},{9,8},{10,11... | collective-permute-start | bytes 61448 | tf_op jit(solution)/shard_map/ppermute | solution.py:533
  13.2 7.7 %copy-start.1 = (f32[40,128]{1,0:T(8,128)S(1)}, f32[40,128]{1,0:T(8,128)}, u32[]{:S(2)}) copy-start(f32[40,128]{1,0:T(8,128)} %constant.59.clone.subs_ref) | copy-start | bytes 61444
  13.2 7.7 %copy-start.2 = (f32[8,128]{1,0:T(8,128)S(1)}, f32[8,128]{1,0:T(8,128)}, u32[]{:S(2)}) copy-start(f32[8,128]{1,0:T(8,128)} %constant.58.clone.lanes_ref) | copy-start | bytes 12292
  13.2 7.7 %collective-permute-start.3 = (f32[40,128]{1,0:T(8,128)S(1)}, f32[40,128]{1,0:T(8,128)S(1)}, u32[]{:S(2)}, u32[]{:S(2)}) collective-permute-start(f32[40,128]{1,0:T(8,128)S(1)} %get-tuple-element.28), channel_id=1, source_target_pairs={{0,15},{1,2},{2,1},{3,4},{4,3},{5,6},{6,5},{7,8},{8,7},{9,10},{10,... | collective-permute-start | bytes 61448 | tf_op jit(solution)/shard_map/ppermute | solution.py:532
  33.3 7.8 %copy-start.7 = (s32[1,128,128]{2,1,0:T(8,128)S(1)}, s32[1,128,128]{2,1,0:T(8,128)}, u32[]{:S(2)}) copy-start(s32[1,128,128]{2,1,0:T(8,128)} %param.17) | copy-start | bytes 196612
  33.3 37.2 %all-to-all-start = ((bf16[128,64,128]{2,1,0:T(8,128)(2,1)}), bf16[128,64,128]{2,1,0:T(8,128)(2,1)S(1)}, u32[]{:S(2)}, u32[]{:S(2)}) async-start(bf16[128,64,128]{2,1,0:T(8,128)(2,1)} %bitcast.12), calls=%async_computation | async-start | bytes 4194304 | tf_op jit(solution)/shard_map/all_to_all | solution.py:576

commit v7 on v6

--- a/solution.py
+++ b/solution.py
@@ -100,7 +100,7 @@
     west_ref[...] = west
 
 
-def corner_kernel(n_lat, first_ref, second_ref, east_ref, west_ref, south_ref, north_ref, out_first, out_second):
+def corner_kernel(n_lat, second_ref, first_ref, east_ref, west_ref, south_ref, north_ref, out_first, out_second):
     height = east_ref.shape[0]
     breadth = first_ref.shape[2]
     lat = lax.axis_index("lat")
@@ -155,11 +155,12 @@
 
 
 def for_windows(list_ref, window, sems, work):
-    count = list_ref.shape[0] // WINDOW
+    lines = WINDOW // 128
+    count = list_ref.shape[0] // lines
 
     def fetch(i, w):
-        source = list_ref.at[pl.ds(pl.multiple_of(i * WINDOW, WINDOW), WINDOW)]
-        return pltpu.make_async_copy(source, window.at[pl.ds(w * WINDOW, WINDOW)], sems.at[w])
+        source = list_ref.at[pl.ds(pl.multiple_of(i * lines, lines), lines), :]
+        return pltpu.make_async_copy(source, window.at[pl.ds(w * lines, lines), :], sems.at[w])
 
     for w in range(2):
         fetch(w, w).start()
@@ -169,14 +170,14 @@
         for w in range(2):
             i = 2 * t + w
             fetch(i, w).wait()
-            work(lambda k, start=w * WINDOW: window[start + k], i)
+            work(lambda k, start=w * lines: window[start + k // 128, k % 128], i)
 
             @pl.when(i + 2 < count)
             def _():
                 fetch(i + 2, w).start()
 
 
-def inside_kernel(courant_ref, cos_ref, sin_ref, x_ref, mov_ref, sea_ref, halves):
+def inside_kernel(courant_ref, heading_ref, x_ref, mov_ref, sea_ref, halves):
     height, breadth = mov_ref.shape
     c0, c1 = courant_ref[0], courant_ref[1]
     moving = mov_ref[...]
@@ -206,8 +207,8 @@
         def step(t, carry):
             p = first + t
             courant = jnp.where(p % 2 == 1, c1, c0)
-            cx = cos_ref[p] * courant
-            cy = sin_ref[p] * courant
+            cx = heading_ref[p] * courant
+            cy = heading_ref[PLANES + p] * courant
             energy = x_ref[p]
             for _ in range(2):
                 flux = moving * energy
@@ -274,9 +275,10 @@
         profile_rows(halves, weight, table, r * group, group, height, breadth)
 
 
-def finish_kernel(courant_ref, cells_ref, mov_ref, sea_ref, weight_ref, edge_ref, south_ref, north_ref, first_ref,
-                  second_ref, lanes_ref, subs_ref, halves_in, table_in, out_ref, picked_ref, halves, table,
-                  lines, picks, window, out_sems, window_sems, pick_sem):
+def finish_kernel(courant_ref, cells_ref, mov_ref, sea_ref, weight_ref, edge_ref, south_ref, north_ref, second_ref,
+                  first_ref, lanes_ref, subs_ref, halves_in, table_in, out_ref, picked_ref, halves, table,
+                  cells, lines, picks, window, out_sems, window_sems, pick_sem):
+    cells[...] = jnp.maximum(cells_ref[...], 0)
     height, breadth = mov_ref.shape
     c0, c1 = courant_ref[0], courant_ref[1]
     even_lon = lax.axis_index("lon") % 2 == 0
@@ -405,17 +407,20 @@
         picks[here, :] = lines[...].astype(jnp.bfloat16)
         pltpu.make_async_copy(picks.at[here, :], picked_ref.at[here, :], pick_sem).start()
 
-    for_windows(cells_ref, window, window_sems, pick)
+    for_windows(cells, window, window_sems, pick)
     pltpu.make_async_copy(picks, picked_ref, pick_sem).wait()
     for write in writes:
         write.wait()
 
 
-def add_kernel(rows_ref, values_ref, out_ref, lines, tile_sums, window, window_sems, out_sem, *sums):
+def add_kernel(rows_ref, values_ref, out_ref, targets, lines, tile_sums, window, window_sems, out_sem, *sums):
     n_acc = len(sums) // 2
     tile = out_ref.shape[1]
     block = 512
     half = WINDOW // 2
+    slot = lax.broadcasted_iota(jnp.int32, targets.shape, 1)
+    spare = tile + (slot // 16 * 8 + slot % 8) % SPARE
+    targets[...] = jnp.where(rows_ref[...] < 0, spare, rows_ref[...])
 
     @pl.loop(0, tile // block)
     def _(i):
@@ -432,7 +437,7 @@
                 left[pl.ds(one, 1), :] = left[pl.ds(one, 1), :] + line
                 right[pl.ds(two, 1), :] = right[pl.ds(two, 1), :] + line
 
-    for_windows(rows_ref, window, window_sems, add)
+    for_windows(targets, window, window_sems, add)
     first_half = lax.broadcasted_iota(jnp.int32, (block, 128), 1) < 64
 
     @pl.loop(0, tile // block)
@@ -466,7 +471,7 @@
     subs = np.zeros((HALF + 4, 128))
     subs[:HALF, 0], subs[:HALF, 1] = cos[:HALF], sin[:HALF]
     subs[:HALF, 2], subs[:HALF, 3] = cos[HALF:], sin[HALF:]
-    return [t.astype(np.float32) for t in (cos, sin, lanes, subs)]
+    return [t.astype(np.float32) for t in (np.concatenate([cos, sin]), lanes, subs)]
 
 
 def body(n_lat, n_lon, spectrum, speed_factor, land_sea_mask, courant, depth_kernel, send_rows, recv_rows):
@@ -484,7 +489,7 @@
     def shape(*dims, kind=f32):
         return jax.ShapeDtypeStruct(dims, kind)
 
-    cos, sin, lanes, subs = constant_tables()
+    headings, lanes, subs = constant_tables()
     row_message = shape(2, ROWS, breadth, kind=jnp.bfloat16)
     row_halo = shape(2, HALF + 4, breadth)
     columns = shape(height, 128)
@@ -515,12 +520,12 @@
     halves = pl.pallas_call(
         inside_kernel,
         out_shape=pltpu.VMEM((breadth // 128, (PLANES + 4) * height, 128), f32),
-        in_specs=[smem] * 3 + [vmem] * 3,
+        in_specs=[smem] * 2 + [vmem] * 3,
         out_specs=vmem,
         compiler_params=params,
         cost_estimate=pl.CostEstimate(flops=4_000_000_000, bytes_accessed=5_000_000, transcendentals=0),
         name="advance_inside",
-    )(courant, cos, sin, x, moving, sea)
+    )(courant, headings, x, moving, sea)
     south, north, first, second = pl.pallas_call(
         functools.partial(corner_kernel, n_lat),
         out_shape=[row_halo] * 2 + [column_message] * 2,
@@ -528,14 +533,11 @@
         out_specs=[vmem] * 4,
         compiler_params=params,
         name="add_corners",
-    )(first, second, east, west)
+    )(second, first, east, west)
     second = lax.ppermute(second, "lon", column_second)
     first = lax.ppermute(first, "lon", column_first)
 
-    cells = jnp.maximum(send_rows, 0).reshape(-1)
-    slot = jnp.arange(slots, dtype=jnp.int32)
-    spare = OUT_DEV + (slot // 16 * 8 + slot % 8) % SPARE
-    targets = jnp.where(recv_rows < 0, spare, recv_rows).reshape(-1)
+    lists = (devices * slots // 128, 128)
     slot_rows = devices * slots // 2
     slot_rows = devices * slots // 2
     table_shape = pltpu.VMEM((height * breadth, 128), f32)
@@ -557,20 +559,21 @@
             pltpu.VMEM(halves.shape, f32),
             table_shape,
         ],
-        in_specs=[smem, hbm] + [vmem] * 12,
+        in_specs=[smem] + [vmem] * 13,
         out_specs=[hbm, hbm, vmem, vmem],
         input_output_aliases={12: 2, 13: 3},
         scratch_shapes=[
+            pltpu.VMEM(lists, jnp.int32),
             pltpu.VMEM((WINDOW // 2, 128), f32),
             pltpu.VMEM((slot_rows, 128), jnp.bfloat16),
-            pltpu.SMEM((2 * WINDOW,), jnp.int32),
+            pltpu.SMEM((2 * WINDOW // 128, 128), jnp.int32),
             pltpu.SemaphoreType.DMA((breadth // 128,)),
             pltpu.SemaphoreType.DMA((2,)),
             pltpu.SemaphoreType.DMA,
         ],
         compiler_params=params,
         name="finish_and_pick",
-    )(courant, cells, moving, sea, weight, edges, south, north, first, second, lanes, subs, halves, table)
+    )(courant, send_rows.reshape(lists), moving, sea, weight, edges, south, north, second, first, lanes, subs, halves, table)
 
     picked = picked.reshape(devices, slots // 2, 128)
     received = lax.all_to_all(picked, both, split_axis=0, concat_axis=0, tiled=True)
@@ -579,19 +582,20 @@
     stokes = pl.pallas_call(
         add_kernel,
         out_shape=pltpu.HBM((components, OUT_DEV), f32),
-        in_specs=[hbm, vmem],
+        in_specs=[vmem] * 2,
         out_specs=hbm,
         scratch_shapes=[
+            pltpu.VMEM(lists, jnp.int32),
             pltpu.VMEM((WINDOW // 2, 128), f32),
             pltpu.VMEM((components, OUT_DEV), f32),
-            pltpu.SMEM((2 * WINDOW,), jnp.int32),
+            pltpu.SMEM((2 * WINDOW // 128, 128), jnp.int32),
             pltpu.SemaphoreType.DMA((2,)),
             pltpu.SemaphoreType.DMA,
         ]
         + [pltpu.VMEM((OUT_DEV + SPARE, 128), f32)] * (2 * N_ACC),
         compiler_params=pltpu.CompilerParams(vmem_limit_bytes=ADD_VMEM_LIMIT),
         name="add_profiles",
-    )(targets, received.reshape(slot_rows, 128))
+    )(recv_rows.reshape(lists), received.reshape(slot_rows, 128))
     return propagated.reshape(DIRS, FREQ, height, breadth), stokes
 
 

time: 85.6 us -> 88.3 us (1.032)
  blocking collectives: 0 us -> 38.1 us
  waiting for transfers between devices: 29.5 us -> 0.01 us
  starting transfers between devices: 18.7 us -> 10.9 us
  local copies, waits for them, and re-layouts: 0.04 us -> 3.02 us
    all_to_all x0 -> x1, blocking collectives: none -> 38.1 us  [body(): lax.all_to_all(picked, both, split_axis=0, concat_axis=0, tiled=True)]
    all_to_all x1 -> x0, waiting for transfers between devices: 29.5 us -> none  [body(): lax.all_to_all(picked, both, split_axis=0, concat_axis=0, tiled=True)]
    all_to_all x1 -> x0, starting transfers between devices: 7.72 us -> none  [body(): lax.all_to_all(picked, both, split_axis=0, concat_axis=0, tiled=True)]
    unnamed x16, local copies, waits for them, and re-layouts: 0.04 us -> 3.02 us
    ppermute x1, starting transfers between devices: 1.72 us -> 0.01 us  [body(): first = lax.ppermute(first, 'lon', column_first)]
    ppermute x1, starting transfers between devices: 4.69 us -> 6.29 us  [body(): second = lax.ppermute(second, 'lon', column_second)]
    ppermute x1, starting transfers between devices: 1.5 us -> 0.09 us  [body(): first = lax.ppermute(first, 'lat', row_first)]
    ppermute x1, starting transfers between devices: 3.1 us -> 4.51 us  [body(): second = lax.ppermute(second, both, row_second)]
  transfers between devices with their start and end apart: 5 -> 4, of which waited for: 1 -> 0; matrix products, arithmetic and copies ran while one was open for 1% -> 0% of each run, Pallas kernels for 8% -> 8%
where the time goes in v7:
time: 88.3 us; the launch traced here: 88 us
  blocking collectives  38.1 us (43%)
  Pallas kernels  35.2 us (40%)
  starting transfers between devices  10.9 us (12%)
  local copies, waits for them, and re-layouts  3.02 us (3%)
    all_to_all x1, blocking collectives, body(): lax.all_to_all(picked, both, split_axis=0, concat_axis=0, tiled=True)  38.1 us
    pallas_call x1, Pallas kernels, body(): pl.pallas_call(add_kernel, out_shape=pltpu.HBM((components, OUT_DEV), f32...  14.8 us
    pallas_call x1, Pallas kernels, body(): pl.pallas_call(finish_kernel, out_shape=[pltpu.HBM((PLANES * height, brea...  12.3 us
    ppermute x1, starting transfers between devices, body(): second = lax.ppermute(second, 'lon', column_second)  6.29 us
    ppermute x1, starting transfers between devices, body(): second = lax.ppermute(second, both, row_second)  4.51 us
    pallas_call x1, Pallas kernels, body(): pl.pallas_call(inside_kernel, out_shape=pltpu.VMEM((breadth // 128, (PLAN...  3.33 us
    unnamed x16, local copies, waits for them, and re-layouts  3.02 us
    pallas_call x1, Pallas kernels, body(): pl.pallas_call(profile_kernel, out_shape=[table_shape, shape(3 * (PLANES...  2.96 us
  transfers between devices with their start and end apart: 4, of which 0 were waited for; matrix products, arithmetic and copies ran while one was open for 0% of the time, Pallas kernels for 8%

profile of v7, /device:TPU:1, one launch (start us, length us, event | category | flops | bytes accessed | tf_op | source)
XLA Modules:
  0.0 88.0 jit_solution(2107313590159102480)
XLA Ops:
  0.6 1.2 %pack_rows.1 = (bf16[2,48,256]{2,1,0:T(8,128)(2,1)S(1)}, bf16[2,48,256]{2,1,0:T(8,128)(2,1)S(1)}, f32[32,256]{1,0:T(8,128)S(1)}, f32[32,256]{1,0:T(8,128)S(1)}) custom-call(f32[72,32,256]{2,1,0:T(8,128)} %bitcast.7, f32[32,256]{1,0:T(8,128)} %speed_hbm.1, s32[32,256]{1,0:T(8,128)} %mask_hbm.1), custom_call_target="tpu_custom_call" | custom-call | tf_op jit(solution)/shard_map/pack_rows/pallas_call | solution.py:498
  1.9 4.5 %collective-permute-start = (bf16[2,48,256]{2,1,0:T(8,128)(2,1)S(1)}, bf16[2,48,256]{2,1,0:T(8,128)(2,1)S(1)}, u32[]{:S(2)}, u32[]{:S(2)}) collective-permute-start(bf16[2,48,256]{2,1,0:T(8,128)(2,1)S(1)} %get-tuple-element.21), channel_id=1, source_target_pairs={{0,0},{112,127},{16,32},{32,16},{48,64},{64,48},{80,96},{96,80},{1... | collective-permute-start | bytes 147464 | tf_op jit(solution)/shard_map/ppermute | solution.py:509
  6.4 0.1 collective-permute-start.1
  6.5 0.0 copy-start
  6.5 1.7 %copy-done = f32[36,2,32,256]{3,2,1,0:T(8,128)S(1)} copy-done((f32[36,2,32,256]{3,2,1,0:T(8,128)S(1)}, f32[36,2,32,256]{3,2,1,0:T(8,128)}, u32[]{:S(2)}) %copy-start) | copy-done | bytes 2359320
  8.1 0.0 copy-start.5
  8.1 0.7 copy-done.5
  8.8 0.0 copy-start.7
  8.8 0.7 copy-done.7
  9.5 3.3 %advance_inside.1.halves.halves_in = f32[2,2432,128]{2,1,0:T(8,128)S(1)} custom-call(f32[2]{0:T(128)S(1)} %copy-done.5, f32[144]{0:T(256)S(1)} %copy-done.7, f32[72,32,256]{2,1,0:T(8,128)S(1)} %bitcast.8, f32[32,256]{1,0:T(8,128)S(1)} %get-tuple-element.17.mov_ref, f32[32,256]{1,0:T(8,128)S(1)} %get-tuple-element.18.sea_ref), custom_call_target="tpu_custom_call" | custom-call | flops 4000000000 | bytes 5000000 | tf_op jit(solution)/shard_map/advance_inside/pallas_call | solution.py:520
  12.8 0.0 copy-start.6
  12.8 0.4 pack_columns.1
  13.2 0.0 collective-permute-done.second_ref
  13.2 0.0 collective-permute-done.1.first_ref
  13.2 0.1 add_corners.1
  13.4 6.3 %collective-permute-start.2 = (f32[40,128]{1,0:T(8,128)S(1)}, f32[40,128]{1,0:T(8,128)S(1)}, u32[]{:S(2)}, u32[]{:S(2)}) collective-permute-start(f32[40,128]{1,0:T(8,128)S(1)} %get-tuple-element.27), channel_id=1, source_target_pairs={{0,15},{1,2},{2,1},{3,4},{4,3},{5,6},{6,5},{7,8},{8,7},{9,10},{10,... | collective-permute-start | bytes 61448 | tf_op jit(solution)/shard_map/ppermute | solution.py:537
  19.7 0.0 copy-start.1
  19.7 0.0 copy-start.3
  19.7 0.0 copy-start.4
  19.7 0.0 collective-permute-start.3
  19.7 0.0 copy-done.6
  19.7 3.0 %profiles_inside.1 = (f32[8192,128]{1,0:T(8,128)S(1)}, bf16[240,128]{1,0:T(8,128)(2,1)S(1)}, f32[2,128,256]{2,1,0:T(8,128)S(1)}) custom-call(f32[2,2432,128]{2,1,0:T(8,128)S(1)} %advance_inside.1.halves.halves_in, f32[64,72]{1,0:T(8,128)S(1)} %copy-done.6), custom_call_target="tpu_custom_call" | custom-call | flops 2000000000 | bytes 5000000 | tf_op jit(solution)/shard_map/profiles_inside/pallas_call | solution.py:544
  22.7 0.0 collective-permute-done.2.second_ref
  22.7 0.0 collective-permute-done.3.first_ref
  22.7 0.0 copy-done.1
  22.7 0.0 copy-done.3
  22.7 0.0 copy-done.4
  22.7 12.3 %finish_and_pick.1 = (f32[2304,256]{1,0:T(8,128)}, bf16[8192,128]{1,0:T(8,128)(2,1)}, f32[2,2432,128]{2,1,0:T(8,128)S(1)}, f32[8192,128]{1,0:T(8,128)S(1)}) custom-call(f32[2]{0:T(128)S(1)} %copy-done.5, s32[128,128]{1,0:T(8,128)S(1)} %bitcast.10, f32[32,256]{1,0:T(8,128)S(1)} %get-tuple-element.17.mov_ref, ...), custom_call_target="tpu_custom_call", output_to_operand_aliasing={{2}: (12, {}), {3}: (13, {})} | custom-call | tf_op jit(solution)/shard_map/finish_and_pick/pallas_call | solution.py:554
  35.1 0.0 copy-start.2
  35.1 38.1 %all_to_all.5 = bf16[128,64,128]{2,1,0:T(8,128)(2,1)S(1)} all-to-all(bf16[128,64,128]{2,1,0:T(8,128)(2,1)} %bitcast.12), channel_id=1, replica_groups=mesh['lat'=8,'lon'=16] {'lat','lon'}, dimensions={0} | all-to-all | bytes 4194304 | tf_op jit(solution)/shard_map/all_to_all | solution.py:579
  73.1 0.0 copy-done.2
  73.1 14.8 %add_profiles.1 = f32[64,4096]{1,0:T(8,128)} custom-call(s32[128,128]{1,0:T(8,128)S(1)} %bitcast.11, bf16[8192,128]{1,0:T(8,128)(2,1)S(1)} %bitcast.6), custom_call_target="tpu_custom_call" | custom-call | tf_op jit(solution)/shard_map/add_profiles/pallas_call | solution.py:582
Async XLA Ops:
  1.9 11.4 %collective-permute-start = (bf16[2,48,256]{2,1,0:T(8,128)(2,1)S(1)}, bf16[2,48,256]{2,1,0:T(8,128)(2,1)S(1)}, u32[]{:S(2)}, u32[]{:S(2)}) collective-permute-start(bf16[2,48,256]{2,1,0:T(8,128)(2,1)S(1)} %get-tuple-element.21), channel_id=1, source_target_pairs={{0,0},{112,127},{16,32},{32,16},{48,64},{64,48},{80,96},{96,80},{1... | collective-permute-start | bytes 147464 | tf_op jit(solution)/shard_map/ppermute | solution.py:509
  6.4 6.9 %collective-permute-start.1 = (bf16[2,48,256]{2,1,0:T(8,128)(2,1)S(1)}, bf16[2,48,256]{2,1,0:T(8,128)(2,1)S(1)}, u32[]{:S(2)}, u32[]{:S(2)}) collective-permute-start(bf16[2,48,256]{2,1,0:T(8,128)(2,1)S(1)} %get-tuple-element.22), channel_id=1, source_target_pairs={{0,16},{16,0},{32,48},{48,32},{64,80},{80,64},{96,112},{112,96},{1... | collective-permute-start | bytes 147464 | tf_op jit(solution)/shard_map/ppermute | solution.py:510
  6.5 1.7 %copy-start = (f32[36,2,32,256]{3,2,1,0:T(8,128)S(1)}, f32[36,2,32,256]{3,2,1,0:T(8,128)}, u32[]{:S(2)}) copy-start(f32[36,2,32,256]{3,2,1,0:T(8,128)} %param.10) | copy-start | bytes 7077892
  8.1 0.7 copy-start.5
  8.8 0.7 copy-start.7
  12.8 6.9 %copy-start.6 = (f32[64,72]{1,0:T(8,128)S(1)}, f32[64,72]{1,0:T(8,128)}, u32[]{:S(2)}) copy-start(f32[64,72]{1,0:T(8,128)} %kernel_ref.1) | copy-start | bytes 55300
  13.4 9.3 %collective-permute-start.2 = (f32[40,128]{1,0:T(8,128)S(1)}, f32[40,128]{1,0:T(8,128)S(1)}, u32[]{:S(2)}, u32[]{:S(2)}) collective-permute-start(f32[40,128]{1,0:T(8,128)S(1)} %get-tuple-element.27), channel_id=1, source_target_pairs={{0,15},{1,2},{2,1},{3,4},{4,3},{5,6},{6,5},{7,8},{8,7},{9,10},{10,... | collective-permute-start | bytes 61448 | tf_op jit(solution)/shard_map/ppermute | solution.py:537
  19.7 3.0 %copy-start.1 = (s32[1,128,128]{2,1,0:T(8,128)S(1)}, s32[1,128,128]{2,1,0:T(8,128)}, u32[]{:S(2)}) copy-start(s32[1,128,128]{2,1,0:T(8,128)} %param.15) | copy-start | bytes 196612
  19.7 3.0 %copy-start.3 = (f32[40,128]{1,0:T(8,128)S(1)}, f32[40,128]{1,0:T(8,128)}, u32[]{:S(2)}) copy-start(f32[40,128]{1,0:T(8,128)} %constant.8.clone.subs_ref) | copy-start | bytes 61444
  19.7 3.0 %copy-start.4 = (f32[8,128]{1,0:T(8,128)S(1)}, f32[8,128]{1,0:T(8,128)}, u32[]{:S(2)}) copy-start(f32[8,128]{1,0:T(8,128)} %constant.7.clone.lanes_ref) | copy-start | bytes 12292
  19.7 3.0 %collective-permute-start.3 = (f32[40,128]{1,0:T(8,128)S(1)}, f32[40,128]{1,0:T(8,128)S(1)}, u32[]{:S(2)}, u32[]{:S(2)}) collective-permute-start(f32[40,128]{1,0:T(8,128)S(1)} %get-tuple-element.28), channel_id=1, source_target_pairs={{0,1},{1,0},{2,3},{3,2},{4,5},{5,4},{6,7},{7,6},{8,9},{9,8},{10,11... | collective-permute-start | bytes 61448 | tf_op jit(solution)/shard_map/ppermute | solution.py:538
  35.1 38.1 %copy-start.2 = (s32[1,128,128]{2,1,0:T(8,128)S(1)}, s32[1,128,128]{2,1,0:T(8,128)}, u32[]{:S(2)}) copy-start(s32[1,128,128]{2,1,0:T(8,128)} %param.16) | copy-start | bytes 196612

commit v8 on v7

--- a/solution.py
+++ b/solution.py
@@ -81,25 +81,6 @@
         second_ref[...] = up_ref[...].astype(jnp.bfloat16)
 
 
-def pack_columns_kernel(x_ref, mov_ref, sea_ref, east_ref, west_ref):
-    height, breadth = mov_ref.shape
-    lane = lax.broadcasted_iota(jnp.int32, (height, 128), 1)
-    east = jnp.zeros((height, 128), jnp.float32)
-    west = jnp.zeros((height, 128), jnp.float32)
-    for q in range(HALF + 2):
-        mine = lane // 2 == q
-        if q < HALF:
-            p_e = q if q < QUAD else q + HALF
-            edge_e, edge_w = x_ref[p_e, :, breadth - 128 :], x_ref[q + QUAD, :, :128]
-        else:
-            field = (mov_ref if q == HALF else sea_ref)[...]
-            edge_e, edge_w = field[:, breadth - 128 :], field[:, :128]
-        east = jnp.where(mine, pltpu.roll(edge_e, (2 * q + 2) % 128, axis=1), east)
-        west = jnp.where(mine, pltpu.roll(edge_w, 2 * q, axis=1), west)
-    east_ref[...] = east
-    west_ref[...] = west
-
-
 def corner_kernel(n_lat, second_ref, first_ref, east_ref, west_ref, south_ref, north_ref, out_first, out_second):
     height = east_ref.shape[0]
     breadth = first_ref.shape[2]
@@ -177,8 +158,21 @@
                 fetch(i + 2, w).start()
 
 
-def inside_kernel(courant_ref, heading_ref, x_ref, mov_ref, sea_ref, halves):
+def inside_kernel(courant_hbm, heading_hbm, x_hbm, mov_ref, sea_ref, halves, east_ref, west_ref,
+                  x_ref, courant_ref, heading_ref, sems):
     height, breadth = mov_ref.shape
+    small = [
+        pltpu.make_async_copy(courant_hbm, courant_ref, sems.at[4]),
+        pltpu.make_async_copy(heading_hbm, heading_ref, sems.at[5]),
+    ]
+    parts = [
+        pltpu.make_async_copy(x_hbm.at[planes], x_ref.at[planes], sems.at[k])
+        for k, planes in enumerate(pl.ds(k * QUAD, QUAD) for k in range(4))
+    ]
+    for copy in small + parts:
+        copy.start()
+    for copy in small:
+        copy.wait()
     c0, c1 = courant_ref[0], courant_ref[1]
     moving = mov_ref[...]
     sea = sea_ref[...]
@@ -223,10 +217,24 @@
 
         lax.fori_loop(0, QUAD, step, 0, unroll=6)
 
-    quadrant(0, True, True)
-    quadrant(QUAD, False, True)
-    quadrant(2 * QUAD, False, False)
-    quadrant(3 * QUAD, True, False)
+    for k, (from_west, from_south) in enumerate(((True, True), (False, True), (False, False), (True, False))):
+        parts[k].wait()
+        quadrant(k * QUAD, from_west, from_south)
+
+    east = jnp.zeros((height, 128), jnp.float32)
+    west = jnp.zeros((height, 128), jnp.float32)
+    for q in range(HALF + 2):
+        mine = lane // 2 == q
+        if q < HALF:
+            p_e = q if q < QUAD else q + HALF
+            edge_e, edge_w = x_ref[p_e, :, breadth - 128 :], x_ref[q + QUAD, :, :128]
+        else:
+            field = moving if q == HALF else sea
+            edge_e, edge_w = field[:, breadth - 128 :], field[:, :128]
+        east = jnp.where(mine, pltpu.roll(edge_e, (2 * q + 2) % 128, axis=1), east)
+        west = jnp.where(mine, pltpu.roll(edge_w, 2 * q, axis=1), west)
+    east_ref[...] = east
+    west_ref[...] = west
 
 
 def profile_rows(halves, weight, table, first_row, count, height, breadth):
@@ -486,6 +494,9 @@
 
     both = ("lat", "lon")
 
+    def in_hbm(*arrays):
+        return [pltpu.with_memory_space_constraint(array, pltpu.HBM) for array in arrays]
+
     def shape(*dims, kind=f32):
         return jax.ShapeDtypeStruct(dims, kind)
 
@@ -505,27 +516,24 @@
         + [pltpu.VMEM((height, breadth), f32), pltpu.VMEM((height, breadth), jnp.int32), pltpu.SemaphoreType.DMA((4,))],
         compiler_params=params,
         name="pack_rows",
-    )(*(pltpu.with_memory_space_constraint(v, pltpu.HBM) for v in (x, speed_factor, land_sea_mask)))
+    )(*in_hbm(x, speed_factor, land_sea_mask))
     second = lax.ppermute(second, both, row_second)
     first = lax.ppermute(first, "lat", row_first)
-    east, west = pl.pallas_call(
-        pack_columns_kernel,
-        out_shape=[columns] * 2,
-        in_specs=[vmem] * 3,
-        out_specs=[vmem] * 2,
-        compiler_params=params,
-        cost_estimate=pl.CostEstimate(flops=2_000_000_000, bytes_accessed=5_000_000, transcendentals=0),
-        name="pack_columns",
-    )(x, moving, sea)
-    halves = pl.pallas_call(
+    halves, east, west = pl.pallas_call(
         inside_kernel,
-        out_shape=pltpu.VMEM((breadth // 128, (PLANES + 4) * height, 128), f32),
-        in_specs=[smem] * 2 + [vmem] * 3,
-        out_specs=vmem,
+        out_shape=[pltpu.VMEM((breadth // 128, (PLANES + 4) * height, 128), f32)] + [columns] * 2,
+        in_specs=[hbm] * 3 + [vmem] * 2,
+        out_specs=[vmem] * 3,
+        scratch_shapes=[
+            pltpu.VMEM((PLANES, height, breadth), f32),
+            pltpu.SMEM(courant.shape, f32),
+            pltpu.SMEM(headings.shape, f32),
+            pltpu.SemaphoreType.DMA((6,)),
+        ],
         compiler_params=params,
         cost_estimate=pl.CostEstimate(flops=4_000_000_000, bytes_accessed=5_000_000, transcendentals=0),
         name="advance_inside",
-    )(courant, headings, x, moving, sea)
+    )(*in_hbm(courant, headings, x), moving, sea)
     south, north, first, second = pl.pallas_call(
         functools.partial(corner_kernel, n_lat),
         out_shape=[row_halo] * 2 + [column_message] * 2,

time: 88.3 us -> 85.8 us (0.972)
  local copies, waits for them, and re-layouts: 3.02 us -> 0.03 us
    unnamed x16 -> x12, local copies, waits for them, and re-layouts: 3.02 us -> 0.03 us
    pallas_call x2 -> x1, Pallas kernels: 3.72 us -> 4.27 us  [body(): pl.pallas_call(inside_kernel, out_shape=[pltpu.VMEM((breadth // 128, (PLA...]
where the time goes in v8:
time: 85.8 us; the launch traced here: 85.5 us
  blocking collectives  38.1 us (44%)
  Pallas kernels  35.8 us (42%)
  starting transfers between devices  10.9 us (13%)
    all_to_all x1, blocking collectives, body(): lax.all_to_all(picked, both, split_axis=0, concat_axis=0, tiled=True)  38.1 us
    pallas_call x1, Pallas kernels, body(): pl.pallas_call(add_kernel, out_shape=pltpu.HBM((components, OUT_DEV), f32...  14.9 us
    pallas_call x1, Pallas kernels, body(): pl.pallas_call(finish_kernel, out_shape=[pltpu.HBM((PLANES * height, brea...  12.3 us
    ppermute x1, starting transfers between devices, body(): second = lax.ppermute(second, 'lon', column_second)  6.29 us
    ppermute x1, starting transfers between devices, body(): second = lax.ppermute(second, both, row_second)  4.51 us
    pallas_call x1, Pallas kernels, body(): pl.pallas_call(inside_kernel, out_shape=[pltpu.VMEM((breadth // 128, (PLA...  4.27 us
    pallas_call x1, Pallas kernels, body(): pl.pallas_call(profile_kernel, out_shape=[table_shape, shape(3 * (PLANES...  2.97 us
  transfers between devices with their start and end apart: 4, of which 0 were waited for; matrix products, arithmetic and copies ran while one was open for 0% of the time, Pallas kernels for 8%

profile of v8, /device:TPU:1, one launch (start us, length us, event | category | flops | bytes accessed | tf_op | source)
XLA Modules:
  0.0 85.5 jit_solution(11281524818537572337)
XLA Ops:
  0.6 1.2 %pack_rows.1 = (bf16[2,48,256]{2,1,0:T(8,128)(2,1)S(1)}, bf16[2,48,256]{2,1,0:T(8,128)(2,1)S(1)}, f32[32,256]{1,0:T(8,128)S(1)}, f32[32,256]{1,0:T(8,128)S(1)}) custom-call(f32[72,32,256]{2,1,0:T(8,128)} %bitcast.9, f32[32,256]{1,0:T(8,128)} %speed_hbm.1, s32[32,256]{1,0:T(8,128)} %mask_hbm.1), custom_call_target="tpu_custom_call" | custom-call | tf_op jit(solution)/shard_map/pack_rows/pallas_call | solution.py:509
  1.9 4.5 %collective-permute-start = (bf16[2,48,256]{2,1,0:T(8,128)(2,1)S(1)}, bf16[2,48,256]{2,1,0:T(8,128)(2,1)S(1)}, u32[]{:S(2)}, u32[]{:S(2)}) collective-permute-start(bf16[2,48,256]{2,1,0:T(8,128)(2,1)S(1)} %get-tuple-element.23), channel_id=1, source_target_pairs={{0,0},{112,127},{16,32},{32,16},{48,64},{64,48},{80,96},{96,80},{1... | collective-permute-start | bytes 147464 | tf_op jit(solution)/shard_map/ppermute | solution.py:520
  6.4 0.1 collective-permute-start.1
  6.5 0.0 copy-start.5
  6.5 4.3 %advance_inside.1 = (f32[2,2432,128]{2,1,0:T(8,128)S(1)}, f32[32,128]{1,0:T(8,128)S(1)}, f32[32,128]{1,0:T(8,128)S(1)}) custom-call(f32[2]{0:T(128)} %courant_ref.1, f32[144]{0:T(256)} %constant.6.clone.heading_hbm, f32[72,32,256]{2,1,0:T(8,128)} %bitcast.10, f32[32,256]{1,0:T(8,128)S(1)} %get-tuple-element.18.mov_ref, f32[32,256]{1,0:T(8,128)S(1)} %get-tuple-element.19.sea_ref), custom_call_target="tpu_custom_call" | custom-call | flops 4000000000 | bytes 5000000 | tf_op jit(solution)/shard_map/advance_inside/pallas_call | solution.py:522
  10.8 0.0 collective-permute-done.second_ref
  10.8 0.0 collective-permute-done.1.first_ref
  10.8 0.1 add_corners.1
  10.9 6.3 %collective-permute-start.2 = (f32[40,128]{1,0:T(8,128)S(1)}, f32[40,128]{1,0:T(8,128)S(1)}, u32[]{:S(2)}, u32[]{:S(2)}) collective-permute-start(f32[40,128]{1,0:T(8,128)S(1)} %get-tuple-element.29), channel_id=1, source_target_pairs={{0,15},{1,2},{2,1},{3,4},{4,3},{5,6},{6,5},{7,8},{8,7},{9,10},{10,... | collective-permute-start | bytes 61448 | tf_op jit(solution)/shard_map/ppermute | solution.py:545
  17.2 0.0 collective-permute-start.3
  17.2 0.0 copy-done.5
  17.2 0.0 copy-start
  17.2 0.0 copy-start.2
  17.2 0.0 copy-start.3
  17.2 0.0 copy-start.4
  17.3 3.0 %profiles_inside.1 = (f32[8192,128]{1,0:T(8,128)S(1)}, bf16[240,128]{1,0:T(8,128)(2,1)S(1)}, f32[2,128,256]{2,1,0:T(8,128)S(1)}) custom-call(f32[2,2432,128]{2,1,0:T(8,128)S(1)} %get-tuple-element.20.halves.halves_in, f32[64,72]{1,0:T(8,128)S(1)} %copy-done.5), custom_call_target="tpu_custom_call" | custom-call | flops 2000000000 | bytes 5000000 | tf_op jit(solution)/shard_map/profiles_inside/pallas_call | solution.py:552
  20.2 0.0 collective-permute-done.2.second_ref
  20.2 0.0 collective-permute-done.3.first_ref
  20.2 0.0 copy-done
  20.3 0.0 copy-done.2
  20.3 0.0 copy-done.3
  20.3 0.0 copy-done.4
  20.3 12.3 %finish_and_pick.1 = (f32[2304,256]{1,0:T(8,128)}, bf16[8192,128]{1,0:T(8,128)(2,1)}, f32[2,2432,128]{2,1,0:T(8,128)S(1)}, f32[8192,128]{1,0:T(8,128)S(1)}) custom-call(f32[2]{0:T(128)S(1)} %copy-done.4, s32[128,128]{1,0:T(8,128)S(1)} %bitcast.7, f32[32,256]{1,0:T(8,128)S(1)} %get-tuple-element.18.mov_ref, ...), custom_call_target="tpu_custom_call", output_to_operand_aliasing={{2}: (12, {}), {3}: (13, {})} | custom-call | tf_op jit(solution)/shard_map/finish_and_pick/pallas_call | solution.py:562
  32.6 0.0 copy-start.1
  32.6 38.1 %all_to_all.5 = bf16[128,64,128]{2,1,0:T(8,128)(2,1)S(1)} all-to-all(bf16[128,64,128]{2,1,0:T(8,128)(2,1)} %bitcast.11), channel_id=1, replica_groups=mesh['lat'=8,'lon'=16] {'lat','lon'}, dimensions={0} | all-to-all | bytes 4194304 | tf_op jit(solution)/shard_map/all_to_all | solution.py:587
  70.7 0.0 copy-done.1
  70.7 14.9 %add_profiles.1 = f32[64,4096]{1,0:T(8,128)} custom-call(s32[128,128]{1,0:T(8,128)S(1)} %bitcast.8, bf16[8192,128]{1,0:T(8,128)(2,1)S(1)} %bitcast.6), custom_call_target="tpu_custom_call" | custom-call | tf_op jit(solution)/shard_map/add_profiles/pallas_call | solution.py:590
Async XLA Ops:
  1.9 8.9 %collective-permute-start = (bf16[2,48,256]{2,1,0:T(8,128)(2,1)S(1)}, bf16[2,48,256]{2,1,0:T(8,128)(2,1)S(1)}, u32[]{:S(2)}, u32[]{:S(2)}) collective-permute-start(bf16[2,48,256]{2,1,0:T(8,128)(2,1)S(1)} %get-tuple-element.23), channel_id=1, source_target_pairs={{0,0},{112,127},{16,32},{32,16},{48,64},{64,48},{80,96},{96,80},{1... | collective-permute-start | bytes 147464 | tf_op jit(solution)/shard_map/ppermute | solution.py:520
  6.4 4.4 %collective-permute-start.1 = (bf16[2,48,256]{2,1,0:T(8,128)(2,1)S(1)}, bf16[2,48,256]{2,1,0:T(8,128)(2,1)S(1)}, u32[]{:S(2)}, u32[]{:S(2)}) collective-permute-start(bf16[2,48,256]{2,1,0:T(8,128)(2,1)S(1)} %get-tuple-element.24), channel_id=1, source_target_pairs={{0,16},{16,0},{32,48},{48,32},{64,80},{80,64},{96,112},{112,96},{1... | collective-permute-start | bytes 147464 | tf_op jit(solution)/shard_map/ppermute | solution.py:521
  6.5 10.7 %copy-start.5 = (f32[64,72]{1,0:T(8,128)S(1)}, f32[64,72]{1,0:T(8,128)}, u32[]{:S(2)}) copy-start(f32[64,72]{1,0:T(8,128)} %kernel_ref.1) | copy-start | bytes 55300
  10.9 9.3 %collective-permute-start.2 = (f32[40,128]{1,0:T(8,128)S(1)}, f32[40,128]{1,0:T(8,128)S(1)}, u32[]{:S(2)}, u32[]{:S(2)}) collective-permute-start(f32[40,128]{1,0:T(8,128)S(1)} %get-tuple-element.29), channel_id=1, source_target_pairs={{0,15},{1,2},{2,1},{3,4},{4,3},{5,6},{6,5},{7,8},{8,7},{9,10},{10,... | collective-permute-start | bytes 61448 | tf_op jit(solution)/shard_map/ppermute | solution.py:545
  17.2 3.0 %collective-permute-start.3 = (f32[40,128]{1,0:T(8,128)S(1)}, f32[40,128]{1,0:T(8,128)S(1)}, u32[]{:S(2)}, u32[]{:S(2)}) collective-permute-start(f32[40,128]{1,0:T(8,128)S(1)} %get-tuple-element.30), channel_id=1, source_target_pairs={{0,1},{1,0},{2,3},{3,2},{4,5},{5,4},{6,7},{7,6},{8,9},{9,8},{10,11... | collective-permute-start | bytes 61448 | tf_op jit(solution)/shard_map/ppermute | solution.py:546
  17.2 3.0 %copy-start = (s32[1,128,128]{2,1,0:T(8,128)S(1)}, s32[1,128,128]{2,1,0:T(8,128)}, u32[]{:S(2)}) copy-start(s32[1,128,128]{2,1,0:T(8,128)} %param.15) | copy-start | bytes 196612
  17.2 3.0 %copy-start.2 = (f32[40,128]{1,0:T(8,128)S(1)}, f32[40,128]{1,0:T(8,128)}, u32[]{:S(2)}) copy-start(f32[40,128]{1,0:T(8,128)} %constant.8.clone.subs_ref) | copy-start | bytes 61444
  17.2 3.0 %copy-start.3 = (f32[8,128]{1,0:T(8,128)S(1)}, f32[8,128]{1,0:T(8,128)}, u32[]{:S(2)}) copy-start(f32[8,128]{1,0:T(8,128)} %constant.7.clone.lanes_ref) | copy-start | bytes 12292
  17.2 3.0 %copy-start.4 = (f32[2]{0:T(128)S(1)}, f32[2]{0:T(128)}, u32[]{:S(2)}) copy-start(f32[2]{0:T(128)} %courant_ref.1) | copy-start | bytes 28
  32.6 38.1 %copy-start.1 = (s32[1,128,128]{2,1,0:T(8,128)S(1)}, s32[1,128,128]{2,1,0:T(8,128)}, u32[]{:S(2)}) copy-start(s32[1,128,128]{2,1,0:T(8,128)} %param.16) | copy-start | bytes 196612

commit v9 on v8

--- a/solution.py
+++ b/solution.py
@@ -38,8 +38,13 @@
     return row_first, row_second, column_first, column_second
 
 
-def pack_rows_kernel(x_hbm, speed_hbm, mask_hbm, first_ref, second_ref, mov_ref, sea_ref,
-                     up_ref, down_ref, top_rows, bottom_rows, speed_ref, mask_ref, sems):
+def is_early():
+    return lax.axis_index("lon") % 4 < 2
+
+
+def pack_rows_kernel(courant_hbm, heading_hbm, x_hbm, speed_hbm, mask_hbm,
+                     first_ref, second_ref, mov_ref, sea_ref, halves, east_ref, west_ref,
+                     up_ref, down_ref, top_rows, bottom_rows, speed_ref, mask_ref, sems, *scratch):
     height, breadth = speed_ref.shape
     copies = [
         pltpu.make_async_copy(source, target, sems.at[k])
@@ -80,8 +85,13 @@
         first_ref[...] = down_ref[...].astype(jnp.bfloat16)
         second_ref[...] = up_ref[...].astype(jnp.bfloat16)
 
-
-def corner_kernel(n_lat, second_ref, first_ref, east_ref, west_ref, south_ref, north_ref, out_first, out_second):
+    @pl.when(is_early())
+    def _():
+        advance_inside(courant_hbm, heading_hbm, x_hbm, mov_ref, sea_ref, halves, east_ref, west_ref, *scratch)
+
+
+def corner_kernel(n_lat, second_ref, first_ref, east_ref, west_ref, halves, kernel_ref,
+                  south_ref, north_ref, out_first, out_second, table, weight_ref, edge_ref, wide_kernel):
     height = east_ref.shape[0]
     breadth = first_ref.shape[2]
     lat = lax.axis_index("lat")
@@ -134,6 +144,10 @@
     out_first[height:] = jnp.where(even_lon, east_edge, west_edge)
     out_second[height:] = jnp.where(even_lon, west_edge, east_edge)
 
+    @pl.when(is_early())
+    def _():
+        profiles_inside(halves, kernel_ref, table, weight_ref, edge_ref, wide_kernel)
+
 
 def for_windows(list_ref, window, sems, work):
     lines = WINDOW // 128
@@ -158,8 +172,14 @@
                 fetch(i + 2, w).start()
 
 
-def inside_kernel(courant_hbm, heading_hbm, x_hbm, mov_ref, sea_ref, halves, east_ref, west_ref,
-                  x_ref, courant_ref, heading_ref, sems):
+def inside_kernel(courant_hbm, heading_hbm, x_hbm, mov_ref, sea_ref, _0, _1, _2, halves, east_ref, west_ref, *scratch):
+    @pl.when(jnp.logical_not(is_early()))
+    def _():
+        advance_inside(courant_hbm, heading_hbm, x_hbm, mov_ref, sea_ref, halves, east_ref, west_ref, *scratch)
+
+
+def advance_inside(courant_hbm, heading_hbm, x_hbm, mov_ref, sea_ref, halves, east_ref, west_ref,
+                   x_ref, courant_ref, heading_ref, sems):
     height, breadth = mov_ref.shape
     small = [
         pltpu.make_async_copy(courant_hbm, courant_ref, sems.at[4]),
@@ -254,7 +274,13 @@
     table[pl.ds(start, count * breadth), :] = profile
 
 
-def profile_kernel(halves, kernel_ref, table, weight_ref, edge_ref, wide_kernel):
+def profile_kernel(halves, kernel_ref, _0, _1, _2, table, weight_ref, edge_ref, wide_kernel):
+    @pl.when(jnp.logical_not(is_early()))
+    def _():
+        profiles_inside(halves, kernel_ref, table, weight_ref, edge_ref, wide_kernel)
+
+
+def profiles_inside(halves, kernel_ref, table, weight_ref, edge_ref, wide_kernel):
     height, breadth = halves.shape[1] // (PLANES + 4), table.shape[0] // (halves.shape[1] // (PLANES + 4))
     pad = jnp.zeros((8, 128), jnp.bfloat16)
     wide_kernel[...] = jnp.zeros((128, 128), jnp.float32)
@@ -506,66 +532,80 @@
     columns = shape(height, 128)
     column_message = shape(height + 8, 128)
     row_first, row_second, column_first, column_second = exchange_pairs(n_lat, n_lon)
-    first, second, moving, sea = pl.pallas_call(
+    inside_shapes = [
+        pltpu.VMEM((breadth // 128, (PLANES + 4) * height, 128), f32),
+        pltpu.VMEM(columns.shape, f32),
+        pltpu.VMEM(columns.shape, f32),
+    ]
+    inside_scratch = [
+        pltpu.VMEM((PLANES, height, breadth), f32),
+        pltpu.SMEM(courant.shape, f32),
+        pltpu.SMEM(headings.shape, f32),
+        pltpu.SemaphoreType.DMA((6,)),
+    ]
+    first, second, moving, sea, *inside = pl.pallas_call(
         pack_rows_kernel,
-        out_shape=[row_message] * 2 + [shape(height, breadth)] * 2,
-        in_specs=[hbm] * 3,
-        out_specs=[vmem] * 4,
+        out_shape=[row_message] * 2 + [shape(height, breadth)] * 2 + inside_shapes,
+        in_specs=[hbm] * 5,
+        out_specs=[vmem] * 7,
         scratch_shapes=[pltpu.VMEM((2, ROWS, breadth), f32)] * 2
         + [pltpu.VMEM((HALF, 8, breadth), f32)] * 2
-        + [pltpu.VMEM((height, breadth), f32), pltpu.VMEM((height, breadth), jnp.int32), pltpu.SemaphoreType.DMA((4,))],
+        + [pltpu.VMEM((height, breadth), f32), pltpu.VMEM((height, breadth), jnp.int32), pltpu.SemaphoreType.DMA((4,))]
+        + inside_scratch,
         compiler_params=params,
         name="pack_rows",
-    )(*in_hbm(x, speed_factor, land_sea_mask))
+    )(*in_hbm(courant, headings, x, speed_factor, land_sea_mask))
     second = lax.ppermute(second, both, row_second)
     first = lax.ppermute(first, "lat", row_first)
     halves, east, west = pl.pallas_call(
         inside_kernel,
-        out_shape=[pltpu.VMEM((breadth // 128, (PLANES + 4) * height, 128), f32)] + [columns] * 2,
-        in_specs=[hbm] * 3 + [vmem] * 2,
+        out_shape=inside_shapes,
+        in_specs=[hbm] * 3 + [vmem] * 5,
         out_specs=[vmem] * 3,
-        scratch_shapes=[
-            pltpu.VMEM((PLANES, height, breadth), f32),
-            pltpu.SMEM(courant.shape, f32),
-            pltpu.SMEM(headings.shape, f32),
-            pltpu.SemaphoreType.DMA((6,)),
-        ],
+        input_output_aliases={5: 0, 6: 1, 7: 2},
+        scratch_shapes=inside_scratch,
         compiler_params=params,
         cost_estimate=pl.CostEstimate(flops=4_000_000_000, bytes_accessed=5_000_000, transcendentals=0),
         name="advance_inside",
-    )(*in_hbm(courant, headings, x), moving, sea)
-    south, north, first, second = pl.pallas_call(
+    )(*in_hbm(courant, headings, x), moving, sea, *inside)
+    profile_shapes = [
+        pltpu.VMEM((height * breadth, 128), f32),
+        pltpu.VMEM((3 * (PLANES + 8), 128), jnp.bfloat16),
+        pltpu.VMEM((2, 128, 256), f32),
+    ]
+    south, north, first, second, *profiles = pl.pallas_call(
         functools.partial(corner_kernel, n_lat),
-        out_shape=[row_halo] * 2 + [column_message] * 2,
-        in_specs=[vmem] * 4,
-        out_specs=[vmem] * 4,
+        out_shape=[row_halo] * 2 + [column_message] * 2 + profile_shapes,
+        in_specs=[vmem] * 6,
+        out_specs=[vmem] * 7,
+        scratch_shapes=[pltpu.VMEM((128, 128), f32)],
         compiler_params=params,
         name="add_corners",
-    )(second, first, east, west)
+    )(second, first, east, west, halves, depth_kernel)
     second = lax.ppermute(second, "lon", column_second)
     first = lax.ppermute(first, "lon", column_first)
 
     lists = (devices * slots // 128, 128)
     slot_rows = devices * slots // 2
     slot_rows = devices * slots // 2
-    table_shape = pltpu.VMEM((height * breadth, 128), f32)
     table, weight, edges = pl.pallas_call(
         profile_kernel,
-        out_shape=[table_shape, shape(3 * (PLANES + 8), 128, kind=jnp.bfloat16), shape(2, 128, 256)],
-        in_specs=[vmem] * 2,
+        out_shape=profile_shapes,
+        in_specs=[vmem] * 5,
         out_specs=[vmem] * 3,
+        input_output_aliases={2: 0, 3: 1, 4: 2},
         scratch_shapes=[pltpu.VMEM((128, 128), f32)],
         compiler_params=params,
         cost_estimate=pl.CostEstimate(flops=2_000_000_000, bytes_accessed=5_000_000, transcendentals=0),
         name="profiles_inside",
-    )(halves, depth_kernel)
+    )(halves, depth_kernel, *profiles)
     propagated, picked, *_ = pl.pallas_call(
         finish_kernel,
         out_shape=[
             pltpu.HBM((PLANES * height, breadth), f32),
             pltpu.HBM((slot_rows, 128), jnp.bfloat16),
-            pltpu.VMEM(halves.shape, f32),
-            table_shape,
+            inside_shapes[0],
+            profile_shapes[0],
         ],
         in_specs=[smem] + [vmem] * 13,
         out_specs=[hbm, hbm, vmem, vmem],

time: 85.8 us -> 89.2 us (1.040)
  waiting for transfers between devices: 0.01 us -> 6.09 us
  starting transfers between devices: 10.9 us -> 6.4 us
  blocking collectives: 38.1 us -> 39.8 us
    pallas_call x2, Pallas kernels: 7.24 us -> 0.09 us  [the longest x1 0.07 us: body(): pl.pallas_call(inside_kernel, out_shape=inside_shapes, in_specs=[hbm] * 3...]
    ppermute x1, waiting for transfers between devices: 0.01 us -> 4.52 us  [body(): second = lax.ppermute(second, 'lon', column_second)]
    ppermute x1, starting transfers between devices: 6.29 us -> 1.8 us  [body(): second = lax.ppermute(second, 'lon', column_second)]
    pallas_call x1, Pallas kernels: 1.23 us -> 5.5 us  [body(): pl.pallas_call(pack_rows_kernel, out_shape=[row_message] * 2 + [shape(hei...]
    pallas_call x1, Pallas kernels: 0.13 us -> 3.07 us  [body(): pl.pallas_call(functools.partial(corner_kernel, n_lat), out_shape=[row_ha...]
    all_to_all x1, blocking collectives: 38.1 us -> 39.8 us  [body(): lax.all_to_all(picked, both, split_axis=0, concat_axis=0, tiled=True)]
    ppermute x1, waiting for transfers between devices: 0.01 us -> 1.57 us  [body(): second = lax.ppermute(second, both, row_second)]
  transfers between devices with their start and end apart: 4 -> 4, of which waited for: 0 -> 2; matrix products, arithmetic and copies ran while one was open for 0% -> 0% of each run, Pallas kernels for 8% -> 0%
where the time goes in v9:
time: 89.2 us; the launch traced here: 88.9 us
  blocking collectives  39.8 us (45%)
  Pallas kernels  35.9 us (40%)
  starting transfers between devices  6.4 us (7%)
  waiting for transfers between devices  6.09 us (7%)
    all_to_all x1, blocking collectives, body(): lax.all_to_all(picked, both, split_axis=0, concat_axis=0, tiled=True)  39.8 us
    pallas_call x1, Pallas kernels, body(): pl.pallas_call(add_kernel, out_shape=pltpu.HBM((components, OUT_DEV), f32...  14.9 us
    pallas_call x1, Pallas kernels, body(): pl.pallas_call(finish_kernel, out_shape=[pltpu.HBM((PLANES * height, brea...  12.4 us
    pallas_call x1, Pallas kernels, body(): pl.pallas_call(pack_rows_kernel, out_shape=[row_message] * 2 + [shape(hei...  5.5 us
    ppermute x1, waiting for transfers between devices, body(): second = lax.ppermute(second, 'lon', column_second)  4.52 us
    ppermute x1, starting transfers between devices, body(): second = lax.ppermute(second, both, row_second)  4.51 us
    pallas_call x1, Pallas kernels, body(): pl.pallas_call(functools.partial(corner_kernel, n_lat), out_shape=[row_ha...  3.07 us
    ppermute x1, starting transfers between devices, body(): second = lax.ppermute(second, 'lon', column_second)  1.8 us
  transfers between devices with their start and end apart: 4, of which 2 were waited for; matrix products, arithmetic and copies ran while one was open for 0% of the time, Pallas kernels for 0%

profile of v9, /device:TPU:1, one launch (start us, length us, event | category | flops | bytes accessed | tf_op | source)
XLA Modules:
  0.0 88.9 jit_solution(12539811077272539046)
XLA Ops:
  0.6 5.5 %pack_rows.1 = (bf16[2,48,256]{2,1,0:T(8,128)(2,1)S(1)}, bf16[2,48,256]{2,1,0:T(8,128)(2,1)S(1)}, f32[32,256]{1,0:T(8,128)S(1)}, f32[32,256]{1,0:T(8,128)S(1)}, ...) custom-call(f32[2]{0:T(128)} %courant_ref.1, f32[144]{0:T(256)} %constant.6.clone.heading_hbm, ...), custom_call_target="tpu_custom_call" | custom-call | tf_op jit(solution)/shard_map/pack_rows/pallas_call | solution.py:546
  6.1 4.5 %collective-permute-start = (bf16[2,48,256]{2,1,0:T(8,128)(2,1)S(1)}, bf16[2,48,256]{2,1,0:T(8,128)(2,1)S(1)}, u32[]{:S(2)}, u32[]{:S(2)}) collective-permute-start(bf16[2,48,256]{2,1,0:T(8,128)(2,1)S(1)} %get-tuple-element.30), channel_id=1, source_target_pairs={{0,0},{112,127},{16,32},{32,16},{48,64},{64,48},{80,96},{96,80},{1... | collective-permute-start | bytes 147464 | tf_op jit(solution)/shard_map/ppermute | solution.py:558
  10.7 0.1 collective-permute-start.1
  10.8 0.0 copy-start.2
  10.8 0.1 advance_inside.1
  10.8 1.6 %collective-permute-done.second_ref = bf16[2,48,256]{2,1,0:T(8,128)(2,1)S(1)} collective-permute-done((bf16[2,48,256]{2,1,0:T(8,128)(2,1)S(1)}, bf16[2,48,256]{2,1,0:T(8,128)(2,1)S(1)}, u32[]{:S(2)}, u32[]{:S(2)}) %collective-permute-start) | collective-permute-done | bytes 49184 | tf_op jit(solution)/shard_map/ppermute | solution.py:558
  12.4 0.0 collective-permute-done.1.first_ref
  12.4 0.0 copy-done.2
  12.4 3.1 %add_corners.1 = (f32[2,40,256]{2,1,0:T(8,128)S(1)}, f32[2,40,256]{2,1,0:T(8,128)S(1)}, f32[40,128]{1,0:T(8,128)S(1)}, f32[40,128]{1,0:T(8,128)S(1)}, f32[8192,1...) custom-call(bf16[2,48,256]{2,1,0:T(8,128)(2,1)S(1)} %collective-permute-done.second_ref, ...), custom_call_target="tpu_custom_call" | custom-call | tf_op jit(solution)/shard_map/add_corners/pallas_call | solution.py:576
  15.5 1.8 %collective-permute-start.2 = (f32[40,128]{1,0:T(8,128)S(1)}, f32[40,128]{1,0:T(8,128)S(1)}, u32[]{:S(2)}, u32[]{:S(2)}) collective-permute-start(f32[40,128]{1,0:T(8,128)S(1)} %get-tuple-element.41), channel_id=1, source_target_pairs={{0,15},{1,2},{2,1},{3,4},{4,3},{5,6},{6,5},{7,8},{8,7},{9,10},{10,... | collective-permute-start | bytes 61448 | tf_op jit(solution)/shard_map/ppermute | solution.py:585
  17.3 0.0 collective-permute-start.3
  17.3 0.0 copy-start
  17.3 0.0 copy-start.3
  17.3 0.0 copy-start.4
  17.3 0.0 copy-start.5
  17.4 4.5 %collective-permute-done.2.second_ref = f32[40,128]{1,0:T(8,128)S(1)} collective-permute-done((f32[40,128]{1,0:T(8,128)S(1)}, f32[40,128]{1,0:T(8,128)S(1)}, u32[]{:S(2)}, u32[]{:S(2)}) %collective-permute-start.2) | collective-permute-done | bytes 20512 | tf_op jit(solution)/shard_map/ppermute | solution.py:585
  21.9 0.0 collective-permute-done.3.first_ref
  21.9 0.0 copy-done
  21.9 0.0 copy-done.3
  21.9 0.0 copy-done.4
  21.9 0.0 copy-done.5
  21.9 12.4 %finish_and_pick.1 = (f32[2304,256]{1,0:T(8,128)}, bf16[8192,128]{1,0:T(8,128)(2,1)}, f32[2,2432,128]{2,1,0:T(8,128)S(1)}, f32[8192,128]{1,0:T(8,128)S(1)}) custom-call(f32[2]{0:T(128)S(1)} %copy-done.5, s32[128,128]{1,0:T(8,128)S(1)} %bitcast.7, f32[32,256]{1,0:T(8,128)S(1)} %get-tuple-element.24.mov_ref, ...), custom_call_target="tpu_custom_call", output_to_operand_aliasing={{2}: (12, {}), {3}: (13, {})} | custom-call | tf_op jit(solution)/shard_map/finish_and_pick/pallas_call | solution.py:602
  34.3 0.0 copy-start.1
  34.3 39.8 %all_to_all.5 = bf16[128,64,128]{2,1,0:T(8,128)(2,1)S(1)} all-to-all(bf16[128,64,128]{2,1,0:T(8,128)(2,1)} %bitcast.11), channel_id=1, replica_groups=mesh['lat'=8,'lon'=16] {'lat','lon'}, dimensions={0} | all-to-all | bytes 4194304 | tf_op jit(solution)/shard_map/all_to_all | solution.py:627
  74.1 0.0 copy-done.1
  74.1 14.9 %add_profiles.1 = f32[64,4096]{1,0:T(8,128)} custom-call(s32[128,128]{1,0:T(8,128)S(1)} %bitcast.8, bf16[8192,128]{1,0:T(8,128)(2,1)S(1)} %bitcast.6), custom_call_target="tpu_custom_call" | custom-call | tf_op jit(solution)/shard_map/add_profiles/pallas_call | solution.py:630
  (1 shorter events, 0.0 us)
Async XLA Ops:
  6.1 6.3 %collective-permute-start = (bf16[2,48,256]{2,1,0:T(8,128)(2,1)S(1)}, bf16[2,48,256]{2,1,0:T(8,128)(2,1)S(1)}, u32[]{:S(2)}, u32[]{:S(2)}) collective-permute-start(bf16[2,48,256]{2,1,0:T(8,128)(2,1)S(1)} %get-tuple-element.30), channel_id=1, source_target_pairs={{0,0},{112,127},{16,32},{32,16},{48,64},{64,48},{80,96},{96,80},{1... | collective-permute-start | bytes 147464 | tf_op jit(solution)/shard_map/ppermute | solution.py:558
  10.7 1.8 %collective-permute-start.1 = (bf16[2,48,256]{2,1,0:T(8,128)(2,1)S(1)}, bf16[2,48,256]{2,1,0:T(8,128)(2,1)S(1)}, u32[]{:S(2)}, u32[]{:S(2)}) collective-permute-start(bf16[2,48,256]{2,1,0:T(8,128)(2,1)S(1)} %get-tuple-element.31), channel_id=1, source_target_pairs={{0,16},{16,0},{32,48},{48,32},{64,80},{80,64},{96,112},{112,96},{1... | collective-permute-start | bytes 147464 | tf_op jit(solution)/shard_map/ppermute | solution.py:559
  10.8 1.7 %copy-start.2 = (f32[64,72]{1,0:T(8,128)S(1)}, f32[64,72]{1,0:T(8,128)}, u32[]{:S(2)}) copy-start(f32[64,72]{1,0:T(8,128)} %kernel_ref.3) | copy-start | bytes 55300
  15.5 6.4 %collective-permute-start.2 = (f32[40,128]{1,0:T(8,128)S(1)}, f32[40,128]{1,0:T(8,128)S(1)}, u32[]{:S(2)}, u32[]{:S(2)}) collective-permute-start(f32[40,128]{1,0:T(8,128)S(1)} %get-tuple-element.41), channel_id=1, source_target_pairs={{0,15},{1,2},{2,1},{3,4},{4,3},{5,6},{6,5},{7,8},{8,7},{9,10},{10,... | collective-permute-start | bytes 61448 | tf_op jit(solution)/shard_map/ppermute | solution.py:585
  17.3 4.6 %collective-permute-start.3 = (f32[40,128]{1,0:T(8,128)S(1)}, f32[40,128]{1,0:T(8,128)S(1)}, u32[]{:S(2)}, u32[]{:S(2)}) collective-permute-start(f32[40,128]{1,0:T(8,128)S(1)} %get-tuple-element.42), channel_id=1, source_target_pairs={{0,1},{1,0},{2,3},{3,2},{4,5},{5,4},{6,7},{7,6},{8,9},{9,8},{10,11... | collective-permute-start | bytes 61448 | tf_op jit(solution)/shard_map/ppermute | solution.py:586
  17.3 4.6 %copy-start = (s32[1,128,128]{2,1,0:T(8,128)S(1)}, s32[1,128,128]{2,1,0:T(8,128)}, u32[]{:S(2)}) copy-start(s32[1,128,128]{2,1,0:T(8,128)} %param.15) | copy-start | bytes 196612
  17.3 4.6 %copy-start.3 = (f32[40,128]{1,0:T(8,128)S(1)}, f32[40,128]{1,0:T(8,128)}, u32[]{:S(2)}) copy-start(f32[40,128]{1,0:T(8,128)} %constant.8.clone.subs_ref) | copy-start | bytes 61444
  17.3 4.6 %copy-start.4 = (f32[8,128]{1,0:T(8,128)S(1)}, f32[8,128]{1,0:T(8,128)}, u32[]{:S(2)}) copy-start(f32[8,128]{1,0:T(8,128)} %constant.7.clone.lanes_ref) | copy-start | bytes 12292
  17.3 4.6 %copy-start.5 = (f32[2]{0:T(128)S(1)}, f32[2]{0:T(128)}, u32[]{:S(2)}) copy-start(f32[2]{0:T(128)} %courant_ref.1) | copy-start | bytes 28
  34.3 39.8 %copy-start.1 = (s32[1,128,128]{2,1,0:T(8,128)S(1)}, s32[1,128,128]{2,1,0:T(8,128)}, u32[]{:S(2)}) copy-start(s32[1,128,128]{2,1,0:T(8,128)} %param.16) | copy-start | bytes 196612

commit v10 on v9

--- a/solution.py
+++ b/solution.py
@@ -39,7 +39,7 @@
 
 
 def is_early():
-    return lax.axis_index("lon") % 4 < 2
+    return lax.axis_index("lon") % 4 == 0
 
 
 def pack_rows_kernel(courant_hbm, heading_hbm, x_hbm, speed_hbm, mask_hbm,

time: 89.2 us -> 89.2 us (level)
  no operation moved by 1% of the time
where the time goes in v10:
time: 89.2 us; the launch traced here: 89 us
  blocking collectives  39.8 us (45%)
  Pallas kernels  35.9 us (40%)
  starting transfers between devices  6.4 us (7%)
  waiting for transfers between devices  6.09 us (7%)
    all_to_all x1, blocking collectives, body(): lax.all_to_all(picked, both, split_axis=0, concat_axis=0, tiled=True)  39.8 us
    pallas_call x1, Pallas kernels, body(): pl.pallas_call(add_kernel, out_shape=pltpu.HBM((components, OUT_DEV), f32...  14.9 us
    pallas_call x1, Pallas kernels, body(): pl.pallas_call(finish_kernel, out_shape=[pltpu.HBM((PLANES * height, brea...  12.4 us
    pallas_call x1, Pallas kernels, body(): pl.pallas_call(pack_rows_kernel, out_shape=[row_message] * 2 + [shape(hei...  5.5 us
    ppermute x1, waiting for transfers between devices, body(): second = lax.ppermute(second, 'lon', column_second)  4.52 us
    ppermute x1, starting transfers between devices, body(): second = lax.ppermute(second, both, row_second)  4.51 us
    pallas_call x1, Pallas kernels, body(): pl.pallas_call(functools.partial(corner_kernel, n_lat), out_shape=[row_ha...  3.07 us
    ppermute x1, starting transfers between devices, body(): second = lax.ppermute(second, 'lon', column_second)  1.8 us
  transfers between devices with their start and end apart: 4, of which 2 were waited for; matrix products, arithmetic and copies ran while one was open for 0% of the time, Pallas kernels for 0%

profile of v10, /device:TPU:1, one launch (start us, length us, event | category | flops | bytes accessed | tf_op | source)
XLA Modules:
  0.0 89.0 jit_solution(17514701253137421936)
XLA Ops:
  0.6 5.5 %pack_rows.1 = (bf16[2,48,256]{2,1,0:T(8,128)(2,1)S(1)}, bf16[2,48,256]{2,1,0:T(8,128)(2,1)S(1)}, f32[32,256]{1,0:T(8,128)S(1)}, f32[32,256]{1,0:T(8,128)S(1)}, ...) custom-call(f32[2]{0:T(128)} %courant_ref.1, f32[144]{0:T(256)} %constant.6.clone.heading_hbm, ...), custom_call_target="tpu_custom_call" | custom-call | tf_op jit(solution)/shard_map/pack_rows/pallas_call | solution.py:546
  6.1 4.5 %collective-permute-start = (bf16[2,48,256]{2,1,0:T(8,128)(2,1)S(1)}, bf16[2,48,256]{2,1,0:T(8,128)(2,1)S(1)}, u32[]{:S(2)}, u32[]{:S(2)}) collective-permute-start(bf16[2,48,256]{2,1,0:T(8,128)(2,1)S(1)} %get-tuple-element.30), channel_id=1, source_target_pairs={{0,0},{112,127},{16,32},{32,16},{48,64},{64,48},{80,96},{96,80},{1... | collective-permute-start | bytes 147464 | tf_op jit(solution)/shard_map/ppermute | solution.py:558
  10.7 0.1 collective-permute-start.1
  10.8 0.0 copy-start.2
  10.8 0.1 advance_inside.1
  10.8 1.6 %collective-permute-done.second_ref = bf16[2,48,256]{2,1,0:T(8,128)(2,1)S(1)} collective-permute-done((bf16[2,48,256]{2,1,0:T(8,128)(2,1)S(1)}, bf16[2,48,256]{2,1,0:T(8,128)(2,1)S(1)}, u32[]{:S(2)}, u32[]{:S(2)}) %collective-permute-start) | collective-permute-done | bytes 49184 | tf_op jit(solution)/shard_map/ppermute | solution.py:558
  12.4 0.0 collective-permute-done.1.first_ref
  12.4 0.0 copy-done.2
  12.4 3.1 %add_corners.1 = (f32[2,40,256]{2,1,0:T(8,128)S(1)}, f32[2,40,256]{2,1,0:T(8,128)S(1)}, f32[40,128]{1,0:T(8,128)S(1)}, f32[40,128]{1,0:T(8,128)S(1)}, f32[8192,1...) custom-call(bf16[2,48,256]{2,1,0:T(8,128)(2,1)S(1)} %collective-permute-done.second_ref, ...), custom_call_target="tpu_custom_call" | custom-call | tf_op jit(solution)/shard_map/add_corners/pallas_call | solution.py:576
  15.5 1.8 %collective-permute-start.2 = (f32[40,128]{1,0:T(8,128)S(1)}, f32[40,128]{1,0:T(8,128)S(1)}, u32[]{:S(2)}, u32[]{:S(2)}) collective-permute-start(f32[40,128]{1,0:T(8,128)S(1)} %get-tuple-element.41), channel_id=1, source_target_pairs={{0,15},{1,2},{2,1},{3,4},{4,3},{5,6},{6,5},{7,8},{8,7},{9,10},{10,... | collective-permute-start | bytes 61448 | tf_op jit(solution)/shard_map/ppermute | solution.py:585
  17.3 0.0 collective-permute-start.3
  17.3 0.0 copy-start
  17.3 0.0 copy-start.3
  17.3 0.0 copy-start.4
  17.3 0.0 copy-start.5
  17.4 4.5 %collective-permute-done.2.second_ref = f32[40,128]{1,0:T(8,128)S(1)} collective-permute-done((f32[40,128]{1,0:T(8,128)S(1)}, f32[40,128]{1,0:T(8,128)S(1)}, u32[]{:S(2)}, u32[]{:S(2)}) %collective-permute-start.2) | collective-permute-done | bytes 20512 | tf_op jit(solution)/shard_map/ppermute | solution.py:585
  21.9 0.0 collective-permute-done.3.first_ref
  21.9 0.0 copy-done
  21.9 0.0 copy-done.3
  21.9 0.0 copy-done.4
  21.9 0.0 copy-done.5
  21.9 12.4 %finish_and_pick.1 = (f32[2304,256]{1,0:T(8,128)}, bf16[8192,128]{1,0:T(8,128)(2,1)}, f32[2,2432,128]{2,1,0:T(8,128)S(1)}, f32[8192,128]{1,0:T(8,128)S(1)}) custom-call(f32[2]{0:T(128)S(1)} %copy-done.5, s32[128,128]{1,0:T(8,128)S(1)} %bitcast.7, f32[32,256]{1,0:T(8,128)S(1)} %get-tuple-element.24.mov_ref, ...), custom_call_target="tpu_custom_call", output_to_operand_aliasing={{2}: (12, {}), {3}: (13, {})} | custom-call | tf_op jit(solution)/shard_map/finish_and_pick/pallas_call | solution.py:602
  34.3 0.0 copy-start.1
  34.3 39.8 %all_to_all.5 = bf16[128,64,128]{2,1,0:T(8,128)(2,1)S(1)} all-to-all(bf16[128,64,128]{2,1,0:T(8,128)(2,1)} %bitcast.11), channel_id=1, replica_groups=mesh['lat'=8,'lon'=16] {'lat','lon'}, dimensions={0} | all-to-all | bytes 4194304 | tf_op jit(solution)/shard_map/all_to_all | solution.py:627
  74.1 0.0 copy-done.1
  74.1 14.9 %add_profiles.1 = f32[64,4096]{1,0:T(8,128)} custom-call(s32[128,128]{1,0:T(8,128)S(1)} %bitcast.8, bf16[8192,128]{1,0:T(8,128)(2,1)S(1)} %bitcast.6), custom_call_target="tpu_custom_call" | custom-call | tf_op jit(solution)/shard_map/add_profiles/pallas_call | solution.py:630
  (1 shorter events, 0.0 us)
Async XLA Ops:
  6.1 6.3 %collective-permute-start = (bf16[2,48,256]{2,1,0:T(8,128)(2,1)S(1)}, bf16[2,48,256]{2,1,0:T(8,128)(2,1)S(1)}, u32[]{:S(2)}, u32[]{:S(2)}) collective-permute-start(bf16[2,48,256]{2,1,0:T(8,128)(2,1)S(1)} %get-tuple-element.30), channel_id=1, source_target_pairs={{0,0},{112,127},{16,32},{32,16},{48,64},{64,48},{80,96},{96,80},{1... | collective-permute-start | bytes 147464 | tf_op jit(solution)/shard_map/ppermute | solution.py:558
  10.7 1.8 %collective-permute-start.1 = (bf16[2,48,256]{2,1,0:T(8,128)(2,1)S(1)}, bf16[2,48,256]{2,1,0:T(8,128)(2,1)S(1)}, u32[]{:S(2)}, u32[]{:S(2)}) collective-permute-start(bf16[2,48,256]{2,1,0:T(8,128)(2,1)S(1)} %get-tuple-element.31), channel_id=1, source_target_pairs={{0,16},{16,0},{32,48},{48,32},{64,80},{80,64},{96,112},{112,96},{1... | collective-permute-start | bytes 147464 | tf_op jit(solution)/shard_map/ppermute | solution.py:559
  10.8 1.7 %copy-start.2 = (f32[64,72]{1,0:T(8,128)S(1)}, f32[64,72]{1,0:T(8,128)}, u32[]{:S(2)}) copy-start(f32[64,72]{1,0:T(8,128)} %kernel_ref.3) | copy-start | bytes 55300
  15.5 6.4 %collective-permute-start.2 = (f32[40,128]{1,0:T(8,128)S(1)}, f32[40,128]{1,0:T(8,128)S(1)}, u32[]{:S(2)}, u32[]{:S(2)}) collective-permute-start(f32[40,128]{1,0:T(8,128)S(1)} %get-tuple-element.41), channel_id=1, source_target_pairs={{0,15},{1,2},{2,1},{3,4},{4,3},{5,6},{6,5},{7,8},{8,7},{9,10},{10,... | collective-permute-start | bytes 61448 | tf_op jit(solution)/shard_map/ppermute | solution.py:585
  17.3 4.6 %collective-permute-start.3 = (f32[40,128]{1,0:T(8,128)S(1)}, f32[40,128]{1,0:T(8,128)S(1)}, u32[]{:S(2)}, u32[]{:S(2)}) collective-permute-start(f32[40,128]{1,0:T(8,128)S(1)} %get-tuple-element.42), channel_id=1, source_target_pairs={{0,1},{1,0},{2,3},{3,2},{4,5},{5,4},{6,7},{7,6},{8,9},{9,8},{10,11... | collective-permute-start | bytes 61448 | tf_op jit(solution)/shard_map/ppermute | solution.py:586
  17.3 4.6 %copy-start = (s32[1,128,128]{2,1,0:T(8,128)S(1)}, s32[1,128,128]{2,1,0:T(8,128)}, u32[]{:S(2)}) copy-start(s32[1,128,128]{2,1,0:T(8,128)} %param.15) | copy-start | bytes 196612
  17.3 4.6 %copy-start.3 = (f32[40,128]{1,0:T(8,128)S(1)}, f32[40,128]{1,0:T(8,128)}, u32[]{:S(2)}) copy-start(f32[40,128]{1,0:T(8,128)} %constant.8.clone.subs_ref) | copy-start | bytes 61444
  17.3 4.6 %copy-start.4 = (f32[8,128]{1,0:T(8,128)S(1)}, f32[8,128]{1,0:T(8,128)}, u32[]{:S(2)}) copy-start(f32[8,128]{1,0:T(8,128)} %constant.7.clone.lanes_ref) | copy-start | bytes 12292
  17.3 4.6 %copy-start.5 = (f32[2]{0:T(128)S(1)}, f32[2]{0:T(128)}, u32[]{:S(2)}) copy-start(f32[2]{0:T(128)} %courant_ref.1) | copy-start | bytes 28
  34.3 39.8 %copy-start.1 = (s32[1,128,128]{2,1,0:T(8,128)S(1)}, s32[1,128,128]{2,1,0:T(8,128)}, u32[]{:S(2)}) copy-start(s32[1,128,128]{2,1,0:T(8,128)} %param.16) | copy-start | bytes 196612

commit v11 on v8

--- a/solution.py
+++ b/solution.py
@@ -254,8 +254,40 @@
     table[pl.ds(start, count * breadth), :] = profile
 
 
-def profile_kernel(halves, kernel_ref, table, weight_ref, edge_ref, wide_kernel):
-    height, breadth = halves.shape[1] // (PLANES + 4), table.shape[0] // (halves.shape[1] // (PLANES + 4))
+def profile_kernel(courant_ref, kernel_ref, mov_ref, sea_ref, south_ref, north_ref, subs_ref, halves_in,
+                   halves, table, edge_ref, wide_kernel):
+    height, breadth = mov_ref.shape
+    wide = lax.broadcasted_iota(jnp.int32, (HALF + 4, breadth), 1)
+    plane = lax.broadcasted_iota(jnp.int32, (HALF + 4, 1), 0)
+    subs = subs_ref[...]
+    sub_courant = jnp.where(plane % 2 == 1, courant_ref[1], courant_ref[0])
+
+    def x_change(flux, cx, west_first):
+        west_flux = jnp.where(wide == 0, 0.0, pltpu.roll(flux, 1, axis=1))
+        east_flux = jnp.where(wide == breadth - 1, 0.0, pltpu.roll(flux, breadth - 1, axis=1))
+        from_west = (plane < QUAD) if west_first else (plane >= QUAD)
+        return jnp.where(from_west, cx * (flux - west_flux), cx * (east_flux - flux))
+
+    def add_rows(first, halo, near, next_row, cx, cy, west_first):
+        rim, far = halo[0], halo[1]
+        rim_mov, rim_sea = rim[HALF : HALF + 1], rim[HALF + 1 : HALF + 2]
+        flux0 = rim_mov * rim
+        div_y = cy * (flux0 - far[HALF : HALF + 1] * far)
+        flux1 = rim_mov * (rim_sea * ((rim - x_change(flux0, cx, west_first)) - div_y))
+        sea0, sea1 = sea_ref[near : near + 1, :], sea_ref[next_row : next_row + 1, :]
+        change = sea0 * (cy * flux0)
+        flux = mov_ref[near : near + 1, :] * change
+        near_change = sea0 * (((change - x_change(flux, cx, west_first)) - cy * flux) + cy * flux1)
+        next_change = sea1 * (cy * flux)
+        for at, delta in ((near, near_change), (next_row, next_change)):
+            for h in range(breadth // 128):
+                place = pl.ds(first * height + at, HALF + 4, stride=height)
+                halves[h, place, :] = halves[h, place, :] + delta[:, h * 128 : (h + 1) * 128]
+
+    cx_s, cy_s, cx_n, cy_n = (subs[:, k : k + 1] * sub_courant for k in range(4))
+    add_rows(0, south_ref, 0, 1, cx_s, cy_s, True)
+    add_rows(HALF, north_ref, height - 1, height - 2, cx_n, -cy_n, False)
+
     pad = jnp.zeros((8, 128), jnp.bfloat16)
     wide_kernel[...] = jnp.zeros((128, 128), jnp.float32)
     wide_kernel[:64, :PLANES] = kernel_ref[...]
@@ -264,18 +296,14 @@
     weight_high = turned[:PLANES].astype(jnp.bfloat16)
     weight_low = (turned[:PLANES] - weight_high.astype(jnp.float32)).astype(jnp.bfloat16)
     weight = jnp.concatenate([weight_high, pad, weight_high, pad, weight_low, pad], axis=0)
-    weight_ref[...] = weight
-
-    lane = lax.broadcasted_iota(jnp.int32, (128, 128), 0)
-    plane = lax.broadcasted_iota(jnp.int32, (128, 128), 1)
-    q = lane // 2
-    used = lane < 2 * HALF
-    for side, owner in ((0, jnp.where(q < QUAD, q, q + HALF)), (1, q + QUAD)):
-        for k in range(2):
-            chosen = used & (plane == owner) & (lane % 2 == (k if side == 0 else 1 - k))
-            edge_ref[side, :, k * 128 : (k + 1) * 128] = jnp.dot(
-                chosen.astype(jnp.float32), turned, precision=lax.Precision.HIGHEST, preferred_element_type=jnp.float32
-            )
+
+    wide_kernel[...] = turned
+    edge_ref[...] = jnp.zeros_like(edge_ref)
+    for q in range(HALF):
+        for side, p in ((0, q if q < QUAD else q + HALF), (1, q + QUAD)):
+            for k in range(2):
+                lane = 2 * q + (k if side == 0 else 1 - k)
+                edge_ref[side, lane : lane + 1, k * 128 : (k + 1) * 128] = wide_kernel[p : p + 1, :]
     group = 8
 
     @pl.loop(0, height // group)
@@ -283,107 +311,66 @@
         profile_rows(halves, weight, table, r * group, group, height, breadth)
 
 
-def finish_kernel(courant_ref, cells_ref, mov_ref, sea_ref, weight_ref, edge_ref, south_ref, north_ref, second_ref,
-                  first_ref, lanes_ref, subs_ref, halves_in, table_in, out_ref, picked_ref, halves, table,
+def finish_kernel(courant_ref, cells_ref, mov_ref, sea_ref, edge_ref, south_ref, north_ref, second_ref, first_ref,
+                  lanes_ref, halves_in, table_in, out_ref, picked_ref, halves, table,
                   cells, lines, picks, window, out_sems, window_sems, pick_sem):
     cells[...] = jnp.maximum(cells_ref[...], 0)
     height, breadth = mov_ref.shape
-    c0, c1 = courant_ref[0], courant_ref[1]
     even_lon = lax.axis_index("lon") % 2 == 0
     from_west = jnp.where(even_lon, second_ref[...], first_ref[...])
     from_east = jnp.where(even_lon, first_ref[...], second_ref[...])
-    corner_w, corner_e = from_west[height : height + 1], from_east[height : height + 1]
-
     lane = lax.broadcasted_iota(jnp.int32, (height, 128), 1)
     row = lax.broadcasted_iota(jnp.int32, (height, 128), 0)
     odd = lane % 2 == 1
-
-    def columns(e0, near, far, corner, cx, cy, sign):
-        mov = jnp.where(odd, e0[:, 2 * HALF + 1 : 2 * HALF + 2], e0[:, 2 * HALF : 2 * HALF + 1])
-        sea = e0[:, 2 * HALF + 2 + near : 2 * HALF + 3 + near]
-        f0 = mov * e0
-        f_far = pltpu.roll(f0, 1 if near > far else 127, axis=1)
-        f_south = jnp.where(row == 0, corner, pltpu.roll(f0, 1, axis=0))
-        f_north = jnp.where(row == height - 1, corner, pltpu.roll(f0, height - 1, axis=0))
-        div_x = cx * (f0 - f_far) if sign > 0 else cx * (f_far - f0)
-        div_y = jnp.where(lane < HALF, cy * (f0 - f_south), cy * (f_north - f0))
-        return f0, mov * (sea * ((e0 - div_x) - div_y))
-
+    southern = lane < HALF
     lanes = lanes_ref[...]
-    lane_courant = jnp.where(lanes[4:5] > 0.5, c1, c0)
-    cx_w, cy_w, cx_e, cy_e = (lanes[k : k + 1] * lane_courant for k in range(4))
-    west_flux0, west_flux1 = columns(from_west[:height], 1, 0, corner_w, cx_w, cy_w, 1)
-    east_flux0, east_flux1 = columns(from_east[:height], 0, 1, corner_e, cx_e, cy_e, -1)
-
-    wide = lax.broadcasted_iota(jnp.int32, (HALF + 4, breadth), 1)
-    plane = lax.broadcasted_iota(jnp.int32, (HALF + 4, 1), 0)
-    plane_l = lax.broadcasted_iota(jnp.int32, (HALF + 4, 128), 0)
-    lane_l = lax.broadcasted_iota(jnp.int32, (HALF + 4, 128), 1)
-    subs = subs_ref[...]
-    sub_courant = jnp.where(plane % 2 == 1, c1, c0)
-
-    def to_sublanes(corner, lane_of):
-        return jnp.sum(jnp.where(lane_l == lane_of, corner, 0.0), axis=1, keepdims=True)
-
-    def rows(near, far, first_west, west_corner, east_corner, cx, cy, sign):
-        mov, sea = near[HALF : HALF + 1], near[HALF + 1 : HALF + 2]
-        f0 = mov * near
-        f_far = far[HALF : HALF + 1] * far
-        f_west = jnp.where(wide == 0, west_corner, pltpu.roll(f0, 1, axis=1))
-        f_east = jnp.where(wide == breadth - 1, east_corner, pltpu.roll(f0, breadth - 1, axis=1))
-        from_west = (plane < QUAD) if first_west else (plane >= QUAD)
-        div_x = jnp.where(from_west, cx * (f0 - f_west), cx * (f_east - f0))
-        div_y = cy * (f0 - f_far) if sign > 0 else cy * (f_far - f0)
-        return f0, mov * (sea * ((near - div_x) - div_y))
-
-    sw = to_sublanes(corner_w, 2 * plane_l + 1)
-    se = to_sublanes(corner_e, 2 * plane_l - HALF)
-    ne = to_sublanes(corner_e, 2 * plane_l + HALF)
-    nw = sw
-    cx_s, cy_s, cx_n, cy_n = (subs[:, k : k + 1] * sub_courant for k in range(4))
-    south_flux0, south_flux1 = rows(south_ref[0], south_ref[1], True, sw, se, cx_s, cy_s, 1)
-    north_flux0, north_flux1 = rows(north_ref[0], north_ref[1], False, nw, ne, cx_n, cy_n, -1)
-
-    def add_rows(first, near, next_row, flux0, flux1, cx, cy, first_west):
-        sea0, sea1 = sea_ref[near : near + 1, :], sea_ref[next_row : next_row + 1, :]
-        change = sea0 * (cy * flux0)
-        flux = mov_ref[near : near + 1, :] * change
-        west_flux = jnp.where(wide == 0, 0.0, pltpu.roll(flux, 1, axis=1))
-        east_flux = jnp.where(wide == breadth - 1, 0.0, pltpu.roll(flux, breadth - 1, axis=1))
-        from_west = (plane < QUAD) if first_west else (plane >= QUAD)
-        div_x = jnp.where(from_west, cx * (flux - west_flux), cx * (east_flux - flux))
-        near_change = sea0 * (((change - div_x) - cy * flux) + cy * flux1)
-        next_change = sea1 * (cy * flux)
-        for at, delta in ((near, near_change), (next_row, next_change)):
-            for h in range(breadth // 128):
-                place = pl.ds(first * height + at, HALF + 4, stride=height)
-                halves[h, place, :] = halves[h, place, :] + delta[:, h * 128 : (h + 1) * 128]
-
-    def add_columns(half, near, next_column, flux0, flux1, cx, cy, from_west):
-        sea0, sea1 = sea_ref[:, near : near + 1], sea_ref[:, next_column : next_column + 1]
+    lane_courant = jnp.where(lanes[4:5] > 0.5, courant_ref[1], courant_ref[0])
+
+    def y_change(flux, cy, rim):
+        south_flux = jnp.where(row == 0, rim, pltpu.roll(flux, 1, axis=0))
+        north_flux = jnp.where(row == height - 1, rim, pltpu.roll(flux, height - 1, axis=0))
+        return jnp.where(southern, cy * (flux - south_flux), cy * (north_flux - flux))
+
+    def add_columns(half, message, near, next_column, cx, cy, west):
+        outer, corner = message[:height], message[height : height + 1]
+        outer_mov = jnp.where(odd, outer[:, 2 * HALF + 1 : 2 * HALF + 2], outer[:, 2 * HALF : 2 * HALF + 1])
+        sea_lane = 2 * HALF + (3 if west else 2)
+        flux0 = outer_mov * outer
+        far = pltpu.roll(flux0, 1 if west else 127, axis=1)
+        energy = (outer - cx * (flux0 - far)) - y_change(flux0, cy, corner)
+        flux1 = outer_mov * (outer[:, sea_lane : sea_lane + 1] * energy)
+        at_column = slice(near, near + 1)
+        rim = jnp.where(
+            southern[:1],
+            south_ref[0, HALF : HALF + 1, at_column] * south_ref[0, HALF + 1 : HALF + 2, at_column],
+            north_ref[0, HALF : HALF + 1, at_column] * north_ref[0, HALF + 1 : HALF + 2, at_column],
+        ) * (cx * corner)
+        sea0, sea1 = sea_ref[:, at_column], sea_ref[:, next_column : next_column + 1]
         change = sea0 * (cx * flux0)
-        flux = mov_ref[:, near : near + 1] * change
-        south_flux = jnp.where(row == 0, 0.0, pltpu.roll(flux, 1, axis=0))
-        north_flux = jnp.where(row == height - 1, 0.0, pltpu.roll(flux, height - 1, axis=0))
-        div_y = jnp.where(lane < HALF, cy * (flux - south_flux), cy * (north_flux - flux))
-        near_change = sea0 * (((change - cx * flux) - div_y) + cx * flux1)
+        flux = mov_ref[:, at_column] * change
+        near_change = sea0 * (((change - cx * flux) - y_change(flux, cy, rim)) + cx * flux1)
         next_change = sea1 * (cx * flux)
-        if from_west:
+        if west:
             both = jnp.where(odd, next_change, pltpu.roll(near_change, 127, axis=1))
         else:
             both = jnp.where(odd, pltpu.roll(near_change, 1, axis=1), next_change)
-        edge = lane < 2 if from_west else lane >= 126
+        edge = lane < 2 if west else lane >= 126
         for q in range(HALF):
-            p = q + QUAD if not from_west else (q if q < QUAD else q + HALF)
-            turned = pltpu.roll(both, ((128 if from_west else 126) - 2 * q) % 128, axis=1)
+            p = q + QUAD if not west else (q if q < QUAD else q + HALF)
+            turned = pltpu.roll(both, ((128 if west else 126) - 2 * q) % 128, axis=1)
             place = pl.ds(p * height, height)
             halves[half, place, :] = halves[half, place, :] + jnp.where(edge, turned, 0.0)
-        return jnp.where(lane < 2 * HALF, both, 0.0)
-
-    add_rows(0, 0, 1, south_flux0, south_flux1, cx_s, cy_s, True)
-    add_rows(HALF, height - 1, height - 2, north_flux0, north_flux1, cx_n, -cy_n, False)
-    change_w = add_columns(0, 0, 1, west_flux0, west_flux1, cx_w, cy_w, True)
-    change_e = add_columns(breadth // 128 - 1, breadth - 1, breadth - 2, east_flux0, east_flux1, -cx_e, cy_e, False)
+        both = jnp.where(lane < 2 * HALF, both, 0.0)
+        profile = jnp.dot(
+            both, edge_ref[0 if west else 1], precision=lax.Precision.HIGHEST, preferred_element_type=jnp.float32
+        )
+        for k, column in enumerate((near, next_column)):
+            place = pl.ds(column, height, stride=breadth)
+            table[place, :] = table[place, :] + profile[:, k * 128 : (k + 1) * 128]
+
+    cx_w, cy_w, cx_e, cy_e = (lanes[k : k + 1] * lane_courant for k in range(4))
+    add_columns(0, from_west, 0, 1, cx_w, cy_w, True)
+    add_columns(breadth // 128 - 1, from_east, breadth - 1, breadth - 2, -cx_e, cy_e, False)
     whole = pl.ds(0, PLANES * height)
     writes = [
         pltpu.make_async_copy(halves.at[h, whole, :], out_ref.at[:, pl.ds(h * 128, 128)], out_sems.at[h])
@@ -392,27 +379,19 @@
     for write in writes:
         write.start()
 
-    for change, columns_of, near, next_column in ((change_w, 0, 0, 1), (change_e, 1, breadth - 1, breadth - 2)):
-        profile = jnp.dot(
-            change, edge_ref[columns_of], precision=lax.Precision.HIGHEST, preferred_element_type=jnp.float32
-        )
-        for k, column in enumerate((near, next_column)):
-            place = pl.ds(column, height, stride=breadth)
-            table[place, :] = table[place, :] + profile[:, k * 128 : (k + 1) * 128]
-    for first_row in (0, height - 2):
-        profile_rows(halves, weight_ref[...], table, first_row, 2, height, breadth)
-
     first_half = lax.broadcasted_iota(jnp.int32, (1, 128), 1) < 64
     half = WINDOW // 2
 
     def pick(cell, i):
-        for g in range(WINDOW // 16):
-            for j in range(8):
-                one, two = cell(16 * g + j), cell(16 * g + 8 + j)
+        start = pl.multiple_of(i * half, half)
+        for g in range(WINDOW // 32):
+            for j in range(16):
+                slot = 32 * g + 16 * (j // 8) + j % 8
+                one, two = cell(slot), cell(slot + 8)
                 line = jnp.where(first_half, table[pl.ds(one, 1), :], table[pl.ds(two, 1), :])
-                lines[8 * g + j : 8 * g + j + 1, :] = line
-        here = pl.ds(pl.multiple_of(i * half, half), half)
-        picks[here, :] = lines[...].astype(jnp.bfloat16)
+                lines[16 * g + j : 16 * g + j + 1, :] = line
+            picks[pl.ds(start + 16 * g, 16), :] = lines[16 * g : 16 * g + 16, :].astype(jnp.bfloat16)
+        here = pl.ds(start, half)
         pltpu.make_async_copy(picks.at[here, :], picked_ref.at[here, :], pick_sem).start()
 
     for_windows(cells, window, window_sems, pick)
@@ -436,11 +415,13 @@
             total[pl.ds(pl.multiple_of(i * block, block), block), :] = jnp.zeros((block, 128), jnp.float32)
 
     def add(row, i):
-        lines[...] = values_ref[pl.ds(pl.multiple_of(i * half, half), half), :].astype(jnp.float32)
-        for g in range(WINDOW // 16):
-            for j in range(8):
-                one, two = row(16 * g + j), row(16 * g + 8 + j)
-                line = lines[8 * g + j : 8 * g + j + 1, :]
+        start = pl.multiple_of(i * half, half)
+        for g in range(WINDOW // 32):
+            lines[16 * g : 16 * g + 16, :] = values_ref[pl.ds(start + 16 * g, 16), :].astype(jnp.float32)
+            for j in range(16):
+                slot = 32 * g + 16 * (j // 8) + j % 8
+                one, two = row(slot), row(slot + 8)
+                line = lines[16 * g + j : 16 * g + j + 1, :]
                 left, right = sums[j % n_acc], sums[n_acc + j % n_acc]
                 left[pl.ds(one, 1), :] = left[pl.ds(one, 1), :] + line
                 right[pl.ds(two, 1), :] = right[pl.ds(two, 1), :] + line
@@ -548,28 +529,30 @@
     lists = (devices * slots // 128, 128)
     slot_rows = devices * slots // 2
     slot_rows = devices * slots // 2
+    halves_shape = pltpu.VMEM(halves.shape, f32)
     table_shape = pltpu.VMEM((height * breadth, 128), f32)
-    table, weight, edges = pl.pallas_call(
+    halves, table, edges = pl.pallas_call(
         profile_kernel,
-        out_shape=[table_shape, shape(3 * (PLANES + 8), 128, kind=jnp.bfloat16), shape(2, 128, 256)],
-        in_specs=[vmem] * 2,
+        out_shape=[halves_shape, table_shape, shape(2, 128, 256)],
+        in_specs=[smem] + [vmem] * 7,
         out_specs=[vmem] * 3,
+        input_output_aliases={7: 0},
         scratch_shapes=[pltpu.VMEM((128, 128), f32)],
         compiler_params=params,
         cost_estimate=pl.CostEstimate(flops=2_000_000_000, bytes_accessed=5_000_000, transcendentals=0),
         name="profiles_inside",
-    )(halves, depth_kernel)
+    )(courant, depth_kernel, moving, sea, south, north, subs, halves)
     propagated, picked, *_ = pl.pallas_call(
         finish_kernel,
         out_shape=[
             pltpu.HBM((PLANES * height, breadth), f32),
             pltpu.HBM((slot_rows, 128), jnp.bfloat16),
-            pltpu.VMEM(halves.shape, f32),
+            halves_shape,
             table_shape,
         ],
-        in_specs=[smem] + [vmem] * 13,
+        in_specs=[smem] + [vmem] * 11,
         out_specs=[hbm, hbm, vmem, vmem],
-        input_output_aliases={12: 2, 13: 3},
+        input_output_aliases={10: 2, 11: 3},
         scratch_shapes=[
             pltpu.VMEM(lists, jnp.int32),
             pltpu.VMEM((WINDOW // 2, 128), f32),
@@ -581,7 +564,7 @@
         ],
         compiler_params=params,
         name="finish_and_pick",
-    )(courant, send_rows.reshape(lists), moving, sea, weight, edges, south, north, second, first, lanes, subs, halves, table)
+    )(courant, send_rows.reshape(lists), moving, sea, edges, south, north, second, first, lanes, halves, table)
 
     picked = picked.reshape(devices, slots // 2, 128)
     received = lax.all_to_all(picked, both, split_axis=0, concat_axis=0, tiled=True)

time: 85.8 us -> 87.2 us (1.016)
  Pallas kernels: 35.8 us -> 37.1 us
  transfers between devices with their start and end apart: 4 -> 4, of which waited for: 0 -> 0; matrix products, arithmetic and copies ran while one was open for 0% -> 0% of each run, Pallas kernels for 8% -> 9%
where the time goes in v11:
time: 87.2 us; the launch traced here: 86.9 us
  blocking collectives  38.1 us (44%)
  Pallas kernels  37.1 us (43%)
  starting transfers between devices  10.9 us (12%)
    all_to_all x1, blocking collectives, body(): lax.all_to_all(picked, both, split_axis=0, concat_axis=0, tiled=True)  38.1 us
    pallas_call x1, Pallas kernels, body(): pl.pallas_call(add_kernel, out_shape=pltpu.HBM((components, OUT_DEV), f32...  14.9 us
    pallas_call x1, Pallas kernels, body(): pl.pallas_call(finish_kernel, out_shape=[pltpu.HBM((PLANES * height, brea...  13.1 us
    ppermute x1, starting transfers between devices, body(): second = lax.ppermute(second, 'lon', column_second)  6.29 us
    ppermute x1, starting transfers between devices, body(): second = lax.ppermute(second, both, row_second)  4.51 us
    pallas_call x1, Pallas kernels, body(): pl.pallas_call(inside_kernel, out_shape=[pltpu.VMEM((breadth // 128, (PLA...  4.28 us
    pallas_call x1, Pallas kernels, body(): pl.pallas_call(profile_kernel, out_shape=[halves_shape, table_shape, shap...  3.47 us
  transfers between devices with their start and end apart: 4, of which 0 were waited for; matrix products, arithmetic and copies ran while one was open for 0% of the time, Pallas kernels for 9%

profile of v11, /device:TPU:1, one launch (start us, length us, event | category | flops | bytes accessed | tf_op | source)
XLA Modules:
  0.0 86.9 jit_solution(7969253243311207212)
XLA Ops:
  0.6 1.2 %pack_rows.1 = (bf16[2,48,256]{2,1,0:T(8,128)(2,1)S(1)}, bf16[2,48,256]{2,1,0:T(8,128)(2,1)S(1)}, f32[32,256]{1,0:T(8,128)S(1)}, f32[32,256]{1,0:T(8,128)S(1)}) custom-call(f32[72,32,256]{2,1,0:T(8,128)} %bitcast.9, f32[32,256]{1,0:T(8,128)} %speed_hbm.1, s32[32,256]{1,0:T(8,128)} %mask_hbm.1), custom_call_target="tpu_custom_call" | custom-call | tf_op jit(solution)/shard_map/pack_rows/pallas_call | solution.py:490
  1.9 4.5 %collective-permute-start = (bf16[2,48,256]{2,1,0:T(8,128)(2,1)S(1)}, bf16[2,48,256]{2,1,0:T(8,128)(2,1)S(1)}, u32[]{:S(2)}, u32[]{:S(2)}) collective-permute-start(bf16[2,48,256]{2,1,0:T(8,128)(2,1)S(1)} %get-tuple-element.20), channel_id=1, source_target_pairs={{0,0},{112,127},{16,32},{32,16},{48,64},{64,48},{80,96},{96,80},{1... | collective-permute-start | bytes 147464 | tf_op jit(solution)/shard_map/ppermute | solution.py:501
  6.4 0.1 collective-permute-start.1
  6.5 0.0 copy-start.3
  6.5 0.0 copy-start.4
  6.5 0.0 copy-start.5
  6.5 4.3 %advance_inside.1 = (f32[2,2432,128]{2,1,0:T(8,128)S(1)}, f32[32,128]{1,0:T(8,128)S(1)}, f32[32,128]{1,0:T(8,128)S(1)}) custom-call(f32[2]{0:T(128)} %courant_ref.3, f32[144]{0:T(256)} %constant.6.clone.heading_hbm, f32[72,32,256]{2,1,0:T(8,128)} %bitcast.10, f32[32,256]{1,0:T(8,128)S(1)} %get-tuple-element.18.mov_ref, f32[32,256]{1,0:T(8,128)S(1)} %get-tuple-element.19.sea_ref), custom_call_target="tpu_custom_call" | custom-call | flops 4000000000 | bytes 5000000 | tf_op jit(solution)/shard_map/advance_inside/pallas_call | solution.py:503
  10.8 0.0 collective-permute-done.second_ref
  10.8 0.0 collective-permute-done.1.first_ref
  10.8 0.1 add_corners.1
  11.0 6.3 %collective-permute-start.2 = (f32[40,128]{1,0:T(8,128)S(1)}, f32[40,128]{1,0:T(8,128)S(1)}, u32[]{:S(2)}, u32[]{:S(2)}) collective-permute-start(f32[40,128]{1,0:T(8,128)S(1)} %get-tuple-element.28), channel_id=1, source_target_pairs={{0,15},{1,2},{2,1},{3,4},{4,3},{5,6},{6,5},{7,8},{8,7},{9,10},{10,... | collective-permute-start | bytes 61448 | tf_op jit(solution)/shard_map/ppermute | solution.py:526
  17.2 0.0 collective-permute-start.3
  17.2 0.0 copy-done.3
  17.2 0.0 copy-done.4
  17.3 0.0 copy-done.5
  17.3 0.0 copy-start
  17.3 0.0 copy-start.2
  17.3 3.5 %profiles_inside.1 = (f32[2,2432,128]{2,1,0:T(8,128)S(1)}, f32[8192,128]{1,0:T(8,128)S(1)}, f32[2,128,256]{2,1,0:T(8,128)S(1)}) custom-call(f32[2]{0:T(128)S(1)} %copy-done.3, f32[64,72]{1,0:T(8,128)S(1)} %copy-done.4, f32[32,256]{1,0:T(8,128)S(1)} %get-tuple-element.18.mov_ref, ...), custom_call_target="tpu_custom_call", output_to_operand_aliasing={{0}: (7, {})} | custom-call | flops 2000000000 | bytes 5000000 | tf_op jit(solution)/shard_map/profiles_inside/pallas_call | solution.py:534
  20.8 0.0 collective-permute-done.2.second_ref
  20.8 0.0 collective-permute-done.3.first_ref
  20.8 0.0 copy-done
  20.8 0.0 copy-done.2
  20.8 13.1 %finish_and_pick.1 = (f32[2304,256]{1,0:T(8,128)}, bf16[8192,128]{1,0:T(8,128)(2,1)}, f32[2,2432,128]{2,1,0:T(8,128)S(1)}, f32[8192,128]{1,0:T(8,128)S(1)}) custom-call(f32[2]{0:T(128)S(1)} %copy-done.3, s32[128,128]{1,0:T(8,128)S(1)} %bitcast.7, f32[32,256]{1,0:T(8,128)S(1)} %get-tuple-element.18.mov_ref, ...), custom_call_target="tpu_custom_call", output_to_operand_aliasing={{2}: (10, {}), {3}: (11, {})} | custom-call | tf_op jit(solution)/shard_map/finish_and_pick/pallas_call | solution.py:545
  33.9 0.0 copy-start.1
  34.0 38.1 %all_to_all.5 = bf16[128,64,128]{2,1,0:T(8,128)(2,1)S(1)} all-to-all(bf16[128,64,128]{2,1,0:T(8,128)(2,1)} %bitcast.11), channel_id=1, replica_groups=mesh['lat'=8,'lon'=16] {'lat','lon'}, dimensions={0} | all-to-all | bytes 4194304 | tf_op jit(solution)/shard_map/all_to_all | solution.py:570
  72.0 0.0 copy-done.1
  72.0 14.9 %add_profiles.1 = f32[64,4096]{1,0:T(8,128)} custom-call(s32[128,128]{1,0:T(8,128)S(1)} %bitcast.8, bf16[8192,128]{1,0:T(8,128)(2,1)S(1)} %bitcast.6), custom_call_target="tpu_custom_call" | custom-call | tf_op jit(solution)/shard_map/add_profiles/pallas_call | solution.py:573
Async XLA Ops:
  1.9 8.9 %collective-permute-start = (bf16[2,48,256]{2,1,0:T(8,128)(2,1)S(1)}, bf16[2,48,256]{2,1,0:T(8,128)(2,1)S(1)}, u32[]{:S(2)}, u32[]{:S(2)}) collective-permute-start(bf16[2,48,256]{2,1,0:T(8,128)(2,1)S(1)} %get-tuple-element.20), channel_id=1, source_target_pairs={{0,0},{112,127},{16,32},{32,16},{48,64},{64,48},{80,96},{96,80},{1... | collective-permute-start | bytes 147464 | tf_op jit(solution)/shard_map/ppermute | solution.py:501
  6.4 4.4 %collective-permute-start.1 = (bf16[2,48,256]{2,1,0:T(8,128)(2,1)S(1)}, bf16[2,48,256]{2,1,0:T(8,128)(2,1)S(1)}, u32[]{:S(2)}, u32[]{:S(2)}) collective-permute-start(bf16[2,48,256]{2,1,0:T(8,128)(2,1)S(1)} %get-tuple-element.21), channel_id=1, source_target_pairs={{0,16},{16,0},{32,48},{48,32},{64,80},{80,64},{96,112},{112,96},{1... | collective-permute-start | bytes 147464 | tf_op jit(solution)/shard_map/ppermute | solution.py:502
  6.5 10.8 %copy-start.3 = (f32[2]{0:T(128)S(1)}, f32[2]{0:T(128)}, u32[]{:S(2)}) copy-start(f32[2]{0:T(128)} %courant_ref.3) | copy-start | bytes 28
  6.5 10.8 %copy-start.4 = (f32[64,72]{1,0:T(8,128)S(1)}, f32[64,72]{1,0:T(8,128)}, u32[]{:S(2)}) copy-start(f32[64,72]{1,0:T(8,128)} %kernel_ref.1) | copy-start | bytes 55300
  6.5 10.8 %copy-start.5 = (f32[40,128]{1,0:T(8,128)S(1)}, f32[40,128]{1,0:T(8,128)}, u32[]{:S(2)}) copy-start(f32[40,128]{1,0:T(8,128)} %constant.7.clone.subs_ref) | copy-start | bytes 61444
  11.0 9.8 %collective-permute-start.2 = (f32[40,128]{1,0:T(8,128)S(1)}, f32[40,128]{1,0:T(8,128)S(1)}, u32[]{:S(2)}, u32[]{:S(2)}) collective-permute-start(f32[40,128]{1,0:T(8,128)S(1)} %get-tuple-element.28), channel_id=1, source_target_pairs={{0,15},{1,2},{2,1},{3,4},{4,3},{5,6},{6,5},{7,8},{8,7},{9,10},{10,... | collective-permute-start | bytes 61448 | tf_op jit(solution)/shard_map/ppermute | solution.py:526
  17.2 3.5 %collective-permute-start.3 = (f32[40,128]{1,0:T(8,128)S(1)}, f32[40,128]{1,0:T(8,128)S(1)}, u32[]{:S(2)}, u32[]{:S(2)}) collective-permute-start(f32[40,128]{1,0:T(8,128)S(1)} %get-tuple-element.29), channel_id=1, source_target_pairs={{0,1},{1,0},{2,3},{3,2},{4,5},{5,4},{6,7},{7,6},{8,9},{9,8},{10,11... | collective-permute-start | bytes 61448 | tf_op jit(solution)/shard_map/ppermute | solution.py:527
  17.3 3.5 %copy-start = (s32[1,128,128]{2,1,0:T(8,128)S(1)}, s32[1,128,128]{2,1,0:T(8,128)}, u32[]{:S(2)}) copy-start(s32[1,128,128]{2,1,0:T(8,128)} %param.15) | copy-start | bytes 196612
  17.3 3.5 %copy-start.2 = (f32[8,128]{1,0:T(8,128)S(1)}, f32[8,128]{1,0:T(8,128)}, u32[]{:S(2)}) copy-start(f32[8,128]{1,0:T(8,128)} %constant.8.clone.lanes_ref) | copy-start | bytes 12292
  33.9 38.1 %copy-start.1 = (s32[1,128,128]{2,1,0:T(8,128)S(1)}, s32[1,128,128]{2,1,0:T(8,128)}, u32[]{:S(2)}) copy-start(s32[1,128,128]{2,1,0:T(8,128)} %param.16) | copy-start | bytes 196612

commit v12 on v11

--- a/solution.py
+++ b/solution.py
@@ -16,7 +16,7 @@
 QUAD = PLANES // 4
 OUT_DEV = 4096
 SPARE = 64
-N_ACC = 4
+N_ACC = 5
 ROWS = HALF + 12
 WINDOW = 1024
 VMEM_LIMIT = 16 * 1024 * 1024
@@ -383,15 +383,13 @@
     half = WINDOW // 2
 
     def pick(cell, i):
-        start = pl.multiple_of(i * half, half)
-        for g in range(WINDOW // 32):
-            for j in range(16):
-                slot = 32 * g + 16 * (j // 8) + j % 8
-                one, two = cell(slot), cell(slot + 8)
-                line = jnp.where(first_half, table[pl.ds(one, 1), :], table[pl.ds(two, 1), :])
-                lines[16 * g + j : 16 * g + j + 1, :] = line
-            picks[pl.ds(start + 16 * g, 16), :] = lines[16 * g : 16 * g + 16, :].astype(jnp.bfloat16)
-        here = pl.ds(start, half)
+        for k in range(half):
+            slot = 16 * (k // 8) + k % 8
+            one, two = cell(slot), cell(slot + 8)
+            line = jnp.where(first_half, table[pl.ds(one, 1), :], table[pl.ds(two, 1), :])
+            lines[k : k + 1, :] = line
+        here = pl.ds(pl.multiple_of(i * half, half), half)
+        picks[here, :] = lines[...].astype(jnp.bfloat16)
         pltpu.make_async_copy(picks.at[here, :], picked_ref.at[here, :], pick_sem).start()
 
     for_windows(cells, window, window_sems, pick)
@@ -415,21 +413,19 @@
             total[pl.ds(pl.multiple_of(i * block, block), block), :] = jnp.zeros((block, 128), jnp.float32)
 
     def add(row, i):
-        start = pl.multiple_of(i * half, half)
-        for g in range(WINDOW // 32):
-            lines[16 * g : 16 * g + 16, :] = values_ref[pl.ds(start + 16 * g, 16), :].astype(jnp.float32)
-            for j in range(16):
-                slot = 32 * g + 16 * (j // 8) + j % 8
-                one, two = row(slot), row(slot + 8)
-                line = lines[16 * g + j : 16 * g + j + 1, :]
-                left, right = sums[j % n_acc], sums[n_acc + j % n_acc]
-                left[pl.ds(one, 1), :] = left[pl.ds(one, 1), :] + line
-                right[pl.ds(two, 1), :] = right[pl.ds(two, 1), :] + line
+        lines[...] = values_ref[pl.ds(pl.multiple_of(i * half, half), half), :].astype(jnp.float32)
+        for k in range(half):
+            slot = 16 * (k // 8) + k % 8
+            one, two = row(slot), row(slot + 8)
+            line = lines[k : k + 1, :]
+            left, right = sums[k % n_acc], sums[n_acc + k % n_acc]
+            left[pl.ds(one, 1), :] = left[pl.ds(one, 1), :] + line
+            right[pl.ds(two, 1), :] = right[pl.ds(two, 1), :] + line
 
     for_windows(targets, window, window_sems, add)
     first_half = lax.broadcasted_iota(jnp.int32, (block, 128), 1) < 64
 
-    @pl.loop(0, tile // block)
+    @pl.loop(0, tile // block, unroll=4)
     def _(i):
         here = pl.ds(pl.multiple_of(i * block, block), block)
         left, right = sums[0][here, :], sums[n_acc][here, :]

time: 87.2 us -> 84.5 us (0.969)
  Pallas kernels: 37.1 us -> 34.4 us
    pallas_call x1, Pallas kernels: 13.1 us -> 11.6 us  [body(): pl.pallas_call(finish_kernel, out_shape=[pltpu.HBM((PLANES * height, brea...]
    pallas_call x1, Pallas kernels: 14.9 us -> 13.7 us  [body(): pl.pallas_call(add_kernel, out_shape=pltpu.HBM((components, OUT_DEV), f32...]
where the time goes in v12:
time: 84.5 us; the launch traced here: 84.2 us
  blocking collectives  38.1 us (45%)
  Pallas kernels  34.4 us (41%)
  starting transfers between devices  10.9 us (13%)
    all_to_all x1, blocking collectives, body(): lax.all_to_all(picked, both, split_axis=0, concat_axis=0, tiled=True)  38.1 us
    pallas_call x1, Pallas kernels, body(): pl.pallas_call(add_kernel, out_shape=pltpu.HBM((components, OUT_DEV), f32...  13.7 us
    pallas_call x1, Pallas kernels, body(): pl.pallas_call(finish_kernel, out_shape=[pltpu.HBM((PLANES * height, brea...  11.6 us
    ppermute x1, starting transfers between devices, body(): second = lax.ppermute(second, 'lon', column_second)  6.29 us
    ppermute x1, starting transfers between devices, body(): second = lax.ppermute(second, both, row_second)  4.51 us
    pallas_call x1, Pallas kernels, body(): pl.pallas_call(inside_kernel, out_shape=[pltpu.VMEM((breadth // 128, (PLA...  4.28 us
    pallas_call x1, Pallas kernels, body(): pl.pallas_call(profile_kernel, out_shape=[halves_shape, table_shape, shap...  3.47 us
  transfers between devices with their start and end apart: 4, of which 0 were waited for; matrix products, arithmetic and copies ran while one was open for 0% of the time, Pallas kernels for 9%

profile of v12, /device:TPU:1, one launch (start us, length us, event | category | flops | bytes accessed | tf_op | source)
XLA Modules:
  0.0 84.2 jit_solution(4830934090498714636)
XLA Ops:
  0.6 1.2 %pack_rows.1 = (bf16[2,48,256]{2,1,0:T(8,128)(2,1)S(1)}, bf16[2,48,256]{2,1,0:T(8,128)(2,1)S(1)}, f32[32,256]{1,0:T(8,128)S(1)}, f32[32,256]{1,0:T(8,128)S(1)}) custom-call(f32[72,32,256]{2,1,0:T(8,128)} %bitcast.9, f32[32,256]{1,0:T(8,128)} %speed_hbm.1, s32[32,256]{1,0:T(8,128)} %mask_hbm.1), custom_call_target="tpu_custom_call" | custom-call | tf_op jit(solution)/shard_map/pack_rows/pallas_call | solution.py:486
  1.9 4.5 %collective-permute-start = (bf16[2,48,256]{2,1,0:T(8,128)(2,1)S(1)}, bf16[2,48,256]{2,1,0:T(8,128)(2,1)S(1)}, u32[]{:S(2)}, u32[]{:S(2)}) collective-permute-start(bf16[2,48,256]{2,1,0:T(8,128)(2,1)S(1)} %get-tuple-element.20), channel_id=1, source_target_pairs={{0,0},{112,127},{16,32},{32,16},{48,64},{64,48},{80,96},{96,80},{1... | collective-permute-start | bytes 147464 | tf_op jit(solution)/shard_map/ppermute | solution.py:497
  6.4 0.1 collective-permute-start.1
  6.5 0.0 copy-start.3
  6.5 0.0 copy-start.4
  6.5 0.0 copy-start.5
  6.5 4.3 %advance_inside.1 = (f32[2,2432,128]{2,1,0:T(8,128)S(1)}, f32[32,128]{1,0:T(8,128)S(1)}, f32[32,128]{1,0:T(8,128)S(1)}) custom-call(f32[2]{0:T(128)} %courant_ref.3, f32[144]{0:T(256)} %constant.6.clone.heading_hbm, f32[72,32,256]{2,1,0:T(8,128)} %bitcast.10, f32[32,256]{1,0:T(8,128)S(1)} %get-tuple-element.18.mov_ref, f32[32,256]{1,0:T(8,128)S(1)} %get-tuple-element.19.sea_ref), custom_call_target="tpu_custom_call" | custom-call | flops 4000000000 | bytes 5000000 | tf_op jit(solution)/shard_map/advance_inside/pallas_call | solution.py:499
  10.8 0.0 collective-permute-done.second_ref
  10.8 0.0 collective-permute-done.1.first_ref
  10.8 0.1 add_corners.1
  11.0 6.3 %collective-permute-start.2 = (f32[40,128]{1,0:T(8,128)S(1)}, f32[40,128]{1,0:T(8,128)S(1)}, u32[]{:S(2)}, u32[]{:S(2)}) collective-permute-start(f32[40,128]{1,0:T(8,128)S(1)} %get-tuple-element.28), channel_id=1, source_target_pairs={{0,15},{1,2},{2,1},{3,4},{4,3},{5,6},{6,5},{7,8},{8,7},{9,10},{10,... | collective-permute-start | bytes 61448 | tf_op jit(solution)/shard_map/ppermute | solution.py:522
  17.2 0.0 collective-permute-start.3
  17.2 0.0 copy-done.3
  17.2 0.0 copy-done.4
  17.3 0.0 copy-done.5
  17.3 0.0 copy-start
  17.3 0.0 copy-start.2
  17.3 3.5 %profiles_inside.1 = (f32[2,2432,128]{2,1,0:T(8,128)S(1)}, f32[8192,128]{1,0:T(8,128)S(1)}, f32[2,128,256]{2,1,0:T(8,128)S(1)}) custom-call(f32[2]{0:T(128)S(1)} %copy-done.3, f32[64,72]{1,0:T(8,128)S(1)} %copy-done.4, f32[32,256]{1,0:T(8,128)S(1)} %get-tuple-element.18.mov_ref, ...), custom_call_target="tpu_custom_call", output_to_operand_aliasing={{0}: (7, {})} | custom-call | flops 2000000000 | bytes 5000000 | tf_op jit(solution)/shard_map/profiles_inside/pallas_call | solution.py:530
  20.8 0.0 collective-permute-done.2.second_ref
  20.8 0.0 collective-permute-done.3.first_ref
  20.8 0.0 copy-done
  20.8 0.0 copy-done.2
  20.8 11.6 %finish_and_pick.1 = (f32[2304,256]{1,0:T(8,128)}, bf16[8192,128]{1,0:T(8,128)(2,1)}, f32[2,2432,128]{2,1,0:T(8,128)S(1)}, f32[8192,128]{1,0:T(8,128)S(1)}) custom-call(f32[2]{0:T(128)S(1)} %copy-done.3, s32[128,128]{1,0:T(8,128)S(1)} %bitcast.7, f32[32,256]{1,0:T(8,128)S(1)} %get-tuple-element.18.mov_ref, ...), custom_call_target="tpu_custom_call", output_to_operand_aliasing={{2}: (10, {}), {3}: (11, {})} | custom-call | tf_op jit(solution)/shard_map/finish_and_pick/pallas_call | solution.py:541
  32.4 0.0 copy-start.1
  32.5 38.1 %all_to_all.5 = bf16[128,64,128]{2,1,0:T(8,128)(2,1)S(1)} all-to-all(bf16[128,64,128]{2,1,0:T(8,128)(2,1)} %bitcast.11), channel_id=1, replica_groups=mesh['lat'=8,'lon'=16] {'lat','lon'}, dimensions={0} | all-to-all | bytes 4194304 | tf_op jit(solution)/shard_map/all_to_all | solution.py:566
  70.5 0.0 copy-done.1
  70.5 13.7 %add_profiles.1 = f32[64,4096]{1,0:T(8,128)} custom-call(s32[128,128]{1,0:T(8,128)S(1)} %bitcast.8, bf16[8192,128]{1,0:T(8,128)(2,1)S(1)} %bitcast.6), custom_call_target="tpu_custom_call" | custom-call | tf_op jit(solution)/shard_map/add_profiles/pallas_call | solution.py:569
Async XLA Ops:
  1.9 8.9 %collective-permute-start = (bf16[2,48,256]{2,1,0:T(8,128)(2,1)S(1)}, bf16[2,48,256]{2,1,0:T(8,128)(2,1)S(1)}, u32[]{:S(2)}, u32[]{:S(2)}) collective-permute-start(bf16[2,48,256]{2,1,0:T(8,128)(2,1)S(1)} %get-tuple-element.20), channel_id=1, source_target_pairs={{0,0},{112,127},{16,32},{32,16},{48,64},{64,48},{80,96},{96,80},{1... | collective-permute-start | bytes 147464 | tf_op jit(solution)/shard_map/ppermute | solution.py:497
  6.4 4.4 %collective-permute-start.1 = (bf16[2,48,256]{2,1,0:T(8,128)(2,1)S(1)}, bf16[2,48,256]{2,1,0:T(8,128)(2,1)S(1)}, u32[]{:S(2)}, u32[]{:S(2)}) collective-permute-start(bf16[2,48,256]{2,1,0:T(8,128)(2,1)S(1)} %get-tuple-element.21), channel_id=1, source_target_pairs={{0,16},{16,0},{32,48},{48,32},{64,80},{80,64},{96,112},{112,96},{1... | collective-permute-start | bytes 147464 | tf_op jit(solution)/shard_map/ppermute | solution.py:498
  6.5 10.8 %copy-start.3 = (f32[2]{0:T(128)S(1)}, f32[2]{0:T(128)}, u32[]{:S(2)}) copy-start(f32[2]{0:T(128)} %courant_ref.3) | copy-start | bytes 28
  6.5 10.8 %copy-start.4 = (f32[64,72]{1,0:T(8,128)S(1)}, f32[64,72]{1,0:T(8,128)}, u32[]{:S(2)}) copy-start(f32[64,72]{1,0:T(8,128)} %kernel_ref.1) | copy-start | bytes 55300
  6.5 10.8 %copy-start.5 = (f32[40,128]{1,0:T(8,128)S(1)}, f32[40,128]{1,0:T(8,128)}, u32[]{:S(2)}) copy-start(f32[40,128]{1,0:T(8,128)} %constant.7.clone.subs_ref) | copy-start | bytes 61444
  11.0 9.8 %collective-permute-start.2 = (f32[40,128]{1,0:T(8,128)S(1)}, f32[40,128]{1,0:T(8,128)S(1)}, u32[]{:S(2)}, u32[]{:S(2)}) collective-permute-start(f32[40,128]{1,0:T(8,128)S(1)} %get-tuple-element.28), channel_id=1, source_target_pairs={{0,15},{1,2},{2,1},{3,4},{4,3},{5,6},{6,5},{7,8},{8,7},{9,10},{10,... | collective-permute-start | bytes 61448 | tf_op jit(solution)/shard_map/ppermute | solution.py:522
  17.2 3.5 %collective-permute-start.3 = (f32[40,128]{1,0:T(8,128)S(1)}, f32[40,128]{1,0:T(8,128)S(1)}, u32[]{:S(2)}, u32[]{:S(2)}) collective-permute-start(f32[40,128]{1,0:T(8,128)S(1)} %get-tuple-element.29), channel_id=1, source_target_pairs={{0,1},{1,0},{2,3},{3,2},{4,5},{5,4},{6,7},{7,6},{8,9},{9,8},{10,11... | collective-permute-start | bytes 61448 | tf_op jit(solution)/shard_map/ppermute | solution.py:523
  17.3 3.5 %copy-start = (s32[1,128,128]{2,1,0:T(8,128)S(1)}, s32[1,128,128]{2,1,0:T(8,128)}, u32[]{:S(2)}) copy-start(s32[1,128,128]{2,1,0:T(8,128)} %param.15) | copy-start | bytes 196612
  17.3 3.5 %copy-start.2 = (f32[8,128]{1,0:T(8,128)S(1)}, f32[8,128]{1,0:T(8,128)}, u32[]{:S(2)}) copy-start(f32[8,128]{1,0:T(8,128)} %constant.8.clone.lanes_ref) | copy-start | bytes 12292
  32.4 38.1 %copy-start.1 = (s32[1,128,128]{2,1,0:T(8,128)S(1)}, s32[1,128,128]{2,1,0:T(8,128)}, u32[]{:S(2)}) copy-start(s32[1,128,128]{2,1,0:T(8,128)} %param.16) | copy-start | bytes 196612

commit v13 on v12

--- a/solution.py
+++ b/solution.py
@@ -162,12 +162,13 @@
                   x_ref, courant_ref, heading_ref, sems):
     height, breadth = mov_ref.shape
     small = [
-        pltpu.make_async_copy(courant_hbm, courant_ref, sems.at[4]),
-        pltpu.make_async_copy(heading_hbm, heading_ref, sems.at[5]),
+        pltpu.make_async_copy(courant_hbm, courant_ref, sems.at[5]),
+        pltpu.make_async_copy(heading_hbm, heading_ref, sems.at[6]),
     ]
+    cuts = (0, 6, QUAD, HALF, 3 * QUAD, PLANES)
     parts = [
-        pltpu.make_async_copy(x_hbm.at[planes], x_ref.at[planes], sems.at[k])
-        for k, planes in enumerate(pl.ds(k * QUAD, QUAD) for k in range(4))
+        pltpu.make_async_copy(x_hbm.at[pl.ds(low, high - low)], x_ref.at[pl.ds(low, high - low)], sems.at[k])
+        for k, (low, high) in enumerate(zip(cuts, cuts[1:]))
     ]
     for copy in small + parts:
         copy.start()
@@ -181,22 +182,25 @@
     for h in range(breadth // 128):
         halves[h, PLANES * height :, :] = jnp.zeros((4 * height, 128), jnp.float32)
 
-    def quadrant(first, from_west, from_south):
+    def quadrant(first, count, from_west, from_south):
         def upstream(flux):
+            turned = [pltpu.roll(flux[:, k : k + 128], 1 if from_west else 127, axis=1) for k in range(0, breadth, 128)]
             if from_west:
-                moved = pltpu.roll(flux, 1, axis=1)
-                side = jnp.concatenate([jnp.where(lane == 0, 0.0, moved[:, :128]), moved[:, 128:]], axis=1)
+                sides = [jnp.where(lane == 0, turned[k - 1] if k else 0.0, turned[k]) for k in range(len(turned))]
             else:
-                moved = pltpu.roll(flux, breadth - 1, axis=1)
-                edge = jnp.where(lane == 127, 0.0, moved[:, breadth - 128 :])
-                side = jnp.concatenate([moved[:, : breadth - 128], edge], axis=1)
+                sides = [
+                    jnp.where(lane == 127, turned[k + 1] if k + 1 < len(turned) else 0.0, turned[k])
+                    for k in range(len(turned))
+                ]
+            moved = [pltpu.roll(flux[k : k + 8], 1 if from_south else 7, axis=0) for k in range(0, height, 8)]
             if from_south:
-                moved = pltpu.roll(flux, 1, axis=0)
-                below = jnp.concatenate([jnp.where(row == 0, 0.0, moved[:8]), moved[8:]], axis=0)
+                below = [jnp.where(row == 0, moved[k - 1] if k else 0.0, moved[k]) for k in range(len(moved))]
             else:
-                moved = pltpu.roll(flux, height - 1, axis=0)
-                below = jnp.concatenate([moved[: height - 8], jnp.where(row == 7, 0.0, moved[height - 8 :])], axis=0)
-            return side, below
+                below = [
+                    jnp.where(row == 7, moved[k + 1] if k + 1 < len(moved) else 0.0, moved[k])
+                    for k in range(len(moved))
+                ]
+            return jnp.concatenate(sides, axis=1), jnp.concatenate(below, axis=0)
 
         def step(t, carry):
             p = first + t
@@ -215,11 +219,11 @@
                 halves[h, start, :] = energy[:, h * 128 : (h + 1) * 128]
             return carry
 
-        lax.fori_loop(0, QUAD, step, 0, unroll=6)
-
-    for k, (from_west, from_south) in enumerate(((True, True), (False, True), (False, False), (True, False))):
-        parts[k].wait()
-        quadrant(k * QUAD, from_west, from_south)
+        lax.fori_loop(0, count, step, 0, unroll=6)
+
+    for copy, low, high in zip(parts, cuts, cuts[1:]):
+        copy.wait()
+        quadrant(low, high - low, low // QUAD in (0, 3), low < HALF)
 
     east = jnp.zeros((height, 128), jnp.float32)
     west = jnp.zeros((height, 128), jnp.float32)
@@ -304,18 +308,16 @@
             for k in range(2):
                 lane = 2 * q + (k if side == 0 else 1 - k)
                 edge_ref[side, lane : lane + 1, k * 128 : (k + 1) * 128] = wide_kernel[p : p + 1, :]
-    group = 8
-
-    @pl.loop(0, height // group)
-    def _(r):
-        profile_rows(halves, weight, table, r * group, group, height, breadth)
+
+    profile_rows(halves, weight, table, 0, height, height, breadth)
+    table[height * breadth :, :] = jnp.zeros((8, 128), jnp.float32)
 
 
 def finish_kernel(courant_ref, cells_ref, mov_ref, sea_ref, edge_ref, south_ref, north_ref, second_ref, first_ref,
                   lanes_ref, halves_in, table_in, out_ref, picked_ref, halves, table,
                   cells, lines, picks, window, out_sems, window_sems, pick_sem):
-    cells[...] = jnp.maximum(cells_ref[...], 0)
     height, breadth = mov_ref.shape
+    cells[...] = jnp.where(cells_ref[...] < 0, height * breadth, cells_ref[...])
     even_lon = lax.axis_index("lon") % 2 == 0
     from_west = jnp.where(even_lon, second_ref[...], first_ref[...])
     from_east = jnp.where(even_lon, first_ref[...], second_ref[...])
@@ -383,15 +385,24 @@
     half = WINDOW // 2
 
     def pick(cell, i):
-        for k in range(half):
-            slot = 16 * (k // 8) + k % 8
-            one, two = cell(slot), cell(slot + 8)
-            line = jnp.where(first_half, table[pl.ds(one, 1), :], table[pl.ds(two, 1), :])
-            lines[k : k + 1, :] = line
+        def read(first, count):
+            for k in range(first, first + count):
+                slot = 16 * (k // 8) + k % 8
+                one, two = cell(slot), cell(slot + 8)
+                lines[k : k + 1, :] = jnp.where(first_half, table[pl.ds(one, 1), :], table[pl.ds(two, 1), :])
+
+        for first in range(0, half, 64):
+            read(first, 32)
+
+            @pl.when(cell(2 * first + 64) < height * breadth)
+            def _():
+                read(first + 32, 32)
+
         here = pl.ds(pl.multiple_of(i * half, half), half)
         picks[here, :] = lines[...].astype(jnp.bfloat16)
         pltpu.make_async_copy(picks.at[here, :], picked_ref.at[here, :], pick_sem).start()
 
+    lines[...] = jnp.zeros_like(lines)
     for_windows(cells, window, window_sems, pick)
     pltpu.make_async_copy(picks, picked_ref, pick_sem).wait()
     for write in writes:
@@ -505,7 +516,7 @@
             pltpu.VMEM((PLANES, height, breadth), f32),
             pltpu.SMEM(courant.shape, f32),
             pltpu.SMEM(headings.shape, f32),
-            pltpu.SemaphoreType.DMA((6,)),
+            pltpu.SemaphoreType.DMA((7,)),
         ],
         compiler_params=params,
         cost_estimate=pl.CostEstimate(flops=4_000_000_000, bytes_accessed=5_000_000, transcendentals=0),
@@ -526,7 +537,7 @@
     slot_rows = devices * slots // 2
     slot_rows = devices * slots // 2
     halves_shape = pltpu.VMEM(halves.shape, f32)
-    table_shape = pltpu.VMEM((height * breadth, 128), f32)
+    table_shape = pltpu.VMEM((height * breadth + 8, 128), f32)
     halves, table, edges = pl.pallas_call(
         profile_kernel,
         out_shape=[halves_shape, table_shape, shape(2, 128, 256)],

time: 84.5 us -> 83.1 us (0.983)
  Pallas kernels: 34.4 us -> 33 us
where the time goes in v13:
time: 83.1 us; the launch traced here: 82.8 us
  blocking collectives  38.1 us (46%)
  Pallas kernels  33 us (40%)
  starting transfers between devices  10.9 us (13%)
    all_to_all x1, blocking collectives, body(): lax.all_to_all(picked, both, split_axis=0, concat_axis=0, tiled=True)  38.1 us
    pallas_call x1, Pallas kernels, body(): pl.pallas_call(add_kernel, out_shape=pltpu.HBM((components, OUT_DEV), f32...  13.7 us
    pallas_call x1, Pallas kernels, body(): pl.pallas_call(finish_kernel, out_shape=[pltpu.HBM((PLANES * height, brea...  10.8 us
    ppermute x1, starting transfers between devices, body(): second = lax.ppermute(second, 'lon', column_second)  6.29 us
    ppermute x1, starting transfers between devices, body(): second = lax.ppermute(second, both, row_second)  4.51 us
    pallas_call x1, Pallas kernels, body(): pl.pallas_call(inside_kernel, out_shape=[pltpu.VMEM((breadth // 128, (PLA...  3.91 us
    pallas_call x1, Pallas kernels, body(): pl.pallas_call(profile_kernel, out_shape=[halves_shape, table_shape, shap...  3.19 us
  transfers between devices with their start and end apart: 4, of which 0 were waited for; matrix products, arithmetic and copies ran while one was open for 0% of the time, Pallas kernels for 9%

profile of v13, /device:TPU:1, one launch (start us, length us, event | category | flops | bytes accessed | tf_op | source)
XLA Modules:
  0.0 82.8 jit_solution(13603212192835459259)
XLA Ops:
  0.6 1.2 %pack_rows.1 = (bf16[2,48,256]{2,1,0:T(8,128)(2,1)S(1)}, bf16[2,48,256]{2,1,0:T(8,128)(2,1)S(1)}, f32[32,256]{1,0:T(8,128)S(1)}, f32[32,256]{1,0:T(8,128)S(1)}) custom-call(f32[72,32,256]{2,1,0:T(8,128)} %bitcast.9, f32[32,256]{1,0:T(8,128)} %speed_hbm.1, s32[32,256]{1,0:T(8,128)} %mask_hbm.1), custom_call_target="tpu_custom_call" | custom-call | tf_op jit(solution)/shard_map/pack_rows/pallas_call | solution.py:497
  1.9 4.5 %collective-permute-start = (bf16[2,48,256]{2,1,0:T(8,128)(2,1)S(1)}, bf16[2,48,256]{2,1,0:T(8,128)(2,1)S(1)}, u32[]{:S(2)}, u32[]{:S(2)}) collective-permute-start(bf16[2,48,256]{2,1,0:T(8,128)(2,1)S(1)} %get-tuple-element.20), channel_id=1, source_target_pairs={{0,0},{112,127},{16,32},{32,16},{48,64},{64,48},{80,96},{96,80},{1... | collective-permute-start | bytes 147464 | tf_op jit(solution)/shard_map/ppermute | solution.py:508
  6.4 0.1 collective-permute-start.1
  6.5 0.0 copy-start.3
  6.5 0.0 copy-start.4
  6.5 0.0 copy-start.5
  6.5 3.9 %advance_inside.1 = (f32[2,2432,128]{2,1,0:T(8,128)S(1)}, f32[32,128]{1,0:T(8,128)S(1)}, f32[32,128]{1,0:T(8,128)S(1)}) custom-call(f32[2]{0:T(128)} %courant_ref.3, f32[144]{0:T(256)} %constant.6.clone.heading_hbm, f32[72,32,256]{2,1,0:T(8,128)} %bitcast.10, f32[32,256]{1,0:T(8,128)S(1)} %get-tuple-element.18.mov_ref, f32[32,256]{1,0:T(8,128)S(1)} %get-tuple-element.19.sea_ref), custom_call_target="tpu_custom_call" | custom-call | flops 4000000000 | bytes 5000000 | tf_op jit(solution)/shard_map/advance_inside/pallas_call | solution.py:510
  10.4 0.0 collective-permute-done.second_ref
  10.4 0.0 collective-permute-done.1.first_ref
  10.5 0.1 add_corners.1
  10.6 6.3 %collective-permute-start.2 = (f32[40,128]{1,0:T(8,128)S(1)}, f32[40,128]{1,0:T(8,128)S(1)}, u32[]{:S(2)}, u32[]{:S(2)}) collective-permute-start(f32[40,128]{1,0:T(8,128)S(1)} %get-tuple-element.28), channel_id=1, source_target_pairs={{0,15},{1,2},{2,1},{3,4},{4,3},{5,6},{6,5},{7,8},{8,7},{9,10},{10,... | collective-permute-start | bytes 61448 | tf_op jit(solution)/shard_map/ppermute | solution.py:533
  16.9 0.0 collective-permute-start.3
  16.9 0.0 copy-done.3
  16.9 0.0 copy-done.4
  16.9 0.0 copy-done.5
  16.9 0.0 copy-start.1
  16.9 0.0 copy-start.2
  16.9 3.2 %profiles_inside.1 = (f32[2,2432,128]{2,1,0:T(8,128)S(1)}, f32[8200,128]{1,0:T(8,128)S(1)}, f32[2,128,256]{2,1,0:T(8,128)S(1)}) custom-call(f32[2]{0:T(128)S(1)} %copy-done.3, f32[64,72]{1,0:T(8,128)S(1)} %copy-done.4, f32[32,256]{1,0:T(8,128)S(1)} %get-tuple-element.18.mov_ref, ...), custom_call_target="tpu_custom_call", output_to_operand_aliasing={{0}: (7, {})} | custom-call | flops 2000000000 | bytes 5000000 | tf_op jit(solution)/shard_map/profiles_inside/pallas_call | solution.py:541
  20.1 0.0 collective-permute-done.2.second_ref
  20.1 0.0 collective-permute-done.3.first_ref
  20.1 0.0 copy-done.1
  20.1 0.0 copy-done.2
  20.2 10.8 %finish_and_pick.1 = (f32[2304,256]{1,0:T(8,128)}, bf16[8192,128]{1,0:T(8,128)(2,1)}, f32[2,2432,128]{2,1,0:T(8,128)S(1)}, f32[8200,128]{1,0:T(8,128)S(1)}) custom-call(f32[2]{0:T(128)S(1)} %copy-done.3, s32[128,128]{1,0:T(8,128)S(1)} %bitcast.8, f32[32,256]{1,0:T(8,128)S(1)} %get-tuple-element.18.mov_ref, ...), custom_call_target="tpu_custom_call", output_to_operand_aliasing={{2}: (10, {}), {3}: (11, {})} | custom-call | tf_op jit(solution)/shard_map/finish_and_pick/pallas_call | solution.py:552
  31.0 0.0 copy-start
  31.0 38.1 %all_to_all.5 = bf16[128,64,128]{2,1,0:T(8,128)(2,1)S(1)} all-to-all(bf16[128,64,128]{2,1,0:T(8,128)(2,1)} %bitcast.11), channel_id=1, replica_groups=mesh['lat'=8,'lon'=16] {'lat','lon'}, dimensions={0} | all-to-all | bytes 4194304 | tf_op jit(solution)/shard_map/all_to_all | solution.py:577
  69.1 0.0 copy-done
  69.1 13.7 %add_profiles.1 = f32[64,4096]{1,0:T(8,128)} custom-call(s32[128,128]{1,0:T(8,128)S(1)} %bitcast.7, bf16[8192,128]{1,0:T(8,128)(2,1)S(1)} %bitcast.6), custom_call_target="tpu_custom_call" | custom-call | tf_op jit(solution)/shard_map/add_profiles/pallas_call | solution.py:580
Async XLA Ops:
  1.9 8.6 %collective-permute-start = (bf16[2,48,256]{2,1,0:T(8,128)(2,1)S(1)}, bf16[2,48,256]{2,1,0:T(8,128)(2,1)S(1)}, u32[]{:S(2)}, u32[]{:S(2)}) collective-permute-start(bf16[2,48,256]{2,1,0:T(8,128)(2,1)S(1)} %get-tuple-element.20), channel_id=1, source_target_pairs={{0,0},{112,127},{16,32},{32,16},{48,64},{64,48},{80,96},{96,80},{1... | collective-permute-start | bytes 147464 | tf_op jit(solution)/shard_map/ppermute | solution.py:508
  6.4 4.1 %collective-permute-start.1 = (bf16[2,48,256]{2,1,0:T(8,128)(2,1)S(1)}, bf16[2,48,256]{2,1,0:T(8,128)(2,1)S(1)}, u32[]{:S(2)}, u32[]{:S(2)}) collective-permute-start(bf16[2,48,256]{2,1,0:T(8,128)(2,1)S(1)} %get-tuple-element.21), channel_id=1, source_target_pairs={{0,16},{16,0},{32,48},{48,32},{64,80},{80,64},{96,112},{112,96},{1... | collective-permute-start | bytes 147464 | tf_op jit(solution)/shard_map/ppermute | solution.py:509
  6.5 10.4 %copy-start.3 = (f32[2]{0:T(128)S(1)}, f32[2]{0:T(128)}, u32[]{:S(2)}) copy-start(f32[2]{0:T(128)} %courant_ref.3) | copy-start | bytes 28
  6.5 10.4 %copy-start.4 = (f32[64,72]{1,0:T(8,128)S(1)}, f32[64,72]{1,0:T(8,128)}, u32[]{:S(2)}) copy-start(f32[64,72]{1,0:T(8,128)} %kernel_ref.1) | copy-start | bytes 55300
  6.5 10.4 %copy-start.5 = (f32[40,128]{1,0:T(8,128)S(1)}, f32[40,128]{1,0:T(8,128)}, u32[]{:S(2)}) copy-start(f32[40,128]{1,0:T(8,128)} %constant.7.clone.subs_ref) | copy-start | bytes 61444
  10.6 9.5 %collective-permute-start.2 = (f32[40,128]{1,0:T(8,128)S(1)}, f32[40,128]{1,0:T(8,128)S(1)}, u32[]{:S(2)}, u32[]{:S(2)}) collective-permute-start(f32[40,128]{1,0:T(8,128)S(1)} %get-tuple-element.28), channel_id=1, source_target_pairs={{0,15},{1,2},{2,1},{3,4},{4,3},{5,6},{6,5},{7,8},{8,7},{9,10},{10,... | collective-permute-start | bytes 61448 | tf_op jit(solution)/shard_map/ppermute | solution.py:533
  16.9 3.3 %collective-permute-start.3 = (f32[40,128]{1,0:T(8,128)S(1)}, f32[40,128]{1,0:T(8,128)S(1)}, u32[]{:S(2)}, u32[]{:S(2)}) collective-permute-start(f32[40,128]{1,0:T(8,128)S(1)} %get-tuple-element.29), channel_id=1, source_target_pairs={{0,1},{1,0},{2,3},{3,2},{4,5},{5,4},{6,7},{7,6},{8,9},{9,8},{10,11... | collective-permute-start | bytes 61448 | tf_op jit(solution)/shard_map/ppermute | solution.py:534
  16.9 3.2 %copy-start.1 = (s32[1,128,128]{2,1,0:T(8,128)S(1)}, s32[1,128,128]{2,1,0:T(8,128)}, u32[]{:S(2)}) copy-start(s32[1,128,128]{2,1,0:T(8,128)} %param.15) | copy-start | bytes 196612
  16.9 3.2 %copy-start.2 = (f32[8,128]{1,0:T(8,128)S(1)}, f32[8,128]{1,0:T(8,128)}, u32[]{:S(2)}) copy-start(f32[8,128]{1,0:T(8,128)} %constant.8.clone.lanes_ref) | copy-start | bytes 12292
  31.0 38.2 %copy-start = (s32[1,128,128]{2,1,0:T(8,128)S(1)}, s32[1,128,128]{2,1,0:T(8,128)}, u32[]{:S(2)}) copy-start(s32[1,128,128]{2,1,0:T(8,128)} %param.16) | copy-start | bytes 196612

commit v14 on v13

--- a/solution.py
+++ b/solution.py
@@ -46,8 +46,8 @@
         for k, (source, target) in enumerate((
             (speed_hbm, speed_ref),
             (mask_hbm, mask_ref),
-            (x_hbm.at[pl.ds(0, HALF), pl.ds(height - 8, 8), :], top_rows),
-            (x_hbm.at[pl.ds(HALF, HALF), pl.ds(0, 8), :], bottom_rows),
+            (x_hbm.at[pl.ds(0, HALF), pl.ds(height - 2, 2), :], top_rows.at[:, pl.ds(6, 2), :]),
+            (x_hbm.at[pl.ds(HALF, HALF), pl.ds(0, 2), :], bottom_rows.at[:, pl.ds(0, 2), :]),
         ))
     ]
     for copy in copies:
@@ -60,9 +60,8 @@
     mov_ref[...] = moving
     sea_ref[...] = sea
     for k in range(2):
-        for q in range(HALF):
-            up_ref[k, q : q + 1, :] = top_rows[q, 7 - k : 8 - k, :]
-            down_ref[k, q : q + 1, :] = bottom_rows[q, k : k + 1, :]
+        up_ref[k, :HALF, :] = top_rows[:, 7 - k, :]
+        down_ref[k, :HALF, :] = bottom_rows[:, k, :]
         up_ref[k, HALF : HALF + 1, :] = moving[height - 1 - k : height - k, :]
         down_ref[k, HALF : HALF + 1, :] = moving[k : k + 1, :]
         up_ref[k, HALF + 1 : HALF + 2, :] = sea[height - 1 - k : height - k, :]
@@ -135,27 +134,31 @@
     out_second[height:] = jnp.where(even_lon, west_edge, east_edge)
 
 
+def fetch_window(list_ref, window, sems, i, w):
+    lines = WINDOW // 128
+    source = list_ref.at[pl.ds(pl.multiple_of(i * lines, lines), lines), :]
+    return pltpu.make_async_copy(source, window.at[pl.ds(w * lines, lines), :], sems.at[w])
+
+
+def start_windows(list_ref, window, sems):
+    for w in range(2):
+        fetch_window(list_ref, window, sems, w, w).start()
+
+
 def for_windows(list_ref, window, sems, work):
     lines = WINDOW // 128
     count = list_ref.shape[0] // lines
-
-    def fetch(i, w):
-        source = list_ref.at[pl.ds(pl.multiple_of(i * lines, lines), lines), :]
-        return pltpu.make_async_copy(source, window.at[pl.ds(w * lines, lines), :], sems.at[w])
-
-    for w in range(2):
-        fetch(w, w).start()
 
     @pl.loop(0, count // 2)
     def _(t):
         for w in range(2):
             i = 2 * t + w
-            fetch(i, w).wait()
+            fetch_window(list_ref, window, sems, i, w).wait()
             work(lambda k, start=w * lines: window[start + k // 128, k % 128], i)
 
             @pl.when(i + 2 < count)
             def _():
-                fetch(i + 2, w).start()
+                fetch_window(list_ref, window, sems, i + 2, w).start()
 
 
 def inside_kernel(courant_hbm, heading_hbm, x_hbm, mov_ref, sea_ref, halves, east_ref, west_ref,
@@ -219,7 +222,7 @@
                 halves[h, start, :] = energy[:, h * 128 : (h + 1) * 128]
             return carry
 
-        lax.fori_loop(0, count, step, 0, unroll=6)
+        lax.fori_loop(0, count, step, 0, unroll=9 if count % 9 == 0 else 6)
 
     for copy, low, high in zip(parts, cuts, cuts[1:]):
         copy.wait()
@@ -318,6 +321,7 @@
                   cells, lines, picks, window, out_sems, window_sems, pick_sem):
     height, breadth = mov_ref.shape
     cells[...] = jnp.where(cells_ref[...] < 0, height * breadth, cells_ref[...])
+    start_windows(cells, window, window_sems)
     even_lon = lax.axis_index("lon") % 2 == 0
     from_west = jnp.where(even_lon, second_ref[...], first_ref[...])
     from_east = jnp.where(even_lon, first_ref[...], second_ref[...])
@@ -394,6 +398,8 @@
         for first in range(0, half, 64):
             read(first, 32)
 
+        for first in range(0, half, 64):
+
             @pl.when(cell(2 * first + 64) < height * breadth)
             def _():
                 read(first + 32, 32)
@@ -417,8 +423,9 @@
     slot = lax.broadcasted_iota(jnp.int32, targets.shape, 1)
     spare = tile + (slot // 16 * 8 + slot % 8) % SPARE
     targets[...] = jnp.where(rows_ref[...] < 0, spare, rows_ref[...])
-
-    @pl.loop(0, tile // block)
+    start_windows(targets, window, window_sems)
+
+    @pl.loop(0, tile // block, unroll=2)
     def _(i):
         for total in sums:
             total[pl.ds(pl.multiple_of(i * block, block), block), :] = jnp.zeros((block, 128), jnp.float32)
@@ -436,7 +443,7 @@
     for_windows(targets, window, window_sems, add)
     first_half = lax.broadcasted_iota(jnp.int32, (block, 128), 1) < 64
 
-    @pl.loop(0, tile // block, unroll=4)
+    @pl.loop(0, tile // block, unroll=8)
     def _(i):
         here = pl.ds(pl.multiple_of(i * block, block), block)
         left, right = sums[0][here, :], sums[n_acc][here, :]

time: 83.1 us -> 82.7 us (level)
  no operation moved by 1% of the time
where the time goes in v14:
time: 82.7 us; the launch traced here: 82.5 us
  blocking collectives  38 us (46%)
  Pallas kernels  32.8 us (40%)
  starting transfers between devices  10.9 us (13%)
    all_to_all x1, blocking collectives, body(): lax.all_to_all(picked, both, split_axis=0, concat_axis=0, tiled=True)  38 us
    pallas_call x1, Pallas kernels, body(): pl.pallas_call(add_kernel, out_shape=pltpu.HBM((components, OUT_DEV), f32...  13.2 us
    pallas_call x1, Pallas kernels, body(): pl.pallas_call(finish_kernel, out_shape=[pltpu.HBM((PLANES * height, brea...  11.3 us
    ppermute x1, starting transfers between devices, body(): second = lax.ppermute(second, 'lon', column_second)  6.29 us
    ppermute x1, starting transfers between devices, body(): second = lax.ppermute(second, both, row_second)  4.51 us
    pallas_call x1, Pallas kernels, body(): pl.pallas_call(inside_kernel, out_shape=[pltpu.VMEM((breadth // 128, (PLA...  3.9 us
    pallas_call x1, Pallas kernels, body(): pl.pallas_call(profile_kernel, out_shape=[halves_shape, table_shape, shap...  3.19 us
  transfers between devices with their start and end apart: 4, of which 0 were waited for; matrix products, arithmetic and copies ran while one was open for 0% of the time, Pallas kernels for 9%

profile of v14, /device:TPU:1, one launch (start us, length us, event | category | flops | bytes accessed | tf_op | source)
XLA Modules:
  0.0 82.5 jit_solution(1879300120638310930)
XLA Ops:
  0.6 1.1 %pack_rows.1 = (bf16[2,48,256]{2,1,0:T(8,128)(2,1)S(1)}, bf16[2,48,256]{2,1,0:T(8,128)(2,1)S(1)}, f32[32,256]{1,0:T(8,128)S(1)}, f32[32,256]{1,0:T(8,128)S(1)}) custom-call(f32[72,32,256]{2,1,0:T(8,128)} %bitcast.9, f32[32,256]{1,0:T(8,128)} %speed_hbm.1, s32[32,256]{1,0:T(8,128)} %mask_hbm.1), custom_call_target="tpu_custom_call" | custom-call | tf_op jit(solution)/shard_map/pack_rows/pallas_call | solution.py:504
  1.7 4.5 %collective-permute-start = (bf16[2,48,256]{2,1,0:T(8,128)(2,1)S(1)}, bf16[2,48,256]{2,1,0:T(8,128)(2,1)S(1)}, u32[]{:S(2)}, u32[]{:S(2)}) collective-permute-start(bf16[2,48,256]{2,1,0:T(8,128)(2,1)S(1)} %get-tuple-element.20), channel_id=1, source_target_pairs={{0,0},{112,127},{16,32},{32,16},{48,64},{64,48},{80,96},{96,80},{1... | collective-permute-start | bytes 147464 | tf_op jit(solution)/shard_map/ppermute | solution.py:515
  6.2 0.1 collective-permute-start.1
  6.3 0.0 copy-start.3
  6.3 0.0 copy-start.4
  6.3 0.0 copy-start.5
  6.4 3.9 %advance_inside.1 = (f32[2,2432,128]{2,1,0:T(8,128)S(1)}, f32[32,128]{1,0:T(8,128)S(1)}, f32[32,128]{1,0:T(8,128)S(1)}) custom-call(f32[2]{0:T(128)} %courant_ref.3, f32[144]{0:T(256)} %constant.6.clone.heading_hbm, f32[72,32,256]{2,1,0:T(8,128)} %bitcast.10, f32[32,256]{1,0:T(8,128)S(1)} %get-tuple-element.18.mov_ref, f32[32,256]{1,0:T(8,128)S(1)} %get-tuple-element.19.sea_ref), custom_call_target="tpu_custom_call" | custom-call | flops 4000000000 | bytes 5000000 | tf_op jit(solution)/shard_map/advance_inside/pallas_call | solution.py:517
  10.3 0.0 collective-permute-done.second_ref
  10.3 0.0 collective-permute-done.1.first_ref
  10.3 0.1 add_corners.1
  10.4 6.3 %collective-permute-start.2 = (f32[40,128]{1,0:T(8,128)S(1)}, f32[40,128]{1,0:T(8,128)S(1)}, u32[]{:S(2)}, u32[]{:S(2)}) collective-permute-start(f32[40,128]{1,0:T(8,128)S(1)} %get-tuple-element.28), channel_id=1, source_target_pairs={{0,15},{1,2},{2,1},{3,4},{4,3},{5,6},{6,5},{7,8},{8,7},{9,10},{10,... | collective-permute-start | bytes 61448 | tf_op jit(solution)/shard_map/ppermute | solution.py:540
  16.7 0.0 collective-permute-start.3
  16.7 0.0 copy-done.3
  16.7 0.0 copy-done.4
  16.7 0.0 copy-done.5
  16.7 0.0 copy-start.1
  16.7 0.0 copy-start.2
  16.8 3.2 %profiles_inside.1 = (f32[2,2432,128]{2,1,0:T(8,128)S(1)}, f32[8200,128]{1,0:T(8,128)S(1)}, f32[2,128,256]{2,1,0:T(8,128)S(1)}) custom-call(f32[2]{0:T(128)S(1)} %copy-done.3, f32[64,72]{1,0:T(8,128)S(1)} %copy-done.4, f32[32,256]{1,0:T(8,128)S(1)} %get-tuple-element.18.mov_ref, ...), custom_call_target="tpu_custom_call", output_to_operand_aliasing={{0}: (7, {})} | custom-call | flops 2000000000 | bytes 5000000 | tf_op jit(solution)/shard_map/profiles_inside/pallas_call | solution.py:548
  19.9 0.0 collective-permute-done.2.second_ref
  20.0 0.0 collective-permute-done.3.first_ref
  20.0 0.0 copy-done.1
  20.0 0.0 copy-done.2
  20.0 11.3 %finish_and_pick.1 = (f32[2304,256]{1,0:T(8,128)}, bf16[8192,128]{1,0:T(8,128)(2,1)}, f32[2,2432,128]{2,1,0:T(8,128)S(1)}, f32[8200,128]{1,0:T(8,128)S(1)}) custom-call(f32[2]{0:T(128)S(1)} %copy-done.3, s32[128,128]{1,0:T(8,128)S(1)} %bitcast.8, f32[32,256]{1,0:T(8,128)S(1)} %get-tuple-element.18.mov_ref, ...), custom_call_target="tpu_custom_call", output_to_operand_aliasing={{2}: (10, {}), {3}: (11, {})} | custom-call | tf_op jit(solution)/shard_map/finish_and_pick/pallas_call | solution.py:559
  31.3 0.0 copy-start
  31.3 38.0 %all_to_all.5 = bf16[128,64,128]{2,1,0:T(8,128)(2,1)S(1)} all-to-all(bf16[128,64,128]{2,1,0:T(8,128)(2,1)} %bitcast.11), channel_id=1, replica_groups=mesh['lat'=8,'lon'=16] {'lat','lon'}, dimensions={0} | all-to-all | bytes 4194304 | tf_op jit(solution)/shard_map/all_to_all | solution.py:584
  69.3 0.0 copy-done
  69.3 13.2 %add_profiles.1 = f32[64,4096]{1,0:T(8,128)} custom-call(s32[128,128]{1,0:T(8,128)S(1)} %bitcast.7, bf16[8192,128]{1,0:T(8,128)(2,1)S(1)} %bitcast.6), custom_call_target="tpu_custom_call" | custom-call | tf_op jit(solution)/shard_map/add_profiles/pallas_call | solution.py:587
Async XLA Ops:
  1.7 8.6 %collective-permute-start = (bf16[2,48,256]{2,1,0:T(8,128)(2,1)S(1)}, bf16[2,48,256]{2,1,0:T(8,128)(2,1)S(1)}, u32[]{:S(2)}, u32[]{:S(2)}) collective-permute-start(bf16[2,48,256]{2,1,0:T(8,128)(2,1)S(1)} %get-tuple-element.20), channel_id=1, source_target_pairs={{0,0},{112,127},{16,32},{32,16},{48,64},{64,48},{80,96},{96,80},{1... | collective-permute-start | bytes 147464 | tf_op jit(solution)/shard_map/ppermute | solution.py:515
  6.2 4.1 %collective-permute-start.1 = (bf16[2,48,256]{2,1,0:T(8,128)(2,1)S(1)}, bf16[2,48,256]{2,1,0:T(8,128)(2,1)S(1)}, u32[]{:S(2)}, u32[]{:S(2)}) collective-permute-start(bf16[2,48,256]{2,1,0:T(8,128)(2,1)S(1)} %get-tuple-element.21), channel_id=1, source_target_pairs={{0,16},{16,0},{32,48},{48,32},{64,80},{80,64},{96,112},{112,96},{1... | collective-permute-start | bytes 147464 | tf_op jit(solution)/shard_map/ppermute | solution.py:516
  6.3 10.4 %copy-start.3 = (f32[2]{0:T(128)S(1)}, f32[2]{0:T(128)}, u32[]{:S(2)}) copy-start(f32[2]{0:T(128)} %courant_ref.3) | copy-start | bytes 28
  6.3 10.4 %copy-start.4 = (f32[64,72]{1,0:T(8,128)S(1)}, f32[64,72]{1,0:T(8,128)}, u32[]{:S(2)}) copy-start(f32[64,72]{1,0:T(8,128)} %kernel_ref.1) | copy-start | bytes 55300
  6.3 10.4 %copy-start.5 = (f32[40,128]{1,0:T(8,128)S(1)}, f32[40,128]{1,0:T(8,128)}, u32[]{:S(2)}) copy-start(f32[40,128]{1,0:T(8,128)} %constant.7.clone.subs_ref) | copy-start | bytes 61444
  10.4 9.5 %collective-permute-start.2 = (f32[40,128]{1,0:T(8,128)S(1)}, f32[40,128]{1,0:T(8,128)S(1)}, u32[]{:S(2)}, u32[]{:S(2)}) collective-permute-start(f32[40,128]{1,0:T(8,128)S(1)} %get-tuple-element.28), channel_id=1, source_target_pairs={{0,15},{1,2},{2,1},{3,4},{4,3},{5,6},{6,5},{7,8},{8,7},{9,10},{10,... | collective-permute-start | bytes 61448 | tf_op jit(solution)/shard_map/ppermute | solution.py:540
  16.7 3.3 %collective-permute-start.3 = (f32[40,128]{1,0:T(8,128)S(1)}, f32[40,128]{1,0:T(8,128)S(1)}, u32[]{:S(2)}, u32[]{:S(2)}) collective-permute-start(f32[40,128]{1,0:T(8,128)S(1)} %get-tuple-element.29), channel_id=1, source_target_pairs={{0,1},{1,0},{2,3},{3,2},{4,5},{5,4},{6,7},{7,6},{8,9},{9,8},{10,11... | collective-permute-start | bytes 61448 | tf_op jit(solution)/shard_map/ppermute | solution.py:541
  16.7 3.2 %copy-start.1 = (s32[1,128,128]{2,1,0:T(8,128)S(1)}, s32[1,128,128]{2,1,0:T(8,128)}, u32[]{:S(2)}) copy-start(s32[1,128,128]{2,1,0:T(8,128)} %param.15) | copy-start | bytes 196612
  16.7 3.2 %copy-start.2 = (f32[8,128]{1,0:T(8,128)S(1)}, f32[8,128]{1,0:T(8,128)}, u32[]{:S(2)}) copy-start(f32[8,128]{1,0:T(8,128)} %constant.8.clone.lanes_ref) | copy-start | bytes 12292
  31.3 38.0 %copy-start = (s32[1,128,128]{2,1,0:T(8,128)S(1)}, s32[1,128,128]{2,1,0:T(8,128)}, u32[]{:S(2)}) copy-start(s32[1,128,128]{2,1,0:T(8,128)} %param.16) | copy-start | bytes 196612

commit v15 on v14

--- a/solution.py
+++ b/solution.py
@@ -397,8 +397,6 @@
 
         for first in range(0, half, 64):
             read(first, 32)
-
-        for first in range(0, half, 64):
 
             @pl.when(cell(2 * first + 64) < height * breadth)
             def _():

time: 82.7 us -> 82.4 us (level)
  no operation moved by 1% of the time
where the time goes in v15:
time: 82.4 us; the launch traced here: 82.1 us
  blocking collectives  37.9 us (46%)
  Pallas kernels  32.5 us (39%)
  starting transfers between devices  10.9 us (13%)
    all_to_all x1, blocking collectives, body(): lax.all_to_all(picked, both, split_axis=0, concat_axis=0, tiled=True)  37.9 us
    pallas_call x1, Pallas kernels, body(): pl.pallas_call(add_kernel, out_shape=pltpu.HBM((components, OUT_DEV), f32...  13.2 us
    pallas_call x1, Pallas kernels, body(): pl.pallas_call(finish_kernel, out_shape=[pltpu.HBM((PLANES * height, brea...  11 us
    ppermute x1, starting transfers between devices, body(): second = lax.ppermute(second, 'lon', column_second)  6.29 us
    ppermute x1, starting transfers between devices, body(): second = lax.ppermute(second, both, row_second)  4.51 us
    pallas_call x1, Pallas kernels, body(): pl.pallas_call(inside_kernel, out_shape=[pltpu.VMEM((breadth // 128, (PLA...  3.9 us
    pallas_call x1, Pallas kernels, body(): pl.pallas_call(profile_kernel, out_shape=[halves_shape, table_shape, shap...  3.19 us
  transfers between devices with their start and end apart: 4, of which 0 were waited for; matrix products, arithmetic and copies ran while one was open for 0% of the time, Pallas kernels for 9%

profile of v15, /device:TPU:1, one launch (start us, length us, event | category | flops | bytes accessed | tf_op | source)
XLA Modules:
  0.0 82.1 jit_solution(4774879034208527589)
XLA Ops:
  0.6 1.1 %pack_rows.1 = (bf16[2,48,256]{2,1,0:T(8,128)(2,1)S(1)}, bf16[2,48,256]{2,1,0:T(8,128)(2,1)S(1)}, f32[32,256]{1,0:T(8,128)S(1)}, f32[32,256]{1,0:T(8,128)S(1)}) custom-call(f32[72,32,256]{2,1,0:T(8,128)} %bitcast.9, f32[32,256]{1,0:T(8,128)} %speed_hbm.1, s32[32,256]{1,0:T(8,128)} %mask_hbm.1), custom_call_target="tpu_custom_call" | custom-call | tf_op jit(solution)/shard_map/pack_rows/pallas_call | solution.py:502
  1.7 4.5 %collective-permute-start = (bf16[2,48,256]{2,1,0:T(8,128)(2,1)S(1)}, bf16[2,48,256]{2,1,0:T(8,128)(2,1)S(1)}, u32[]{:S(2)}, u32[]{:S(2)}) collective-permute-start(bf16[2,48,256]{2,1,0:T(8,128)(2,1)S(1)} %get-tuple-element.20), channel_id=1, source_target_pairs={{0,0},{112,127},{16,32},{32,16},{48,64},{64,48},{80,96},{96,80},{1... | collective-permute-start | bytes 147464 | tf_op jit(solution)/shard_map/ppermute | solution.py:513
  6.2 0.1 collective-permute-start.1
  6.3 0.0 copy-start.3
  6.3 0.0 copy-start.4
  6.3 0.0 copy-start.5
  6.4 3.9 %advance_inside.1 = (f32[2,2432,128]{2,1,0:T(8,128)S(1)}, f32[32,128]{1,0:T(8,128)S(1)}, f32[32,128]{1,0:T(8,128)S(1)}) custom-call(f32[2]{0:T(128)} %courant_ref.3, f32[144]{0:T(256)} %constant.6.clone.heading_hbm, f32[72,32,256]{2,1,0:T(8,128)} %bitcast.10, f32[32,256]{1,0:T(8,128)S(1)} %get-tuple-element.18.mov_ref, f32[32,256]{1,0:T(8,128)S(1)} %get-tuple-element.19.sea_ref), custom_call_target="tpu_custom_call" | custom-call | flops 4000000000 | bytes 5000000 | tf_op jit(solution)/shard_map/advance_inside/pallas_call | solution.py:515
  10.3 0.0 collective-permute-done.second_ref
  10.3 0.0 collective-permute-done.1.first_ref
  10.3 0.1 add_corners.1
  10.4 6.3 %collective-permute-start.2 = (f32[40,128]{1,0:T(8,128)S(1)}, f32[40,128]{1,0:T(8,128)S(1)}, u32[]{:S(2)}, u32[]{:S(2)}) collective-permute-start(f32[40,128]{1,0:T(8,128)S(1)} %get-tuple-element.28), channel_id=1, source_target_pairs={{0,15},{1,2},{2,1},{3,4},{4,3},{5,6},{6,5},{7,8},{8,7},{9,10},{10,... | collective-permute-start | bytes 61448 | tf_op jit(solution)/shard_map/ppermute | solution.py:538
  16.7 0.0 collective-permute-start.3
  16.7 0.0 copy-done.3
  16.7 0.0 copy-done.4
  16.7 0.0 copy-done.5
  16.7 0.0 copy-start.1
  16.7 0.0 copy-start.2
  16.8 3.2 %profiles_inside.1 = (f32[2,2432,128]{2,1,0:T(8,128)S(1)}, f32[8200,128]{1,0:T(8,128)S(1)}, f32[2,128,256]{2,1,0:T(8,128)S(1)}) custom-call(f32[2]{0:T(128)S(1)} %copy-done.3, f32[64,72]{1,0:T(8,128)S(1)} %copy-done.4, f32[32,256]{1,0:T(8,128)S(1)} %get-tuple-element.18.mov_ref, ...), custom_call_target="tpu_custom_call", output_to_operand_aliasing={{0}: (7, {})} | custom-call | flops 2000000000 | bytes 5000000 | tf_op jit(solution)/shard_map/profiles_inside/pallas_call | solution.py:546
  19.9 0.0 collective-permute-done.2.second_ref
  20.0 0.0 collective-permute-done.3.first_ref
  20.0 0.0 copy-done.1
  20.0 0.0 copy-done.2
  20.0 11.0 %finish_and_pick.1 = (f32[2304,256]{1,0:T(8,128)}, bf16[8192,128]{1,0:T(8,128)(2,1)}, f32[2,2432,128]{2,1,0:T(8,128)S(1)}, f32[8200,128]{1,0:T(8,128)S(1)}) custom-call(f32[2]{0:T(128)S(1)} %copy-done.3, s32[128,128]{1,0:T(8,128)S(1)} %bitcast.8, f32[32,256]{1,0:T(8,128)S(1)} %get-tuple-element.18.mov_ref, ...), custom_call_target="tpu_custom_call", output_to_operand_aliasing={{2}: (10, {}), {3}: (11, {})} | custom-call | tf_op jit(solution)/shard_map/finish_and_pick/pallas_call | solution.py:557
  31.0 0.0 copy-start
  31.0 37.9 %all_to_all.5 = bf16[128,64,128]{2,1,0:T(8,128)(2,1)S(1)} all-to-all(bf16[128,64,128]{2,1,0:T(8,128)(2,1)} %bitcast.11), channel_id=1, replica_groups=mesh['lat'=8,'lon'=16] {'lat','lon'}, dimensions={0} | all-to-all | bytes 4194304 | tf_op jit(solution)/shard_map/all_to_all | solution.py:582
  69.0 0.0 copy-done
  69.0 13.2 %add_profiles.1 = f32[64,4096]{1,0:T(8,128)} custom-call(s32[128,128]{1,0:T(8,128)S(1)} %bitcast.7, bf16[8192,128]{1,0:T(8,128)(2,1)S(1)} %bitcast.6), custom_call_target="tpu_custom_call" | custom-call | tf_op jit(solution)/shard_map/add_profiles/pallas_call | solution.py:585
Async XLA Ops:
  1.7 8.6 %collective-permute-start = (bf16[2,48,256]{2,1,0:T(8,128)(2,1)S(1)}, bf16[2,48,256]{2,1,0:T(8,128)(2,1)S(1)}, u32[]{:S(2)}, u32[]{:S(2)}) collective-permute-start(bf16[2,48,256]{2,1,0:T(8,128)(2,1)S(1)} %get-tuple-element.20), channel_id=1, source_target_pairs={{0,0},{112,127},{16,32},{32,16},{48,64},{64,48},{80,96},{96,80},{1... | collective-permute-start | bytes 147464 | tf_op jit(solution)/shard_map/ppermute | solution.py:513
  6.2 4.1 %collective-permute-start.1 = (bf16[2,48,256]{2,1,0:T(8,128)(2,1)S(1)}, bf16[2,48,256]{2,1,0:T(8,128)(2,1)S(1)}, u32[]{:S(2)}, u32[]{:S(2)}) collective-permute-start(bf16[2,48,256]{2,1,0:T(8,128)(2,1)S(1)} %get-tuple-element.21), channel_id=1, source_target_pairs={{0,16},{16,0},{32,48},{48,32},{64,80},{80,64},{96,112},{112,96},{1... | collective-permute-start | bytes 147464 | tf_op jit(solution)/shard_map/ppermute | solution.py:514
  6.3 10.4 %copy-start.3 = (f32[2]{0:T(128)S(1)}, f32[2]{0:T(128)}, u32[]{:S(2)}) copy-start(f32[2]{0:T(128)} %courant_ref.3) | copy-start | bytes 28
  6.3 10.4 %copy-start.4 = (f32[64,72]{1,0:T(8,128)S(1)}, f32[64,72]{1,0:T(8,128)}, u32[]{:S(2)}) copy-start(f32[64,72]{1,0:T(8,128)} %kernel_ref.1) | copy-start | bytes 55300
  6.3 10.4 %copy-start.5 = (f32[40,128]{1,0:T(8,128)S(1)}, f32[40,128]{1,0:T(8,128)}, u32[]{:S(2)}) copy-start(f32[40,128]{1,0:T(8,128)} %constant.7.clone.subs_ref) | copy-start | bytes 61444
  10.4 9.5 %collective-permute-start.2 = (f32[40,128]{1,0:T(8,128)S(1)}, f32[40,128]{1,0:T(8,128)S(1)}, u32[]{:S(2)}, u32[]{:S(2)}) collective-permute-start(f32[40,128]{1,0:T(8,128)S(1)} %get-tuple-element.28), channel_id=1, source_target_pairs={{0,15},{1,2},{2,1},{3,4},{4,3},{5,6},{6,5},{7,8},{8,7},{9,10},{10,... | collective-permute-start | bytes 61448 | tf_op jit(solution)/shard_map/ppermute | solution.py:538
  16.7 3.3 %collective-permute-start.3 = (f32[40,128]{1,0:T(8,128)S(1)}, f32[40,128]{1,0:T(8,128)S(1)}, u32[]{:S(2)}, u32[]{:S(2)}) collective-permute-start(f32[40,128]{1,0:T(8,128)S(1)} %get-tuple-element.29), channel_id=1, source_target_pairs={{0,1},{1,0},{2,3},{3,2},{4,5},{5,4},{6,7},{7,6},{8,9},{9,8},{10,11... | collective-permute-start | bytes 61448 | tf_op jit(solution)/shard_map/ppermute | solution.py:539
  16.7 3.2 %copy-start.1 = (s32[1,128,128]{2,1,0:T(8,128)S(1)}, s32[1,128,128]{2,1,0:T(8,128)}, u32[]{:S(2)}) copy-start(s32[1,128,128]{2,1,0:T(8,128)} %param.15) | copy-start | bytes 196612
  16.7 3.2 %copy-start.2 = (f32[8,128]{1,0:T(8,128)S(1)}, f32[8,128]{1,0:T(8,128)}, u32[]{:S(2)}) copy-start(f32[8,128]{1,0:T(8,128)} %constant.8.clone.lanes_ref) | copy-start | bytes 12292
  31.0 37.9 %copy-start = (s32[1,128,128]{2,1,0:T(8,128)S(1)}, s32[1,128,128]{2,1,0:T(8,128)}, u32[]{:S(2)}) copy-start(s32[1,128,128]{2,1,0:T(8,128)} %param.16) | copy-start | bytes 196612

commit v16 on v15

--- a/solution.py
+++ b/solution.py
@@ -183,7 +183,7 @@
     lane = lax.broadcasted_iota(jnp.int32, (height, 128), 1)
     row = lax.broadcasted_iota(jnp.int32, (8, breadth), 0)
     for h in range(breadth // 128):
-        halves[h, PLANES * height :, :] = jnp.zeros((4 * height, 128), jnp.float32)
+        halves[h, PLANES * height :, :] = jnp.zeros((5 * height, 128), jnp.float32)
 
     def quadrant(first, count, from_west, from_south):
         def upstream(flux):
@@ -313,7 +313,7 @@
                 edge_ref[side, lane : lane + 1, k * 128 : (k + 1) * 128] = wide_kernel[p : p + 1, :]
 
     profile_rows(halves, weight, table, 0, height, height, breadth)
-    table[height * breadth :, :] = jnp.zeros((8, 128), jnp.float32)
+    table[height * breadth :, :] = jnp.zeros((breadth, 128), jnp.float32)
 
 
 def finish_kernel(courant_ref, cells_ref, mov_ref, sea_ref, edge_ref, south_ref, north_ref, second_ref, first_ref,
@@ -514,7 +514,7 @@
     first = lax.ppermute(first, "lat", row_first)
     halves, east, west = pl.pallas_call(
         inside_kernel,
-        out_shape=[pltpu.VMEM((breadth // 128, (PLANES + 4) * height, 128), f32)] + [columns] * 2,
+        out_shape=[pltpu.VMEM((breadth // 128, (PLANES + 5) * height, 128), f32)] + [columns] * 2,
         in_specs=[hbm] * 3 + [vmem] * 2,
         out_specs=[vmem] * 3,
         scratch_shapes=[
@@ -542,7 +542,7 @@
     slot_rows = devices * slots // 2
     slot_rows = devices * slots // 2
     halves_shape = pltpu.VMEM(halves.shape, f32)
-    table_shape = pltpu.VMEM((height * breadth + 8, 128), f32)
+    table_shape = pltpu.VMEM((height * breadth + breadth, 128), f32)
     halves, table, edges = pl.pallas_call(
         profile_kernel,
         out_shape=[halves_shape, table_shape, shape(2, 128, 256)],
@@ -595,7 +595,7 @@
             pltpu.SemaphoreType.DMA((2,)),
             pltpu.SemaphoreType.DMA,
         ]
-        + [pltpu.VMEM((OUT_DEV + SPARE, 128), f32)] * (2 * N_ACC),
+        + [pltpu.VMEM((OUT_DEV + SPARE + 8, 128), f32)] * (2 * N_ACC),
         compiler_params=pltpu.CompilerParams(vmem_limit_bytes=ADD_VMEM_LIMIT),
         name="add_profiles",
     )(recv_rows.reshape(lists), received.reshape(slot_rows, 128))

time: 82.4 us -> 82.6 us (level)
  no operation moved by 1% of the time
where the time goes in v16:
time: 82.6 us; the launch traced here: 82.2 us
  blocking collectives  38 us (46%)
  Pallas kernels  32.5 us (39%)
  starting transfers between devices  10.9 us (13%)
    all_to_all x1, blocking collectives, body(): lax.all_to_all(picked, both, split_axis=0, concat_axis=0, tiled=True)  38 us
    pallas_call x1, Pallas kernels, body(): pl.pallas_call(add_kernel, out_shape=pltpu.HBM((components, OUT_DEV), f32...  13.2 us
    pallas_call x1, Pallas kernels, body(): pl.pallas_call(finish_kernel, out_shape=[pltpu.HBM((PLANES * height, brea...  11 us
    ppermute x1, starting transfers between devices, body(): second = lax.ppermute(second, 'lon', column_second)  6.29 us
    ppermute x1, starting transfers between devices, body(): second = lax.ppermute(second, both, row_second)  4.51 us
    pallas_call x1, Pallas kernels, body(): pl.pallas_call(inside_kernel, out_shape=[pltpu.VMEM((breadth // 128, (PLA...  3.9 us
    pallas_call x1, Pallas kernels, body(): pl.pallas_call(profile_kernel, out_shape=[halves_shape, table_shape, shap...  3.2 us
  transfers between devices with their start and end apart: 4, of which 0 were waited for; matrix products, arithmetic and copies ran while one was open for 0% of the time, Pallas kernels for 9%

profile of v16, /device:TPU:1, one launch (start us, length us, event | category | flops | bytes accessed | tf_op | source)
XLA Modules:
  0.0 82.2 jit_solution(4928962473581740752)
XLA Ops:
  0.6 1.1 %pack_rows.1 = (bf16[2,48,256]{2,1,0:T(8,128)(2,1)S(1)}, bf16[2,48,256]{2,1,0:T(8,128)(2,1)S(1)}, f32[32,256]{1,0:T(8,128)S(1)}, f32[32,256]{1,0:T(8,128)S(1)}) custom-call(f32[72,32,256]{2,1,0:T(8,128)} %bitcast.9, f32[32,256]{1,0:T(8,128)} %speed_hbm.1, s32[32,256]{1,0:T(8,128)} %mask_hbm.1), custom_call_target="tpu_custom_call" | custom-call | tf_op jit(solution)/shard_map/pack_rows/pallas_call | solution.py:502
  1.7 4.5 %collective-permute-start = (bf16[2,48,256]{2,1,0:T(8,128)(2,1)S(1)}, bf16[2,48,256]{2,1,0:T(8,128)(2,1)S(1)}, u32[]{:S(2)}, u32[]{:S(2)}) collective-permute-start(bf16[2,48,256]{2,1,0:T(8,128)(2,1)S(1)} %get-tuple-element.20), channel_id=1, source_target_pairs={{0,0},{112,127},{16,32},{32,16},{48,64},{64,48},{80,96},{96,80},{1... | collective-permute-start | bytes 147464 | tf_op jit(solution)/shard_map/ppermute | solution.py:513
  6.2 0.1 collective-permute-start.1
  6.3 0.0 copy-start.3
  6.3 0.0 copy-start.4
  6.3 0.0 copy-start.5
  6.4 3.9 %advance_inside.1 = (f32[2,2464,128]{2,1,0:T(8,128)S(1)}, f32[32,128]{1,0:T(8,128)S(1)}, f32[32,128]{1,0:T(8,128)S(1)}) custom-call(f32[2]{0:T(128)} %courant_ref.3, f32[144]{0:T(256)} %constant.6.clone.heading_hbm, f32[72,32,256]{2,1,0:T(8,128)} %bitcast.10, f32[32,256]{1,0:T(8,128)S(1)} %get-tuple-element.18.mov_ref, f32[32,256]{1,0:T(8,128)S(1)} %get-tuple-element.19.sea_ref), custom_call_target="tpu_custom_call" | custom-call | flops 4000000000 | bytes 5000000 | tf_op jit(solution)/shard_map/advance_inside/pallas_call | solution.py:515
  10.3 0.0 collective-permute-done.second_ref
  10.3 0.0 collective-permute-done.1.first_ref
  10.3 0.1 add_corners.1
  10.4 6.3 %collective-permute-start.2 = (f32[40,128]{1,0:T(8,128)S(1)}, f32[40,128]{1,0:T(8,128)S(1)}, u32[]{:S(2)}, u32[]{:S(2)}) collective-permute-start(f32[40,128]{1,0:T(8,128)S(1)} %get-tuple-element.28), channel_id=1, source_target_pairs={{0,15},{1,2},{2,1},{3,4},{4,3},{5,6},{6,5},{7,8},{8,7},{9,10},{10,... | collective-permute-start | bytes 61448 | tf_op jit(solution)/shard_map/ppermute | solution.py:538
  16.7 0.0 collective-permute-start.3
  16.7 0.0 copy-done.3
  16.7 0.0 copy-done.4
  16.7 0.0 copy-done.5
  16.7 0.0 copy-start
  16.7 0.0 copy-start.2
  16.8 3.2 %profiles_inside.1 = (f32[2,2464,128]{2,1,0:T(8,128)S(1)}, f32[8448,128]{1,0:T(8,128)S(1)}, f32[2,128,256]{2,1,0:T(8,128)S(1)}) custom-call(f32[2]{0:T(128)S(1)} %copy-done.3, f32[64,72]{1,0:T(8,128)S(1)} %copy-done.4, f32[32,256]{1,0:T(8,128)S(1)} %get-tuple-element.18.mov_ref, ...), custom_call_target="tpu_custom_call", output_to_operand_aliasing={{0}: (7, {})} | custom-call | flops 2000000000 | bytes 5000000 | tf_op jit(solution)/shard_map/profiles_inside/pallas_call | solution.py:546
  20.0 0.0 collective-permute-done.2.second_ref
  20.0 0.0 collective-permute-done.3.first_ref
  20.0 0.0 copy-done
  20.0 0.0 copy-done.2
  20.0 11.0 %finish_and_pick.1 = (f32[2304,256]{1,0:T(8,128)}, bf16[8192,128]{1,0:T(8,128)(2,1)}, f32[2,2464,128]{2,1,0:T(8,128)S(1)}, f32[8448,128]{1,0:T(8,128)S(1)}) custom-call(f32[2]{0:T(128)S(1)} %copy-done.3, s32[128,128]{1,0:T(8,128)S(1)} %bitcast.7, f32[32,256]{1,0:T(8,128)S(1)} %get-tuple-element.18.mov_ref, ...), custom_call_target="tpu_custom_call", output_to_operand_aliasing={{2}: (10, {}), {3}: (11, {})} | custom-call | tf_op jit(solution)/shard_map/finish_and_pick/pallas_call | solution.py:557
  31.1 0.0 copy-start.1
  31.1 38.0 %all_to_all.5 = bf16[128,64,128]{2,1,0:T(8,128)(2,1)S(1)} all-to-all(bf16[128,64,128]{2,1,0:T(8,128)(2,1)} %bitcast.11), channel_id=1, replica_groups=mesh['lat'=8,'lon'=16] {'lat','lon'}, dimensions={0} | all-to-all | bytes 4194304 | tf_op jit(solution)/shard_map/all_to_all | solution.py:582
  69.0 0.0 copy-done.1
  69.0 13.2 %add_profiles.1 = f32[64,4096]{1,0:T(8,128)} custom-call(s32[128,128]{1,0:T(8,128)S(1)} %bitcast.8, bf16[8192,128]{1,0:T(8,128)(2,1)S(1)} %bitcast.6), custom_call_target="tpu_custom_call" | custom-call | tf_op jit(solution)/shard_map/add_profiles/pallas_call | solution.py:585
Async XLA Ops:
  1.7 8.6 %collective-permute-start = (bf16[2,48,256]{2,1,0:T(8,128)(2,1)S(1)}, bf16[2,48,256]{2,1,0:T(8,128)(2,1)S(1)}, u32[]{:S(2)}, u32[]{:S(2)}) collective-permute-start(bf16[2,48,256]{2,1,0:T(8,128)(2,1)S(1)} %get-tuple-element.20), channel_id=1, source_target_pairs={{0,0},{112,127},{16,32},{32,16},{48,64},{64,48},{80,96},{96,80},{1... | collective-permute-start | bytes 147464 | tf_op jit(solution)/shard_map/ppermute | solution.py:513
  6.2 4.1 %collective-permute-start.1 = (bf16[2,48,256]{2,1,0:T(8,128)(2,1)S(1)}, bf16[2,48,256]{2,1,0:T(8,128)(2,1)S(1)}, u32[]{:S(2)}, u32[]{:S(2)}) collective-permute-start(bf16[2,48,256]{2,1,0:T(8,128)(2,1)S(1)} %get-tuple-element.21), channel_id=1, source_target_pairs={{0,16},{16,0},{32,48},{48,32},{64,80},{80,64},{96,112},{112,96},{1... | collective-permute-start | bytes 147464 | tf_op jit(solution)/shard_map/ppermute | solution.py:514
  6.3 10.4 %copy-start.3 = (f32[2]{0:T(128)S(1)}, f32[2]{0:T(128)}, u32[]{:S(2)}) copy-start(f32[2]{0:T(128)} %courant_ref.3) | copy-start | bytes 28
  6.3 10.4 %copy-start.4 = (f32[64,72]{1,0:T(8,128)S(1)}, f32[64,72]{1,0:T(8,128)}, u32[]{:S(2)}) copy-start(f32[64,72]{1,0:T(8,128)} %kernel_ref.1) | copy-start | bytes 55300
  6.3 10.4 %copy-start.5 = (f32[40,128]{1,0:T(8,128)S(1)}, f32[40,128]{1,0:T(8,128)}, u32[]{:S(2)}) copy-start(f32[40,128]{1,0:T(8,128)} %constant.7.clone.subs_ref) | copy-start | bytes 61444
  10.4 9.5 %collective-permute-start.2 = (f32[40,128]{1,0:T(8,128)S(1)}, f32[40,128]{1,0:T(8,128)S(1)}, u32[]{:S(2)}, u32[]{:S(2)}) collective-permute-start(f32[40,128]{1,0:T(8,128)S(1)} %get-tuple-element.28), channel_id=1, source_target_pairs={{0,15},{1,2},{2,1},{3,4},{4,3},{5,6},{6,5},{7,8},{8,7},{9,10},{10,... | collective-permute-start | bytes 61448 | tf_op jit(solution)/shard_map/ppermute | solution.py:538
  16.7 3.3 %collective-permute-start.3 = (f32[40,128]{1,0:T(8,128)S(1)}, f32[40,128]{1,0:T(8,128)S(1)}, u32[]{:S(2)}, u32[]{:S(2)}) collective-permute-start(f32[40,128]{1,0:T(8,128)S(1)} %get-tuple-element.29), channel_id=1, source_target_pairs={{0,1},{1,0},{2,3},{3,2},{4,5},{5,4},{6,7},{7,6},{8,9},{9,8},{10,11... | collective-permute-start | bytes 61448 | tf_op jit(solution)/shard_map/ppermute | solution.py:539
  16.7 3.3 %copy-start = (s32[1,128,128]{2,1,0:T(8,128)S(1)}, s32[1,128,128]{2,1,0:T(8,128)}, u32[]{:S(2)}) copy-start(s32[1,128,128]{2,1,0:T(8,128)} %param.15) | copy-start | bytes 196612
  16.7 3.3 %copy-start.2 = (f32[8,128]{1,0:T(8,128)S(1)}, f32[8,128]{1,0:T(8,128)}, u32[]{:S(2)}) copy-start(f32[8,128]{1,0:T(8,128)} %constant.8.clone.lanes_ref) | copy-start | bytes 12292
  31.1 38.0 %copy-start.1 = (s32[1,128,128]{2,1,0:T(8,128)S(1)}, s32[1,128,128]{2,1,0:T(8,128)}, u32[]{:S(2)}) copy-start(s32[1,128,128]{2,1,0:T(8,128)} %param.16) | copy-start | bytes 196612
